TPU v7x, 32 devices: a whole 2x2x4 slice. The times are simulated.
32 devices in a mesh: rep: 8 (over y, x, core), tp: 4 (over z).
Axes of the slice: x: 2, y: 2, z: 4, core: 2. Of those that a mesh axis runs over, the one named last changes fastest.
Arguments:
- queries: bfloat16 [104, 48, 4096], P('rep', None, 'tp'), may hold values from -33 to 33
- tree_cache: bfloat16 [104, 2, 48, 4096], P('rep', None, None, 'tp'), may hold values from -11 to 11
- tree_mask: int32 [104, 48, 48], P('rep'), may hold values from 0 to 1, as said below
- dest_group: int32 [104, 1], P('rep'), may hold values from 0 to 7; in each aligned block of 13 rows (0 to 12, 13 to 25, ...) at most 2 rows name the same one
- accepted_path: int32 [104, 8], P('rep'), may hold values from 0 to 47
- prompt_cache: bfloat16 [8, 2, 152, 4096], P('rep', None, None, 'tp'), may hold values from -11 to 11
- first_len: int32 [8], P('rep'), may hold values from 2 to 152
- spill_cache: bfloat16 [8, 2, 152, 4096], P('rep', None, None, 'tp'), may hold values from -6 to 6
- spill_len: int32 [8], P('rep'), may hold values from 76 to 152
- out_weight: bfloat16 [4096, 4096], P(None, 'tp'), may hold values from -0.09375 to 0.09375
Outputs:
- projected: bfloat16 [104, 48, 4096], P('rep', None, 'tp')
- accepted_cache: bfloat16 [104, 2, 8, 4096], P('rep', None, None, 'tp')
Inputs may be any that keep to these rules, and one draw needn't show every extreme that they name: `dest_group`: in each aligned block of 13 requests (those of one index of rep) no group is named more than 2 times. Row t of tree_mask[r] marks token t and its ancestors in a tree whose parents come before their children.
All inputs are finite; a program needn't handle non-finite values.
Results may differ from a plain program's by a relative error of at most 0.014.
Values may be sent and summed in bfloat16 or wider, within the bound.
No kernel may reach another device: no remote copies, remote signals or barrier semaphores. Data moves between devices by JAX's collectives and lax.ppermute only.
A program may use at most 128 MiB of HBM per device.

v0:
```python
import math

import jax
import jax.numpy as jnp
from jax import lax
from jax.sharding import PartitionSpec as P

HD = 128
TREE = 48
PCAP = 152


NEG_FILL = -1e30


def swapped(value, axis, apart):
    mask = 2**apart
    pairs = [(source, source ^ mask) for source in range(lax.axis_size(axis))]
    return lax.ppermute(value, axis, pairs)


def attend_part(query_rows, key_rows, value_rows, visible, head_size):
    heads_here = query_rows.shape[2] // head_size
    maxima = []
    totals = []
    partial_sums = []
    for head_index in range(heads_here):
        lower = head_index * head_size
        upper = lower + head_size
        scores = lax.dot_general(
            query_rows[:, :, lower:upper],
            key_rows[:, :, lower:upper],
            (((2,), (2,)), ((0,), (0,))),
            preferred_element_type=jnp.float32,
        ) * (1.0 / math.sqrt(head_size))
        scores = jnp.where(visible, scores, NEG_FILL)
        peaks = jnp.max(scores, axis=2)
        raw_weights = jnp.where(visible, jnp.exp(scores - peaks[:, :, None]), 0.0)
        maxima.append(peaks)
        totals.append(jnp.sum(raw_weights, axis=2))
        partial_sums.append(
            lax.dot_general(
                raw_weights.astype(jnp.bfloat16),
                value_rows[:, :, lower:upper],
                (((2,), (1,)), ((0,), (0,))),
                preferred_element_type=jnp.float32,
            )
        )
    return (
        jnp.stack(maxima, axis=-1),
        jnp.stack(totals, axis=-1),
        jnp.concatenate(partial_sums, axis=-1),
    )


def combine_parts(first_part, second_part, head_size):
    max_first, total_first, accum_first = first_part
    max_second, total_second, accum_second = second_part
    peaks = jnp.maximum(max_first, max_second)
    factor_first = jnp.exp(max_first - peaks)
    factor_second = jnp.exp(max_second - peaks)
    totals = total_first * factor_first + total_second * factor_second
    full_shape = accum_first.shape
    split_shape = full_shape[:-1] + (full_shape[-1] // head_size, head_size)
    accum = (
        accum_first.reshape(split_shape) * factor_first[..., None]
        + accum_second.reshape(split_shape) * factor_second[..., None]
    )
    return (peaks, totals, accum.reshape(full_shape))


def local(
    queries,
    tree_cache,
    tree_mask,
    dest_group,
    accepted_path,
    prompt_cache,
    first_len,
    spill_cache,
    spill_len,
    out_weight,
):
    req_here = queries.shape[0]
    local_cols = queries.shape[2]
    heads_here = local_cols // HD
    groups = lax.axis_size("rep")
    per_group = max(2, (req_here + groups - 1) // groups)
    n_slots = groups * per_group
    target = dest_group[:, 0]
    same_target = target[:, None] == target[None, :]
    earlier = jnp.arange(req_here)[None, :] < jnp.arange(req_here)[:, None]
    rank_index = jnp.sum(jnp.logical_and(same_target, earlier), axis=1)
    slot_index = target * per_group + rank_index
    selector = (jnp.arange(n_slots, dtype=jnp.int32)[:, None] == slot_index[None, :]).astype(
        jnp.bfloat16
    )
    outbound = jnp.einsum(
        "sr,rtc->stc", selector, queries, preferred_element_type=jnp.float32
    ).astype(jnp.bfloat16)
    outbound = outbound.reshape(groups, per_group, TREE, local_cols)
    inbound = lax.all_to_all(outbound, "rep", split_axis=0, concat_axis=0, tiled=True)
    routed_rows = inbound.reshape(1, n_slots * TREE, local_cols)
    positions = jnp.arange(PCAP, dtype=jnp.int32)
    prompt_seen = (positions < first_len[0])[None, None, :]
    prompt_part = attend_part(routed_rows, prompt_cache[:, 0], prompt_cache[:, 1], prompt_seen, HD)
    partner_rows = swapped(routed_rows, "rep", 0)
    spill_seen = (positions < spill_len[0])[None, None, :]
    spill_max, spill_total, spill_accum = attend_part(
        partner_rows, spill_cache[:, 0], spill_cache[:, 1], spill_seen, HD
    )
    spill_part = (
        swapped(spill_max.astype(jnp.bfloat16), "rep", 0).astype(spill_max.dtype),
        swapped(spill_total.astype(jnp.bfloat16), "rep", 0).astype(spill_total.dtype),
        swapped(spill_accum.astype(jnp.bfloat16), "rep", 0).astype(spill_accum.dtype),
    )
    merged_max, merged_total, merged_accum = combine_parts(prompt_part, spill_part, HD)
    back_max, back_total, back_accum = (
        lax.all_to_all(
            merged_max.reshape(groups, per_group, TREE, heads_here),
            "rep",
            split_axis=0,
            concat_axis=0,
            tiled=True,
        ),
        lax.all_to_all(
            merged_total.reshape(groups, per_group, TREE, heads_here),
            "rep",
            split_axis=0,
            concat_axis=0,
            tiled=True,
        ),
        lax.all_to_all(
            merged_accum.reshape(groups, per_group, TREE, local_cols),
            "rep",
            split_axis=0,
            concat_axis=0,
            tiled=True,
        ),
    )
    remote_part = (
        jnp.take(back_max.reshape(n_slots, TREE, heads_here), slot_index, axis=0),
        jnp.take(back_total.reshape(n_slots, TREE, heads_here), slot_index, axis=0),
        jnp.take(back_accum.reshape(n_slots, TREE, local_cols), slot_index, axis=0),
    )
    tree_seen = tree_mask == 1
    tree_part = attend_part(queries, tree_cache[:, 0], tree_cache[:, 1], tree_seen, HD)
    final_max, final_total, final_accum = combine_parts(remote_part, tree_part, HD)
    attn = final_accum.reshape(req_here, TREE, heads_here, HD) / final_total[..., None]
    attn = attn.reshape(req_here * TREE, local_cols).astype(jnp.bfloat16)
    summed = jnp.dot(
        lax.all_gather(attn, "tp", axis=1, tiled=True),
        out_weight,
        preferred_element_type=jnp.float32,
    )
    projected = summed.astype(jnp.bfloat16).reshape(req_here, TREE, out_weight.shape[1])
    accepted_cache = jnp.take_along_axis(tree_cache, accepted_path[:, None, :, None], axis=2)
    return (projected, accepted_cache)


def solution(mesh):
    return jax.shard_map(
        local,
        mesh=mesh,
        in_specs=(
            P("rep", None, "tp"),
            P("rep", None, None, "tp"),
            P("rep", None, None),
            P("rep", None),
            P("rep", None),
            P("rep", None, None, "tp"),
            P("rep"),
            P("rep", None, None, "tp"),
            P("rep"),
            P(None, "tp"),
        ),
        out_specs=(P("rep", None, "tp"), P("rep", None, None, "tp")),
        check_vma=False,
    )
```

profile of v0, /device:TPU:0, one launch (start us, length us, event | category | flops | bytes accessed | tf_op | source)
XLA Modules:
  0.0 307.1 jit_solution(11455234567655455256)
XLA Ops:
  9.3 2.4 convolution_convert_fusion
  11.7 2.0 copy.118
  13.7 5.4 %all-to-all-start = ((bf16[8,2,48,1024]{3,2,1,0:T(8,128)(2,1)}), bf16[8,2,48,1024]{3,2,1,0:T(8,128)(2,1)}, u32[]{:S(2)}, u32[]{:S(2)}) async-start(bf16[8,2,48,1024]{3,2,1,0:T(8,128)(2,1)} %bitcast.387), calls=%async_computation | async-start | bytes 3145728 | tf_op jit(solution)/shard_map/all_to_all | solution.py:102
  19.3 1.4 slice_bitcast_fusion
  26.6 1.4 fusion.122
  28.1 12.2 %all-to-all-done = bf16[8,2,48,1024]{3,2,1,0:T(8,128)(2,1)} async-done(((bf16[8,2,48,1024]{3,2,1,0:T(8,128)(2,1)}), bf16[8,2,48,1024]{3,2,1,0:T(8,128)(2,1)}, u32[]{:S(2)}, u32[]{:S(2)}) %all-to-all-start) | async-done | bytes 1572896 | tf_op jit(solution)/shard_map/all_to_all | solution.py:102
  41.5 1.3 fusion.201
  44.0 1.3 fusion.203
  45.3 1.3 fusion.204
  47.9 1.2 fusion.206
  49.2 1.3 fusion.207
  50.5 2.3 fusion.58
  55.9 2.0 convolution_dynamic-update-slice_fusion.7
  57.9 2.0 convolution_dynamic-update-slice_fusion.6
  59.9 1.8 convolution_dynamic-update-slice_fusion.5
  61.8 1.3 fusion.208
  63.1 1.8 fusion.28
  66.2 1.8 fusion.30
  69.3 1.8 fusion.32
  72.3 1.8 fusion.34
  75.4 1.8 fusion.36
  78.5 1.8 fusion.38
  81.6 1.8 fusion.40
  84.7 1.8 fusion.42
  87.0 1.8 convolution_dynamic-update-slice_fusion.4
  90.0 1.9 copy.77
  93.0 1.9 convolution_dynamic-update-slice_fusion.3
  95.0 2.0 convolution_dynamic-update-slice_fusion.2
  97.2 2.3 fusion.74
  100.6 1.8 convolution_dynamic-update-slice_fusion.1
  104.1 3.3 %all-to-all-start.2 = ((f32[8,1,768]{2,1,0:T(1,128)}), f32[8,1,768]{2,1,0:T(1,128)S(1)}, u32[]{:S(2)}, u32[]{:S(2)}) async-start(f32[8,1,768]{2,1,0:T(1,128)} %reshape.1099), calls=%async_computation.2 | async-start | bytes 49152 | tf_op jit(solution)/shard_map/all_to_all | solution.py:119
  107.5 1.8 convolution_dynamic-update-slice_fusion
  109.4 2.2 mul.182
  111.6 4.6 %mul.183 = f32[8,2,48,1024]{3,2,1,0:T(8,128)} reshape(f32[768,8,128]{2,1,0:T(8,128)} %mul.182) | data formatting | bytes 6291456 | tf_op jit(solution)/shard_map/mul | solution.py:66
  116.3 2.2 mul.186
  118.5 4.6 %mul.187 = f32[8,2,48,1024]{3,2,1,0:T(8,128)} reshape(f32[768,8,128]{2,1,0:T(8,128)} %mul.186) | data formatting | bytes 6291456 | tf_op jit(solution)/shard_map/mul | solution.py:67
  124.1 3.1 %copy.81 = f32[1,768,1024]{2,1,0:T(8,128)} copy(bf16[1,768,1024]{1,2,0:T(8,128)(2,1)} %collective-permute-done.2) | data formatting | bytes 4718592 | tf_op jit(solution)/shard_map/reshape | solution.py:67
  127.2 4.1 %all-to-all-start.3 = ((f32[8,1,768]{2,1,0:T(1,128)}), f32[8,1,768]{2,1,0:T(1,128)S(1)}, u32[]{:S(2)}, u32[]{:S(2)}) async-start(f32[8,1,768]{2,1,0:T(1,128)} %reshape.1101), calls=%async_computation.3 | async-start | bytes 49152 | tf_op jit(solution)/shard_map/all_to_all | solution.py:126
  131.3 8.2 %multiply_add_fusion = f32[8,2,48,1024]{3,2,1,0:T(8,128)} fusion(f32[8,2,48,1024]{3,2,1,0:T(8,128)} %bitcast.383, f32[8,2,48,1024]{3,2,1,0:T(8,128)} %mul.187, f32[8,2,48,1024]{3,2,1,0:T(8,128)} %convolution_dynamic-update-slice_fusion, f32[8,2,48,1024]{3,2,1,0:T(8,128)} %mul.183), kind=kLoop, calls=%fused_computation.4 | loop fusion | flops 2359296 | bytes 15728640 | tf_op jit(solution)/shard_map/add | solution.py:66
  139.5 4.6 %all-to-all-start.1 = ((f32[8,2,48,1024]{3,2,1,0:T(8,128)}), f32[8,2,48,1024]{3,2,1,0:T(8,128)}, u32[]{:S(2)}, u32[]{:S(2)}) async-start(f32[8,2,48,1024]{3,2,1,0:T(8,128)} %multiply_add_fusion), calls=%async_computation.1 | async-start | bytes 6291456 | tf_op jit(solution)/shard_map/all_to_all | solution.py:133
  152.3 2.1 convolution_dynamic-update-slice_fusion.15
  154.4 2.1 convolution_dynamic-update-slice_fusion.14
  167.9 14.1 %all-to-all-done.1 = f32[8,2,48,1024]{3,2,1,0:T(8,128)} async-done(((f32[8,2,48,1024]{3,2,1,0:T(8,128)}), f32[8,2,48,1024]{3,2,1,0:T(8,128)}, u32[]{:S(2)}, u32[]{:S(2)}) %all-to-all-start.1) | async-done | bytes 3145760 | tf_op jit(solution)/shard_map/all_to_all | solution.py:133
  182.0 4.1 %gather_fusion = f32[13,48,1024]{2,1,0:T(8,128)} fusion(f32[16,48,1024]{2,1,0:T(8,128)} %bitcast.95, s32[1024]{0:T(1024)S(1)} %pad_clamp_fusion.1), kind=kCustom, calls=%fused_computation.2 | custom fusion | bytes 5111860 | tf_op jit(solution)/shard_map/jit(_take)/gather | solution.py:144
  189.2 4.8 %fusion = bf16[624,1024]{1,0:T(8,128)(2,1)} fusion(f32[78,8,8,128]{3,2,1,0:T(8,128)S(1)} %bitcast.386, f32[78,8,8,128]{3,2,1,0:T(8,128)S(1)} %bitcast.385, f32[78,8,8,128]{3,2,1,0:T(8,128)S(1)} %bitcast.384, f32[13,48,1024]{2,1,0:T(8,128)} %convolution_dynamic-update-slice_fusion.8, f32[13,48,1024]{2,1,0:T(8,128)S(1)} %copy-done.1, ...), kind=kLoop, calls=%fused_computation.6 | loop fusion | flops 3833856 | bytes 14058096 | tf_op jit(solution)/shard_map/convert_element_type | solution.py:150
  194.3 2.7 gather_fusion.1
  198.0 92.1 %all-gather.2.cloned.1.call-done = bf16[624,4096]{1,0:T(8,128)(2,1)} async-done(((bf16[624,1024]{1,0:T(8,128)(2,1)}), bf16[624,4096]{1,0:T(8,128)(2,1)}) %all-gather.2.cloned.1.call-update) | async-done | bytes 5111824 | tf_op jit(solution)/shard_map/all_gather | solution.py:152
  290.1 10.2 %convolution_convert_fusion.1 = bf16[624,1024]{1,0:T(8,128)(2,1)} fusion(bf16[624,4096]{1,0:T(8,128)(2,1)} %all-gather.2.cloned.1.call-done, bf16[4096,1024]{1,0:T(8,128)(2,1)} %param.21), kind=kOutput, calls=%fused_computation.12 | convolution fusion | flops 5235130368 | bytes 14778368 | tf_op jit(solution)/shard_map/dot_general | solution.py:151
  (303 shorter events, 52.6 us)
Async XLA Ops:
  13.7 5.4 %copy-start.32 = (s32[13,48,48]{2,1,0:T(8,128)S(1)}, s32[13,48,48]{2,1,0:T(8,128)}, u32[]{:S(2)}) copy-start(s32[13,48,48]{2,1,0:T(8,128)} %param.14) | copy-start | bytes 359428
  13.7 5.6 %copy-start = (bf16[13,2,48,1024]{3,2,1,0:T(8,128)(2,1)S(1)}, bf16[13,2,48,1024]{3,2,1,0:T(8,128)(2,1)}, u32[]{:S(2)}) copy-start(bf16[13,2,48,1024]{3,2,1,0:T(8,128)(2,1)} %param.13) | copy-start | bytes 7667716
  13.7 26.6 %all-to-all-start = ((bf16[8,2,48,1024]{3,2,1,0:T(8,128)(2,1)}), bf16[8,2,48,1024]{3,2,1,0:T(8,128)(2,1)}, u32[]{:S(2)}, u32[]{:S(2)}) async-start(bf16[8,2,48,1024]{3,2,1,0:T(8,128)(2,1)} %bitcast.387), calls=%async_computation | async-start | bytes 3145728 | tf_op jit(solution)/shard_map/all_to_all | solution.py:102
  21.0 5.6 %copy-start.14 = (f32[13,48,48]{1,2,0:T(8,128)}, f32[13,48,48]{1,2,0:T(8,128)S(1)}, u32[]{:S(2)}) copy-start(f32[13,48,48]{1,2,0:T(8,128)S(1)} %get-tuple-element.103) | copy-start | bytes 359428
  21.2 5.3 %copy-start.15 = (f32[13,48,48]{1,2,0:T(8,128)}, f32[13,48,48]{1,2,0:T(8,128)S(1)}, u32[]{:S(2)}) copy-start(f32[13,48,48]{1,2,0:T(8,128)S(1)} %get-tuple-element.101) | copy-start | bytes 359428
  21.5 5.1 %copy-start.12 = (f32[13,48,48]{1,2,0:T(8,128)}, f32[13,48,48]{1,2,0:T(8,128)S(1)}, u32[]{:S(2)}) copy-start(f32[13,48,48]{1,2,0:T(8,128)S(1)} %get-tuple-element.99) | copy-start | bytes 359428
  44.0 6.4 %copy-start.35 = (f32[768]{0:T(1024)}, f32[768]{0:T(1024)S(1)}, u32[]{:S(2)}) copy-start(f32[768]{0:T(1024)S(1)} %get-tuple-element.60) | copy-start | bytes 9220
  45.3 7.4 %copy-start.37 = (f32[768]{0:T(1024)}, f32[768]{0:T(1024)S(1)}, u32[]{:S(2)}) copy-start(f32[768]{0:T(1024)S(1)} %get-tuple-element.62) | copy-start | bytes 9220
  46.6 6.2 %copy-start.39 = (f32[768]{0:T(1024)}, f32[768]{0:T(1024)S(1)}, u32[]{:S(2)}) copy-start(f32[768]{0:T(1024)S(1)} %get-tuple-element.64) | copy-start | bytes 9220
  47.8 4.9 %copy-start.41 = (f32[768]{0:T(1024)}, f32[768]{0:T(1024)S(1)}, u32[]{:S(2)}) copy-start(f32[768]{0:T(1024)S(1)} %get-tuple-element.66) | copy-start | bytes 9220
  47.8 13.9 %collective-permute-start = (bf16[1,768,1024]{2,1,0:T(8,128)(2,1)}, bf16[1,768,1024]{2,1,0:T(8,128)(2,1)}, u32[]{:S(2)}, u32[]{:S(2)}) collective-permute-start(bf16[1,768,1024]{2,1,0:T(8,128)(2,1)} %bitcast.6), channel_id=1, source_target_pairs={{0,4},{4,0},{8,12},{12,8},{16,20},{20,16},{24,28},{28,24},{1,5},{5... | collective-permute-start | bytes 4718600 | tf_op jit(solution)/shard_map/ppermute | solution.py:19
  55.9 7.2 %copy-start.76 = (pred[152]{0:T(512)(128)(4,1)S(1)}, pred[152]{0:T(512)(128)(4,1)}, u32[]{:S(2)}) copy-start(pred[152]{0:T(512)(128)(4,1)} %iota_compare_fusion.2) | copy-start | bytes 460
  63.0 6.2 %copy-start.21 = (f32[768,152]{0,1:T(8,128)}, f32[768,152]{0,1:T(8,128)S(1)}, u32[]{:S(2)}) copy-start(f32[768,152]{0,1:T(8,128)S(1)} %get-tuple-element.73) | copy-start | bytes 1400836
  63.1 6.2 %copy-start.55 = (f32[768]{0:T(1024)}, f32[768]{0:T(1024)S(1)}, u32[]{:S(2)}) copy-start(f32[768]{0:T(1024)S(1)} %get-tuple-element.72) | copy-start | bytes 9220
  66.1 8.0 %copy-start.23 = (f32[768,152]{0,1:T(8,128)}, f32[768,152]{0,1:T(8,128)S(1)}, u32[]{:S(2)}) copy-start(f32[768,152]{0,1:T(8,128)S(1)} %get-tuple-element.75) | copy-start | bytes 1400836
  66.1 8.0 %copy-start.57 = (f32[768]{0:T(1024)}, f32[768]{0:T(1024)S(1)}, u32[]{:S(2)}) copy-start(f32[768]{0:T(1024)S(1)} %get-tuple-element.74) | copy-start | bytes 9220
  69.2 8.0 %copy-start.25 = (f32[768,152]{0,1:T(8,128)}, f32[768,152]{0,1:T(8,128)S(1)}, u32[]{:S(2)}) copy-start(f32[768,152]{0,1:T(8,128)S(1)} %get-tuple-element.77) | copy-start | bytes 1400836
  69.2 8.0 %copy-start.59 = (f32[768]{0:T(1024)}, f32[768]{0:T(1024)S(1)}, u32[]{:S(2)}) copy-start(f32[768]{0:T(1024)S(1)} %get-tuple-element.76) | copy-start | bytes 9220
  72.3 8.0 %copy-start.27 = (f32[768,152]{0,1:T(8,128)}, f32[768,152]{0,1:T(8,128)S(1)}, u32[]{:S(2)}) copy-start(f32[768,152]{0,1:T(8,128)S(1)} %get-tuple-element.79) | copy-start | bytes 1400836
  72.3 8.0 %copy-start.61 = (f32[768]{0:T(1024)}, f32[768]{0:T(1024)S(1)}, u32[]{:S(2)}) copy-start(f32[768]{0:T(1024)S(1)} %get-tuple-element.78) | copy-start | bytes 9220
  75.4 8.0 %copy-start.28 = (f32[768,152]{0,1:T(8,128)}, f32[768,152]{0,1:T(8,128)S(1)}, u32[]{:S(2)}) copy-start(f32[768,152]{0,1:T(8,128)S(1)} %get-tuple-element.81) | copy-start | bytes 1400836
  75.4 8.0 %copy-start.63 = (f32[768]{0:T(1024)}, f32[768]{0:T(1024)S(1)}, u32[]{:S(2)}) copy-start(f32[768]{0:T(1024)S(1)} %get-tuple-element.80) | copy-start | bytes 9220
  78.5 8.0 %copy-start.29 = (f32[768,152]{0,1:T(8,128)}, f32[768,152]{0,1:T(8,128)S(1)}, u32[]{:S(2)}) copy-start(f32[768,152]{0,1:T(8,128)S(1)} %get-tuple-element.83) | copy-start | bytes 1400836
  78.5 8.0 %copy-start.65 = (f32[768]{0:T(1024)}, f32[768]{0:T(1024)S(1)}, u32[]{:S(2)}) copy-start(f32[768]{0:T(1024)S(1)} %get-tuple-element.82) | copy-start | bytes 9220
  81.6 7.2 %copy-start.30 = (f32[768,152]{0,1:T(8,128)}, f32[768,152]{0,1:T(8,128)S(1)}, u32[]{:S(2)}) copy-start(f32[768,152]{0,1:T(8,128)S(1)} %get-tuple-element.85) | copy-start | bytes 1400836
  81.6 7.2 %copy-start.67 = (f32[768]{0:T(1024)}, f32[768]{0:T(1024)S(1)}, u32[]{:S(2)}) copy-start(f32[768]{0:T(1024)S(1)} %get-tuple-element.84) | copy-start | bytes 9220
  86.5 37.5 %collective-permute-start.2 = (bf16[1,768,1024]{1,2,0:T(8,128)(2,1)}, bf16[1,768,1024]{1,2,0:T(8,128)(2,1)}, u32[]{:S(2)}, u32[]{:S(2)}) collective-permute-start(bf16[1,768,1024]{1,2,0:T(8,128)(2,1)} %fusion.42), channel_id=1, source_target_pairs={{0,4},{4,0},{8,12},{12,8},{16,20},{20,16},{24,28},{28,24},{1,5},{5... | collective-permute-start | bytes 4718600 | tf_op jit(solution)/shard_map/ppermute | solution.py:19
  97.2 5.3 %copy-start.36 = (f32[768]{0:T(1024)S(1)}, f32[768]{0:T(1024)}, u32[]{:S(2)}) copy-start(f32[768]{0:T(1024)} %copy-done.35) | copy-start | bytes 9220
  97.2 5.3 %copy-start.38 = (f32[768]{0:T(1024)S(1)}, f32[768]{0:T(1024)}, u32[]{:S(2)}) copy-start(f32[768]{0:T(1024)} %copy-done.37) | copy-start | bytes 9220
  97.2 5.3 %copy-start.40 = (f32[768]{0:T(1024)S(1)}, f32[768]{0:T(1024)}, u32[]{:S(2)}) copy-start(f32[768]{0:T(1024)} %copy-done.39) | copy-start | bytes 9220
  97.2 5.3 %copy-start.42 = (f32[768]{0:T(1024)S(1)}, f32[768]{0:T(1024)}, u32[]{:S(2)}) copy-start(f32[768]{0:T(1024)} %copy-done.41) | copy-start | bytes 9220
  97.2 5.3 %copy-start.44 = (f32[768]{0:T(1024)S(1)}, f32[768]{0:T(1024)}, u32[]{:S(2)}) copy-start(f32[768]{0:T(1024)} %copy-done.43) | copy-start | bytes 9220
  97.2 5.3 %copy-start.46 = (f32[768]{0:T(1024)S(1)}, f32[768]{0:T(1024)}, u32[]{:S(2)}) copy-start(f32[768]{0:T(1024)} %copy-done.45) | copy-start | bytes 9220
  97.2 5.3 %copy-start.18 = (bf16[768,152]{0,1:T(8,128)(2,1)S(1)}, bf16[768,152]{0,1:T(8,128)(2,1)}, u32[]{:S(2)}) copy-start(bf16[768,152]{0,1:T(8,128)(2,1)} %get-tuple-element.44) | copy-start | bytes 700420
  99.8 3.4 %collective-permute-start.3 = (bf16[1,768,8]{1,2,0:T(8,128)(2,1)S(1)}, bf16[1,768,8]{1,2,0:T(8,128)(2,1)S(1)}, u32[]{:S(2)}, u32[]{:S(2)}) collective-permute-start(bf16[1,768,8]{1,2,0:T(8,128)(2,1)S(1)} %stack.182), channel_id=1, source_target_pairs={{0,4},{4,0},{8,12},{12,8},{16,20},{20,16},{24,28},{28,24},{1,5},{5... | collective-permute-start | bytes 36872 | tf_op jit(solution)/shard_map/ppermute | solution.py:19
  100.1 3.1 %collective-permute-start.1 = (bf16[1,768,8]{1,2,0:T(8,128)(2,1)S(1)}, bf16[1,768,8]{1,2,0:T(8,128)(2,1)S(1)}, u32[]{:S(2)}, u32[]{:S(2)}) collective-permute-start(bf16[1,768,8]{1,2,0:T(8,128)(2,1)S(1)} %stack.155), channel_id=1, source_target_pairs={{0,4},{4,0},{8,12},{12,8},{16,20},{20,16},{24,28},{28,24},{1,5},{5... | collective-permute-start | bytes 36872 | tf_op jit(solution)/shard_map/ppermute | solution.py:19
  104.1 23.0 %all-to-all-start.2 = ((f32[8,1,768]{2,1,0:T(1,128)}), f32[8,1,768]{2,1,0:T(1,128)S(1)}, u32[]{:S(2)}, u32[]{:S(2)}) async-start(f32[8,1,768]{2,1,0:T(1,128)} %reshape.1099), calls=%async_computation.2 | async-start | bytes 49152 | tf_op jit(solution)/shard_map/all_to_all | solution.py:119
  127.2 12.3 %all-to-all-start.3 = ((f32[8,1,768]{2,1,0:T(1,128)}), f32[8,1,768]{2,1,0:T(1,128)S(1)}, u32[]{:S(2)}, u32[]{:S(2)}) async-start(f32[8,1,768]{2,1,0:T(1,128)} %reshape.1101), calls=%async_computation.3 | async-start | bytes 49152 | tf_op jit(solution)/shard_map/all_to_all | solution.py:126
  139.5 10.0 %copy-start.33 = (f32[13,48]{1,0:T(8,128)S(1)}, f32[13,48]{1,0:T(8,128)}, u32[]{:S(2)}) copy-start(f32[13,48]{1,0:T(8,128)} %get-tuple-element.14) | copy-start | bytes 7492
  139.5 42.5 %all-to-all-start.1 = ((f32[8,2,48,1024]{3,2,1,0:T(8,128)}), f32[8,2,48,1024]{3,2,1,0:T(8,128)}, u32[]{:S(2)}, u32[]{:S(2)}) async-start(f32[8,2,48,1024]{3,2,1,0:T(8,128)} %multiply_add_fusion), calls=%async_computation.1 | async-start | bytes 6291456 | tf_op jit(solution)/shard_map/all_to_all | solution.py:133
  144.1 12.3 %copy-start.13 = (f32[13,48,48]{1,2,0:T(8,128)S(1)}, f32[13,48,48]{1,2,0:T(8,128)}, u32[]{:S(2)}) copy-start(f32[13,48,48]{1,2,0:T(8,128)} %copy-done.12) | copy-start | bytes 359428
  144.1 146.0 %all-gather.2.cloned.1.call-start = ((), (), s32[]{:S(2)}) async-start(), calls=%async_computation.4 | async-start | bytes 6389760 | tf_op jit(solution)/shard_map/all_gather | solution.py:152
  144.8 12.7 %copy-start.9 = (f32[13,48,48]{1,2,0:T(8,128)S(1)}, f32[13,48,48]{1,2,0:T(8,128)}, u32[]{:S(2)}) copy-start(f32[13,48,48]{1,2,0:T(8,128)} %copy-done.8) | copy-start | bytes 359428
  150.8 5.6 %copy-start.2 = (bf16[13,48,1024]{2,1,0:T(8,128)(2,1)S(1)}, bf16[13,48,1024]{2,1,0:T(8,128)(2,1)}, u32[]{:S(2)}) copy-start(bf16[13,48,1024]{2,1,0:T(8,128)(2,1)} %get-tuple-element.38) | copy-start | bytes 3833860
  152.3 6.2 %copy-start.7 = (f32[13,48,48]{1,2,0:T(8,128)S(1)}, f32[13,48,48]{1,2,0:T(8,128)}, u32[]{:S(2)}) copy-start(f32[13,48,48]{1,2,0:T(8,128)} %copy-done.6) | copy-start | bytes 359428
  154.3 5.2 %copy-start.5 = (f32[13,48,48]{1,2,0:T(8,128)S(1)}, f32[13,48,48]{1,2,0:T(8,128)}, u32[]{:S(2)}) copy-start(f32[13,48,48]{1,2,0:T(8,128)} %copy-done.4) | copy-start | bytes 359428
  160.6 5.3 %copy-start.71 = (pred[13]{0:T(512)(128)(4,1)S(1)}, pred[13]{0:T(512)(128)(4,1)}, u32[]{:S(2)}) copy-start(pred[13]{0:T(512)(128)(4,1)} %get-tuple-element.36) | copy-start | bytes 43
  189.2 4.9 %copy-start.34 = (s32[13,8]{0,1:T(8,128)S(1)}, s32[13,8]{0,1:T(8,128)}, u32[]{:S(2)}) copy-start(s32[13,8]{0,1:T(8,128)} %param.16) | copy-start | bytes 1252
  (38 other events, 134.6 us)
Sparse Core Ops, SparseCore 0:
  194.2 95.8 all-gather.1
where the time goes:
time: 310 us; the launch traced here: 307 us
  waiting for transfers between devices  118 us (38%)
  matrix products  74.5 us (24%)
  local copies, waits for them, and re-layouts  52.3 us (17%)
  other arithmetic  26.2 us (8%)
  starting transfers between devices  18.7 us (6%)
  between operations  17.1 us (6%)
    all_gather x1, waiting for transfers between devices, local(): lax.all_gather(attn, 'tp', axis=1, tiled=True)  92.1 us
    dot_general x24, matrix products, attend_part(): lax.dot_general(raw_weights.astype(jnp.bfloat16), value_rows[:, :, lower:...  40.1 us
    dot_general x24, matrix products, attend_part(): lax.dot_general(query_rows[:, :, lower:upper], key_rows[:, :, lower:upper...  22 us
    all_to_all x1, waiting for transfers between devices, local(): lax.all_to_all(merged_accum.reshape(groups, per_group, TREE, local_cols),...  14.1 us
    all_to_all x1, waiting for transfers between devices, local(): lax.all_to_all(outbound, 'rep', split_axis=0, concat_axis=0, tiled=True)  12.2 us
    dot_general x1, matrix products, local(): jnp.dot(lax.all_gather(attn, 'tp', axis=1, tiled=True), out_weight, prefe...  10.2 us
    add x1, other arithmetic, combine_parts(): accum_first.reshape(split_shape) * factor_first[..., None]  8.19 us
    mul x4, local copies, waits for them, and re-layouts, combine_parts(): accum_second.reshape(split_shape) * factor_second[..., None]  7.7 us
  transfers between devices with their start and end apart: 9, of which 3 were waited for; matrix products, arithmetic and copies ran while one was open for 30% of the time, Pallas kernels for 0%

commit v1 on v0

v1 whole, which is shorter than its diff:
```python
import math
from functools import partial

import jax
import jax.numpy as jnp
from jax import lax
from jax.experimental import pallas as pl
from jax.experimental.pallas import tpu as pltpu
from jax.sharding import PartitionSpec as P

HD = 128
NEG_FILL = -1e30
SCALE = 1.0 / math.sqrt(HD)
VMEM_BYTES = 48 * 1024 * 1024


def attend_kernel(idx_ref, q_ref, tree_ref, bias_ref, *rest, n_caches):
    cache_refs = rest[:n_caches]
    out_ref, held, sems = rest[n_caches:]
    copies = []
    at = 0
    for i, ref in enumerate(cache_refs):
        size = ref.shape[0]
        copies.append(pltpu.make_async_copy(ref, held.at[pl.ds(at, size)], sems.at[i]))
        at += size
    for copy in copies:
        copy.start()
    for copy in copies:
        copy.wait()
    requests, _, width = q_ref.shape
    padded = held.shape[3]
    n_keys = bias_ref.shape[2]
    position = lax.broadcasted_iota(jnp.int32, (1, n_keys), 1).astype(jnp.float32)
    repeats = -(-n_keys // HD)

    def length_row(block, part):
        tail = held[block, part, 0, pl.ds(padded - 16, 16), 0:HD].astype(jnp.float32)[15:16]
        return jnp.concatenate([tail] * repeats, axis=1)[:, :n_keys]

    def body(r, carry):
        first = idx_ref[0, r]
        second = idx_ref[1, r]
        limit = jnp.where(position < padded, length_row(first, 0), length_row(second, 1) + padded)
        limit = jnp.where(position < 2 * padded, limit, n_keys)
        bias = bias_ref[r] + jnp.where(position < limit, 0.0, NEG_FILL)
        for h in range(width // HD):
            cols = slice(h * HD, (h + 1) * HD)
            keys = jnp.concatenate(
                [held[first, 0, 0, :, cols], held[second, 1, 0, :, cols], tree_ref[r, 0, :, cols]], axis=0
            )
            values = jnp.concatenate(
                [held[first, 0, 1, :, cols], held[second, 1, 1, :, cols], tree_ref[r, 1, :, cols]], axis=0
            )
            scores = lax.dot_general(
                q_ref[r, :, cols], keys, (((1,), (1,)), ((), ())), preferred_element_type=jnp.float32
            )
            scores = scores * SCALE + bias
            raw = jnp.exp(scores - jnp.max(scores, axis=1, keepdims=True))
            total = jnp.sum(raw, axis=1, keepdims=True)
            accum = jnp.dot(raw.astype(jnp.bfloat16), values, preferred_element_type=jnp.float32)
            out_ref[r, :, cols] = (accum / total).astype(out_ref.dtype)
        return carry

    lax.fori_loop(0, requests, body, 0)


def attend(idx, queries, tree_cache, bias, caches, start, width):
    req, tree, _ = queries.shape
    block = start // width
    n_blocks = sum(c.shape[0] for c in caches)
    keys = bias.shape[2]
    return pl.pallas_call(
        partial(attend_kernel, n_caches=len(caches)),
        grid=(1,),
        in_specs=[
            pl.BlockSpec(memory_space=pltpu.SMEM),
            pl.BlockSpec((req, tree, width), lambda i: (0, 0, block)),
            pl.BlockSpec((req, 2, tree, width), lambda i: (0, 0, 0, block)),
            pl.BlockSpec(bias.shape, lambda i: (0, 0, 0)),
        ]
        + [pl.BlockSpec(memory_space=pl.ANY)] * len(caches),
        out_specs=pl.BlockSpec((req, tree, width), lambda i: (0, 0, 0)),
        out_shape=jax.ShapeDtypeStruct((req, tree, width), jnp.bfloat16),
        scratch_shapes=[
            pltpu.VMEM((n_blocks,) + caches[0].shape[1:], jnp.bfloat16),
            pltpu.SemaphoreType.DMA((len(caches),)),
        ],
        compiler_params=pltpu.CompilerParams(vmem_limit_bytes=VMEM_BYTES),
        cost_estimate=pl.CostEstimate(
            flops=4 * req * tree * keys * width * 16, bytes_accessed=8 * n_blocks * 320 * width, transcendentals=0
        ),
    )(idx, queries, tree_cache, bias, *caches)


def project_kernel(z_ref, own, p1, p2, p3, p4, p5, w_ref, *rest, has_acc):
    out_ref = rest[-1]
    z = z_ref[0]
    middle = jnp.logical_and(z > 0, z < 3)
    lower = z < 2
    src_a = jnp.where(lower, 2, 1)
    src_b = jnp.where(lower, 3, 0)
    total = jnp.dot(own[...], w_ref[z], preferred_element_type=jnp.float32)
    total += jnp.dot(p1[...], w_ref[jnp.bitwise_xor(z, 1)], preferred_element_type=jnp.float32)
    total += jnp.dot(jnp.where(middle, p2[...], p4[...]), w_ref[src_a], preferred_element_type=jnp.float32)
    total += jnp.dot(jnp.where(middle, p3[...], p5[...]), w_ref[src_b], preferred_element_type=jnp.float32)
    if has_acc:
        total += rest[0][...]
    out_ref[...] = total.astype(out_ref.dtype)


def project(z, pieces, weight, acc, start, width, last):
    rows = pieces[0].shape[0]
    _, _, cols = weight.shape
    tile = 256
    block = start // width
    whole = pl.BlockSpec((rows, width), lambda n: (0, 0))
    args = [z, *pieces, weight] + ([acc] if acc is not None else [])
    out_type = jnp.bfloat16 if last else jnp.float32
    in_place = {7 + 1: 0} if acc is not None and not last else {}
    return pl.pallas_call(
        partial(project_kernel, has_acc=acc is not None),
        grid=(cols // tile,),
        in_specs=[pl.BlockSpec(memory_space=pltpu.SMEM)]
        + [whole] * 6
        + [pl.BlockSpec((weight.shape[0], width, tile), lambda n: (0, block, n))]
        + ([pl.BlockSpec((rows, tile), lambda n: (0, n))] if acc is not None else []),
        out_specs=pl.BlockSpec((rows, tile), lambda n: (0, n)),
        out_shape=jax.ShapeDtypeStruct((rows, cols), out_type),
        input_output_aliases=in_place,
        compiler_params=pltpu.CompilerParams(vmem_limit_bytes=VMEM_BYTES),
        cost_estimate=pl.CostEstimate(
            flops=2 * rows * 4 * width * cols, bytes_accessed=8 * width * cols + 8 * rows * cols, transcendentals=0
        ),
    )(*args)


def cache_block(prompt_cache, spill_cache, lens, start, width, padded):
    both = jnp.stack([prompt_cache[..., start : start + width], spill_cache[..., start : start + width]], axis=1)
    both = jnp.pad(both, ((0, 0), (0, 0), (0, 0), (0, padded - both.shape[3]), (0, 0)))
    row = lax.broadcasted_iota(jnp.int32, both.shape, 3)
    return jnp.where(row == padded - 1, lens[None, :, None, None, None], both)


def gather_caches(block):
    def across(value, mask):
        return lax.ppermute(value, "rep", [(i, i ^ mask) for i in range(lax.axis_size("rep"))])

    same = [block] + [across(block, m) for m in (2, 4, 6)]
    other = [across(value, 1) for value in same]
    return [value for pair in zip(same, other) for value in pair]


def exchange(attn):
    def send(value, pairs):
        return lax.ppermute(value, "tp", pairs)

    p1 = send(attn, [(0, 1), (1, 0), (2, 3), (3, 2)])
    p2 = send(attn, [(1, 2), (2, 1)])
    p3 = send(p1, [(1, 2), (2, 1)])
    p4 = send(p2, [(1, 0), (2, 3)])
    p5 = send(p3, [(1, 0), (2, 3)])
    return [attn, p1, p2, p3, p4, p5]


def local(
    queries,
    tree_cache,
    tree_mask,
    dest_group,
    accepted_path,
    prompt_cache,
    first_len,
    spill_cache,
    spill_len,
    out_weight,
    *,
    tuned,
):
    req, tree, cols = queries.shape
    prompt = prompt_cache.shape[2]
    padded = (prompt // 16 + 1) * 16
    group = dest_group[:, 0]
    partner = jnp.bitwise_xor(group, 1)
    lens = jnp.stack([first_len[0], spill_len[0]]).astype(jnp.bfloat16)
    bias = jnp.pad(jnp.where(tree_mask == 1, 0.0, NEG_FILL), ((0, 0), (0, 0), (2 * padded, 0)))
    if tuned:
        base = lax.axis_index("rep").astype(jnp.int32)
    else:
        base = jnp.zeros((), jnp.int32)
    idx = jnp.stack([jnp.bitwise_xor(group, base), jnp.bitwise_xor(partner, base)])
    accepted_cache = jnp.take_along_axis(tree_cache, accepted_path[:, None, :, None], axis=2)

    if not tuned:
        block = cache_block(prompt_cache, spill_cache, lens, 0, cols, padded)
        caches = [lax.all_gather(block, "rep", axis=0, tiled=True)]
        attn = attend(idx, queries, tree_cache, bias, caches, 0, cols).reshape(req * tree, cols)
        whole = lax.all_gather(attn, "tp", axis=1, tiled=True)
        summed = jnp.dot(whole, out_weight, preferred_element_type=jnp.float32)
        return summed.astype(jnp.bfloat16).reshape(req, tree, out_weight.shape[1]), accepted_cache

    z = lax.axis_index("tp").astype(jnp.int32).reshape(1)
    weight = out_weight.reshape(lax.axis_size("tp"), cols, out_weight.shape[1])
    chunks = []
    start = 0
    for heads in (1, 1, 2, 2, 2):
        chunks.append((start, heads * HD))
        start += heads * HD
    acc = None
    for i, (start, width) in enumerate(chunks):
        block = cache_block(prompt_cache, spill_cache, lens, start, width, padded)
        caches = gather_caches(block)
        attn = attend(idx, queries, tree_cache, bias, caches, start, width).reshape(req * tree, width)
        pieces = exchange(attn)
        acc = project(z, pieces, weight, acc, start, width, i == len(chunks) - 1)
    return acc.reshape(req, tree, out_weight.shape[1]), accepted_cache


def solution(mesh):
    heads_here = 32 // mesh.shape["tp"]
    tuned = mesh.shape["rep"] == 8 and mesh.shape["tp"] == 4 and heads_here == 8
    return jax.shard_map(
        partial(local, tuned=tuned),
        mesh=mesh,
        in_specs=(
            P("rep", None, "tp"),
            P("rep", None, None, "tp"),
            P("rep", None, None),
            P("rep", None),
            P("rep", None),
            P("rep", None, None, "tp"),
            P("rep"),
            P("rep", None, None, "tp"),
            P("rep"),
            P(None, "tp"),
        ),
        out_specs=(P("rep", None, "tp"), P("rep", None, None, "tp")),
        check_vma=False,
    )
```

time: 310 us -> 209 us (0.67)
  the two profiles are of different devices: /device:TPU:0 before, /device:TPU:10 now
where the time goes in v1:
time: 209 us; the launch traced here: 207 us
  starting transfers between devices  69.8 us (33%)
  Pallas kernels  67.2 us (32%)
  waiting for transfers between devices  35.6 us (17%)
  local copies, waits for them, and re-layouts  28.2 us (13%)
  other arithmetic  3.61 us (2%)
  between operations  2.9 us (1%)
    pallas_call x5, Pallas kernels, attend(): pl.pallas_call(partial(attend_kernel, n_caches=len(caches)), grid=(1,), i...  46.9 us
    ppermute x25, starting transfers between devices, send(): return lax.ppermute(value, 'tp', pairs)  46.8 us
    ppermute x35, waiting for transfers between devices, across(): lax.ppermute(value, 'rep', [(i, i ^ mask) for i in range(lax.axis_size('r...  23.2 us
    ppermute x35, starting transfers between devices, across(): lax.ppermute(value, 'rep', [(i, i ^ mask) for i in range(lax.axis_size('r...  23 us
    unnamed x113, local copies, waits for them, and re-layouts  20.5 us
    pallas_call x5, Pallas kernels, project(): pl.pallas_call(partial(project_kernel, has_acc=acc is not None), grid=(co...  20.3 us
    ppermute x25, waiting for transfers between devices, send(): return lax.ppermute(value, 'tp', pairs)  12.3 us
    gather x3, local copies, waits for them, and re-layouts, local(): jnp.take_along_axis(tree_cache, accepted_path[:, None, :, None], axis=2)  5.08 us
  transfers between devices with their start and end apart: 60, of which 11 were waited for; matrix products, arithmetic and copies ran while one was open for 6% of the time, Pallas kernels for 30%

profile of v1, /device:TPU:10, one launch (start us, length us, event | category | flops | bytes accessed | tf_op | source)
XLA Modules:
  0.0 207.3 jit_solution(7056282885724739761)
XLA Ops:
  3.9 1.5 collective-permute-start.51
  5.4 1.4 collective-permute-start.53
  7.4 3.1 %collective-permute-done.49.rest_2_ = bf16[1,2,2,160,128]{4,3,2,1,0:T(8,128)(2,1)S(1)} collective-permute-done((bf16[1,2,2,160,128]{4,3,2,1,0:T(8,128)(2,1)S(1)}, bf16[1,2,2,160,128]{4,3,2,1,0:T(8,128)(2,1)S(1)}, u32[]{:S(2)}, u32[]{:S(2)}) %collective-permute-start.49) | collective-permute-done | bytes 163872 | tf_op jit(solution)/shard_map/ppermute | solution.py:146
  10.4 1.5 collective-permute-start.39
  12.0 1.3 slice_bitcast_fusion
  13.3 3.3 %collective-permute-start.41 = (bf16[1,2,2,160,128]{4,3,2,1,0:T(8,128)(2,1)S(1)}, bf16[1,2,2,160,128]{4,3,2,1,0:T(8,128)(2,1)S(1)}, u32[]{:S(2)}, u32[]{:S(2)}) collective-permute-start(bf16[1,2,2,160,128]{4,3,2,1,0:T(8,128)(2,1)S(1)} %get-tuple-element.15.rest_0_), channel_id=1, source_target_pairs={{0,24},{4,28},{8,16},{12,20},{16,8},{20,12},{24,0},{28,4},{1,25},{... | collective-permute-start | bytes 491528 | tf_op jit(solution)/shard_map/ppermute | solution.py:146
  18.5 2.4 %collective-permute-done.41.rest_6_ = bf16[1,2,2,160,128]{4,3,2,1,0:T(8,128)(2,1)S(1)} collective-permute-done((bf16[1,2,2,160,128]{4,3,2,1,0:T(8,128)(2,1)S(1)}, bf16[1,2,2,160,128]{4,3,2,1,0:T(8,128)(2,1)S(1)}, u32[]{:S(2)}, u32[]{:S(2)}) %collective-permute-start.41) | collective-permute-done | bytes 163872 | tf_op jit(solution)/shard_map/ppermute | solution.py:146
  22.8 1.3 collective-permute-start.27
  31.7 1.3 collective-permute-start.15
  33.0 7.1 %collective-permute-done.27.rest_4_ = bf16[1,2,2,160,256]{4,3,2,1,0:T(8,128)(2,1)S(1)} collective-permute-done((bf16[1,2,2,160,256]{4,3,2,1,0:T(8,128)(2,1)S(1)}, bf16[1,2,2,160,256]{4,3,2,1,0:T(8,128)(2,1)S(1)}, u32[]{:S(2)}, u32[]{:S(2)}) %collective-permute-start.27) | collective-permute-done | bytes 327712 | tf_op jit(solution)/shard_map/ppermute | solution.py:146
  40.1 1.7 collective-permute-start.17
  43.0 2.8 %collective-permute-done.13.rest_2_ = bf16[1,2,2,160,256]{4,3,2,1,0:T(8,128)(2,1)} collective-permute-done((bf16[1,2,2,160,256]{4,3,2,1,0:T(8,128)(2,1)S(1)}, bf16[1,2,2,160,256]{4,3,2,1,0:T(8,128)(2,1)}, u32[]{:S(2)}, u32[]{:S(2)}) %collective-permute-start.13) | collective-permute-done | bytes 327712 | tf_op jit(solution)/shard_map/ppermute | solution.py:146
  45.8 1.3 collective-permute-start.3
  47.1 7.2 %collective-permute-done.15.rest_4_ = bf16[1,2,2,160,256]{4,3,2,1,0:T(8,128)(2,1)} collective-permute-done((bf16[1,2,2,160,256]{4,3,2,1,0:T(8,128)(2,1)S(1)}, bf16[1,2,2,160,256]{4,3,2,1,0:T(8,128)(2,1)}, u32[]{:S(2)}, u32[]{:S(2)}) %collective-permute-start.15) | collective-permute-done | bytes 327712 | tf_op jit(solution)/shard_map/ppermute | solution.py:146
  54.3 1.7 collective-permute-start.5
  62.6 7.7 %shard_map.117 = bf16[13,48,128]{2,1,0:T(8,128)(2,1)S(1)} custom-call(s32[2,13]{1,0:T(2,128)S(1)} %pad_add_fusion.idx_ref, bf16[13,48,1024]{2,1,0:T(8,128)(2,1)S(1)} %copy-done.24, bf16[13,2,48,1024]{3,2,1,0:T(8,128)(2,1)} %tree_ref.9, f32[13,48,368]{2,1,0:T(8,128)S(1)} %pad.21.bias_ref, bf16[1,2,2,160,128]{4,3,2,1,0:T(8,128)(2,1)S(1)} %get-tuple-element.14.rest_0_, ...), custom_call_target="tpu_custom_call" | custom-call | flops 1881145344 | bytes 2621440 | tf_op jit(solution)/shard_map/pallas_call | solution.py:72
  70.9 4.6 %collective-permute-start.56 = (bf16[624,128]{1,0:T(8,128)(2,1)S(1)}, bf16[624,128]{1,0:T(8,128)(2,1)S(1)}, u32[]{:S(2)}, u32[]{:S(2)}) collective-permute-start(bf16[624,128]{1,0:T(8,128)(2,1)S(1)} %bitcast.52), channel_id=1, source_target_pairs={{1,2},{2,1},{5,6},{6,5},{9,10},{10,9},{13,14},{14,13},{17,18},{18,... | collective-permute-start | bytes 479240 | tf_op jit(solution)/shard_map/ppermute | solution.py:155
  76.2 7.6 %shard_map.116 = bf16[13,48,128]{2,1,0:T(8,128)(2,1)S(1)} custom-call(s32[2,13]{1,0:T(2,128)S(1)} %pad_add_fusion.idx_ref, bf16[13,48,1024]{2,1,0:T(8,128)(2,1)S(1)} %copy-done.24, bf16[13,2,48,1024]{3,2,1,0:T(8,128)(2,1)} %tree_ref.9, f32[13,48,368]{2,1,0:T(8,128)S(1)} %pad.21.bias_ref, bf16[1,2,2,160,128]{4,3,2,1,0:T(8,128)(2,1)S(1)} %get-tuple-element.15.rest_0_, ...), custom_call_target="tpu_custom_call" | custom-call | flops 1881145344 | bytes 2621440 | tf_op jit(solution)/shard_map/pallas_call | solution.py:72
  84.0 2.0 collective-permute-start.44
  86.1 4.4 %collective-permute-done.43.p1 = bf16[624,128]{1,0:T(8,128)(2,1)S(1)} collective-permute-done((bf16[624,128]{1,0:T(8,128)(2,1)S(1)}, bf16[624,128]{1,0:T(8,128)(2,1)S(1)}, u32[]{:S(2)}, u32[]{:S(2)}) %collective-permute-start.43) | collective-permute-done | bytes 159776 | tf_op jit(solution)/shard_map/ppermute | solution.py:155
  90.4 1.9 collective-permute-done.44.p2
  92.9 2.2 %collective-permute-start.57 = (bf16[624,128]{1,0:T(8,128)(2,1)S(1)}, bf16[624,128]{1,0:T(8,128)(2,1)S(1)}, u32[]{:S(2)}, u32[]{:S(2)}) collective-permute-start(bf16[624,128]{1,0:T(8,128)(2,1)S(1)} %collective-permute-done.55.p1), channel_id=1, source_target_pairs={{1,2},{2,1},{5,6},{6,5},{9,10},{10,9},{13,14},{14,13},{17,18},{18,... | collective-permute-start | bytes 479240 | tf_op jit(solution)/shard_map/ppermute | solution.py:155
  95.1 1.3 collective-permute-start.58
  96.4 10.8 %shard_map.115 = bf16[13,48,256]{2,1,0:T(8,128)(2,1)S(1)} custom-call(s32[2,13]{1,0:T(2,128)S(1)} %pad_add_fusion.idx_ref, bf16[13,48,1024]{2,1,0:T(8,128)(2,1)S(1)} %copy-done.24, bf16[13,2,48,1024]{3,2,1,0:T(8,128)(2,1)} %tree_ref.9, f32[13,48,368]{2,1,0:T(8,128)S(1)} %pad.21.bias_ref, bf16[1,2,2,160,256]{4,3,2,1,0:T(8,128)(2,1)S(1)} %get-tuple-element.16.rest_0_, ...), custom_call_target="tpu_custom_call" | custom-call | flops 3762290688 | bytes 5242880 | tf_op jit(solution)/shard_map/pallas_call | solution.py:72
  107.9 3.6 %collective-permute-start.45 = (bf16[624,128]{1,0:T(8,128)(2,1)S(1)}, bf16[624,128]{1,0:T(8,128)(2,1)S(1)}, u32[]{:S(2)}, u32[]{:S(2)}) collective-permute-start(bf16[624,128]{1,0:T(8,128)(2,1)S(1)} %collective-permute-done.43.p1), channel_id=1, source_target_pairs={{1,2},{2,1},{5,6},{6,5},{9,10},{10,9},{13,14},{14,13},{17,18},{18,... | collective-permute-start | bytes 479240 | tf_op jit(solution)/shard_map/ppermute | solution.py:155
  111.6 1.3 collective-permute-start.46
  112.9 10.7 %shard_map.114 = bf16[13,48,256]{2,1,0:T(8,128)(2,1)S(1)} custom-call(s32[2,13]{1,0:T(2,128)S(1)} %pad_add_fusion.idx_ref, bf16[13,48,1024]{2,1,0:T(8,128)(2,1)S(1)} %copy-done.24, bf16[13,2,48,1024]{3,2,1,0:T(8,128)(2,1)} %tree_ref.9, f32[13,48,368]{2,1,0:T(8,128)S(1)} %pad.21.bias_ref, bf16[1,2,2,160,256]{4,3,2,1,0:T(8,128)(2,1)S(1)} %get-tuple-element.17.rest_0_, ...), custom_call_target="tpu_custom_call" | custom-call | flops 3762290688 | bytes 5242880 | tf_op jit(solution)/shard_map/pallas_call | solution.py:72
  126.4 2.2 %collective-permute-start.32 = (bf16[624,256]{1,0:T(8,128)(2,1)S(1)}, bf16[624,256]{1,0:T(8,128)(2,1)S(1)}, u32[]{:S(2)}, u32[]{:S(2)}) collective-permute-start(bf16[624,256]{1,0:T(8,128)(2,1)S(1)} %bitcast.46), channel_id=1, source_target_pairs={{1,2},{2,1},{5,6},{6,5},{9,10},{10,9},{13,14},{14,13},{17,18},{18,... | collective-permute-start | bytes 958472 | tf_op jit(solution)/shard_map/ppermute | solution.py:155
  129.1 10.1 %shard_map.113 = bf16[13,48,256]{2,1,0:T(8,128)(2,1)S(1)} custom-call(s32[2,13]{1,0:T(2,128)S(1)} %pad_add_fusion.idx_ref, bf16[13,48,1024]{2,1,0:T(8,128)(2,1)S(1)} %copy-done.25, bf16[13,2,48,1024]{3,2,1,0:T(8,128)(2,1)} %tree_ref.9, f32[13,48,368]{2,1,0:T(8,128)S(1)} %pad.21.bias_ref, bf16[1,2,2,160,256]{4,3,2,1,0:T(8,128)(2,1)S(1)} %get-tuple-element.18.rest_0_, ...), custom_call_target="tpu_custom_call" | custom-call | flops 3762290688 | bytes 5242880 | tf_op jit(solution)/shard_map/pallas_call | solution.py:72
  139.9 3.2 %collective-permute-start.20 = (bf16[624,256]{1,0:T(8,128)(2,1)S(1)}, bf16[624,256]{1,0:T(8,128)(2,1)S(1)}, u32[]{:S(2)}, u32[]{:S(2)}) collective-permute-start(bf16[624,256]{1,0:T(8,128)(2,1)S(1)} %bitcast.49), channel_id=1, source_target_pairs={{1,2},{2,1},{5,6},{6,5},{9,10},{10,9},{13,14},{14,13},{17,18},{18,... | collective-permute-start | bytes 958472 | tf_op jit(solution)/shard_map/ppermute | solution.py:155
  143.8 2.7 %collective-permute-start.8 = (bf16[624,256]{1,0:T(8,128)(2,1)S(1)}, bf16[624,256]{1,0:T(8,128)(2,1)S(1)}, u32[]{:S(2)}, u32[]{:S(2)}) collective-permute-start(bf16[624,256]{1,0:T(8,128)(2,1)S(1)} %bitcast.43), channel_id=1, source_target_pairs={{1,2},{2,1},{5,6},{6,5},{9,10},{10,9},{13,14},{14,13},{17,18},{18,... | collective-permute-start | bytes 958472 | tf_op jit(solution)/shard_map/ppermute | solution.py:155
  146.5 3.2 %collective-permute-start.33 = (bf16[624,256]{1,0:T(8,128)(2,1)S(1)}, bf16[624,256]{1,0:T(8,128)(2,1)}, u32[]{:S(2)}, u32[]{:S(2)}) collective-permute-start(bf16[624,256]{1,0:T(8,128)(2,1)S(1)} %collective-permute-done.31.p1), channel_id=1, source_target_pairs={{1,2},{2,1},{5,6},{6,5},{9,10},{10,9},{13,14},{14,13},{17,18},{18,... | collective-permute-start | bytes 958472 | tf_op jit(solution)/shard_map/ppermute | solution.py:155
  149.7 2.7 %collective-permute-start.21 = (bf16[624,256]{1,0:T(8,128)(2,1)S(1)}, bf16[624,256]{1,0:T(8,128)(2,1)S(1)}, u32[]{:S(2)}, u32[]{:S(2)}) collective-permute-start(bf16[624,256]{1,0:T(8,128)(2,1)S(1)} %collective-permute-done.19.p1), channel_id=1, source_target_pairs={{1,2},{2,1},{5,6},{6,5},{9,10},{10,9},{13,14},{14,13},{17,18},{18,... | collective-permute-start | bytes 958472 | tf_op jit(solution)/shard_map/ppermute | solution.py:155
  152.4 2.0 collective-permute-start.34
  154.4 3.2 %collective-permute-start.9 = (bf16[624,256]{1,0:T(8,128)(2,1)S(1)}, bf16[624,256]{1,0:T(8,128)(2,1)S(1)}, u32[]{:S(2)}, u32[]{:S(2)}) collective-permute-start(bf16[624,256]{1,0:T(8,128)(2,1)S(1)} %collective-permute-done.7.p1), channel_id=1, source_target_pairs={{1,2},{2,1},{5,6},{6,5},{9,10},{10,9},{13,14},{14,13},{17,18},{18,... | collective-permute-start | bytes 958472 | tf_op jit(solution)/shard_map/ppermute | solution.py:155
  157.8 4.9 %gather_fusion = bf16[104,2,1024]{2,0,1:T(8,128)(2,1)} fusion(bf16[13,2,48,1024]{3,2,1,0:T(8,128)(2,1)} %tree_ref.9, s32[104]{0:T(128)S(1)} %reshape.105), kind=kCustom, calls=%fused_computation | custom fusion | bytes 852800 | tf_op jit(solution)/shard_map/jit(take_along_axis)/gather | solution.py:191
  162.8 2.0 collective-permute-start.22
  166.1 2.0 collective-permute-start.35
  168.1 4.7 %collective-permute-done.21.p3 = bf16[624,256]{1,0:T(8,128)(2,1)S(1)} collective-permute-done((bf16[624,256]{1,0:T(8,128)(2,1)S(1)}, bf16[624,256]{1,0:T(8,128)(2,1)S(1)}, u32[]{:S(2)}, u32[]{:S(2)}) %collective-permute-start.21) | collective-permute-done | bytes 319520 | tf_op jit(solution)/shard_map/ppermute | solution.py:155
  172.8 2.0 collective-permute-start.23
  174.8 1.9 fusion.6
  176.7 1.8 copy.19
  179.8 1.5 collective-permute-start.11
  186.8 3.6 %shard_map.118.rest_0_ = f32[624,1024]{1,0:T(8,128)S(1)} custom-call(s32[1]{0:T(128)} %bitcast.z_ref, bf16[624,128]{1,0:T(8,128)(2,1)S(1)} %bitcast.53, bf16[624,128]{1,0:T(8,128)(2,1)S(1)} %copy-done.3, bf16[624,128]{1,0:T(8,128)(2,1)S(1)} %copy-done.5, bf16[624,128]{1,0:T(8,128)(2,1)S(1)} %copy-done.7, bf16[624,128]{1,0:T(8,128)(2,1)S(1)} %copy-done.9, ...), custom_call_target="tpu_custom_call" | custom-call | flops 654311424 | bytes 6160384 | tf_op jit(solution)/shard_map/pallas_call | solution.py:120
  190.5 3.7 %shard_map.119.rest_0_ = f32[624,1024]{1,0:T(8,128)S(1)} custom-call(s32[1]{0:T(128)} %bitcast.z_ref, bf16[624,128]{1,0:T(8,128)(2,1)S(1)} %bitcast.56, bf16[624,128]{1,0:T(8,128)(2,1)S(1)} %copy-done.15, bf16[624,128]{1,0:T(8,128)(2,1)S(1)} %copy-done.17, bf16[624,128]{1,0:T(8,128)(2,1)S(1)} %copy-done.19, ...), custom_call_target="tpu_custom_call", output_to_operand_aliasing={{}: (8, {})} | custom-call | flops 654311424 | bytes 6160384 | tf_op jit(solution)/shard_map/pallas_call | solution.py:120
  194.2 4.2 %shard_map.120.rest_0_ = f32[624,1024]{1,0:T(8,128)S(1)} custom-call(s32[1]{0:T(128)} %bitcast.z_ref, bf16[624,256]{1,0:T(8,128)(2,1)S(1)} %bitcast.47, bf16[624,256]{1,0:T(8,128)(2,1)S(1)} %collective-permute-done.31.p1, bf16[624,256]{1,0:T(8,128)(2,1)S(1)} %collective-permute-done.32.p2, ...), custom_call_target="tpu_custom_call", output_to_operand_aliasing={{}: (8, {})} | custom-call | flops 1308622848 | bytes 7208960 | tf_op jit(solution)/shard_map/pallas_call | solution.py:120
  198.5 4.1 %shard_map.121.rest_0_ = f32[624,1024]{1,0:T(8,128)S(1)} custom-call(s32[1]{0:T(128)} %bitcast.z_ref, bf16[624,256]{1,0:T(8,128)(2,1)S(1)} %bitcast.50, bf16[624,256]{1,0:T(8,128)(2,1)S(1)} %collective-permute-done.19.p1, bf16[624,256]{1,0:T(8,128)(2,1)S(1)} %collective-permute-done.20.p2, ...), custom_call_target="tpu_custom_call", output_to_operand_aliasing={{}: (8, {})} | custom-call | flops 1308622848 | bytes 7208960 | tf_op jit(solution)/shard_map/pallas_call | solution.py:120
  202.6 4.6 %shard_map.122 = bf16[624,1024]{1,0:T(8,128)(2,1)} custom-call(s32[1]{0:T(128)} %bitcast.z_ref, bf16[624,256]{1,0:T(8,128)(2,1)S(1)} %bitcast.44, bf16[624,256]{1,0:T(8,128)(2,1)S(1)} %collective-permute-done.7.p1, bf16[624,256]{1,0:T(8,128)(2,1)S(1)} %collective-permute-done.8.p2, bf16[624,256]{1,0:T(8,128)(2,1)S(1)} %collective-permute-done.9.p3, ...), custom_call_target="tpu_custom_call" | custom-call | flops 1308622848 | bytes 7208960 | tf_op jit(solution)/shard_map/pallas_call | solution.py:120
  (212 shorter events, 37.0 us)
Async XLA Ops:
  3.9 9.4 %collective-permute-start.51 = (bf16[1,2,2,160,128]{4,3,2,1,0:T(8,128)(2,1)S(1)}, bf16[1,2,2,160,128]{4,3,2,1,0:T(8,128)(2,1)S(1)}, u32[]{:S(2)}, u32[]{:S(2)}) collective-permute-start(bf16[1,2,2,160,128]{4,3,2,1,0:T(8,128)(2,1)S(1)} %get-tuple-element.14.rest_0_), channel_id=1, source_target_pairs={{0,16},{4,20},{8,24},{12,28},{16,0},{20,4},{24,8},{28,12},{1,17},{... | collective-permute-start | bytes 491528 | tf_op jit(solution)/shard_map/ppermute | solution.py:146
  5.4 11.2 %collective-permute-start.53 = (bf16[1,2,2,160,128]{4,3,2,1,0:T(8,128)(2,1)S(1)}, bf16[1,2,2,160,128]{4,3,2,1,0:T(8,128)(2,1)S(1)}, u32[]{:S(2)}, u32[]{:S(2)}) collective-permute-start(bf16[1,2,2,160,128]{4,3,2,1,0:T(8,128)(2,1)S(1)} %get-tuple-element.14.rest_0_), channel_id=1, source_target_pairs={{0,24},{4,28},{8,16},{12,20},{16,8},{20,12},{24,0},{28,4},{1,25},{... | collective-permute-start | bytes 491528 | tf_op jit(solution)/shard_map/ppermute | solution.py:146
  6.8 9.8 %collective-permute-start.48 = (bf16[1,2,2,160,128]{4,3,2,1,0:T(8,128)(2,1)S(1)}, bf16[1,2,2,160,128]{4,3,2,1,0:T(8,128)(2,1)S(1)}, u32[]{:S(2)}, u32[]{:S(2)}) collective-permute-start(bf16[1,2,2,160,128]{4,3,2,1,0:T(8,128)(2,1)S(1)} %get-tuple-element.14.rest_0_), channel_id=1, source_target_pairs={{0,4},{4,0},{8,12},{12,8},{16,20},{20,16},{24,28},{28,24},{1,5},{5... | collective-permute-start | bytes 491528 | tf_op jit(solution)/shard_map/ppermute | solution.py:146
  6.8 10.7 %collective-permute-start.37 = (bf16[1,2,2,160,128]{4,3,2,1,0:T(8,128)(2,1)S(1)}, bf16[1,2,2,160,128]{4,3,2,1,0:T(8,128)(2,1)S(1)}, u32[]{:S(2)}, u32[]{:S(2)}) collective-permute-start(bf16[1,2,2,160,128]{4,3,2,1,0:T(8,128)(2,1)S(1)} %get-tuple-element.15.rest_0_), channel_id=1, source_target_pairs={{0,8},{4,12},{8,0},{12,4},{16,24},{20,28},{24,16},{28,20},{1,9},{5... | collective-permute-start | bytes 491528 | tf_op jit(solution)/shard_map/ppermute | solution.py:146
  20.8 10.9 %collective-permute-start.25 = (bf16[1,2,2,160,256]{4,3,2,1,0:T(8,128)(2,1)S(1)}, bf16[1,2,2,160,256]{4,3,2,1,0:T(8,128)(2,1)S(1)}, u32[]{:S(2)}, u32[]{:S(2)}) collective-permute-start(bf16[1,2,2,160,256]{4,3,2,1,0:T(8,128)(2,1)S(1)} %get-tuple-element.16.rest_0_), channel_id=1, source_target_pairs={{0,8},{4,12},{8,0},{12,4},{16,24},{20,28},{24,16},{28,20},{1,9},{5... | collective-permute-start | bytes 983048 | tf_op jit(solution)/shard_map/ppermute | solution.py:146
  22.8 17.4 %collective-permute-start.27 = (bf16[1,2,2,160,256]{4,3,2,1,0:T(8,128)(2,1)S(1)}, bf16[1,2,2,160,256]{4,3,2,1,0:T(8,128)(2,1)S(1)}, u32[]{:S(2)}, u32[]{:S(2)}) collective-permute-start(bf16[1,2,2,160,256]{4,3,2,1,0:T(8,128)(2,1)S(1)} %get-tuple-element.16.rest_0_), channel_id=1, source_target_pairs={{0,16},{4,20},{8,24},{12,28},{16,0},{20,4},{24,8},{28,12},{1,17},{... | collective-permute-start | bytes 983048 | tf_op jit(solution)/shard_map/ppermute | solution.py:146
  27.9 14.9 %collective-permute-start.29 = (bf16[1,2,2,160,256]{4,3,2,1,0:T(8,128)(2,1)S(1)}, bf16[1,2,2,160,256]{4,3,2,1,0:T(8,128)(2,1)}, u32[]{:S(2)}, u32[]{:S(2)}) collective-permute-start(bf16[1,2,2,160,256]{4,3,2,1,0:T(8,128)(2,1)S(1)} %get-tuple-element.16.rest_0_), channel_id=1, source_target_pairs={{0,24},{4,28},{8,16},{12,20},{16,8},{20,12},{24,0},{28,4},{1,25},{... | collective-permute-start | bytes 983048 | tf_op jit(solution)/shard_map/ppermute | solution.py:146
  29.5 13.4 %collective-permute-start.24 = (bf16[1,2,2,160,256]{4,3,2,1,0:T(8,128)(2,1)S(1)}, bf16[1,2,2,160,256]{4,3,2,1,0:T(8,128)(2,1)}, u32[]{:S(2)}, u32[]{:S(2)}) collective-permute-start(bf16[1,2,2,160,256]{4,3,2,1,0:T(8,128)(2,1)S(1)} %get-tuple-element.16.rest_0_), channel_id=1, source_target_pairs={{0,4},{4,0},{8,12},{12,8},{16,20},{20,16},{24,28},{28,24},{1,5},{5... | collective-permute-start | bytes 983048 | tf_op jit(solution)/shard_map/ppermute | solution.py:146
  30.4 15.3 %collective-permute-start.13 = (bf16[1,2,2,160,256]{4,3,2,1,0:T(8,128)(2,1)S(1)}, bf16[1,2,2,160,256]{4,3,2,1,0:T(8,128)(2,1)}, u32[]{:S(2)}, u32[]{:S(2)}) collective-permute-start(bf16[1,2,2,160,256]{4,3,2,1,0:T(8,128)(2,1)S(1)} %get-tuple-element.17.rest_0_), channel_id=1, source_target_pairs={{0,8},{4,12},{8,0},{12,4},{16,24},{20,28},{24,16},{28,20},{1,9},{5... | collective-permute-start | bytes 983048 | tf_op jit(solution)/shard_map/ppermute | solution.py:146
  31.7 22.6 %collective-permute-start.15 = (bf16[1,2,2,160,256]{4,3,2,1,0:T(8,128)(2,1)S(1)}, bf16[1,2,2,160,256]{4,3,2,1,0:T(8,128)(2,1)}, u32[]{:S(2)}, u32[]{:S(2)}) collective-permute-start(bf16[1,2,2,160,256]{4,3,2,1,0:T(8,128)(2,1)S(1)} %get-tuple-element.17.rest_0_), channel_id=1, source_target_pairs={{0,16},{4,20},{8,24},{12,28},{16,0},{20,4},{24,8},{28,12},{1,17},{... | collective-permute-start | bytes 983048 | tf_op jit(solution)/shard_map/ppermute | solution.py:146
  40.1 15.8 %collective-permute-start.17 = (bf16[1,2,2,160,256]{4,3,2,1,0:T(8,128)(2,1)S(1)}, bf16[1,2,2,160,256]{4,3,2,1,0:T(8,128)(2,1)}, u32[]{:S(2)}, u32[]{:S(2)}) collective-permute-start(bf16[1,2,2,160,256]{4,3,2,1,0:T(8,128)(2,1)S(1)} %get-tuple-element.17.rest_0_), channel_id=1, source_target_pairs={{0,24},{4,28},{8,16},{12,20},{16,8},{20,12},{24,0},{28,4},{1,25},{... | collective-permute-start | bytes 983048 | tf_op jit(solution)/shard_map/ppermute | solution.py:146
  42.8 27.5 %collective-permute-start.12 = (bf16[1,2,2,160,256]{4,3,2,1,0:T(8,128)(2,1)S(1)}, bf16[1,2,2,160,256]{4,3,2,1,0:T(8,128)(2,1)S(1)}, u32[]{:S(2)}, u32[]{:S(2)}) collective-permute-start(bf16[1,2,2,160,256]{4,3,2,1,0:T(8,128)(2,1)S(1)} %get-tuple-element.17.rest_0_), channel_id=1, source_target_pairs={{0,4},{4,0},{8,12},{12,8},{16,20},{20,16},{24,28},{28,24},{1,5},{5... | collective-permute-start | bytes 983048 | tf_op jit(solution)/shard_map/ppermute | solution.py:146
  42.9 28.0 %collective-permute-start.1 = (bf16[1,2,2,160,256]{4,3,2,1,0:T(8,128)(2,1)S(1)}, bf16[1,2,2,160,256]{4,3,2,1,0:T(8,128)(2,1)S(1)}, u32[]{:S(2)}, u32[]{:S(2)}) collective-permute-start(bf16[1,2,2,160,256]{4,3,2,1,0:T(8,128)(2,1)S(1)} %get-tuple-element.18.rest_0_), channel_id=1, source_target_pairs={{0,8},{4,12},{8,0},{12,4},{16,24},{20,28},{24,16},{28,20},{1,9},{5... | collective-permute-start | bytes 983048 | tf_op jit(solution)/shard_map/ppermute | solution.py:146
  45.8 29.7 %collective-permute-start.3 = (bf16[1,2,2,160,256]{4,3,2,1,0:T(8,128)(2,1)S(1)}, bf16[1,2,2,160,256]{4,3,2,1,0:T(8,128)(2,1)S(1)}, u32[]{:S(2)}, u32[]{:S(2)}) collective-permute-start(bf16[1,2,2,160,256]{4,3,2,1,0:T(8,128)(2,1)S(1)} %get-tuple-element.18.rest_0_), channel_id=1, source_target_pairs={{0,16},{4,20},{8,24},{12,28},{16,0},{20,4},{24,8},{28,12},{1,17},{... | collective-permute-start | bytes 983048 | tf_op jit(solution)/shard_map/ppermute | solution.py:146
  54.3 21.3 %collective-permute-start.5 = (bf16[1,2,2,160,256]{4,3,2,1,0:T(8,128)(2,1)S(1)}, bf16[1,2,2,160,256]{4,3,2,1,0:T(8,128)(2,1)S(1)}, u32[]{:S(2)}, u32[]{:S(2)}) collective-permute-start(bf16[1,2,2,160,256]{4,3,2,1,0:T(8,128)(2,1)S(1)} %get-tuple-element.18.rest_0_), channel_id=1, source_target_pairs={{0,24},{4,28},{8,16},{12,20},{16,8},{20,12},{24,0},{28,4},{1,25},{... | collective-permute-start | bytes 983048 | tf_op jit(solution)/shard_map/ppermute | solution.py:146
  56.0 20.1 %collective-permute-start = (bf16[1,2,2,160,256]{4,3,2,1,0:T(8,128)(2,1)S(1)}, bf16[1,2,2,160,256]{4,3,2,1,0:T(8,128)(2,1)S(1)}, u32[]{:S(2)}, u32[]{:S(2)}) collective-permute-start(bf16[1,2,2,160,256]{4,3,2,1,0:T(8,128)(2,1)S(1)} %get-tuple-element.18.rest_0_), channel_id=1, source_target_pairs={{0,4},{4,0},{8,12},{12,8},{16,20},{20,16},{24,28},{28,24},{1,5},{5... | collective-permute-start | bytes 983048 | tf_op jit(solution)/shard_map/ppermute | solution.py:146
  70.4 13.5 %collective-permute-start.55 = (bf16[624,128]{1,0:T(8,128)(2,1)S(1)}, bf16[624,128]{1,0:T(8,128)(2,1)S(1)}, u32[]{:S(2)}, u32[]{:S(2)}) collective-permute-start(bf16[624,128]{1,0:T(8,128)(2,1)S(1)} %bitcast.51), channel_id=1, source_target_pairs={{0,1},{1,0},{2,3},{3,2},{4,5},{5,4},{6,7},{7,6},{8,9},{9,8},{10,11... | collective-permute-start | bytes 479240 | tf_op jit(solution)/shard_map/ppermute | solution.py:155
  70.9 13.1 %collective-permute-start.56 = (bf16[624,128]{1,0:T(8,128)(2,1)S(1)}, bf16[624,128]{1,0:T(8,128)(2,1)S(1)}, u32[]{:S(2)}, u32[]{:S(2)}) collective-permute-start(bf16[624,128]{1,0:T(8,128)(2,1)S(1)} %bitcast.52), channel_id=1, source_target_pairs={{1,2},{2,1},{5,6},{6,5},{9,10},{10,9},{13,14},{14,13},{17,18},{18,... | collective-permute-start | bytes 479240 | tf_op jit(solution)/shard_map/ppermute | solution.py:155
  75.5 16.8 %collective-permute-start.26 = (bf16[1,2,2,160,256]{4,3,2,1,0:T(8,128)(2,1)S(1)}, bf16[1,2,2,160,256]{4,3,2,1,0:T(8,128)(2,1)S(1)}, u32[]{:S(2)}, u32[]{:S(2)}) collective-permute-start(bf16[1,2,2,160,256]{4,3,2,1,0:T(8,128)(2,1)S(1)} %collective-permute-done.25.rest_2_), channel_id=1, source_target_pairs={{0,4},{4,0},{8,12},{12,8},{16,20},{20,16},{24,28},{28,24},{1,5},{5... | collective-permute-start | bytes 983048 | tf_op jit(solution)/shard_map/ppermute | solution.py:146
  75.6 17.3 %collective-permute-start.28 = (bf16[1,2,2,160,256]{4,3,2,1,0:T(8,128)(2,1)S(1)}, bf16[1,2,2,160,256]{4,3,2,1,0:T(8,128)(2,1)S(1)}, u32[]{:S(2)}, u32[]{:S(2)}) collective-permute-start(bf16[1,2,2,160,256]{4,3,2,1,0:T(8,128)(2,1)S(1)} %collective-permute-done.27.rest_4_), channel_id=1, source_target_pairs={{0,4},{4,0},{8,12},{12,8},{16,20},{20,16},{24,28},{28,24},{1,5},{5... | collective-permute-start | bytes 983048 | tf_op jit(solution)/shard_map/ppermute | solution.py:146
  76.1 18.9 %collective-permute-start.30 = (bf16[1,2,2,160,256]{4,3,2,1,0:T(8,128)(2,1)}, bf16[1,2,2,160,256]{4,3,2,1,0:T(8,128)(2,1)S(1)}, u32[]{:S(2)}, u32[]{:S(2)}) collective-permute-start(bf16[1,2,2,160,256]{4,3,2,1,0:T(8,128)(2,1)} %collective-permute-done.29.rest_6_), channel_id=1, source_target_pairs={{0,4},{4,0},{8,12},{12,8},{16,20},{20,16},{24,28},{28,24},{1,5},{5... | collective-permute-start | bytes 983048 | tf_op jit(solution)/shard_map/ppermute | solution.py:146
  90.4 17.4 %collective-permute-start.14 = (bf16[1,2,2,160,256]{4,3,2,1,0:T(8,128)(2,1)}, bf16[1,2,2,160,256]{4,3,2,1,0:T(8,128)(2,1)S(1)}, u32[]{:S(2)}, u32[]{:S(2)}) collective-permute-start(bf16[1,2,2,160,256]{4,3,2,1,0:T(8,128)(2,1)} %collective-permute-done.13.rest_2_), channel_id=1, source_target_pairs={{0,4},{4,0},{8,12},{12,8},{16,20},{20,16},{24,28},{28,24},{1,5},{5... | collective-permute-start | bytes 983048 | tf_op jit(solution)/shard_map/ppermute | solution.py:146
  92.3 15.6 %collective-permute-start.16 = (bf16[1,2,2,160,256]{4,3,2,1,0:T(8,128)(2,1)}, bf16[1,2,2,160,256]{4,3,2,1,0:T(8,128)(2,1)S(1)}, u32[]{:S(2)}, u32[]{:S(2)}) collective-permute-start(bf16[1,2,2,160,256]{4,3,2,1,0:T(8,128)(2,1)} %collective-permute-done.15.rest_4_), channel_id=1, source_target_pairs={{0,4},{4,0},{8,12},{12,8},{16,20},{20,16},{24,28},{28,24},{1,5},{5... | collective-permute-start | bytes 983048 | tf_op jit(solution)/shard_map/ppermute | solution.py:146
  92.4 19.2 %collective-permute-start.18 = (bf16[1,2,2,160,256]{4,3,2,1,0:T(8,128)(2,1)}, bf16[1,2,2,160,256]{4,3,2,1,0:T(8,128)(2,1)S(1)}, u32[]{:S(2)}, u32[]{:S(2)}) collective-permute-start(bf16[1,2,2,160,256]{4,3,2,1,0:T(8,128)(2,1)} %collective-permute-done.17.rest_6_), channel_id=1, source_target_pairs={{0,4},{4,0},{8,12},{12,8},{16,20},{20,16},{24,28},{28,24},{1,5},{5... | collective-permute-start | bytes 983048 | tf_op jit(solution)/shard_map/ppermute | solution.py:146
  92.9 14.3 %collective-permute-start.57 = (bf16[624,128]{1,0:T(8,128)(2,1)S(1)}, bf16[624,128]{1,0:T(8,128)(2,1)S(1)}, u32[]{:S(2)}, u32[]{:S(2)}) collective-permute-start(bf16[624,128]{1,0:T(8,128)(2,1)S(1)} %collective-permute-done.55.p1), channel_id=1, source_target_pairs={{1,2},{2,1},{5,6},{6,5},{9,10},{10,9},{13,14},{14,13},{17,18},{18,... | collective-permute-start | bytes 479240 | tf_op jit(solution)/shard_map/ppermute | solution.py:155
  95.1 12.2 %collective-permute-start.58 = (bf16[624,128]{1,0:T(8,128)(2,1)S(1)}, bf16[624,128]{1,0:T(8,128)(2,1)S(1)}, u32[]{:S(2)}, u32[]{:S(2)}) collective-permute-start(bf16[624,128]{1,0:T(8,128)(2,1)S(1)} %collective-permute-done.56.p2), channel_id=1, source_target_pairs={{1,0},{2,3},{5,4},{6,7},{9,8},{10,11},{13,12},{14,15},{17,16},{18,... | collective-permute-start | bytes 479240 | tf_op jit(solution)/shard_map/ppermute | solution.py:155
  107.2 19.1 %collective-permute-start.2 = (bf16[1,2,2,160,256]{4,3,2,1,0:T(8,128)(2,1)S(1)}, bf16[1,2,2,160,256]{4,3,2,1,0:T(8,128)(2,1)S(1)}, u32[]{:S(2)}, u32[]{:S(2)}) collective-permute-start(bf16[1,2,2,160,256]{4,3,2,1,0:T(8,128)(2,1)S(1)} %collective-permute-done.1.rest_2_), channel_id=1, source_target_pairs={{0,4},{4,0},{8,12},{12,8},{16,20},{20,16},{24,28},{28,24},{1,5},{5... | collective-permute-start | bytes 983048 | tf_op jit(solution)/shard_map/ppermute | solution.py:146
  107.3 19.0 %collective-permute-start.4 = (bf16[1,2,2,160,256]{4,3,2,1,0:T(8,128)(2,1)S(1)}, bf16[1,2,2,160,256]{4,3,2,1,0:T(8,128)(2,1)S(1)}, u32[]{:S(2)}, u32[]{:S(2)}) collective-permute-start(bf16[1,2,2,160,256]{4,3,2,1,0:T(8,128)(2,1)S(1)} %collective-permute-done.3.rest_4_), channel_id=1, source_target_pairs={{0,4},{4,0},{8,12},{12,8},{16,20},{20,16},{24,28},{28,24},{1,5},{5... | collective-permute-start | bytes 983048 | tf_op jit(solution)/shard_map/ppermute | solution.py:146
  107.8 20.8 %collective-permute-start.6 = (bf16[1,2,2,160,256]{4,3,2,1,0:T(8,128)(2,1)S(1)}, bf16[1,2,2,160,256]{4,3,2,1,0:T(8,128)(2,1)S(1)}, u32[]{:S(2)}, u32[]{:S(2)}) collective-permute-start(bf16[1,2,2,160,256]{4,3,2,1,0:T(8,128)(2,1)S(1)} %collective-permute-done.5.rest_6_), channel_id=1, source_target_pairs={{0,4},{4,0},{8,12},{12,8},{16,20},{20,16},{24,28},{28,24},{1,5},{5... | collective-permute-start | bytes 983048 | tf_op jit(solution)/shard_map/ppermute | solution.py:146
  107.9 15.7 %collective-permute-start.45 = (bf16[624,128]{1,0:T(8,128)(2,1)S(1)}, bf16[624,128]{1,0:T(8,128)(2,1)S(1)}, u32[]{:S(2)}, u32[]{:S(2)}) collective-permute-start(bf16[624,128]{1,0:T(8,128)(2,1)S(1)} %collective-permute-done.43.p1), channel_id=1, source_target_pairs={{1,2},{2,1},{5,6},{6,5},{9,10},{10,9},{13,14},{14,13},{17,18},{18,... | collective-permute-start | bytes 479240 | tf_op jit(solution)/shard_map/ppermute | solution.py:155
  111.6 13.4 %collective-permute-start.46 = (bf16[624,128]{1,0:T(8,128)(2,1)S(1)}, bf16[624,128]{1,0:T(8,128)(2,1)S(1)}, u32[]{:S(2)}, u32[]{:S(2)}) collective-permute-start(bf16[624,128]{1,0:T(8,128)(2,1)S(1)} %collective-permute-done.44.p2), channel_id=1, source_target_pairs={{1,0},{2,3},{5,4},{6,7},{9,8},{10,11},{13,12},{14,15},{17,16},{18,... | collective-permute-start | bytes 479240 | tf_op jit(solution)/shard_map/ppermute | solution.py:155
  123.6 15.6 %collective-permute-start.59 = (bf16[624,128]{1,0:T(8,128)(2,1)S(1)}, bf16[624,128]{1,0:T(8,128)(2,1)S(1)}, u32[]{:S(2)}, u32[]{:S(2)}) collective-permute-start(bf16[624,128]{1,0:T(8,128)(2,1)S(1)} %collective-permute-done.57.p3), channel_id=1, source_target_pairs={{1,0},{2,3},{5,4},{6,7},{9,8},{10,11},{13,12},{14,15},{17,16},{18,... | collective-permute-start | bytes 479240 | tf_op jit(solution)/shard_map/ppermute | solution.py:155
  125.0 18.2 %collective-permute-start.47 = (bf16[624,128]{1,0:T(8,128)(2,1)S(1)}, bf16[624,128]{1,0:T(8,128)(2,1)S(1)}, u32[]{:S(2)}, u32[]{:S(2)}) collective-permute-start(bf16[624,128]{1,0:T(8,128)(2,1)S(1)} %collective-permute-done.45.p3), channel_id=1, source_target_pairs={{1,0},{2,3},{5,4},{6,7},{9,8},{10,11},{13,12},{14,15},{17,16},{18,... | collective-permute-start | bytes 479240 | tf_op jit(solution)/shard_map/ppermute | solution.py:155
  126.3 17.5 %collective-permute-start.31 = (bf16[624,256]{1,0:T(8,128)(2,1)S(1)}, bf16[624,256]{1,0:T(8,128)(2,1)S(1)}, u32[]{:S(2)}, u32[]{:S(2)}) collective-permute-start(bf16[624,256]{1,0:T(8,128)(2,1)S(1)} %bitcast.45), channel_id=1, source_target_pairs={{0,1},{1,0},{2,3},{3,2},{4,5},{5,4},{6,7},{7,6},{8,9},{9,8},{10,11... | collective-permute-start | bytes 958472 | tf_op jit(solution)/shard_map/ppermute | solution.py:155
  126.4 20.1 %collective-permute-start.32 = (bf16[624,256]{1,0:T(8,128)(2,1)S(1)}, bf16[624,256]{1,0:T(8,128)(2,1)S(1)}, u32[]{:S(2)}, u32[]{:S(2)}) collective-permute-start(bf16[624,256]{1,0:T(8,128)(2,1)S(1)} %bitcast.46), channel_id=1, source_target_pairs={{1,2},{2,1},{5,6},{6,5},{9,10},{10,9},{13,14},{14,13},{17,18},{18,... | collective-permute-start | bytes 958472 | tf_op jit(solution)/shard_map/ppermute | solution.py:155
  128.6 21.1 %collective-permute-start.19 = (bf16[624,256]{1,0:T(8,128)(2,1)S(1)}, bf16[624,256]{1,0:T(8,128)(2,1)S(1)}, u32[]{:S(2)}, u32[]{:S(2)}) collective-permute-start(bf16[624,256]{1,0:T(8,128)(2,1)S(1)} %bitcast.48), channel_id=1, source_target_pairs={{0,1},{1,0},{2,3},{3,2},{4,5},{5,4},{6,7},{7,6},{8,9},{9,8},{10,11... | collective-permute-start | bytes 958472 | tf_op jit(solution)/shard_map/ppermute | solution.py:155
  139.9 12.5 %collective-permute-start.20 = (bf16[624,256]{1,0:T(8,128)(2,1)S(1)}, bf16[624,256]{1,0:T(8,128)(2,1)S(1)}, u32[]{:S(2)}, u32[]{:S(2)}) collective-permute-start(bf16[624,256]{1,0:T(8,128)(2,1)S(1)} %bitcast.49), channel_id=1, source_target_pairs={{1,2},{2,1},{5,6},{6,5},{9,10},{10,9},{13,14},{14,13},{17,18},{18,... | collective-permute-start | bytes 958472 | tf_op jit(solution)/shard_map/ppermute | solution.py:155
  143.8 10.6 %collective-permute-start.7 = (bf16[624,256]{1,0:T(8,128)(2,1)S(1)}, bf16[624,256]{1,0:T(8,128)(2,1)S(1)}, u32[]{:S(2)}, u32[]{:S(2)}) collective-permute-start(bf16[624,256]{1,0:T(8,128)(2,1)S(1)} %bitcast.42), channel_id=1, source_target_pairs={{0,1},{1,0},{2,3},{3,2},{4,5},{5,4},{6,7},{7,6},{8,9},{9,8},{10,11... | collective-permute-start | bytes 958472 | tf_op jit(solution)/shard_map/ppermute | solution.py:155
  143.8 19.0 %collective-permute-start.8 = (bf16[624,256]{1,0:T(8,128)(2,1)S(1)}, bf16[624,256]{1,0:T(8,128)(2,1)S(1)}, u32[]{:S(2)}, u32[]{:S(2)}) collective-permute-start(bf16[624,256]{1,0:T(8,128)(2,1)S(1)} %bitcast.43), channel_id=1, source_target_pairs={{1,2},{2,1},{5,6},{6,5},{9,10},{10,9},{13,14},{14,13},{17,18},{18,... | collective-permute-start | bytes 958472 | tf_op jit(solution)/shard_map/ppermute | solution.py:155
  146.5 19.6 %collective-permute-start.33 = (bf16[624,256]{1,0:T(8,128)(2,1)S(1)}, bf16[624,256]{1,0:T(8,128)(2,1)}, u32[]{:S(2)}, u32[]{:S(2)}) collective-permute-start(bf16[624,256]{1,0:T(8,128)(2,1)S(1)} %collective-permute-done.31.p1), channel_id=1, source_target_pairs={{1,2},{2,1},{5,6},{6,5},{9,10},{10,9},{13,14},{14,13},{17,18},{18,... | collective-permute-start | bytes 958472 | tf_op jit(solution)/shard_map/ppermute | solution.py:155
  149.7 23.1 %collective-permute-start.21 = (bf16[624,256]{1,0:T(8,128)(2,1)S(1)}, bf16[624,256]{1,0:T(8,128)(2,1)S(1)}, u32[]{:S(2)}, u32[]{:S(2)}) collective-permute-start(bf16[624,256]{1,0:T(8,128)(2,1)S(1)} %collective-permute-done.19.p1), channel_id=1, source_target_pairs={{1,2},{2,1},{5,6},{6,5},{9,10},{10,9},{13,14},{14,13},{17,18},{18,... | collective-permute-start | bytes 958472 | tf_op jit(solution)/shard_map/ppermute | solution.py:155
  152.4 26.1 %collective-permute-start.34 = (bf16[624,256]{1,0:T(8,128)(2,1)S(1)}, bf16[624,256]{1,0:T(8,128)(2,1)}, u32[]{:S(2)}, u32[]{:S(2)}) collective-permute-start(bf16[624,256]{1,0:T(8,128)(2,1)S(1)} %collective-permute-done.32.p2), channel_id=1, source_target_pairs={{1,0},{2,3},{5,4},{6,7},{9,8},{10,11},{13,12},{14,15},{17,16},{18,... | collective-permute-start | bytes 958472 | tf_op jit(solution)/shard_map/ppermute | solution.py:155
  154.4 25.4 %collective-permute-start.9 = (bf16[624,256]{1,0:T(8,128)(2,1)S(1)}, bf16[624,256]{1,0:T(8,128)(2,1)S(1)}, u32[]{:S(2)}, u32[]{:S(2)}) collective-permute-start(bf16[624,256]{1,0:T(8,128)(2,1)S(1)} %collective-permute-done.7.p1), channel_id=1, source_target_pairs={{1,2},{2,1},{5,6},{6,5},{9,10},{10,9},{13,14},{14,13},{17,18},{18,... | collective-permute-start | bytes 958472 | tf_op jit(solution)/shard_map/ppermute | solution.py:155
  162.8 35.7 %collective-permute-start.22 = (bf16[624,256]{1,0:T(8,128)(2,1)S(1)}, bf16[624,256]{1,0:T(8,128)(2,1)}, u32[]{:S(2)}, u32[]{:S(2)}) collective-permute-start(bf16[624,256]{1,0:T(8,128)(2,1)S(1)} %collective-permute-done.20.p2), channel_id=1, source_target_pairs={{1,0},{2,3},{5,4},{6,7},{9,8},{10,11},{13,12},{14,15},{17,16},{18,... | collective-permute-start | bytes 958472 | tf_op jit(solution)/shard_map/ppermute | solution.py:155
  166.1 28.1 %collective-permute-start.35 = (bf16[624,256]{1,0:T(8,128)(2,1)}, bf16[624,256]{1,0:T(8,128)(2,1)}, u32[]{:S(2)}, u32[]{:S(2)}) collective-permute-start(bf16[624,256]{1,0:T(8,128)(2,1)} %collective-permute-done.33.p3), channel_id=1, source_target_pairs={{1,0},{2,3},{5,4},{6,7},{9,8},{10,11},{13,12},{14,15},{17,16},{18,... | collective-permute-start | bytes 958472 | tf_op jit(solution)/shard_map/ppermute | solution.py:155
  172.8 25.7 %collective-permute-start.23 = (bf16[624,256]{1,0:T(8,128)(2,1)S(1)}, bf16[624,256]{1,0:T(8,128)(2,1)}, u32[]{:S(2)}, u32[]{:S(2)}) collective-permute-start(bf16[624,256]{1,0:T(8,128)(2,1)S(1)} %collective-permute-done.21.p3), channel_id=1, source_target_pairs={{1,0},{2,3},{5,4},{6,7},{9,8},{10,11},{13,12},{14,15},{17,16},{18,... | collective-permute-start | bytes 958472 | tf_op jit(solution)/shard_map/ppermute | solution.py:155
  178.5 24.1 %collective-permute-start.10 = (bf16[624,256]{1,0:T(8,128)(2,1)S(1)}, bf16[624,256]{1,0:T(8,128)(2,1)S(1)}, u32[]{:S(2)}, u32[]{:S(2)}) collective-permute-start(bf16[624,256]{1,0:T(8,128)(2,1)S(1)} %collective-permute-done.8.p2), channel_id=1, source_target_pairs={{1,0},{2,3},{5,4},{6,7},{9,8},{10,11},{13,12},{14,15},{17,16},{18,... | collective-permute-start | bytes 958472 | tf_op jit(solution)/shard_map/ppermute | solution.py:155
  179.8 22.8 %collective-permute-start.11 = (bf16[624,256]{1,0:T(8,128)(2,1)S(1)}, bf16[624,256]{1,0:T(8,128)(2,1)S(1)}, u32[]{:S(2)}, u32[]{:S(2)}) collective-permute-start(bf16[624,256]{1,0:T(8,128)(2,1)S(1)} %collective-permute-done.9.p3), channel_id=1, source_target_pairs={{1,0},{2,3},{5,4},{6,7},{9,8},{10,11},{13,12},{14,15},{17,16},{18,... | collective-permute-start | bytes 958472 | tf_op jit(solution)/shard_map/ppermute | solution.py:155
  (68 other events, 696.1 us)

commit v2 on v1

v2 whole, which is shorter than its diff:
```python
import math
from functools import partial

import jax
import jax.numpy as jnp
from jax import lax
from jax.experimental import pallas as pl
from jax.experimental.pallas import tpu as pltpu
from jax.sharding import PartitionSpec as P

HD = 128
NEG_FILL = -1e30
HEAD_CHUNKS = (1, 1, 2, 2, 2)


K_FLOPS = 2_700_000_000
J_FLOPS = 2_000_000_000
GATE = (1, 1, 1)


def cost(flops):
    return pl.CostEstimate(flops=flops, bytes_accessed=1000, transcendentals=0)


SCALE = 1.0 / math.sqrt(HD)
VMEM_BYTES = 6 * 1024 * 1024


def attend_kernel(idx_ref, q_ref, tree_ref, bias_ref, *rest, n_caches):
    cache_refs = rest[:n_caches]
    out_ref, held, sems = rest[n_caches:]
    copies = []
    at = 0
    for i, ref in enumerate(cache_refs):
        size = ref.shape[0]
        copies.append(pltpu.make_async_copy(ref, held.at[pl.ds(at, size)], sems.at[i]))
        at += size
    for copy in copies:
        copy.start()
    for copy in copies:
        copy.wait()
    requests, _, width = q_ref.shape
    padded = held.shape[3]
    n_keys = bias_ref.shape[2]
    position = lax.broadcasted_iota(jnp.int32, (1, n_keys), 1).astype(jnp.float32)
    repeats = -(-n_keys // HD)

    def length_row(block, part):
        tail = held[block, part, 0, pl.ds(padded - 16, 16), 0:HD].astype(jnp.float32)[15:16]
        return jnp.concatenate([tail] * repeats, axis=1)[:, :n_keys]

    def body(r, carry):
        first = idx_ref[0, r]
        second = idx_ref[1, r]
        limit = jnp.where(position < padded, length_row(first, 0), length_row(second, 1) + padded)
        limit = jnp.where(position < 2 * padded, limit, n_keys)
        bias = bias_ref[r] + jnp.where(position < limit, 0.0, NEG_FILL)
        for h in range(width // HD):
            cols = slice(h * HD, (h + 1) * HD)
            keys = jnp.concatenate(
                [held[first, 0, 0, :, cols], held[second, 1, 0, :, cols], tree_ref[r, 0, :, cols]], axis=0
            )
            values = jnp.concatenate(
                [held[first, 0, 1, :, cols], held[second, 1, 1, :, cols], tree_ref[r, 1, :, cols]], axis=0
            )
            scores = lax.dot_general(
                q_ref[r, :, cols], keys, (((1,), (1,)), ((), ())), preferred_element_type=jnp.float32
            )
            scores = scores * SCALE + bias
            raw = jnp.exp(scores - jnp.max(scores, axis=1, keepdims=True))
            total = jnp.sum(raw, axis=1, keepdims=True)
            accum = jnp.dot(raw.astype(jnp.bfloat16), values, preferred_element_type=jnp.float32)
            out_ref[r, :, cols] = (accum / total).astype(out_ref.dtype)
        return carry

    lax.fori_loop(0, requests, body, 0)


def attend(idx, queries, tree_cache, bias, caches, start, width):
    req, tree, _ = queries.shape
    block = start // width
    n_blocks = sum(c.shape[0] for c in caches)
    keys = bias.shape[2]
    return pl.pallas_call(
        partial(attend_kernel, n_caches=len(caches)),
        grid=(1,),
        in_specs=[
            pl.BlockSpec(memory_space=pltpu.SMEM),
            pl.BlockSpec((req, tree, width), lambda i: (0, 0, block)),
            pl.BlockSpec((req, 2, tree, width), lambda i: (0, 0, 0, block)),
            pl.BlockSpec(bias.shape, lambda i: (0, 0, 0)),
        ]
        + [pl.BlockSpec(memory_space=pl.ANY)] * len(caches),
        out_specs=pl.BlockSpec((req, tree, width), lambda i: (0, 0, 0)),
        out_shape=jax.ShapeDtypeStruct((req, tree, width), jnp.bfloat16),
        scratch_shapes=[
            pltpu.VMEM((n_blocks,) + caches[0].shape[1:], jnp.bfloat16),
            pltpu.SemaphoreType.DMA((len(caches),)),
        ],
        compiler_params=pltpu.CompilerParams(vmem_limit_bytes=8 * VMEM_BYTES),
        cost_estimate=pl.CostEstimate(
            flops=4 * req * tree * keys * width * 16, bytes_accessed=8 * n_blocks * 320 * width, transcendentals=0
        ),
    )(idx, queries, tree_cache, bias, *caches)


def paired_kernel(slot_ref, *rest, start, inside, n_caches):
    sides, caches, outs = rest[:6], rest[6 : 6 + n_caches], rest[6 + n_caches :]
    width = outs[0].shape[2]
    tree = outs[0].shape[1]
    padded = caches[0].shape[2]
    n_keys = 2 * tree + 2 * padded
    position = lax.broadcasted_iota(jnp.int32, (1, n_keys), 1).astype(jnp.float32)
    repeats = -(-n_keys // HD)

    def length_row(ref, part):
        tail = ref[part, 0, padded - 16 : padded, 0:HD].astype(jnp.float32)[15:16]
        return jnp.concatenate([tail] * repeats, axis=1)[:, :n_keys]

    lane = lax.broadcasted_iota(jnp.int32, (tree, HD), 1)
    for m, cache in enumerate(caches):
        spill_at = 2 * tree + padded
        limit = jnp.where(position < spill_at, length_row(cache, 0) + 2 * tree, length_row(cache, 1) + spill_at)
        limit = jnp.where(position < 2 * tree, n_keys, limit)
        unseen = jnp.where(position < limit, 0.0, NEG_FILL)
        for side in range(2):
            q_ref, tree_ref, bias_ref = sides[3 * side : 3 * side + 3]
            out_ref = outs[side]
            r0, r1, used = [slot_ref[3 * side + k, m] for k in range(3)]
            used = used > 0
            rolled = jnp.where(lane < tree, NEG_FILL, pltpu.roll(bias_ref[r1], tree, 1))
            rolled = jnp.where(lane < 2 * tree, rolled, 0.0)
            head_bias = jnp.concatenate([bias_ref[r0], rolled], axis=0) + unseen[:, :HD]
            bias = jnp.concatenate(
                [head_bias, jnp.broadcast_to(unseen[:, HD:], (2 * tree, n_keys - HD))], axis=1
            )
            for h in range(width // HD):
                here = slice(h * HD, (h + 1) * HD)
                held = slice(inside + h * HD, inside + (h + 1) * HD)
                cols = slice(start + h * HD, start + (h + 1) * HD)

                def stored(k):
                    return jnp.concatenate(
                        [tree_ref[r0, k, :, cols], tree_ref[r1, k, :, cols], cache[0, k, :, held], cache[1, k, :, held]],
                        axis=0,
                    )

                both = jnp.concatenate([q_ref[r0, :, cols], q_ref[r1, :, cols]], axis=0)
                scores = lax.dot_general(
                    both, stored(0), (((1,), (1,)), ((), ())), preferred_element_type=jnp.float32
                )
                scores = scores * SCALE + bias
                raw = jnp.exp(scores - jnp.max(scores, axis=1, keepdims=True))
                total = jnp.sum(raw, axis=1, keepdims=True)
                accum = jnp.dot(raw.astype(jnp.bfloat16), stored(1), preferred_element_type=jnp.float32)
                attn = (accum / total).astype(out_ref.dtype)
                out_ref[r0, :, here] = jnp.where(used, attn[:tree], out_ref[r0, :, here])
                out_ref[r1, :, here] = jnp.where(used, attn[tree:], out_ref[r1, :, here])


def attend_pairs(slots, sides, caches, start, inside, width):
    req, tree, _ = sides[0].shape
    vmem = pl.BlockSpec(memory_space=pltpu.VMEM)
    return pl.pallas_call(
        partial(paired_kernel, start=start, inside=inside, n_caches=len(caches)),
        in_specs=[pl.BlockSpec(memory_space=pltpu.SMEM)] + [vmem] * (len(sides) + len(caches)),
        out_specs=[vmem, vmem],
        out_shape=[jax.ShapeDtypeStruct((req, tree, width), jnp.bfloat16)] * 2,
        compiler_params=pltpu.CompilerParams(vmem_limit_bytes=VMEM_BYTES),
        cost_estimate=cost(K_FLOPS + K_FLOPS * width // HD),
    )(slots, *sides, *caches)


def project_kernel(z_ref, w_hbm, *rest, parts, counts):
    has_own, has_middle, has_acc = counts
    rest = list(rest)
    own = rest.pop(0) if has_own else None
    outer = rest.pop(0)
    between = rest.pop(0) if has_middle else None
    acc = rest.pop(0) if has_acc else None
    out_ref, w_ref, sems = rest
    z = z_ref[0]
    lower = z < 2
    sources = (z, jnp.bitwise_xor(z, 1), jnp.where(lower, 2, 1), jnp.where(lower, 3, 0))
    tile = w_ref.shape[2]
    tiles = w_ref.shape[0]
    copies = []
    for n in range(tiles):
        at = 0
        for which, start, width in parts:
            copies.append(
                pltpu.make_async_copy(
                    w_hbm.at[sources[which], pl.ds(start, width), pl.ds(n * tile, tile)],
                    w_ref.at[n, pl.ds(at, width), :],
                    sems.at[len(copies)],
                )
            )
            at += width
    for copy in copies:
        copy.start()
    pieces = [own[...]] if has_own else []
    fresh = own.shape[1] if has_own else 0
    if has_own:
        pieces.append(outer[:, :fresh])
    if has_middle:
        middle = jnp.logical_and(z > 0, z < 3)
        pieces.append(jnp.where(middle, between[...], outer[:, fresh:]))
    attn = jnp.concatenate(pieces, axis=1)
    for n in range(tiles):
        for copy in copies[n * len(parts) : (n + 1) * len(parts)]:
            copy.wait()
        cols = slice(n * tile, (n + 1) * tile)
        total = jnp.dot(attn, w_ref[n], preferred_element_type=jnp.float32)
        if has_acc:
            total += acc[:, cols]
        out_ref[:, cols] = total.astype(out_ref.dtype)


def project(z, weight, own, outer, between, acc, parts, last):
    _, _, cols = weight.shape
    rows = outer.shape[0]
    depth = sum(width for _, _, width in parts)
    tile = 256
    tiles = cols // tile
    given = [v for v in (own, outer, between, acc) if v is not None]
    in_place = {1 + len(given): 0} if acc is not None and not last else {}
    vmem = pl.BlockSpec(memory_space=pltpu.VMEM)
    return pl.pallas_call(
        partial(
            project_kernel, parts=parts, counts=(own is not None, between is not None, acc is not None)
        ),
        in_specs=[pl.BlockSpec(memory_space=pltpu.SMEM), pl.BlockSpec(memory_space=pltpu.HBM)] + [vmem] * len(given),
        out_specs=vmem,
        out_shape=jax.ShapeDtypeStruct((rows, cols), jnp.bfloat16 if last else jnp.float32),
        scratch_shapes=[
            pltpu.VMEM((tiles, depth, tile), jnp.bfloat16),
            pltpu.SemaphoreType.DMA((tiles * len(parts),)),
        ],
        input_output_aliases=in_place,
        compiler_params=pltpu.CompilerParams(vmem_limit_bytes=VMEM_BYTES),
        cost_estimate=cost(J_FLOPS),
    )(z, weight, *given)


def cache_block(prompt, spill, lens, start, width, padded):
    both = jnp.stack([prompt[0, ..., start : start + width], spill[0, ..., start : start + width]])
    both = jnp.pad(both, ((0, 0), (0, 0), (0, padded - both.shape[2]), (0, 0)))
    row = lax.broadcasted_iota(jnp.int32, both.shape, 2)
    return jnp.where(row == padded - 1, lens[:, None, None, None], both)


def across(value, mask):
    return lax.ppermute(value, "rep", [(i, i ^ mask) for i in range(lax.axis_size("rep"))])


def along(value, pairs):
    return lax.ppermute(value, "tp", pairs)


def after(value, *earlier):
    return lax.optimization_barrier((value, *earlier))[0]


def pair_slots(group, blocks):
    match = blocks[:, None] == group[None, :]
    order = jnp.arange(group.shape[0], dtype=jnp.int32)[None, :]
    lowest = jnp.min(jnp.where(match, order, group.shape[0]), axis=1)
    highest = jnp.max(jnp.where(match, order, -1), axis=1)
    used = highest >= 0
    return [jnp.where(used, lowest, 0), jnp.where(used, highest, 0), used.astype(jnp.int32)]


def pair_bias(tree_mask):
    bias = jnp.where(tree_mask == 1, 0.0, NEG_FILL).astype(jnp.float32)
    tree = bias.shape[1]
    bias = jnp.pad(bias, ((0, 0), (0, 0), (0, tree)), constant_values=NEG_FILL)
    return jnp.pad(bias, ((0, 0), (0, 0), (0, HD - 2 * tree)))


def local(
    queries,
    tree_cache,
    tree_mask,
    dest_group,
    accepted_path,
    prompt_cache,
    first_len,
    spill_cache,
    spill_len,
    out_weight,
    *,
    tuned,
):
    req, tree, cols = queries.shape
    prompt = prompt_cache.shape[2]
    padded = (prompt // 16 + 1) * 16
    group = dest_group[:, 0]

    if not tuned:
        accepted_cache = jnp.take_along_axis(tree_cache, accepted_path[:, None, :, None], axis=2)
        lens = jnp.stack([first_len[0], spill_len[0]]).astype(jnp.bfloat16)
        idx = jnp.stack([group, jnp.bitwise_xor(group, 1)])
        bias = jnp.where(tree_mask == 1, 0.0, NEG_FILL).astype(jnp.float32)
        bias = jnp.pad(bias, ((0, 0), (0, 0), (2 * padded, 0)))
        block = cache_block(prompt_cache, spill_cache, lens, 0, cols, padded)
        caches = lax.all_gather(block, "rep", axis=0, tiled=False)
        attn = attend(idx, queries, tree_cache, bias, [caches], 0, cols).reshape(req * tree, cols)
        whole = lax.all_gather(attn, "tp", axis=1, tiled=True)
        summed = jnp.dot(whole, out_weight, preferred_element_type=jnp.float32)
        return summed.astype(jnp.bfloat16).reshape(req, tree, out_weight.shape[1]), accepted_cache

    spill = across(spill_cache, 1)
    lens = jnp.stack([first_len[0], across(spill_len, 1)[0]]).astype(jnp.bfloat16)
    other_queries = across(queries, 1)
    other_tree = across(tree_cache, 1)
    other_mask = across(tree_mask, 1)
    other_group = across(dest_group, 1)

    chunks = []
    start = 0
    for heads in HEAD_CHUNKS:
        chunks.append((start, heads * HD))
        start += heads * HD
    n = len(chunks)
    gathered, owns, raws = [], [], []

    def gather(i):
        start, width = chunks[i]
        block = cache_block(prompt_cache, spill, lens, start, width, padded)
        if i > 0:
            block = after(block, *gathered[i - 1][1:], *raws[max(i - 2, 0) : i - 1])
        gathered.append([block] + [across(block, m) for m in (2, 4, 6)])

    gather(0)
    group, other_group, tree_mask, other_mask = lax.optimization_barrier(
        (group, other_group[:, 0], tree_mask, other_mask, gathered[0][0])
    )[:4]
    me = lax.axis_index("rep").astype(jnp.int32)
    blocks = jnp.bitwise_xor(me, jnp.array([0, 2, 4, 6], jnp.int32))
    slots = jnp.stack(pair_slots(group, blocks) + pair_slots(other_group, blocks))
    sides = [queries, tree_cache, pair_bias(tree_mask), other_queries, other_tree, pair_bias(other_mask)]
    mine = jnp.bitwise_and(jnp.bitwise_xor(group, me), 1) == 0

    z = lax.axis_index("tp").astype(jnp.int32).reshape(1)
    weight = out_weight.reshape(lax.axis_size("tp"), cols, out_weight.shape[1])
    acc = None
    accs, outer, between = [], [], []
    for i in range(n + 2):
        fresh = []
        if i < n:
            start, width = chunks[i]
            ready = slots
            if i > 0:
                gates = [owns[i - 1]] + between[max(i - 2, 0) : i - 1] + accs[max(i - 3, 0) : i - 2]
                ready = after(slots, *gates)
            own, theirs = attend_pairs(ready, sides, gathered[i], start, 0, width)
            raws.append(theirs)
            if i + 1 < n:
                gather(i + 1)
                if GATE[0]:
                    theirs = after(theirs, *gathered[i + 1][1:])
            if i > 0 and GATE[1]:
                theirs = after(theirs, between[i - 1])
            if i > 0 and GATE[2]:
                theirs = after(theirs, outer[i - 1])
            attn = jnp.where(mine[:, None, None], own, across(theirs, 1)).reshape(req * tree, width)
            owns.append(attn)
            fresh = [attn]
        payload = fresh + ([between[i - 1]] if i > 0 else [])
        payload = jnp.concatenate(payload, axis=1)
        if i > 1:
            payload = after(payload, accs[i - 2])
        outer.append(along(payload, [(0, 1), (1, 0), (2, 3), (3, 2)] if i < n else [(1, 0), (2, 3)]))
        if i <= n:
            relayed = [outer[i - 1][:, : chunks[i - 1][1]]] if i > 0 else []
            between.append(along(jnp.concatenate(fresh + relayed, axis=1), [(1, 2), (2, 1)]))
        parts = [(0, *chunks[i]), (1, *chunks[i])] if i < n else []
        parts += [(2, *chunks[i - 1])] if 0 < i <= n else []
        parts += [(3, *chunks[i - 2])] if i > 1 else []
        acc = project(
            z, weight, owns[i] if i < n else None, outer[i], between[i - 1] if i > 0 else None, acc, parts, i == n + 1
        )
        accs.append(acc)
    path = after(accepted_path, owns[-1])
    accepted_cache = jnp.take_along_axis(tree_cache, path[:, None, :, None], axis=2)
    return acc.reshape(req, tree, out_weight.shape[1]), accepted_cache


def solution(mesh):
    heads_here = 32 // mesh.shape["tp"]
    tuned = mesh.shape["rep"] == 8 and mesh.shape["tp"] == 4 and heads_here == sum(HEAD_CHUNKS)
    return jax.shard_map(
        partial(local, tuned=tuned),
        mesh=mesh,
        in_specs=(
            P("rep", None, "tp"),
            P("rep", None, None, "tp"),
            P("rep", None, None),
            P("rep", None),
            P("rep", None),
            P("rep", None, None, "tp"),
            P("rep"),
            P("rep", None, None, "tp"),
            P("rep"),
            P(None, "tp"),
        ),
        out_specs=(P("rep", None, "tp"), P("rep", None, None, "tp")),
        check_vma=False,
    )
```

time: 209 us -> 173 us (0.83)
  the two profiles are of different devices: /device:TPU:10 before, /device:TPU:0 now
where the time goes in v2:
time: 173 us; the launch traced here: 172 us
  Pallas kernels  52.4 us (30%)
  starting transfers between devices  42.5 us (25%)
  waiting for transfers between devices  33.3 us (19%)
  local copies, waits for them, and re-layouts  32.8 us (19%)
  other arithmetic  8.43 us (5%)
  between operations  2.9 us (2%)
    pallas_call x5, Pallas kernels, attend_pairs(): pl.pallas_call(partial(paired_kernel, start=start, inside=inside, n_cache...  30.8 us
    unnamed x95, local copies, waits for them, and re-layouts  22.9 us
    ppermute x13, starting transfers between devices, along(): return lax.ppermute(value, 'tp', pairs)  22 us
    pallas_call x7, Pallas kernels, project(): pl.pallas_call(partial(project_kernel, parts=parts, counts=(own is not No...  21.6 us
    ppermute x13, waiting for transfers between devices, along(): return lax.ppermute(value, 'tp', pairs)  20.7 us
    ppermute x26, starting transfers between devices, across(): lax.ppermute(value, 'rep', [(i, i ^ mask) for i in range(lax.axis_size('r...  20.5 us
    ppermute x26, waiting for transfers between devices, across(): lax.ppermute(value, 'rep', [(i, i ^ mask) for i in range(lax.axis_size('r...  12.5 us
    gather x3, local copies, waits for them, and re-layouts, local(): jnp.take_along_axis(tree_cache, path[:, None, :, None], axis=2)  5.88 us
  transfers between devices with their start and end apart: 39, of which 13 were waited for; matrix products, arithmetic and copies ran while one was open for 10% of the time, Pallas kernels for 29%

profile of v2, /device:TPU:0, one launch (start us, length us, event | category | flops | bytes accessed | tf_op | source)
XLA Modules:
  0.0 172.2 jit_solution(6625122390767381769)
XLA Ops:
  6.8 2.9 %collective-permute-start.6 = (bf16[2,2,160,128]{3,2,1,0:T(8,128)(2,1)}, bf16[2,2,160,128]{3,2,1,0:T(8,128)(2,1)}, u32[]{:S(2)}, u32[]{:S(2)}) collective-permute-start(bf16[2,2,160,128]{3,2,1,0:T(8,128)(2,1)} %get-tuple-element.108.rest_6_), channel_id=1, source_target_pairs={{0,8},{4,12},{8,0},{12,4},{16,24},{20,28},{24,16},{28,20},{1,9},{5... | collective-permute-start | bytes 491528 | tf_op jit(solution)/shard_map/ppermute | solution.py:253
  9.7 1.5 collective-permute-start.7
  11.5 1.2 fusion.12
  13.6 1.3 pad_select_fusion.rest_5_
  15.0 4.4 %collective-permute-done.7.rest_8_ = bf16[2,2,160,128]{3,2,1,0:T(8,128)(2,1)} collective-permute-done((bf16[2,2,160,128]{3,2,1,0:T(8,128)(2,1)}, bf16[2,2,160,128]{3,2,1,0:T(8,128)(2,1)}, u32[]{:S(2)}, u32[]{:S(2)}) %collective-permute-start.7) | collective-permute-done | bytes 163872 | tf_op jit(solution)/shard_map/ppermute | solution.py:253
  19.4 1.2 collective-permute-start.9
  21.5 1.4 collective-permute-start.11
  22.9 1.3 copy-done.32
  24.3 4.7 %shard_map.122 = (bf16[13,48,128]{2,1,0:T(8,128)(2,1)S(1)}, bf16[13,48,128]{2,1,0:T(8,128)(2,1)S(1)}) custom-call(s32[6,4]{1,0:T(8,128)S(1)} %stack.29.slot_ref, bf16[13,48,1024]{2,1,0:T(8,128)(2,1)S(1)} %copy-done.32, bf16[13,2,48,1024]{3,2,1,0:T(8,128)(2,1)S(1)} %copy-done.4, f32[13,48,128]{2,1,0:T(8,128)S(1)} %fusion.17.rest_2_, ...), custom_call_target="tpu_custom_call" | custom-call | flops 5400000000 | bytes 1000 | tf_op jit(solution)/shard_map/pallas_call | solution.py:164
  29.2 1.2 collective-permute-start.13
  31.4 1.4 collective-permute-start.15
  33.6 4.5 %collective-permute-start.17 = (bf16[624,128]{1,0:T(8,128)(2,1)S(1)}, bf16[624,128]{1,0:T(8,128)(2,1)S(1)}, u32[]{:S(2)}, u32[]{:S(2)}) collective-permute-start(bf16[624,128]{1,0:T(8,128)(2,1)S(1)} %bitcast.53), channel_id=1, source_target_pairs={{0,1},{1,0},{2,3},{3,2},{4,5},{5,4},{6,7},{7,6},{8,9},{9,8},{10,11... | collective-permute-start | bytes 479240 | tf_op jit(solution)/shard_map/ppermute | solution.py:257
  38.0 4.5 %shard_map.123 = (bf16[13,48,128]{2,1,0:T(8,128)(2,1)S(1)}, bf16[13,48,128]{2,1,0:T(8,128)(2,1)S(1)}) custom-call(s32[6,4]{1,0:T(8,128)S(1)} %stack.29.slot_ref, bf16[13,48,1024]{2,1,0:T(8,128)(2,1)S(1)} %copy-done.33, bf16[13,2,48,1024]{3,2,1,0:T(8,128)(2,1)S(1)} %copy-done.4, f32[13,48,128]{2,1,0:T(8,128)S(1)} %fusion.17.rest_2_, ...), custom_call_target="tpu_custom_call" | custom-call | flops 5400000000 | bytes 1000 | tf_op jit(solution)/shard_map/pallas_call | solution.py:164
  42.6 3.2 %collective-permute-done.14.rest_8_ = bf16[2,2,160,256]{3,2,1,0:T(8,128)(2,1)S(1)} collective-permute-done((bf16[2,2,160,256]{3,2,1,0:T(8,128)(2,1)S(1)}, bf16[2,2,160,256]{3,2,1,0:T(8,128)(2,1)S(1)}, u32[]{:S(2)}, u32[]{:S(2)}) %collective-permute-start.14) | collective-permute-done | bytes 327712 | tf_op jit(solution)/shard_map/ppermute | solution.py:253
  45.8 1.4 collective-permute-done.15.rest_9_
  48.3 1.4 collective-permute-start.20
  51.7 4.4 %collective-permute-start.23 = (bf16[624,256]{1,0:T(8,128)(2,1)S(1)}, bf16[624,256]{1,0:T(8,128)(2,1)S(1)}, u32[]{:S(2)}, u32[]{:S(2)}) collective-permute-start(bf16[624,256]{1,0:T(8,128)(2,1)S(1)} %get-tuple-element.102), channel_id=1, source_target_pairs={{0,1},{1,0},{2,3},{3,2},{4,5},{5,4},{6,7},{7,6},{8,9},{9,8},{10,11... | collective-permute-start | bytes 958472 | tf_op jit(solution)/shard_map/ppermute | solution.py:257
  56.2 7.5 %shard_map.124 = (bf16[13,48,256]{2,1,0:T(8,128)(2,1)S(1)}, bf16[13,48,256]{2,1,0:T(8,128)(2,1)}) custom-call(s32[6,4]{1,0:T(8,128)S(1)} %stack.29.slot_ref, bf16[13,48,1024]{2,1,0:T(8,128)(2,1)S(1)} %copy-done.33, bf16[13,2,48,1024]{3,2,1,0:T(8,128)(2,1)S(1)} %copy-done.4, f32[13,48,128]{2,1,0:T(8,128)S(1)} %copy-done.26, ...), custom_call_target="tpu_custom_call" | custom-call | flops 8099999744 | bytes 1000 | tf_op jit(solution)/shard_map/pallas_call | solution.py:164
  66.9 3.4 %copy-done = bf16[4096,1024]{1,0:T(8,128)(2,1)S(1)} copy-done((bf16[4096,1024]{1,0:T(8,128)(2,1)S(1)}, bf16[4096,1024]{1,0:T(8,128)(2,1)}, u32[]{:S(2)}) %copy-start) | copy-done | bytes 8388632
  71.2 1.4 shard_map.125.rest_3_
  73.5 1.4 collective-permute-start.26
  74.9 1.3 collective-permute-start.27
  76.3 1.2 broadcast_select_fusion.2
  77.6 1.6 collective-permute-start.29
  80.4 7.3 %shard_map.126 = (bf16[13,48,256]{2,1,0:T(8,128)(2,1)S(1)}, bf16[13,48,256]{2,1,0:T(8,128)(2,1)S(1)}) custom-call(s32[6,4]{1,0:T(8,128)S(1)} %stack.29.slot_ref, bf16[13,48,1024]{2,1,0:T(8,128)(2,1)S(1)} %copy-done.34, bf16[13,2,48,1024]{3,2,1,0:T(8,128)(2,1)S(1)} %copy-done.5, f32[13,48,128]{2,1,0:T(8,128)S(1)} %copy-done.27, ...), custom_call_target="tpu_custom_call" | custom-call | flops 8099999744 | bytes 1000 | tf_op jit(solution)/shard_map/pallas_call | solution.py:164
  87.7 1.5 collective-permute-done.26.rest_8_
  89.3 1.4 collective-permute-done.27.rest_9_
  90.7 2.9 %collective-permute-done.29.rest_1_ = bf16[624,512]{1,0:T(8,128)(2,1)S(1)} collective-permute-done((bf16[624,512]{1,0:T(8,128)(2,1)S(1)}, bf16[624,512]{1,0:T(8,128)(2,1)S(1)}, u32[]{:S(2)}, u32[]{:S(2)}) %collective-permute-start.29) | collective-permute-done | bytes 639008 | tf_op jit(solution)/shard_map/ppermute | solution.py:257
  93.6 2.3 %shard_map.127.rest_3_ = f32[624,1024]{1,0:T(8,128)S(1)} custom-call(s32[1]{0:T(128)} %bitcast.z_ref, bf16[4,1024,1024]{2,1,0:T(8,128)(2,1)S(1)} %bitcast.35, bf16[624,128]{1,0:T(8,128)(2,1)S(1)} %bitcast.51, bf16[624,256]{1,0:T(8,128)(2,1)S(1)} %copy-done.15, bf16[624,128]{1,0:T(8,128)(2,1)S(1)} %copy-done.17, ...), custom_call_target="tpu_custom_call", output_to_operand_aliasing={{}: (5, {})} | custom-call | flops 2000000000 | bytes 1000 | tf_op jit(solution)/shard_map/pallas_call | solution.py:228
  96.1 1.8 %collective-permute-start.32 = (bf16[624,640]{1,0:T(8,128)(2,1)S(1)}, bf16[624,640]{1,0:T(8,128)(2,1)S(1)}, u32[]{:S(2)}, u32[]{:S(2)}) collective-permute-start(bf16[624,640]{1,0:T(8,128)(2,1)S(1)} %pad_maximum_fusion.1), channel_id=1, source_target_pairs={{0,1},{1,0},{2,3},{3,2},{4,5},{5,4},{6,7},{7,6},{8,9},{9,8},{10,11... | collective-permute-start | bytes 2396168 | tf_op jit(solution)/shard_map/ppermute | solution.py:257
  98.8 6.8 %shard_map.128 = (bf16[13,48,256]{2,1,0:T(8,128)(2,1)S(1)}, bf16[13,48,256]{2,1,0:T(8,128)(2,1)S(1)}) custom-call(s32[6,4]{1,0:T(8,128)S(1)} %stack.29.slot_ref, bf16[13,48,1024]{2,1,0:T(8,128)(2,1)S(1)} %copy-done.34, bf16[13,2,48,1024]{3,2,1,0:T(8,128)(2,1)S(1)} %copy-done.5, f32[13,48,128]{2,1,0:T(8,128)S(1)} %copy-done.27, ...), custom_call_target="tpu_custom_call" | custom-call | flops 8099999744 | bytes 1000 | tf_op jit(solution)/shard_map/pallas_call | solution.py:164
  105.6 10.7 %collective-permute-done.32.rest_1_ = bf16[624,640]{1,0:T(8,128)(2,1)S(1)} collective-permute-done((bf16[624,640]{1,0:T(8,128)(2,1)S(1)}, bf16[624,640]{1,0:T(8,128)(2,1)S(1)}, u32[]{:S(2)}, u32[]{:S(2)}) %collective-permute-start.32) | collective-permute-done | bytes 798752 | tf_op jit(solution)/shard_map/ppermute | solution.py:257
  116.4 3.1 %shard_map.129.rest_3_ = f32[624,1024]{1,0:T(8,128)S(1)} custom-call(s32[1]{0:T(128)} %bitcast.z_ref, bf16[4,1024,1024]{2,1,0:T(8,128)(2,1)S(1)} %bitcast.36, bf16[624,256]{1,0:T(8,128)(2,1)S(1)} %bitcast.46, bf16[624,512]{1,0:T(8,128)(2,1)S(1)} %copy-done.13, bf16[624,256]{1,0:T(8,128)(2,1)S(1)} %collective-permute-done.22.rest_2_, ...), custom_call_target="tpu_custom_call", output_to_operand_aliasing={{}: (5, {})} | custom-call | flops 2000000000 | bytes 1000 | tf_op jit(solution)/shard_map/pallas_call | solution.py:228
  120.6 1.7 %collective-permute-start.34 = (bf16[624,768]{1,0:T(8,128)(2,1)}, bf16[624,768]{1,0:T(8,128)(2,1)}, u32[]{:S(2)}, u32[]{:S(2)}) collective-permute-start(bf16[624,768]{1,0:T(8,128)(2,1)} %pad_maximum_fusion), channel_id=1, source_target_pairs={{0,1},{1,0},{2,3},{3,2},{4,5},{5,4},{6,7},{7,6},{8,9},{9,8},{10,11... | collective-permute-start | bytes 2875400 | tf_op jit(solution)/shard_map/ppermute | solution.py:257
  123.2 1.5 collective-permute-start.37
  124.9 5.7 %gather_fusion = bf16[104,2,1024]{2,0,1:T(8,128)(2,1)} fusion(bf16[13,2,48,1024]{3,2,1,0:T(8,128)(2,1)} %rest_1_.9, s32[104]{0:T(128)S(1)} %reshape.132), kind=kCustom, calls=%fused_computation | custom fusion | bytes 852800 | tf_op jit(solution)/shard_map/jit(take_along_axis)/gather | solution.py:385
  130.6 3.4 %copy-done.1 = bf16[4096,1024]{1,0:T(8,128)(2,1)S(1)} copy-done((bf16[4096,1024]{1,0:T(8,128)(2,1)S(1)}, bf16[4096,1024]{1,0:T(8,128)(2,1)}, u32[]{:S(2)}) %copy-start.1) | copy-done | bytes 8388632
  136.2 3.8 %shard_map.130.rest_3_ = f32[624,1024]{1,0:T(8,128)S(1)} custom-call(s32[1]{0:T(128)} %bitcast.z_ref, bf16[4,1024,1024]{2,1,0:T(8,128)(2,1)S(1)} %bitcast.37, bf16[624,256]{1,0:T(8,128)(2,1)S(1)} %bitcast.43, bf16[624,640]{1,0:T(8,128)(2,1)S(1)} %copy-done.11, bf16[624,384]{1,0:T(8,128)(2,1)S(1)} %copy-done.9, ...), custom_call_target="tpu_custom_call", output_to_operand_aliasing={{}: (5, {})} | custom-call | flops 2000000000 | bytes 1000 | tf_op jit(solution)/shard_map/pallas_call | solution.py:228
  140.0 1.3 collective-permute-start.38
  141.3 3.3 %collective-permute-done.34.rest_1_ = bf16[624,768]{1,0:T(8,128)(2,1)} collective-permute-done((bf16[624,768]{1,0:T(8,128)(2,1)}, bf16[624,768]{1,0:T(8,128)(2,1)}, u32[]{:S(2)}, u32[]{:S(2)}) %collective-permute-start.34) | collective-permute-done | bytes 958496 | tf_op jit(solution)/shard_map/ppermute | solution.py:257
  144.5 1.7 slice.65
  147.0 3.4 %copy-done.2 = bf16[4096,1024]{1,0:T(8,128)(2,1)S(1)} copy-done((bf16[4096,1024]{1,0:T(8,128)(2,1)S(1)}, bf16[4096,1024]{1,0:T(8,128)(2,1)}, u32[]{:S(2)}) %copy-start.2) | copy-done | bytes 8388632
  151.5 5.1 %shard_map.131.rest_2_ = f32[624,1024]{1,0:T(8,128)S(1)} custom-call(s32[1]{0:T(128)} %bitcast.z_ref, bf16[4,1024,1024]{2,1,0:T(8,128)(2,1)S(1)} %bitcast.38, bf16[624,256]{1,0:T(8,128)(2,1)S(1)} %bitcast.49, bf16[624,768]{1,0:T(8,128)(2,1)} %collective-permute-done.34.rest_1_, bf16[624,512]{1,0:T(8,128)(2,1)S(1)} %copy-done.7, ...), custom_call_target="tpu_custom_call", output_to_operand_aliasing={{}: (5, {})} | custom-call | flops 2000000000 | bytes 1000 | tf_op jit(solution)/shard_map/pallas_call | solution.py:228
  156.6 1.3 collective-permute-start.36
  159.0 3.4 %copy-done.3 = bf16[4096,1024]{1,0:T(8,128)(2,1)S(1)} copy-done((bf16[4096,1024]{1,0:T(8,128)(2,1)S(1)}, bf16[4096,1024]{1,0:T(8,128)(2,1)}, u32[]{:S(2)}) %copy-start.3) | copy-done | bytes 8388632
  162.4 3.5 %shard_map.132.rest_2_ = f32[624,1024]{1,0:T(8,128)S(1)} custom-call(s32[1]{0:T(128)} %bitcast.z_ref, bf16[4,1024,1024]{2,1,0:T(8,128)(2,1)S(1)} %bitcast.39, bf16[624,512]{1,0:T(8,128)(2,1)} %collective-permute-done.38.rest_0_, bf16[624,512]{1,0:T(8,128)(2,1)} %collective-permute-done.37.rest_1_, ...), custom_call_target="tpu_custom_call", output_to_operand_aliasing={{}: (4, {})} | custom-call | flops 2000000000 | bytes 1000 | tf_op jit(solution)/shard_map/pallas_call | solution.py:228
  165.9 3.7 %collective-permute-done.36.rest_0_ = bf16[624,256]{1,0:T(8,128)(2,1)S(1)} collective-permute-done((bf16[624,256]{1,0:T(8,128)(2,1)S(1)}, bf16[624,256]{1,0:T(8,128)(2,1)S(1)}, u32[]{:S(2)}, u32[]{:S(2)}) %collective-permute-start.36) | collective-permute-done | bytes 319520 | tf_op jit(solution)/shard_map/ppermute | solution.py:257
  169.6 2.4 %shard_map.133 = bf16[624,1024]{1,0:T(8,128)(2,1)} custom-call(s32[1]{0:T(128)} %bitcast.z_ref, bf16[4,1024,1024]{2,1,0:T(8,128)(2,1)S(1)} %bitcast.40, bf16[624,256]{1,0:T(8,128)(2,1)S(1)} %collective-permute-done.36.rest_0_, bf16[624,256]{1,0:T(8,128)(2,1)S(1)} %collective-permute-done.35.rest_1_, f32[624,1024]{1,0:T(8,128)S(1)} %shard_map.132.rest_2_), custom_call_target="tpu_custom_call" | custom-call | flops 2000000000 | bytes 1000 | tf_op jit(solution)/shard_map/pallas_call | solution.py:228
  (180 shorter events, 26.4 us)
Async XLA Ops:
  0.6 9.0 %collective-permute-start = (s32[13,1]{0,1:T(1,128)}, s32[13,1]{0,1:T(1,128)S(1)}, u32[]{:S(2)}, u32[]{:S(2)}) collective-permute-start(s32[13,1]{0,1:T(1,128)} %param.14), channel_id=1, source_target_pairs={{0,4},{4,0},{8,12},{12,8},{16,20},{20,16},{24,28},{28,24},{1,5},{5... | collective-permute-start | bytes 164 | tf_op jit(solution)/shard_map/ppermute | solution.py:253
  1.2 10.0 %collective-permute-start.1 = (s32[13,48,48]{2,1,0:T(8,128)}, s32[13,48,48]{2,1,0:T(8,128)S(1)}, u32[]{:S(2)}, u32[]{:S(2)}) collective-permute-start(s32[13,48,48]{2,1,0:T(8,128)} %param.13), channel_id=1, source_target_pairs={{0,4},{4,0},{8,12},{12,8},{16,20},{20,16},{24,28},{28,24},{1,5},{5... | collective-permute-start | bytes 359432 | tf_op jit(solution)/shard_map/ppermute | solution.py:253
  1.2 4.6 %collective-permute-start.3 = (bf16[1,2,152,1024]{3,2,1,0:T(8,128)(2,1)}, bf16[1,2,152,1024]{3,2,1,0:T(8,128)(2,1)S(1)}, u32[]{:S(2)}, u32[]{:S(2)}) collective-permute-start(bf16[1,2,152,1024]{3,2,1,0:T(8,128)(2,1)} %param.18), channel_id=1, source_target_pairs={{0,4},{4,0},{8,12},{12,8},{16,20},{20,16},{24,28},{28,24},{1,5},{5... | collective-permute-start | bytes 1867784 | tf_op jit(solution)/shard_map/ppermute | solution.py:253
  1.7 3.2 %collective-permute-start.2 = (s32[1]{0:T(128)}, s32[1]{0:T(128)}, u32[]{:S(2)}, u32[]{:S(2)}) collective-permute-start(s32[1]{0:T(128)} %param.19), channel_id=1, source_target_pairs={{0,4},{4,0},{8,12},{12,8},{16,20},{20,16},{24,28},{28,24},{1,5},{5... | collective-permute-start | bytes 20 | tf_op jit(solution)/shard_map/ppermute | solution.py:253
  1.7 21.2 %collective-permute-start.5 = (bf16[13,2,48,1024]{3,2,1,0:T(8,128)(2,1)}, bf16[13,2,48,1024]{3,2,1,0:T(8,128)(2,1)}, u32[]{:S(2)}, u32[]{:S(2)}) collective-permute-start(bf16[13,2,48,1024]{3,2,1,0:T(8,128)(2,1)} %rest_1_.9), channel_id=1, source_target_pairs={{0,4},{4,0},{8,12},{12,8},{16,20},{20,16},{24,28},{28,24},{1,5},{5... | collective-permute-start | bytes 7667720 | tf_op jit(solution)/shard_map/ppermute | solution.py:253
  4.9 18.0 %collective-permute-start.4 = (bf16[13,48,1024]{2,1,0:T(8,128)(2,1)}, bf16[13,48,1024]{2,1,0:T(8,128)(2,1)}, u32[]{:S(2)}, u32[]{:S(2)}) collective-permute-start(bf16[13,48,1024]{2,1,0:T(8,128)(2,1)} %rest_0_.9), channel_id=1, source_target_pairs={{0,4},{4,0},{8,12},{12,8},{16,20},{20,16},{24,28},{28,24},{1,5},{5... | collective-permute-start | bytes 3833864 | tf_op jit(solution)/shard_map/ppermute | solution.py:253
  6.8 14.7 %copy-start.30 = (bf16[2,2,160,128]{3,2,1,0:T(8,128)(2,1)}, bf16[2,2,160,128]{3,2,1,0:T(8,128)(2,1)S(1)}, u32[]{:S(2)}) copy-start(bf16[2,2,160,128]{3,2,1,0:T(8,128)(2,1)S(1)} %get-tuple-element.48.rest_6_) | copy-start | bytes 491524
  6.8 8.2 %collective-permute-start.6 = (bf16[2,2,160,128]{3,2,1,0:T(8,128)(2,1)}, bf16[2,2,160,128]{3,2,1,0:T(8,128)(2,1)}, u32[]{:S(2)}, u32[]{:S(2)}) collective-permute-start(bf16[2,2,160,128]{3,2,1,0:T(8,128)(2,1)} %get-tuple-element.108.rest_6_), channel_id=1, source_target_pairs={{0,8},{4,12},{8,0},{12,4},{16,24},{20,28},{24,16},{28,20},{1,9},{5... | collective-permute-start | bytes 491528 | tf_op jit(solution)/shard_map/ppermute | solution.py:253
  9.7 9.7 %collective-permute-start.7 = (bf16[2,2,160,128]{3,2,1,0:T(8,128)(2,1)}, bf16[2,2,160,128]{3,2,1,0:T(8,128)(2,1)}, u32[]{:S(2)}, u32[]{:S(2)}) collective-permute-start(bf16[2,2,160,128]{3,2,1,0:T(8,128)(2,1)} %get-tuple-element.108.rest_6_), channel_id=1, source_target_pairs={{0,16},{4,20},{8,24},{12,28},{16,0},{20,4},{24,8},{28,12},{1,17},{... | collective-permute-start | bytes 491528 | tf_op jit(solution)/shard_map/ppermute | solution.py:253
  11.2 8.2 %collective-permute-start.8 = (bf16[2,2,160,128]{3,2,1,0:T(8,128)(2,1)}, bf16[2,2,160,128]{3,2,1,0:T(8,128)(2,1)}, u32[]{:S(2)}, u32[]{:S(2)}) collective-permute-start(bf16[2,2,160,128]{3,2,1,0:T(8,128)(2,1)} %get-tuple-element.108.rest_6_), channel_id=1, source_target_pairs={{0,24},{4,28},{8,16},{12,20},{16,8},{20,12},{24,0},{28,4},{1,25},{... | collective-permute-start | bytes 491528 | tf_op jit(solution)/shard_map/ppermute | solution.py:253
  12.8 18.7 %copy-start.21 = (bf16[2,2,160,256]{3,2,1,0:T(8,128)(2,1)}, bf16[2,2,160,256]{3,2,1,0:T(8,128)(2,1)S(1)}, u32[]{:S(2)}) copy-start(bf16[2,2,160,256]{3,2,1,0:T(8,128)(2,1)S(1)} %get-tuple-element.53.rest_6_) | copy-start | bytes 983044
  13.6 24.4 %copy-start.25 = (f32[13,48,128]{2,1,0:T(8,128)}, f32[13,48,128]{2,1,0:T(8,128)S(1)}, u32[]{:S(2)}) copy-start(f32[13,48,128]{2,1,0:T(8,128)S(1)} %fusion.17.rest_2_) | copy-start | bytes 958468
  14.9 41.3 %copy-start.28 = (f32[13,48,128]{2,1,0:T(8,128)}, f32[13,48,128]{2,1,0:T(8,128)S(1)}, u32[]{:S(2)}) copy-start(f32[13,48,128]{2,1,0:T(8,128)S(1)} %pad_select_fusion.rest_5_) | copy-start | bytes 958468
  19.4 9.6 %collective-permute-start.9 = (bf16[2,2,160,128]{3,2,1,0:T(8,128)(2,1)S(1)}, bf16[2,2,160,128]{3,2,1,0:T(8,128)(2,1)S(1)}, u32[]{:S(2)}, u32[]{:S(2)}) collective-permute-start(bf16[2,2,160,128]{3,2,1,0:T(8,128)(2,1)S(1)} %get-tuple-element.48.rest_6_), channel_id=1, source_target_pairs={{0,8},{4,12},{8,0},{12,4},{16,24},{20,28},{24,16},{28,20},{1,9},{5... | collective-permute-start | bytes 491528 | tf_op jit(solution)/shard_map/ppermute | solution.py:253
  20.6 8.6 %collective-permute-start.10 = (bf16[2,2,160,128]{3,2,1,0:T(8,128)(2,1)S(1)}, bf16[2,2,160,128]{3,2,1,0:T(8,128)(2,1)S(1)}, u32[]{:S(2)}, u32[]{:S(2)}) collective-permute-start(bf16[2,2,160,128]{3,2,1,0:T(8,128)(2,1)S(1)} %get-tuple-element.48.rest_6_), channel_id=1, source_target_pairs={{0,16},{4,20},{8,24},{12,28},{16,0},{20,4},{24,8},{28,12},{1,17},{... | collective-permute-start | bytes 491528 | tf_op jit(solution)/shard_map/ppermute | solution.py:253
  21.5 7.7 %collective-permute-start.11 = (bf16[2,2,160,128]{3,2,1,0:T(8,128)(2,1)S(1)}, bf16[2,2,160,128]{3,2,1,0:T(8,128)(2,1)S(1)}, u32[]{:S(2)}, u32[]{:S(2)}) collective-permute-start(bf16[2,2,160,128]{3,2,1,0:T(8,128)(2,1)S(1)} %get-tuple-element.48.rest_6_), channel_id=1, source_target_pairs={{0,24},{4,28},{8,16},{12,20},{16,8},{20,12},{24,0},{28,4},{1,25},{... | collective-permute-start | bytes 491528 | tf_op jit(solution)/shard_map/ppermute | solution.py:253
  22.9 15.1 %copy-start.31 = (bf16[2,2,160,128]{3,2,1,0:T(8,128)(2,1)S(1)}, bf16[2,2,160,128]{3,2,1,0:T(8,128)(2,1)}, u32[]{:S(2)}) copy-start(bf16[2,2,160,128]{3,2,1,0:T(8,128)(2,1)} %copy-done.30) | copy-start | bytes 491524
  29.2 3.6 %collective-permute-start.12 = (bf16[13,48,128]{2,1,0:T(8,128)(2,1)S(1)}, bf16[13,48,128]{2,1,0:T(8,128)(2,1)S(1)}, u32[]{:S(2)}, u32[]{:S(2)}) collective-permute-start(bf16[13,48,128]{2,1,0:T(8,128)(2,1)S(1)} %get-tuple-element.49), channel_id=1, source_target_pairs={{0,4},{4,0},{8,12},{12,8},{16,20},{20,16},{24,28},{28,24},{1,5},{5... | collective-permute-start | bytes 479240 | tf_op jit(solution)/shard_map/ppermute | solution.py:253
  29.2 13.4 %collective-permute-start.13 = (bf16[2,2,160,256]{3,2,1,0:T(8,128)(2,1)S(1)}, bf16[2,2,160,256]{3,2,1,0:T(8,128)(2,1)S(1)}, u32[]{:S(2)}, u32[]{:S(2)}) collective-permute-start(bf16[2,2,160,256]{3,2,1,0:T(8,128)(2,1)S(1)} %get-tuple-element.53.rest_6_), channel_id=1, source_target_pairs={{0,8},{4,12},{8,0},{12,4},{16,24},{20,28},{24,16},{28,20},{1,9},{5... | collective-permute-start | bytes 983048 | tf_op jit(solution)/shard_map/ppermute | solution.py:253
  30.4 15.4 %collective-permute-start.14 = (bf16[2,2,160,256]{3,2,1,0:T(8,128)(2,1)S(1)}, bf16[2,2,160,256]{3,2,1,0:T(8,128)(2,1)S(1)}, u32[]{:S(2)}, u32[]{:S(2)}) collective-permute-start(bf16[2,2,160,256]{3,2,1,0:T(8,128)(2,1)S(1)} %get-tuple-element.53.rest_6_), channel_id=1, source_target_pairs={{0,16},{4,20},{8,24},{12,28},{16,0},{20,4},{24,8},{28,12},{1,17},{... | collective-permute-start | bytes 983048 | tf_op jit(solution)/shard_map/ppermute | solution.py:253
  31.4 15.8 %collective-permute-start.15 = (bf16[2,2,160,256]{3,2,1,0:T(8,128)(2,1)S(1)}, bf16[2,2,160,256]{3,2,1,0:T(8,128)(2,1)S(1)}, u32[]{:S(2)}, u32[]{:S(2)}) collective-permute-start(bf16[2,2,160,256]{3,2,1,0:T(8,128)(2,1)S(1)} %get-tuple-element.53.rest_6_), channel_id=1, source_target_pairs={{0,24},{4,28},{8,16},{12,20},{16,8},{20,12},{24,0},{28,4},{1,25},{... | collective-permute-start | bytes 983048 | tf_op jit(solution)/shard_map/ppermute | solution.py:253
  32.9 14.3 %collective-permute-start.16 = (bf16[624,128]{1,0:T(8,128)(2,1)S(1)}, bf16[624,128]{1,0:T(8,128)(2,1)S(1)}, u32[]{:S(2)}, u32[]{:S(2)}) collective-permute-start(bf16[624,128]{1,0:T(8,128)(2,1)S(1)} %bitcast.52), channel_id=1, source_target_pairs={{1,2},{2,1},{5,6},{6,5},{9,10},{10,9},{13,14},{14,13},{17,18},{18,... | collective-permute-start | bytes 479240 | tf_op jit(solution)/shard_map/ppermute | solution.py:257
  33.6 13.6 %collective-permute-start.17 = (bf16[624,128]{1,0:T(8,128)(2,1)S(1)}, bf16[624,128]{1,0:T(8,128)(2,1)S(1)}, u32[]{:S(2)}, u32[]{:S(2)}) collective-permute-start(bf16[624,128]{1,0:T(8,128)(2,1)S(1)} %bitcast.53), channel_id=1, source_target_pairs={{0,1},{1,0},{2,3},{3,2},{4,5},{5,4},{6,7},{7,6},{8,9},{9,8},{10,11... | collective-permute-start | bytes 479240 | tf_op jit(solution)/shard_map/ppermute | solution.py:257
  47.2 3.6 %collective-permute-start.18 = (bf16[13,48,128]{2,1,0:T(8,128)(2,1)S(1)}, bf16[13,48,128]{2,1,0:T(8,128)(2,1)S(1)}, u32[]{:S(2)}, u32[]{:S(2)}) collective-permute-start(bf16[13,48,128]{2,1,0:T(8,128)(2,1)S(1)} %get-tuple-element.56), channel_id=1, source_target_pairs={{0,4},{4,0},{8,12},{12,8},{16,20},{20,16},{24,28},{28,24},{1,5},{5... | collective-permute-start | bytes 479240 | tf_op jit(solution)/shard_map/ppermute | solution.py:253
  47.3 17.1 %collective-permute-start.19 = (bf16[2,2,160,256]{3,2,1,0:T(8,128)(2,1)}, bf16[2,2,160,256]{3,2,1,0:T(8,128)(2,1)S(1)}, u32[]{:S(2)}, u32[]{:S(2)}) collective-permute-start(bf16[2,2,160,256]{3,2,1,0:T(8,128)(2,1)} %get-tuple-element.60.rest_6_), channel_id=1, source_target_pairs={{0,8},{4,12},{8,0},{12,4},{16,24},{20,28},{24,16},{28,20},{1,9},{5... | collective-permute-start | bytes 983048 | tf_op jit(solution)/shard_map/ppermute | solution.py:253
  48.3 17.0 %collective-permute-start.20 = (bf16[2,2,160,256]{3,2,1,0:T(8,128)(2,1)}, bf16[2,2,160,256]{3,2,1,0:T(8,128)(2,1)S(1)}, u32[]{:S(2)}, u32[]{:S(2)}) collective-permute-start(bf16[2,2,160,256]{3,2,1,0:T(8,128)(2,1)} %get-tuple-element.60.rest_6_), channel_id=1, source_target_pairs={{0,16},{4,20},{8,24},{12,28},{16,0},{20,4},{24,8},{28,12},{1,17},{... | collective-permute-start | bytes 983048 | tf_op jit(solution)/shard_map/ppermute | solution.py:253
  49.7 16.3 %collective-permute-start.21 = (bf16[2,2,160,256]{3,2,1,0:T(8,128)(2,1)}, bf16[2,2,160,256]{3,2,1,0:T(8,128)(2,1)S(1)}, u32[]{:S(2)}, u32[]{:S(2)}) collective-permute-start(bf16[2,2,160,256]{3,2,1,0:T(8,128)(2,1)} %get-tuple-element.60.rest_6_), channel_id=1, source_target_pairs={{0,24},{4,28},{8,16},{12,20},{16,8},{20,12},{24,0},{28,4},{1,25},{... | collective-permute-start | bytes 983048 | tf_op jit(solution)/shard_map/ppermute | solution.py:253
  51.0 15.8 %collective-permute-start.22 = (bf16[624,256]{1,0:T(8,128)(2,1)S(1)}, bf16[624,256]{1,0:T(8,128)(2,1)S(1)}, u32[]{:S(2)}, u32[]{:S(2)}) collective-permute-start(bf16[624,256]{1,0:T(8,128)(2,1)S(1)} %get-tuple-element.103), channel_id=1, source_target_pairs={{1,2},{2,1},{5,6},{6,5},{9,10},{10,9},{13,14},{14,13},{17,18},{18,... | collective-permute-start | bytes 958472 | tf_op jit(solution)/shard_map/ppermute | solution.py:257
  51.7 15.1 %collective-permute-start.23 = (bf16[624,256]{1,0:T(8,128)(2,1)S(1)}, bf16[624,256]{1,0:T(8,128)(2,1)S(1)}, u32[]{:S(2)}, u32[]{:S(2)}) collective-permute-start(bf16[624,256]{1,0:T(8,128)(2,1)S(1)} %get-tuple-element.102), channel_id=1, source_target_pairs={{0,1},{1,0},{2,3},{3,2},{4,5},{5,4},{6,7},{7,6},{8,9},{9,8},{10,11... | collective-permute-start | bytes 958472 | tf_op jit(solution)/shard_map/ppermute | solution.py:257
  66.8 9.5 %collective-permute-start.24 = (bf16[13,48,256]{2,1,0:T(8,128)(2,1)}, bf16[13,48,256]{2,1,0:T(8,128)(2,1)}, u32[]{:S(2)}, u32[]{:S(2)}) collective-permute-start(bf16[13,48,256]{2,1,0:T(8,128)(2,1)} %get-tuple-element.63), channel_id=1, source_target_pairs={{0,4},{4,0},{8,12},{12,8},{16,20},{20,16},{24,28},{28,24},{1,5},{5... | collective-permute-start | bytes 958472 | tf_op jit(solution)/shard_map/ppermute | solution.py:253
  72.7 15.0 %collective-permute-start.25 = (bf16[2,2,160,256]{3,2,1,0:T(8,128)(2,1)S(1)}, bf16[2,2,160,256]{3,2,1,0:T(8,128)(2,1)S(1)}, u32[]{:S(2)}, u32[]{:S(2)}) collective-permute-start(bf16[2,2,160,256]{3,2,1,0:T(8,128)(2,1)S(1)} %copy-done.20), channel_id=1, source_target_pairs={{0,8},{4,12},{8,0},{12,4},{16,24},{20,28},{24,16},{28,20},{1,9},{5... | collective-permute-start | bytes 983048 | tf_op jit(solution)/shard_map/ppermute | solution.py:253
  73.5 15.8 %collective-permute-start.26 = (bf16[2,2,160,256]{3,2,1,0:T(8,128)(2,1)S(1)}, bf16[2,2,160,256]{3,2,1,0:T(8,128)(2,1)S(1)}, u32[]{:S(2)}, u32[]{:S(2)}) collective-permute-start(bf16[2,2,160,256]{3,2,1,0:T(8,128)(2,1)S(1)} %copy-done.20), channel_id=1, source_target_pairs={{0,16},{4,20},{8,24},{12,28},{16,0},{20,4},{24,8},{28,12},{1,17},{... | collective-permute-start | bytes 983048 | tf_op jit(solution)/shard_map/ppermute | solution.py:253
  74.9 15.8 %collective-permute-start.27 = (bf16[2,2,160,256]{3,2,1,0:T(8,128)(2,1)S(1)}, bf16[2,2,160,256]{3,2,1,0:T(8,128)(2,1)S(1)}, u32[]{:S(2)}, u32[]{:S(2)}) collective-permute-start(bf16[2,2,160,256]{3,2,1,0:T(8,128)(2,1)S(1)} %copy-done.20), channel_id=1, source_target_pairs={{0,24},{4,28},{8,16},{12,20},{16,8},{20,12},{24,0},{28,4},{1,25},{... | collective-permute-start | bytes 983048 | tf_op jit(solution)/shard_map/ppermute | solution.py:253
  77.6 16.0 %collective-permute-start.29 = (bf16[624,512]{1,0:T(8,128)(2,1)S(1)}, bf16[624,512]{1,0:T(8,128)(2,1)S(1)}, u32[]{:S(2)}, u32[]{:S(2)}) collective-permute-start(bf16[624,512]{1,0:T(8,128)(2,1)S(1)} %pad_maximum_fusion.2), channel_id=1, source_target_pairs={{0,1},{1,0},{2,3},{3,2},{4,5},{5,4},{6,7},{7,6},{8,9},{9,8},{10,11... | collective-permute-start | bytes 1916936 | tf_op jit(solution)/shard_map/ppermute | solution.py:257
  79.2 14.3 %slice-start = ((s8[8388608]{0:T(1024)(128)(4,1)}), s8[4194304]{0:T(1024)(128)(4,1)S(1)}, s32[]{:S(2)}) async-start(s8[8388608]{0:T(1024)(128)(4,1)} %bitcast.33), calls=%async_computation | async-start | bytes 8388608
  79.3 14.3 %slice-start.1 = ((s8[8388608]{0:T(1024)(128)(4,1)}), s8[4194304]{0:T(1024)(128)(4,1)S(1)}, s32[]{:S(2)}) async-start(s8[8388608]{0:T(1024)(128)(4,1)} %bitcast.33), calls=%async_computation.1 | async-start | bytes 8388608
  79.3 14.3 %copy-start.15 = (bf16[624,256]{1,0:T(8,128)(2,1)S(1)}, bf16[624,256]{1,0:T(8,128)(2,1)}, u32[]{:S(2)}) copy-start(bf16[624,256]{1,0:T(8,128)(2,1)} %copy-done.14) | copy-start | bytes 958468
  79.3 11.4 %collective-permute-start.28 = (bf16[624,384]{1,0:T(8,128)(2,1)S(1)}, bf16[624,384]{1,0:T(8,128)(2,1)S(1)}, u32[]{:S(2)}, u32[]{:S(2)}) collective-permute-start(bf16[624,384]{1,0:T(8,128)(2,1)S(1)} %pad_maximum_fusion.5), channel_id=1, source_target_pairs={{1,2},{2,1},{5,6},{6,5},{9,10},{10,9},{13,14},{14,13},{17,18},{18,... | collective-permute-start | bytes 1437704 | tf_op jit(solution)/shard_map/ppermute | solution.py:257
  93.5 2.3 %collective-permute-start.30 = (bf16[13,48,256]{2,1,0:T(8,128)(2,1)S(1)}, bf16[13,48,256]{2,1,0:T(8,128)(2,1)S(1)}, u32[]{:S(2)}, u32[]{:S(2)}) collective-permute-start(bf16[13,48,256]{2,1,0:T(8,128)(2,1)S(1)} %get-tuple-element.71), channel_id=1, source_target_pairs={{0,4},{4,0},{8,12},{12,8},{16,20},{20,16},{24,28},{28,24},{1,5},{5... | collective-permute-start | bytes 958472 | tf_op jit(solution)/shard_map/ppermute | solution.py:253
  96.1 20.3 %collective-permute-start.32 = (bf16[624,640]{1,0:T(8,128)(2,1)S(1)}, bf16[624,640]{1,0:T(8,128)(2,1)S(1)}, u32[]{:S(2)}, u32[]{:S(2)}) collective-permute-start(bf16[624,640]{1,0:T(8,128)(2,1)S(1)} %pad_maximum_fusion.1), channel_id=1, source_target_pairs={{0,1},{1,0},{2,3},{3,2},{4,5},{5,4},{6,7},{7,6},{8,9},{9,8},{10,11... | collective-permute-start | bytes 2396168 | tf_op jit(solution)/shard_map/ppermute | solution.py:257
  98.0 18.4 %copy-start.13 = (bf16[624,512]{1,0:T(8,128)(2,1)S(1)}, bf16[624,512]{1,0:T(8,128)(2,1)}, u32[]{:S(2)}) copy-start(bf16[624,512]{1,0:T(8,128)(2,1)} %copy-done.12) | copy-start | bytes 1916932
  98.0 7.6 %collective-permute-start.31 = (bf16[624,512]{1,0:T(8,128)(2,1)S(1)}, bf16[624,512]{1,0:T(8,128)(2,1)S(1)}, u32[]{:S(2)}, u32[]{:S(2)}) collective-permute-start(bf16[624,512]{1,0:T(8,128)(2,1)S(1)} %pad_maximum_fusion.3), channel_id=1, source_target_pairs={{1,2},{2,1},{5,6},{6,5},{9,10},{10,9},{13,14},{14,13},{17,18},{18,... | collective-permute-start | bytes 1916936 | tf_op jit(solution)/shard_map/ppermute | solution.py:257
  116.3 3.1 %collective-permute-start.33 = (bf16[13,48,256]{2,1,0:T(8,128)(2,1)S(1)}, bf16[13,48,256]{2,1,0:T(8,128)(2,1)S(1)}, u32[]{:S(2)}, u32[]{:S(2)}) collective-permute-start(bf16[13,48,256]{2,1,0:T(8,128)(2,1)S(1)} %get-tuple-element.77), channel_id=1, source_target_pairs={{0,4},{4,0},{8,12},{12,8},{16,20},{20,16},{24,28},{28,24},{1,5},{5... | collective-permute-start | bytes 958472 | tf_op jit(solution)/shard_map/ppermute | solution.py:253
  120.6 23.9 %collective-permute-start.34 = (bf16[624,768]{1,0:T(8,128)(2,1)}, bf16[624,768]{1,0:T(8,128)(2,1)}, u32[]{:S(2)}, u32[]{:S(2)}) collective-permute-start(bf16[624,768]{1,0:T(8,128)(2,1)} %pad_maximum_fusion), channel_id=1, source_target_pairs={{0,1},{1,0},{2,3},{3,2},{4,5},{5,4},{6,7},{7,6},{8,9},{9,8},{10,11... | collective-permute-start | bytes 2875400 | tf_op jit(solution)/shard_map/ppermute | solution.py:257
  123.2 16.7 %collective-permute-start.37 = (bf16[624,512]{1,0:T(8,128)(2,1)}, bf16[624,512]{1,0:T(8,128)(2,1)}, u32[]{:S(2)}, u32[]{:S(2)}) collective-permute-start(bf16[624,512]{1,0:T(8,128)(2,1)} %pad_maximum_fusion.4), channel_id=1, source_target_pairs={{1,2},{2,1},{5,6},{6,5},{9,10},{10,9},{13,14},{14,13},{17,18},{18,... | collective-permute-start | bytes 1916936 | tf_op jit(solution)/shard_map/ppermute | solution.py:257
  140.0 19.1 %collective-permute-start.38 = (bf16[624,512]{1,0:T(8,128)(2,1)}, bf16[624,512]{1,0:T(8,128)(2,1)}, u32[]{:S(2)}, u32[]{:S(2)}) collective-permute-start(bf16[624,512]{1,0:T(8,128)(2,1)} %collective-permute-done.37.rest_1_), channel_id=1, source_target_pairs={{1,0},{2,3},{5,4},{6,7},{9,8},{10,11},{13,12},{14,15},{17,16},{18,... | collective-permute-start | bytes 1916936 | tf_op jit(solution)/shard_map/ppermute | solution.py:257
  146.2 10.4 %collective-permute-start.35 = (bf16[624,256]{1,0:T(8,128)(2,1)}, bf16[624,256]{1,0:T(8,128)(2,1)S(1)}, u32[]{:S(2)}, u32[]{:S(2)}) collective-permute-start(bf16[624,256]{1,0:T(8,128)(2,1)} %slice.65), channel_id=1, source_target_pairs={{1,2},{2,1},{5,6},{6,5},{9,10},{10,9},{13,14},{14,13},{17,18},{18,... | collective-permute-start | bytes 958472 | tf_op jit(solution)/shard_map/ppermute | solution.py:257
  156.6 13.0 %collective-permute-start.36 = (bf16[624,256]{1,0:T(8,128)(2,1)S(1)}, bf16[624,256]{1,0:T(8,128)(2,1)S(1)}, u32[]{:S(2)}, u32[]{:S(2)}) collective-permute-start(bf16[624,256]{1,0:T(8,128)(2,1)S(1)} %collective-permute-done.35.rest_1_), channel_id=1, source_target_pairs={{1,0},{2,3},{5,4},{6,7},{9,8},{10,11},{13,12},{14,15},{17,16},{18,... | collective-permute-start | bytes 958472 | tf_op jit(solution)/shard_map/ppermute | solution.py:257
  (40 other events, 227.2 us)

commit v3 on v2

--- a/solution.py
+++ b/solution.py
@@ -10,12 +10,13 @@
 
 HD = 128
 NEG_FILL = -1e30
-HEAD_CHUNKS = (1, 1, 2, 2, 2)
+HEAD_CHUNKS = (2, 2, 2, 2)
+SPLITS = (2, 3, 4, 5)
 
 
 K_FLOPS = 2_700_000_000
 J_FLOPS = 2_000_000_000
-GATE = (1, 1, 1)
+GATE = (0, 1, 1)
 
 
 def cost(flops):
@@ -23,7 +24,9 @@
 
 
 SCALE = 1.0 / math.sqrt(HD)
-VMEM_BYTES = 6 * 1024 * 1024
+LOG2E = math.log2(math.e)
+VMEM_BYTES = 10 * 1024 * 1024
+J_VMEM = 12 * 1024 * 1024
 
 
 def attend_kernel(idx_ref, q_ref, tree_ref, bias_ref, *rest, n_caches):
@@ -109,53 +112,63 @@
     width = outs[0].shape[2]
     tree = outs[0].shape[1]
     padded = caches[0].shape[2]
-    n_keys = 2 * tree + 2 * padded
+    own_keys = 4 * tree
+    n_keys = own_keys + 2 * padded
+    spill_at = own_keys + padded
+    lanes = sides[2].shape[2]
     position = lax.broadcasted_iota(jnp.int32, (1, n_keys), 1).astype(jnp.float32)
+    lane = lax.broadcasted_iota(jnp.int32, (tree, lanes), 1)
     repeats = -(-n_keys // HD)
 
     def length_row(ref, part):
         tail = ref[part, 0, padded - 16 : padded, 0:HD].astype(jnp.float32)[15:16]
         return jnp.concatenate([tail] * repeats, axis=1)[:, :n_keys]
 
-    lane = lax.broadcasted_iota(jnp.int32, (tree, HD), 1)
     for m, cache in enumerate(caches):
-        spill_at = 2 * tree + padded
-        limit = jnp.where(position < spill_at, length_row(cache, 0) + 2 * tree, length_row(cache, 1) + spill_at)
-        limit = jnp.where(position < 2 * tree, n_keys, limit)
+        limit = jnp.where(position < spill_at, length_row(cache, 0) + own_keys, length_row(cache, 1) + spill_at)
+        limit = jnp.where(position < own_keys, n_keys, limit)
         unseen = jnp.where(position < limit, 0.0, NEG_FILL)
+        rows, used = [], []
         for side in range(2):
-            q_ref, tree_ref, bias_ref = sides[3 * side : 3 * side + 3]
-            out_ref = outs[side]
-            r0, r1, used = [slot_ref[3 * side + k, m] for k in range(3)]
-            used = used > 0
-            rolled = jnp.where(lane < tree, NEG_FILL, pltpu.roll(bias_ref[r1], tree, 1))
-            rolled = jnp.where(lane < 2 * tree, rolled, 0.0)
-            head_bias = jnp.concatenate([bias_ref[r0], rolled], axis=0) + unseen[:, :HD]
-            bias = jnp.concatenate(
-                [head_bias, jnp.broadcast_to(unseen[:, HD:], (2 * tree, n_keys - HD))], axis=1
+            for k in range(2):
+                rows.append((side, slot_ref[3 * side + k, m]))
+                used.append(slot_ref[3 * side + 2, m] > 0)
+        head_bias = []
+        for i, (side, r) in enumerate(rows):
+            block = sides[3 * side + 2][r]
+            block = block if i == 0 else pltpu.roll(block, i * tree, 1)
+            here = jnp.logical_and(lane >= i * tree, lane < (i + 1) * tree)
+            head_bias.append(jnp.where(here, block, jnp.where(lane < own_keys, NEG_FILL, 0.0)))
+        bias = jnp.concatenate(
+            [
+                jnp.concatenate(head_bias, axis=0) + unseen[:, :lanes],
+                jnp.broadcast_to(unseen[:, lanes:], (own_keys, n_keys - lanes)),
+            ],
+            axis=1,
+        )
+        results = []
+        for h in range(width // HD):
+            here = slice(h * HD, (h + 1) * HD)
+            held = slice(inside + h * HD, inside + (h + 1) * HD)
+            cols = slice(start + h * HD, start + (h + 1) * HD)
+
+            def stored(k):
+                own = [sides[3 * side + 1][r, k, :, cols] for side, r in rows]
+                return jnp.concatenate(own + [cache[0, k, :, held], cache[1, k, :, held]], axis=0)
+
+            asked = jnp.concatenate([sides[3 * side][r, :, cols] for side, r in rows], axis=0)
+            scores = lax.dot_general(
+                asked, stored(0), (((1,), (1,)), ((), ())), preferred_element_type=jnp.float32
             )
-            for h in range(width // HD):
-                here = slice(h * HD, (h + 1) * HD)
-                held = slice(inside + h * HD, inside + (h + 1) * HD)
-                cols = slice(start + h * HD, start + (h + 1) * HD)
-
-                def stored(k):
-                    return jnp.concatenate(
-                        [tree_ref[r0, k, :, cols], tree_ref[r1, k, :, cols], cache[0, k, :, held], cache[1, k, :, held]],
-                        axis=0,
-                    )
-
-                both = jnp.concatenate([q_ref[r0, :, cols], q_ref[r1, :, cols]], axis=0)
-                scores = lax.dot_general(
-                    both, stored(0), (((1,), (1,)), ((), ())), preferred_element_type=jnp.float32
-                )
-                scores = scores * SCALE + bias
-                raw = jnp.exp(scores - jnp.max(scores, axis=1, keepdims=True))
-                total = jnp.sum(raw, axis=1, keepdims=True)
-                accum = jnp.dot(raw.astype(jnp.bfloat16), stored(1), preferred_element_type=jnp.float32)
-                attn = (accum / total).astype(out_ref.dtype)
-                out_ref[r0, :, here] = jnp.where(used, attn[:tree], out_ref[r0, :, here])
-                out_ref[r1, :, here] = jnp.where(used, attn[tree:], out_ref[r1, :, here])
+            scores = scores * (SCALE * LOG2E) + bias
+            raw = jnp.exp2(scores - jnp.max(scores, axis=1, keepdims=True))
+            total = jnp.sum(raw, axis=1, keepdims=True)
+            accum = jnp.dot(raw.astype(jnp.bfloat16), stored(1), preferred_element_type=jnp.float32)
+            results.append((here, (accum / total).astype(jnp.bfloat16)))
+        for here, attn in results:
+            for i, (side, r) in enumerate(rows):
+                mine = attn[i * tree : (i + 1) * tree]
+                outs[side][r, :, here] = jnp.where(used[i], mine, outs[side][r, :, here])
 
 
 def attend_pairs(slots, sides, caches, start, inside, width):
@@ -171,73 +184,70 @@
     )(slots, *sides, *caches)
 
 
-def project_kernel(z_ref, w_hbm, *rest, parts, counts):
-    has_own, has_middle, has_acc = counts
+def project_kernel(z_ref, w_hbm, *rest, steps, has_acc):
     rest = list(rest)
-    own = rest.pop(0) if has_own else None
-    outer = rest.pop(0)
-    between = rest.pop(0) if has_middle else None
     acc = rest.pop(0) if has_acc else None
-    out_ref, w_ref, sems = rest
+    out_ref, w_ref, sems = rest[-3:]
     z = z_ref[0]
     lower = z < 2
+    middle = jnp.logical_and(z > 0, z < 3)
     sources = (z, jnp.bitwise_xor(z, 1), jnp.where(lower, 2, 1), jnp.where(lower, 3, 0))
-    tile = w_ref.shape[2]
-    tiles = w_ref.shape[0]
     copies = []
-    for n in range(tiles):
-        at = 0
-        for which, start, width in parts:
+    at = 0
+    for _, _, step in steps:
+        for which, start, width in step:
             copies.append(
                 pltpu.make_async_copy(
-                    w_hbm.at[sources[which], pl.ds(start, width), pl.ds(n * tile, tile)],
-                    w_ref.at[n, pl.ds(at, width), :],
+                    w_hbm.at[sources[which], pl.ds(start, width), :],
+                    w_ref.at[pl.ds(at, width), :],
                     sems.at[len(copies)],
                 )
             )
+            copies[-1].start()
             at += width
+    pieces = []
+    for has_own, has_middle, _ in steps:
+        own = rest.pop(0) if has_own else None
+        outer = rest.pop(0)
+        fresh = own.shape[1] if has_own else 0
+        if has_own:
+            pieces += [own[...], outer[:, :fresh]]
+        if has_middle:
+            pieces.append(jnp.where(middle, rest.pop(0)[...], outer[:, fresh:]))
+    attn = jnp.concatenate(pieces, axis=1)
     for copy in copies:
-        copy.start()
-    pieces = [own[...]] if has_own else []
-    fresh = own.shape[1] if has_own else 0
-    if has_own:
-        pieces.append(outer[:, :fresh])
-    if has_middle:
-        middle = jnp.logical_and(z > 0, z < 3)
-        pieces.append(jnp.where(middle, between[...], outer[:, fresh:]))
-    attn = jnp.concatenate(pieces, axis=1)
-    for n in range(tiles):
-        for copy in copies[n * len(parts) : (n + 1) * len(parts)]:
-            copy.wait()
+        copy.wait()
+    tile = 256
+    for n in range(out_ref.shape[1] // tile):
         cols = slice(n * tile, (n + 1) * tile)
-        total = jnp.dot(attn, w_ref[n], preferred_element_type=jnp.float32)
+        total = jnp.dot(attn, w_ref[:, cols], preferred_element_type=jnp.float32)
         if has_acc:
             total += acc[:, cols]
         out_ref[:, cols] = total.astype(out_ref.dtype)
 
 
-def project(z, weight, own, outer, between, acc, parts, last):
+def project(z, weight, steps, acc, last):
     _, _, cols = weight.shape
-    rows = outer.shape[0]
-    depth = sum(width for _, _, width in parts)
-    tile = 256
-    tiles = cols // tile
-    given = [v for v in (own, outer, between, acc) if v is not None]
-    in_place = {1 + len(given): 0} if acc is not None and not last else {}
+    given = [] if acc is None else [acc]
+    shape = []
+    for own, outer, between, parts in steps:
+        given += [v for v in (own, outer, between) if v is not None]
+        shape.append((own is not None, between is not None, tuple(parts)))
+    count = sum(len(step[2]) for step in shape)
+    depth = sum(width for step in shape for _, _, width in step[2])
+    rows = steps[0][1].shape[0]
     vmem = pl.BlockSpec(memory_space=pltpu.VMEM)
     return pl.pallas_call(
-        partial(
-            project_kernel, parts=parts, counts=(own is not None, between is not None, acc is not None)
-        ),
+        partial(project_kernel, steps=tuple(shape), has_acc=acc is not None),
         in_specs=[pl.BlockSpec(memory_space=pltpu.SMEM), pl.BlockSpec(memory_space=pltpu.HBM)] + [vmem] * len(given),
         out_specs=vmem,
         out_shape=jax.ShapeDtypeStruct((rows, cols), jnp.bfloat16 if last else jnp.float32),
         scratch_shapes=[
-            pltpu.VMEM((tiles, depth, tile), jnp.bfloat16),
-            pltpu.SemaphoreType.DMA((tiles * len(parts),)),
+            pltpu.VMEM((depth, cols), jnp.bfloat16),
+            pltpu.SemaphoreType.DMA((count,)),
         ],
-        input_output_aliases=in_place,
-        compiler_params=pltpu.CompilerParams(vmem_limit_bytes=VMEM_BYTES),
+        input_output_aliases={2: 0} if acc is not None and not last else {},
+        compiler_params=pltpu.CompilerParams(vmem_limit_bytes=J_VMEM),
         cost_estimate=cost(J_FLOPS),
     )(z, weight, *given)
 
@@ -273,8 +283,7 @@
 def pair_bias(tree_mask):
     bias = jnp.where(tree_mask == 1, 0.0, NEG_FILL).astype(jnp.float32)
     tree = bias.shape[1]
-    bias = jnp.pad(bias, ((0, 0), (0, 0), (0, tree)), constant_values=NEG_FILL)
-    return jnp.pad(bias, ((0, 0), (0, 0), (0, HD - 2 * tree)))
+    return jnp.pad(bias, ((0, 0), (0, 0), (0, -(-4 * tree // HD) * HD - tree)))
 
 
 def local(
@@ -311,11 +320,6 @@
 
     spill = across(spill_cache, 1)
     lens = jnp.stack([first_len[0], across(spill_len, 1)[0]]).astype(jnp.bfloat16)
-    other_queries = across(queries, 1)
-    other_tree = across(tree_cache, 1)
-    other_mask = across(tree_mask, 1)
-    other_group = across(dest_group, 1)
-
     chunks = []
     start = 0
     for heads in HEAD_CHUNKS:
@@ -332,9 +336,13 @@
         gathered.append([block] + [across(block, m) for m in (2, 4, 6)])
 
     gather(0)
-    group, other_group, tree_mask, other_mask = lax.optimization_barrier(
-        (group, other_group[:, 0], tree_mask, other_mask, gathered[0][0])
+    queries, tree_cache, tree_mask, dest_group = lax.optimization_barrier(
+        (queries, tree_cache, tree_mask, dest_group, gathered[0][0])
     )[:4]
+    other_queries = across(queries, 1)
+    other_tree = across(tree_cache, 1)
+    other_mask = across(tree_mask, 1)
+    group, other_group = dest_group[:, 0], across(dest_group, 1)[:, 0]
     me = lax.axis_index("rep").astype(jnp.int32)
     blocks = jnp.bitwise_xor(me, jnp.array([0, 2, 4, 6], jnp.int32))
     slots = jnp.stack(pair_slots(group, blocks) + pair_slots(other_group, blocks))
@@ -344,32 +352,30 @@
     z = lax.axis_index("tp").astype(jnp.int32).reshape(1)
     weight = out_weight.reshape(lax.axis_size("tp"), cols, out_weight.shape[1])
     acc = None
-    accs, outer, between = [], [], []
+    steps, outer, between = [], [], []
     for i in range(n + 2):
         fresh = []
         if i < n:
             start, width = chunks[i]
             ready = slots
             if i > 0:
-                gates = [owns[i - 1]] + between[max(i - 2, 0) : i - 1] + accs[max(i - 3, 0) : i - 2]
+                gates = [owns[i - 1]] + between[max(i - 2, 0) : i - 1]
                 ready = after(slots, *gates)
             own, theirs = attend_pairs(ready, sides, gathered[i], start, 0, width)
             raws.append(theirs)
             if i + 1 < n:
                 gather(i + 1)
-                if GATE[0]:
+                if GATE[0] == 1 or i > 0 and GATE[0] == 2:
                     theirs = after(theirs, *gathered[i + 1][1:])
             if i > 0 and GATE[1]:
                 theirs = after(theirs, between[i - 1])
-            if i > 0 and GATE[2]:
+            if i > 0 and (GATE[2] == 1 or i < n - 1 and GATE[2] == 2 or i == 1 and GATE[2] == 3):
                 theirs = after(theirs, outer[i - 1])
             attn = jnp.where(mine[:, None, None], own, across(theirs, 1)).reshape(req * tree, width)
             owns.append(attn)
             fresh = [attn]
         payload = fresh + ([between[i - 1]] if i > 0 else [])
         payload = jnp.concatenate(payload, axis=1)
-        if i > 1:
-            payload = after(payload, accs[i - 2])
         outer.append(along(payload, [(0, 1), (1, 0), (2, 3), (3, 2)] if i < n else [(1, 0), (2, 3)]))
         if i <= n:
             relayed = [outer[i - 1][:, : chunks[i - 1][1]]] if i > 0 else []
@@ -377,10 +383,12 @@
         parts = [(0, *chunks[i]), (1, *chunks[i])] if i < n else []
         parts += [(2, *chunks[i - 1])] if 0 < i <= n else []
         parts += [(3, *chunks[i - 2])] if i > 1 else []
-        acc = project(
-            z, weight, owns[i] if i < n else None, outer[i], between[i - 1] if i > 0 else None, acc, parts, i == n + 1
+        steps.append(
+            (owns[i] if i < n else None, outer[i], between[i - 1] if i > 0 else None, parts)
         )
-        accs.append(acc)
+        if i in SPLITS:
+            acc = project(after(z, raws[-1]), weight, steps, acc, i == n + 1)
+            steps = []
     path = after(accepted_path, owns[-1])
     accepted_cache = jnp.take_along_axis(tree_cache, path[:, None, :, None], axis=2)
     return acc.reshape(req, tree, out_weight.shape[1]), accepted_cache

time: 173 us -> 161 us (0.931)
  waiting for transfers between devices: 33.3 us -> 56.2 us
  Pallas kernels: 52.4 us -> 31.9 us
  local copies, waits for them, and re-layouts: 32.8 us -> 21.1 us
  starting transfers between devices: 42.5 us -> 39.6 us
    ppermute x26 -> x22, waiting for transfers between devices: 12.5 us -> 44.7 us  [across(): lax.ppermute(value, 'rep', [(i, i ^ mask) for i in range(lax.axis_size('r...]
    unnamed x95 -> x49, local copies, waits for them, and re-layouts: 22.9 us -> 9.8 us
    pallas_call x7 -> x4, Pallas kernels: 21.6 us -> 11.1 us  [project(): pl.pallas_call(partial(project_kernel, steps=tuple(shape), has_acc=acc is...]
    pallas_call x5 -> x4, Pallas kernels: 30.8 us -> 20.8 us  [attend_pairs(): pl.pallas_call(partial(paired_kernel, start=start, inside=inside, n_cache...]
    ppermute x13 -> x11, waiting for transfers between devices: 20.7 us -> 11.4 us  [along(): return lax.ppermute(value, 'tp', pairs)]
    optimization_barrier x0 -> x1, local copies, waits for them, and re-layouts: none -> 4.11 us  [local(): lax.optimization_barrier((queries, tree_cache, tree_mask, dest_group, gat...]
    ppermute x13 -> x11, starting transfers between devices: 22 us -> 19.6 us  [along(): return lax.ppermute(value, 'tp', pairs)]
    ppermute x26 -> x22, starting transfers between devices: 20.5 us -> 20.1 us  [across(): lax.ppermute(value, 'rep', [(i, i ^ mask) for i in range(lax.axis_size('r...]
  transfers between devices with their start and end apart: 39 -> 33, of which waited for: 13 -> 13; matrix products, arithmetic and copies ran while one was open for 10% -> 11% of each run, Pallas kernels for 29% -> 16%
where the time goes in v3:
time: 161 us; the launch traced here: 159 us
  waiting for transfers between devices  56.2 us (35%)
  starting transfers between devices  39.6 us (25%)
  Pallas kernels  31.9 us (20%)
  local copies, waits for them, and re-layouts  21.1 us (13%)
  other arithmetic  7.3 us (5%)
  between operations  2.87 us (2%)
    ppermute x22, waiting for transfers between devices, across(): lax.ppermute(value, 'rep', [(i, i ^ mask) for i in range(lax.axis_size('r...  44.7 us
    pallas_call x4, Pallas kernels, attend_pairs(): pl.pallas_call(partial(paired_kernel, start=start, inside=inside, n_cache...  20.8 us
    ppermute x22, starting transfers between devices, across(): lax.ppermute(value, 'rep', [(i, i ^ mask) for i in range(lax.axis_size('r...  20.1 us
    ppermute x11, starting transfers between devices, along(): return lax.ppermute(value, 'tp', pairs)  19.6 us
    ppermute x11, waiting for transfers between devices, along(): return lax.ppermute(value, 'tp', pairs)  11.4 us
    pallas_call x4, Pallas kernels, project(): pl.pallas_call(partial(project_kernel, steps=tuple(shape), has_acc=acc is...  11.1 us
    unnamed x49, local copies, waits for them, and re-layouts  9.8 us
    gather x3, local copies, waits for them, and re-layouts, local(): jnp.take_along_axis(tree_cache, path[:, None, :, None], axis=2)  4.66 us
  transfers between devices with their start and end apart: 33, of which 13 were waited for; matrix products, arithmetic and copies ran while one was open for 11% of the time, Pallas kernels for 16%

profile of v3, /device:TPU:0, one launch (start us, length us, event | category | flops | bytes accessed | tf_op | source)
XLA Modules:
  0.0 159.0 jit_solution(838627720228245609)
XLA Ops:
  1.9 1.2 fusion.21
  4.1 1.4 fusion.16
  6.0 2.9 %collective-permute-start.6 = (bf16[2,2,160,256]{3,2,1,0:T(8,128)(2,1)}, bf16[2,2,160,256]{3,2,1,0:T(8,128)(2,1)}, u32[]{:S(2)}, u32[]{:S(2)}) collective-permute-start(bf16[2,2,160,256]{3,2,1,0:T(8,128)(2,1)} %get-tuple-element.79.rest_6_), channel_id=1, source_target_pairs={{0,8},{4,12},{8,0},{12,4},{16,24},{20,28},{24,16},{28,20},{1,9},{5... | collective-permute-start | bytes 983048 | tf_op jit(solution)/shard_map/ppermute | solution.py:263
  9.4 1.0 compare_select_fusion.1
  11.1 2.8 %collective-permute-start.7 = (bf16[2,2,160,256]{3,2,1,0:T(8,128)(2,1)}, bf16[2,2,160,256]{3,2,1,0:T(8,128)(2,1)}, u32[]{:S(2)}, u32[]{:S(2)}) collective-permute-start(bf16[2,2,160,256]{3,2,1,0:T(8,128)(2,1)} %get-tuple-element.79.rest_6_), channel_id=1, source_target_pairs={{0,16},{4,20},{8,24},{12,28},{16,0},{20,4},{24,8},{28,12},{1,17},{... | collective-permute-start | bytes 983048 | tf_op jit(solution)/shard_map/ppermute | solution.py:263
  14.2 1.8 %collective-permute-start.8 = (bf16[2,2,160,256]{3,2,1,0:T(8,128)(2,1)}, bf16[2,2,160,256]{3,2,1,0:T(8,128)(2,1)}, u32[]{:S(2)}, u32[]{:S(2)}) collective-permute-start(bf16[2,2,160,256]{3,2,1,0:T(8,128)(2,1)} %get-tuple-element.79.rest_6_), channel_id=1, source_target_pairs={{0,24},{4,28},{8,16},{12,20},{16,8},{20,12},{24,0},{28,4},{1,25},{... | collective-permute-start | bytes 983048 | tf_op jit(solution)/shard_map/ppermute | solution.py:263
  16.1 1.0 compare_select_fusion
  17.1 12.2 %collective-permute-done.7.rest_8_ = bf16[2,2,160,256]{3,2,1,0:T(8,128)(2,1)} collective-permute-done((bf16[2,2,160,256]{3,2,1,0:T(8,128)(2,1)}, bf16[2,2,160,256]{3,2,1,0:T(8,128)(2,1)}, u32[]{:S(2)}, u32[]{:S(2)}) %collective-permute-start.7) | collective-permute-done | bytes 327712 | tf_op jit(solution)/shard_map/ppermute | solution.py:263
  29.3 5.4 %shard_map.122 = (bf16[13,48,256]{2,1,0:T(8,128)(2,1)S(1)}, bf16[13,48,256]{2,1,0:T(8,128)(2,1)S(1)}) custom-call(s32[6,4]{1,0:T(8,128)S(1)} %stack.26.slot_ref, bf16[13,48,1024]{2,1,0:T(8,128)(2,1)} %rest_0_.3, bf16[13,2,48,1024]{3,2,1,0:T(8,128)(2,1)S(1)} %copy-done.2, f32[13,48,256]{2,1,0:T(8,128)S(1)} %pad.21.rest_2_, ...), custom_call_target="tpu_custom_call" | custom-call | flops 8099999744 | bytes 1000 | tf_op jit(solution)/shard_map/pallas_call | solution.py:177
  34.9 1.8 %collective-permute-start.10 = (bf16[2,2,160,256]{3,2,1,0:T(8,128)(2,1)S(1)}, bf16[2,2,160,256]{3,2,1,0:T(8,128)(2,1)S(1)}, u32[]{:S(2)}, u32[]{:S(2)}) collective-permute-start(bf16[2,2,160,256]{3,2,1,0:T(8,128)(2,1)S(1)} %get-tuple-element.36.rest_6_), channel_id=1, source_target_pairs={{0,8},{4,12},{8,0},{12,4},{16,24},{20,28},{24,16},{28,20},{1,9},{5... | collective-permute-start | bytes 983048 | tf_op jit(solution)/shard_map/ppermute | solution.py:263
  36.6 1.5 collective-permute-start.11
  39.2 4.7 %collective-permute-start.14 = (bf16[624,256]{1,0:T(8,128)(2,1)S(1)}, bf16[624,256]{1,0:T(8,128)(2,1)S(1)}, u32[]{:S(2)}, u32[]{:S(2)}) collective-permute-start(bf16[624,256]{1,0:T(8,128)(2,1)S(1)} %bitcast.45), channel_id=1, source_target_pairs={{0,1},{1,0},{2,3},{3,2},{4,5},{5,4},{6,7},{7,6},{8,9},{9,8},{10,11... | collective-permute-start | bytes 958472 | tf_op jit(solution)/shard_map/ppermute | solution.py:267
  43.9 1.5 collective-permute-done.10.rest_7_
  45.4 8.0 %collective-permute-done.11.rest_8_ = bf16[2,2,160,256]{3,2,1,0:T(8,128)(2,1)S(1)} collective-permute-done((bf16[2,2,160,256]{3,2,1,0:T(8,128)(2,1)S(1)}, bf16[2,2,160,256]{3,2,1,0:T(8,128)(2,1)S(1)}, u32[]{:S(2)}, u32[]{:S(2)}) %collective-permute-start.11) | collective-permute-done | bytes 327712 | tf_op jit(solution)/shard_map/ppermute | solution.py:263
  53.4 1.1 copy-done.18
  54.5 5.1 %shard_map.123 = (bf16[13,48,256]{2,1,0:T(8,128)(2,1)S(1)}, bf16[13,48,256]{2,1,0:T(8,128)(2,1)S(1)}) custom-call(s32[6,4]{1,0:T(8,128)S(1)} %stack.26.slot_ref, bf16[13,48,1024]{2,1,0:T(8,128)(2,1)} %rest_0_.3, bf16[13,2,48,1024]{3,2,1,0:T(8,128)(2,1)S(1)} %copy-done.2, f32[13,48,256]{2,1,0:T(8,128)S(1)} %copy-done.18, ...), custom_call_target="tpu_custom_call" | custom-call | flops 8099999744 | bytes 1000 | tf_op jit(solution)/shard_map/pallas_call | solution.py:177
  59.8 1.3 collective-permute-start.16
  61.9 1.4 collective-permute-start.18
  64.3 4.4 %collective-permute-start.20 = (bf16[624,512]{1,0:T(8,128)(2,1)S(1)}, bf16[624,512]{1,0:T(8,128)(2,1)S(1)}, u32[]{:S(2)}, u32[]{:S(2)}) collective-permute-start(bf16[624,512]{1,0:T(8,128)(2,1)S(1)} %get-tuple-element.74), channel_id=1, source_target_pairs={{0,1},{1,0},{2,3},{3,2},{4,5},{5,4},{6,7},{7,6},{8,9},{9,8},{10,11... | collective-permute-start | bytes 1916936 | tf_op jit(solution)/shard_map/ppermute | solution.py:267
  68.7 1.9 %collective-permute-done.16.rest_7_ = bf16[2,2,160,256]{3,2,1,0:T(8,128)(2,1)S(1)} collective-permute-done((bf16[2,2,160,256]{3,2,1,0:T(8,128)(2,1)}, bf16[2,2,160,256]{3,2,1,0:T(8,128)(2,1)S(1)}, u32[]{:S(2)}, u32[]{:S(2)}) %collective-permute-start.16) | collective-permute-done | bytes 327712 | tf_op jit(solution)/shard_map/ppermute | solution.py:263
  70.6 6.0 %collective-permute-done.17.rest_8_ = bf16[2,2,160,256]{3,2,1,0:T(8,128)(2,1)S(1)} collective-permute-done((bf16[2,2,160,256]{3,2,1,0:T(8,128)(2,1)}, bf16[2,2,160,256]{3,2,1,0:T(8,128)(2,1)S(1)}, u32[]{:S(2)}, u32[]{:S(2)}) %collective-permute-start.17) | collective-permute-done | bytes 327712 | tf_op jit(solution)/shard_map/ppermute | solution.py:263
  76.6 1.5 collective-permute-done.18.rest_9_
  78.1 5.1 %shard_map.124 = (bf16[13,48,256]{2,1,0:T(8,128)(2,1)S(1)}, bf16[13,48,256]{2,1,0:T(8,128)(2,1)S(1)}) custom-call(s32[6,4]{1,0:T(8,128)S(1)} %stack.26.slot_ref, bf16[13,48,1024]{2,1,0:T(8,128)(2,1)} %rest_0_.3, bf16[13,2,48,1024]{3,2,1,0:T(8,128)(2,1)S(1)} %copy-done.2, f32[13,48,256]{2,1,0:T(8,128)S(1)} %copy-done.19, ...), custom_call_target="tpu_custom_call" | custom-call | flops 8099999744 | bytes 1000 | tf_op jit(solution)/shard_map/pallas_call | solution.py:177
  84.3 1.5 collective-permute-start.23
  85.8 1.2 collective-permute-start.24
  87.2 1.6 %collective-permute-start.25 = (bf16[624,768]{1,0:T(8,128)(2,1)S(1)}, bf16[624,768]{1,0:T(8,128)(2,1)S(1)}, u32[]{:S(2)}, u32[]{:S(2)}) collective-permute-start(bf16[624,768]{1,0:T(8,128)(2,1)S(1)} %pad_maximum_fusion), channel_id=1, source_target_pairs={{0,1},{1,0},{2,3},{3,2},{4,5},{5,4},{6,7},{7,6},{8,9},{9,8},{10,11... | collective-permute-start | bytes 2875400 | tf_op jit(solution)/shard_map/ppermute | solution.py:267
  89.8 4.2 %collective-permute-done.22.rest_7_ = bf16[2,2,160,256]{3,2,1,0:T(8,128)(2,1)S(1)} collective-permute-done((bf16[2,2,160,256]{3,2,1,0:T(8,128)(2,1)S(1)}, bf16[2,2,160,256]{3,2,1,0:T(8,128)(2,1)S(1)}, u32[]{:S(2)}, u32[]{:S(2)}) %collective-permute-start.22) | collective-permute-done | bytes 327712 | tf_op jit(solution)/shard_map/ppermute | solution.py:263
  94.0 7.1 %collective-permute-done.23.rest_8_ = bf16[2,2,160,256]{3,2,1,0:T(8,128)(2,1)S(1)} collective-permute-done((bf16[2,2,160,256]{3,2,1,0:T(8,128)(2,1)S(1)}, bf16[2,2,160,256]{3,2,1,0:T(8,128)(2,1)S(1)}, u32[]{:S(2)}, u32[]{:S(2)}) %collective-permute-start.23) | collective-permute-done | bytes 327712 | tf_op jit(solution)/shard_map/ppermute | solution.py:263
  101.1 5.1 %shard_map.125 = (bf16[13,48,256]{2,1,0:T(8,128)(2,1)S(1)}, bf16[13,48,256]{2,1,0:T(8,128)(2,1)S(1)}) custom-call(s32[6,4]{1,0:T(8,128)S(1)} %stack.26.slot_ref, bf16[13,48,1024]{2,1,0:T(8,128)(2,1)} %rest_0_.3, bf16[13,2,48,1024]{3,2,1,0:T(8,128)(2,1)S(1)} %copy-done.2, f32[13,48,256]{2,1,0:T(8,128)S(1)} %copy-done.19, ...), custom_call_target="tpu_custom_call" | custom-call | flops 8099999744 | bytes 1000 | tf_op jit(solution)/shard_map/pallas_call | solution.py:177
  106.3 3.7 %collective-permute-done.25.rest_6_ = bf16[624,768]{1,0:T(8,128)(2,1)S(1)} collective-permute-done((bf16[624,768]{1,0:T(8,128)(2,1)S(1)}, bf16[624,768]{1,0:T(8,128)(2,1)S(1)}, u32[]{:S(2)}, u32[]{:S(2)}) %collective-permute-start.25) | collective-permute-done | bytes 958496 | tf_op jit(solution)/shard_map/ppermute | solution.py:267
  110.0 1.6 %collective-permute-done.27 = bf16[13,48,256]{2,1,0:T(8,128)(2,1)S(1)} collective-permute-done((bf16[13,48,256]{2,1,0:T(8,128)(2,1)S(1)}, bf16[13,48,256]{2,1,0:T(8,128)(2,1)S(1)}, u32[]{:S(2)}, u32[]{:S(2)}) %collective-permute-start.27) | collective-permute-done | bytes 319520 | tf_op jit(solution)/shard_map/ppermute | solution.py:263
  111.7 1.0 pad_maximum_fusion.1
  112.7 1.6 collective-permute-start.28
  115.2 1.5 collective-permute-start.29
  116.7 4.1 %copy.24 = bf16[13,2,48,1024]{3,1,2,0:T(2,128)(2,1)} copy(bf16[13,2,48,1024]{3,2,1,0:T(8,128)(2,1)S(1)} %copy-done.2) | data formatting | bytes 5111808 | tf_op jit(solution)/shard_map/optimization_barrier | solution.py:339
  120.9 3.4 %copy-done = bf16[4096,1024]{1,0:T(8,128)(2,1)S(1)} copy-done((bf16[4096,1024]{1,0:T(8,128)(2,1)S(1)}, bf16[4096,1024]{1,0:T(8,128)(2,1)}, u32[]{:S(2)}) %copy-start) | copy-done | bytes 8388632
  124.3 3.9 %shard_map.126.rest_0_ = f32[624,1024]{1,0:T(8,128)S(1)} custom-call(s32[1]{0:T(128)} %bitcast.z_ref, bf16[4,1024,1024]{2,1,0:T(8,128)(2,1)S(1)} %bitcast.32, bf16[624,256]{1,0:T(8,128)(2,1)S(1)} %bitcast.46, bf16[624,256]{1,0:T(8,128)(2,1)S(1)} %copy-done.16, bf16[624,256]{1,0:T(8,128)(2,1)S(1)} %bitcast.43, bf16[624,512]{1,0:T(8,128)(2,1)S(1)} %copy-done.10, ...), custom_call_target="tpu_custom_call" | custom-call | flops 2000000000 | bytes 1000 | tf_op jit(solution)/shard_map/pallas_call | solution.py:240
  128.2 1.3 collective-permute-start.30
  129.5 6.8 %collective-permute-done.28.rest_2_ = bf16[624,768]{1,0:T(8,128)(2,1)} collective-permute-done((bf16[624,768]{1,0:T(8,128)(2,1)}, bf16[624,768]{1,0:T(8,128)(2,1)}, u32[]{:S(2)}, u32[]{:S(2)}) %collective-permute-start.28) | collective-permute-done | bytes 958496 | tf_op jit(solution)/shard_map/ppermute | solution.py:267
  136.3 1.0 slice.52
  138.2 4.5 %gather_fusion = bf16[104,2,1024]{2,1,0:T(2,128)(2,1)} fusion(bf16[13,2,48,1024]{3,1,2,0:T(2,128)(2,1)} %copy.24, s32[104]{0:T(128)S(1)} %reshape.134), kind=kCustom, calls=%fused_computation | custom fusion | bytes 852800 | tf_op jit(solution)/shard_map/jit(take_along_axis)/gather | solution.py:393
  142.7 1.1 fusion.8
  144.6 1.5 collective-permute-start.32
  146.2 3.4 %copy-done.1 = bf16[4096,1024]{1,0:T(8,128)(2,1)S(1)} copy-done((bf16[4096,1024]{1,0:T(8,128)(2,1)S(1)}, bf16[4096,1024]{1,0:T(8,128)(2,1)}, u32[]{:S(2)}) %copy-start.1) | copy-done | bytes 8388632
  149.5 1.1 copy-done.6
  150.6 3.2 %shard_map.127.rest_0_ = f32[624,1024]{1,0:T(8,128)S(1)} custom-call(s32[1]{0:T(128)} %bitcast.z_ref, bf16[4,1024,1024]{2,1,0:T(8,128)(2,1)S(1)} %bitcast.33, f32[624,1024]{1,0:T(8,128)S(1)} %shard_map.126.rest_0_, bf16[624,256]{1,0:T(8,128)(2,1)S(1)} %bitcast.41, bf16[624,768]{1,0:T(8,128)(2,1)} %collective-permute-done.28.rest_2_, ...), custom_call_target="tpu_custom_call", output_to_operand_aliasing={{}: (2, {})} | custom-call | flops 2000000000 | bytes 1000 | tf_op jit(solution)/shard_map/pallas_call | solution.py:240
  153.8 2.4 %shard_map.128.rest_0_ = f32[624,1024]{1,0:T(8,128)S(1)} custom-call(s32[1]{0:T(128)} %bitcast.z_ref, bf16[4,1024,1024]{2,1,0:T(8,128)(2,1)S(1)} %bitcast.34, f32[624,1024]{1,0:T(8,128)S(1)} %shard_map.127.rest_0_, bf16[624,512]{1,0:T(8,128)(2,1)} %collective-permute-done.30.rest_1_, ...), custom_call_target="tpu_custom_call", output_to_operand_aliasing={{}: (2, {})} | custom-call | flops 2000000000 | bytes 1000 | tf_op jit(solution)/shard_map/pallas_call | solution.py:240
  157.2 1.6 %shard_map.129 = bf16[624,1024]{1,0:T(8,128)(2,1)} custom-call(s32[1]{0:T(128)} %bitcast.z_ref, bf16[4,1024,1024]{2,1,0:T(8,128)(2,1)S(1)} %bitcast.35, f32[624,1024]{1,0:T(8,128)S(1)} %shard_map.128.rest_0_, bf16[624,256]{1,0:T(8,128)(2,1)S(1)} %collective-permute-done.32.rest_1_, bf16[624,256]{1,0:T(8,128)(2,1)S(1)} %collective-permute-done.31.rest_2_), custom_call_target="tpu_custom_call" | custom-call | flops 2000000000 | bytes 1000 | tf_op jit(solution)/shard_map/pallas_call | solution.py:240
  (110 shorter events, 11.6 us)
Async XLA Ops:
  0.6 3.4 %collective-permute-start.1 = (bf16[1,2,152,1024]{3,2,1,0:T(8,128)(2,1)}, bf16[1,2,152,1024]{3,2,1,0:T(8,128)(2,1)S(1)}, u32[]{:S(2)}, u32[]{:S(2)}) collective-permute-start(bf16[1,2,152,1024]{3,2,1,0:T(8,128)(2,1)} %param.18), channel_id=1, source_target_pairs={{0,4},{4,0},{8,12},{12,8},{16,20},{20,16},{24,28},{28,24},{1,5},{5... | collective-permute-start | bytes 1867784 | tf_op jit(solution)/shard_map/ppermute | solution.py:263
  1.1 2.0 %collective-permute-start = (s32[1]{0:T(128)}, s32[1]{0:T(128)}, u32[]{:S(2)}, u32[]{:S(2)}) collective-permute-start(s32[1]{0:T(128)} %param.19), channel_id=1, source_target_pairs={{0,4},{4,0},{8,12},{12,8},{16,20},{20,16},{24,28},{28,24},{1,5},{5... | collective-permute-start | bytes 20 | tf_op jit(solution)/shard_map/ppermute | solution.py:263
  3.1 5.8 %copy-start.23 = (s32[13,1]{0,1:T(1,128)S(1)}, s32[13,1]{0,1:T(1,128)}, u32[]{:S(2)}) copy-start(s32[13,1]{0,1:T(1,128)} %param.14) | copy-start | bytes 160
  5.4 23.9 %collective-permute-start.4 = (bf16[13,2,48,1024]{3,2,1,0:T(8,128)(2,1)S(1)}, bf16[13,2,48,1024]{3,2,1,0:T(8,128)(2,1)}, u32[]{:S(2)}, u32[]{:S(2)}) collective-permute-start(bf16[13,2,48,1024]{3,2,1,0:T(8,128)(2,1)S(1)} %copy-done.2), channel_id=1, source_target_pairs={{0,4},{4,0},{8,12},{12,8},{16,20},{20,16},{24,28},{28,24},{1,5},{5... | collective-permute-start | bytes 7667720 | tf_op jit(solution)/shard_map/ppermute | solution.py:263
  5.9 23.5 %collective-permute-start.3 = (bf16[13,48,1024]{2,1,0:T(8,128)(2,1)}, bf16[13,48,1024]{2,1,0:T(8,128)(2,1)}, u32[]{:S(2)}, u32[]{:S(2)}) collective-permute-start(bf16[13,48,1024]{2,1,0:T(8,128)(2,1)} %rest_0_.3), channel_id=1, source_target_pairs={{0,4},{4,0},{8,12},{12,8},{16,20},{20,16},{24,28},{28,24},{1,5},{5... | collective-permute-start | bytes 3833864 | tf_op jit(solution)/shard_map/ppermute | solution.py:263
  6.0 11.2 %collective-permute-start.6 = (bf16[2,2,160,256]{3,2,1,0:T(8,128)(2,1)}, bf16[2,2,160,256]{3,2,1,0:T(8,128)(2,1)}, u32[]{:S(2)}, u32[]{:S(2)}) collective-permute-start(bf16[2,2,160,256]{3,2,1,0:T(8,128)(2,1)} %get-tuple-element.79.rest_6_), channel_id=1, source_target_pairs={{0,8},{4,12},{8,0},{12,4},{16,24},{20,28},{24,16},{28,20},{1,9},{5... | collective-permute-start | bytes 983048 | tf_op jit(solution)/shard_map/ppermute | solution.py:263
  8.9 2.2 %collective-permute-start.2 = (s32[13,1]{0,1:T(1,128)S(1)}, s32[13,1]{0,1:T(1,128)S(1)}, u32[]{:S(2)}, u32[]{:S(2)}) collective-permute-start(s32[13,1]{0,1:T(1,128)S(1)} %copy-done.23), channel_id=1, source_target_pairs={{0,4},{4,0},{8,12},{12,8},{16,20},{20,16},{24,28},{28,24},{1,5},{5... | collective-permute-start | bytes 164 | tf_op jit(solution)/shard_map/ppermute | solution.py:263
  8.9 5.3 %collective-permute-start.5 = (s32[13,48,48]{2,1,0:T(8,128)}, s32[13,48,48]{2,1,0:T(8,128)S(1)}, u32[]{:S(2)}, u32[]{:S(2)}) collective-permute-start(s32[13,48,48]{2,1,0:T(8,128)} %param.13), channel_id=1, source_target_pairs={{0,4},{4,0},{8,12},{12,8},{16,20},{20,16},{24,28},{28,24},{1,5},{5... | collective-permute-start | bytes 359432 | tf_op jit(solution)/shard_map/ppermute | solution.py:263
  10.4 24.3 %copy-start.17 = (f32[13,48,256]{2,1,0:T(8,128)}, f32[13,48,256]{2,1,0:T(8,128)S(1)}, u32[]{:S(2)}) copy-start(f32[13,48,256]{2,1,0:T(8,128)S(1)} %pad.21.rest_2_) | copy-start | bytes 1916932
  11.1 18.2 %collective-permute-start.7 = (bf16[2,2,160,256]{3,2,1,0:T(8,128)(2,1)}, bf16[2,2,160,256]{3,2,1,0:T(8,128)(2,1)}, u32[]{:S(2)}, u32[]{:S(2)}) collective-permute-start(bf16[2,2,160,256]{3,2,1,0:T(8,128)(2,1)} %get-tuple-element.79.rest_6_), channel_id=1, source_target_pairs={{0,16},{4,20},{8,24},{12,28},{16,0},{20,4},{24,8},{28,12},{1,17},{... | collective-permute-start | bytes 983048 | tf_op jit(solution)/shard_map/ppermute | solution.py:263
  14.2 15.1 %collective-permute-start.8 = (bf16[2,2,160,256]{3,2,1,0:T(8,128)(2,1)}, bf16[2,2,160,256]{3,2,1,0:T(8,128)(2,1)}, u32[]{:S(2)}, u32[]{:S(2)}) collective-permute-start(bf16[2,2,160,256]{3,2,1,0:T(8,128)(2,1)} %get-tuple-element.79.rest_6_), channel_id=1, source_target_pairs={{0,24},{4,28},{8,16},{12,20},{16,8},{20,12},{24,0},{28,4},{1,25},{... | collective-permute-start | bytes 983048 | tf_op jit(solution)/shard_map/ppermute | solution.py:263
  34.8 3.6 %collective-permute-start.9 = (bf16[13,48,256]{2,1,0:T(8,128)(2,1)S(1)}, bf16[13,48,256]{2,1,0:T(8,128)(2,1)S(1)}, u32[]{:S(2)}, u32[]{:S(2)}) collective-permute-start(bf16[13,48,256]{2,1,0:T(8,128)(2,1)S(1)} %get-tuple-element.34), channel_id=1, source_target_pairs={{0,4},{4,0},{8,12},{12,8},{16,20},{20,16},{24,28},{28,24},{1,5},{5... | collective-permute-start | bytes 958472 | tf_op jit(solution)/shard_map/ppermute | solution.py:263
  34.9 10.6 %collective-permute-start.10 = (bf16[2,2,160,256]{3,2,1,0:T(8,128)(2,1)S(1)}, bf16[2,2,160,256]{3,2,1,0:T(8,128)(2,1)S(1)}, u32[]{:S(2)}, u32[]{:S(2)}) collective-permute-start(bf16[2,2,160,256]{3,2,1,0:T(8,128)(2,1)S(1)} %get-tuple-element.36.rest_6_), channel_id=1, source_target_pairs={{0,8},{4,12},{8,0},{12,4},{16,24},{20,28},{24,16},{28,20},{1,9},{5... | collective-permute-start | bytes 983048 | tf_op jit(solution)/shard_map/ppermute | solution.py:263
  36.6 16.8 %collective-permute-start.11 = (bf16[2,2,160,256]{3,2,1,0:T(8,128)(2,1)S(1)}, bf16[2,2,160,256]{3,2,1,0:T(8,128)(2,1)S(1)}, u32[]{:S(2)}, u32[]{:S(2)}) collective-permute-start(bf16[2,2,160,256]{3,2,1,0:T(8,128)(2,1)S(1)} %get-tuple-element.36.rest_6_), channel_id=1, source_target_pairs={{0,16},{4,20},{8,24},{12,28},{16,0},{20,4},{24,8},{28,12},{1,17},{... | collective-permute-start | bytes 983048 | tf_op jit(solution)/shard_map/ppermute | solution.py:263
  38.2 15.3 %collective-permute-start.12 = (bf16[2,2,160,256]{3,2,1,0:T(8,128)(2,1)S(1)}, bf16[2,2,160,256]{3,2,1,0:T(8,128)(2,1)S(1)}, u32[]{:S(2)}, u32[]{:S(2)}) collective-permute-start(bf16[2,2,160,256]{3,2,1,0:T(8,128)(2,1)S(1)} %get-tuple-element.36.rest_6_), channel_id=1, source_target_pairs={{0,24},{4,28},{8,16},{12,20},{16,8},{20,12},{24,0},{28,4},{1,25},{... | collective-permute-start | bytes 983048 | tf_op jit(solution)/shard_map/ppermute | solution.py:263
  38.5 21.2 %copy-start.11 = (bf16[13,48,256]{2,1,0:T(8,128)(2,1)}, bf16[13,48,256]{2,1,0:T(8,128)(2,1)S(1)}, u32[]{:S(2)}) copy-start(bf16[13,48,256]{2,1,0:T(8,128)(2,1)S(1)} %broadcast_select_fusion.3) | copy-start | bytes 958468
  38.5 21.2 %collective-permute-start.13 = (bf16[624,256]{1,0:T(8,128)(2,1)S(1)}, bf16[624,256]{1,0:T(8,128)(2,1)S(1)}, u32[]{:S(2)}, u32[]{:S(2)}) collective-permute-start(bf16[624,256]{1,0:T(8,128)(2,1)S(1)} %bitcast.44), channel_id=1, source_target_pairs={{1,2},{2,1},{5,6},{6,5},{9,10},{10,9},{13,14},{14,13},{17,18},{18,... | collective-permute-start | bytes 958472 | tf_op jit(solution)/shard_map/ppermute | solution.py:267
  39.2 20.5 %collective-permute-start.14 = (bf16[624,256]{1,0:T(8,128)(2,1)S(1)}, bf16[624,256]{1,0:T(8,128)(2,1)S(1)}, u32[]{:S(2)}, u32[]{:S(2)}) collective-permute-start(bf16[624,256]{1,0:T(8,128)(2,1)S(1)} %bitcast.45), channel_id=1, source_target_pairs={{0,1},{1,0},{2,3},{3,2},{4,5},{5,4},{6,7},{7,6},{8,9},{9,8},{10,11... | collective-permute-start | bytes 958472 | tf_op jit(solution)/shard_map/ppermute | solution.py:267
  59.7 18.4 %copy-start.19 = (f32[13,48,256]{2,1,0:T(8,128)S(1)}, f32[13,48,256]{2,1,0:T(8,128)}, u32[]{:S(2)}) copy-start(f32[13,48,256]{2,1,0:T(8,128)} %copy-done.17) | copy-start | bytes 1916932
  59.7 23.6 %copy-start.13 = (bf16[624,256]{1,0:T(8,128)(2,1)}, bf16[624,256]{1,0:T(8,128)(2,1)S(1)}, u32[]{:S(2)}) copy-start(bf16[624,256]{1,0:T(8,128)(2,1)S(1)} %collective-permute-done.13.rest_4_) | copy-start | bytes 958468
  59.7 23.6 %copy-start.15 = (bf16[624,256]{1,0:T(8,128)(2,1)}, bf16[624,256]{1,0:T(8,128)(2,1)S(1)}, u32[]{:S(2)}) copy-start(bf16[624,256]{1,0:T(8,128)(2,1)S(1)} %collective-permute-done.14.rest_1_) | copy-start | bytes 958468
  59.7 3.6 %collective-permute-start.15 = (bf16[13,48,256]{2,1,0:T(8,128)(2,1)S(1)}, bf16[13,48,256]{2,1,0:T(8,128)(2,1)S(1)}, u32[]{:S(2)}, u32[]{:S(2)}) collective-permute-start(bf16[13,48,256]{2,1,0:T(8,128)(2,1)S(1)} %get-tuple-element.40), channel_id=1, source_target_pairs={{0,4},{4,0},{8,12},{12,8},{16,20},{20,16},{24,28},{28,24},{1,5},{5... | collective-permute-start | bytes 958472 | tf_op jit(solution)/shard_map/ppermute | solution.py:263
  59.8 10.8 %collective-permute-start.16 = (bf16[2,2,160,256]{3,2,1,0:T(8,128)(2,1)}, bf16[2,2,160,256]{3,2,1,0:T(8,128)(2,1)S(1)}, u32[]{:S(2)}, u32[]{:S(2)}) collective-permute-start(bf16[2,2,160,256]{3,2,1,0:T(8,128)(2,1)} %get-tuple-element.42.rest_6_), channel_id=1, source_target_pairs={{0,8},{4,12},{8,0},{12,4},{16,24},{20,28},{24,16},{28,20},{1,9},{5... | collective-permute-start | bytes 983048 | tf_op jit(solution)/shard_map/ppermute | solution.py:263
  61.1 15.5 %collective-permute-start.17 = (bf16[2,2,160,256]{3,2,1,0:T(8,128)(2,1)}, bf16[2,2,160,256]{3,2,1,0:T(8,128)(2,1)S(1)}, u32[]{:S(2)}, u32[]{:S(2)}) collective-permute-start(bf16[2,2,160,256]{3,2,1,0:T(8,128)(2,1)} %get-tuple-element.42.rest_6_), channel_id=1, source_target_pairs={{0,16},{4,20},{8,24},{12,28},{16,0},{20,4},{24,8},{28,12},{1,17},{... | collective-permute-start | bytes 983048 | tf_op jit(solution)/shard_map/ppermute | solution.py:263
  61.9 16.2 %collective-permute-start.18 = (bf16[2,2,160,256]{3,2,1,0:T(8,128)(2,1)}, bf16[2,2,160,256]{3,2,1,0:T(8,128)(2,1)S(1)}, u32[]{:S(2)}, u32[]{:S(2)}) collective-permute-start(bf16[2,2,160,256]{3,2,1,0:T(8,128)(2,1)} %get-tuple-element.42.rest_6_), channel_id=1, source_target_pairs={{0,24},{4,28},{8,16},{12,20},{16,8},{20,12},{24,0},{28,4},{1,25},{... | collective-permute-start | bytes 983048 | tf_op jit(solution)/shard_map/ppermute | solution.py:263
  63.6 19.7 %collective-permute-start.19 = (bf16[624,512]{1,0:T(8,128)(2,1)S(1)}, bf16[624,512]{1,0:T(8,128)(2,1)S(1)}, u32[]{:S(2)}, u32[]{:S(2)}) collective-permute-start(bf16[624,512]{1,0:T(8,128)(2,1)S(1)} %get-tuple-element.75), channel_id=1, source_target_pairs={{1,2},{2,1},{5,6},{6,5},{9,10},{10,9},{13,14},{14,13},{17,18},{18,... | collective-permute-start | bytes 1916936 | tf_op jit(solution)/shard_map/ppermute | solution.py:267
  64.3 19.1 %copy-start.20 = (bf16[2,2,160,256]{3,2,1,0:T(8,128)(2,1)S(1)}, bf16[2,2,160,256]{3,2,1,0:T(8,128)(2,1)}, u32[]{:S(2)}) copy-start(bf16[2,2,160,256]{3,2,1,0:T(8,128)(2,1)} %get-tuple-element.48.rest_6_) | copy-start | bytes 983044
  64.3 19.0 %collective-permute-start.20 = (bf16[624,512]{1,0:T(8,128)(2,1)S(1)}, bf16[624,512]{1,0:T(8,128)(2,1)S(1)}, u32[]{:S(2)}, u32[]{:S(2)}) collective-permute-start(bf16[624,512]{1,0:T(8,128)(2,1)S(1)} %get-tuple-element.74), channel_id=1, source_target_pairs={{0,1},{1,0},{2,3},{3,2},{4,5},{5,4},{6,7},{7,6},{8,9},{9,8},{10,11... | collective-permute-start | bytes 1916936 | tf_op jit(solution)/shard_map/ppermute | solution.py:267
  83.3 5.6 %copy-start.3 = (bf16[624,512]{1,0:T(8,128)(2,1)}, bf16[624,512]{1,0:T(8,128)(2,1)S(1)}, u32[]{:S(2)}) copy-start(bf16[624,512]{1,0:T(8,128)(2,1)S(1)} %collective-permute-done.19.rest_7_) | copy-start | bytes 1916932
  83.3 5.5 %copy-start.9 = (bf16[624,512]{1,0:T(8,128)(2,1)}, bf16[624,512]{1,0:T(8,128)(2,1)S(1)}, u32[]{:S(2)}) copy-start(bf16[624,512]{1,0:T(8,128)(2,1)S(1)} %collective-permute-done.20.rest_3_) | copy-start | bytes 1916932
  83.3 3.6 %collective-permute-start.21 = (bf16[13,48,256]{2,1,0:T(8,128)(2,1)S(1)}, bf16[13,48,256]{2,1,0:T(8,128)(2,1)S(1)}, u32[]{:S(2)}, u32[]{:S(2)}) collective-permute-start(bf16[13,48,256]{2,1,0:T(8,128)(2,1)S(1)} %get-tuple-element.46), channel_id=1, source_target_pairs={{0,4},{4,0},{8,12},{12,8},{16,20},{20,16},{24,28},{28,24},{1,5},{5... | collective-permute-start | bytes 958472 | tf_op jit(solution)/shard_map/ppermute | solution.py:263
  83.4 10.6 %collective-permute-start.22 = (bf16[2,2,160,256]{3,2,1,0:T(8,128)(2,1)S(1)}, bf16[2,2,160,256]{3,2,1,0:T(8,128)(2,1)S(1)}, u32[]{:S(2)}, u32[]{:S(2)}) collective-permute-start(bf16[2,2,160,256]{3,2,1,0:T(8,128)(2,1)S(1)} %copy-done.20), channel_id=1, source_target_pairs={{0,8},{4,12},{8,0},{12,4},{16,24},{20,28},{24,16},{28,20},{1,9},{5... | collective-permute-start | bytes 983048 | tf_op jit(solution)/shard_map/ppermute | solution.py:263
  84.3 16.8 %collective-permute-start.23 = (bf16[2,2,160,256]{3,2,1,0:T(8,128)(2,1)S(1)}, bf16[2,2,160,256]{3,2,1,0:T(8,128)(2,1)S(1)}, u32[]{:S(2)}, u32[]{:S(2)}) collective-permute-start(bf16[2,2,160,256]{3,2,1,0:T(8,128)(2,1)S(1)} %copy-done.20), channel_id=1, source_target_pairs={{0,16},{4,20},{8,24},{12,28},{16,0},{20,4},{24,8},{28,12},{1,17},{... | collective-permute-start | bytes 983048 | tf_op jit(solution)/shard_map/ppermute | solution.py:263
  85.8 15.3 %collective-permute-start.24 = (bf16[2,2,160,256]{3,2,1,0:T(8,128)(2,1)S(1)}, bf16[2,2,160,256]{3,2,1,0:T(8,128)(2,1)S(1)}, u32[]{:S(2)}, u32[]{:S(2)}) collective-permute-start(bf16[2,2,160,256]{3,2,1,0:T(8,128)(2,1)S(1)} %copy-done.20), channel_id=1, source_target_pairs={{0,24},{4,28},{8,16},{12,20},{16,8},{20,12},{24,0},{28,4},{1,25},{... | collective-permute-start | bytes 983048 | tf_op jit(solution)/shard_map/ppermute | solution.py:263
  87.2 22.8 %collective-permute-start.25 = (bf16[624,768]{1,0:T(8,128)(2,1)S(1)}, bf16[624,768]{1,0:T(8,128)(2,1)S(1)}, u32[]{:S(2)}, u32[]{:S(2)}) collective-permute-start(bf16[624,768]{1,0:T(8,128)(2,1)S(1)} %pad_maximum_fusion), channel_id=1, source_target_pairs={{0,1},{1,0},{2,3},{3,2},{4,5},{5,4},{6,7},{7,6},{8,9},{9,8},{10,11... | collective-permute-start | bytes 2875400 | tf_op jit(solution)/shard_map/ppermute | solution.py:267
  88.9 17.3 %collective-permute-start.26 = (bf16[624,512]{1,0:T(8,128)(2,1)S(1)}, bf16[624,512]{1,0:T(8,128)(2,1)S(1)}, u32[]{:S(2)}, u32[]{:S(2)}) collective-permute-start(bf16[624,512]{1,0:T(8,128)(2,1)S(1)} %pad_maximum_fusion.4), channel_id=1, source_target_pairs={{1,2},{2,1},{5,6},{6,5},{9,10},{10,9},{13,14},{14,13},{17,18},{18,... | collective-permute-start | bytes 1916936 | tf_op jit(solution)/shard_map/ppermute | solution.py:267
  106.2 9.0 %copy-start.5 = (bf16[624,512]{1,0:T(8,128)(2,1)}, bf16[624,512]{1,0:T(8,128)(2,1)S(1)}, u32[]{:S(2)}) copy-start(bf16[624,512]{1,0:T(8,128)(2,1)S(1)} %collective-permute-done.26.rest_3_) | copy-start | bytes 1916932
  110.0 5.3 %copy-start.7 = (bf16[624,768]{1,0:T(8,128)(2,1)}, bf16[624,768]{1,0:T(8,128)(2,1)S(1)}, u32[]{:S(2)}) copy-start(bf16[624,768]{1,0:T(8,128)(2,1)S(1)} %collective-permute-done.25.rest_6_) | copy-start | bytes 2875396
  110.0 1.6 %collective-permute-start.27 = (bf16[13,48,256]{2,1,0:T(8,128)(2,1)S(1)}, bf16[13,48,256]{2,1,0:T(8,128)(2,1)S(1)}, u32[]{:S(2)}, u32[]{:S(2)}) collective-permute-start(bf16[13,48,256]{2,1,0:T(8,128)(2,1)S(1)} %get-tuple-element.54), channel_id=1, source_target_pairs={{0,4},{4,0},{8,12},{12,8},{16,20},{20,16},{24,28},{28,24},{1,5},{5... | collective-permute-start | bytes 958472 | tf_op jit(solution)/shard_map/ppermute | solution.py:263
  112.7 23.6 %collective-permute-start.28 = (bf16[624,768]{1,0:T(8,128)(2,1)}, bf16[624,768]{1,0:T(8,128)(2,1)}, u32[]{:S(2)}, u32[]{:S(2)}) collective-permute-start(bf16[624,768]{1,0:T(8,128)(2,1)} %pad_maximum_fusion.1), channel_id=1, source_target_pairs={{0,1},{1,0},{2,3},{3,2},{4,5},{5,4},{6,7},{7,6},{8,9},{9,8},{10,11... | collective-permute-start | bytes 2875400 | tf_op jit(solution)/shard_map/ppermute | solution.py:267
  115.2 13.0 %collective-permute-start.29 = (bf16[624,512]{1,0:T(8,128)(2,1)}, bf16[624,512]{1,0:T(8,128)(2,1)}, u32[]{:S(2)}, u32[]{:S(2)}) collective-permute-start(bf16[624,512]{1,0:T(8,128)(2,1)} %pad_maximum_fusion.5), channel_id=1, source_target_pairs={{1,2},{2,1},{5,6},{6,5},{9,10},{10,9},{13,14},{14,13},{17,18},{18,... | collective-permute-start | bytes 1916936 | tf_op jit(solution)/shard_map/ppermute | solution.py:267
  116.7 4.1 %copy-start.10 = (bf16[624,512]{1,0:T(8,128)(2,1)S(1)}, bf16[624,512]{1,0:T(8,128)(2,1)}, u32[]{:S(2)}) copy-start(bf16[624,512]{1,0:T(8,128)(2,1)} %copy-done.9) | copy-start | bytes 1916932
  116.7 4.1 %copy-start.12 = (bf16[13,48,256]{2,1,0:T(8,128)(2,1)S(1)}, bf16[13,48,256]{2,1,0:T(8,128)(2,1)}, u32[]{:S(2)}) copy-start(bf16[13,48,256]{2,1,0:T(8,128)(2,1)} %copy-done.11) | copy-start | bytes 958468
  116.7 4.1 %copy-start.14 = (bf16[624,256]{1,0:T(8,128)(2,1)S(1)}, bf16[624,256]{1,0:T(8,128)(2,1)}, u32[]{:S(2)}) copy-start(bf16[624,256]{1,0:T(8,128)(2,1)} %copy-done.13) | copy-start | bytes 958468
  116.7 4.1 %copy-start.16 = (bf16[624,256]{1,0:T(8,128)(2,1)S(1)}, bf16[624,256]{1,0:T(8,128)(2,1)}, u32[]{:S(2)}) copy-start(bf16[624,256]{1,0:T(8,128)(2,1)} %copy-done.15) | copy-start | bytes 958468
  128.2 25.6 %collective-permute-start.30 = (bf16[624,512]{1,0:T(8,128)(2,1)}, bf16[624,512]{1,0:T(8,128)(2,1)}, u32[]{:S(2)}, u32[]{:S(2)}) collective-permute-start(bf16[624,512]{1,0:T(8,128)(2,1)} %collective-permute-done.29.rest_2_), channel_id=1, source_target_pairs={{1,0},{2,3},{5,4},{6,7},{9,8},{10,11},{13,12},{14,15},{17,16},{18,... | collective-permute-start | bytes 1916936 | tf_op jit(solution)/shard_map/ppermute | solution.py:267
  137.3 7.4 %collective-permute-start.31 = (bf16[624,256]{1,0:T(8,128)(2,1)S(1)}, bf16[624,256]{1,0:T(8,128)(2,1)S(1)}, u32[]{:S(2)}, u32[]{:S(2)}) collective-permute-start(bf16[624,256]{1,0:T(8,128)(2,1)S(1)} %slice.52), channel_id=1, source_target_pairs={{1,2},{2,1},{5,6},{6,5},{9,10},{10,9},{13,14},{14,13},{17,18},{18,... | collective-permute-start | bytes 958472 | tf_op jit(solution)/shard_map/ppermute | solution.py:267
  144.6 12.5 %collective-permute-start.32 = (bf16[624,256]{1,0:T(8,128)(2,1)S(1)}, bf16[624,256]{1,0:T(8,128)(2,1)S(1)}, u32[]{:S(2)}, u32[]{:S(2)}) collective-permute-start(bf16[624,256]{1,0:T(8,128)(2,1)S(1)} %collective-permute-done.31.rest_2_), channel_id=1, source_target_pairs={{1,0},{2,3},{5,4},{6,7},{9,8},{10,11},{13,12},{14,15},{17,16},{18,... | collective-permute-start | bytes 958472 | tf_op jit(solution)/shard_map/ppermute | solution.py:267
  (9 other events, 25.3 us)

commit v4 on v3

--- a/solution.py
+++ b/solution.py
@@ -12,6 +12,7 @@
 NEG_FILL = -1e30
 HEAD_CHUNKS = (2, 2, 2, 2)
 SPLITS = (2, 3, 4, 5)
+FRONT = 1
 
 
 K_FLOPS = 2_700_000_000
@@ -336,11 +337,10 @@
         gathered.append([block] + [across(block, m) for m in (2, 4, 6)])
 
     gather(0)
-    queries, tree_cache, tree_mask, dest_group = lax.optimization_barrier(
-        (queries, tree_cache, tree_mask, dest_group, gathered[0][0])
-    )[:4]
+    queries, tree_cache = lax.optimization_barrier((queries, tree_cache, gathered[0][0]))[:2]
     other_queries = across(queries, 1)
     other_tree = across(tree_cache, 1)
+    tree_mask, dest_group = lax.optimization_barrier((tree_mask, dest_group, gathered[0][FRONT]))[:2]
     other_mask = across(tree_mask, 1)
     group, other_group = dest_group[:, 0], across(dest_group, 1)[:, 0]
     me = lax.axis_index("rep").astype(jnp.int32)

time: 161 us -> 157 us (0.975)
  starting transfers between devices: 39.6 us -> 35.9 us
    ppermute x22, starting transfers between devices: 20.1 us -> 16.6 us  [across(): lax.ppermute(value, 'rep', [(i, i ^ mask) for i in range(lax.axis_size('r...]
    unnamed x49 -> x53, local copies, waits for them, and re-layouts: 9.8 us -> 11.5 us
  transfers between devices with their start and end apart: 33 -> 33, of which waited for: 13 -> 16; matrix products, arithmetic and copies ran while one was open for 11% -> 10% of each run, Pallas kernels for 16% -> 16%
where the time goes in v4:
time: 157 us; the launch traced here: 155 us
  waiting for transfers between devices  55.8 us (36%)
  starting transfers between devices  35.9 us (23%)
  Pallas kernels  31.8 us (20%)
  local copies, waits for them, and re-layouts  22.7 us (14%)
  other arithmetic  6.33 us (4%)
  between operations  2.84 us (2%)
    ppermute x22, waiting for transfers between devices, across(): lax.ppermute(value, 'rep', [(i, i ^ mask) for i in range(lax.axis_size('r...  44.8 us
    pallas_call x4, Pallas kernels, attend_pairs(): pl.pallas_call(partial(paired_kernel, start=start, inside=inside, n_cache...  20.7 us
    ppermute x11, starting transfers between devices, along(): return lax.ppermute(value, 'tp', pairs)  19.3 us
    ppermute x22, starting transfers between devices, across(): lax.ppermute(value, 'rep', [(i, i ^ mask) for i in range(lax.axis_size('r...  16.6 us
    unnamed x53, local copies, waits for them, and re-layouts  11.5 us
    pallas_call x4, Pallas kernels, project(): pl.pallas_call(partial(project_kernel, steps=tuple(shape), has_acc=acc is...  11.1 us
    ppermute x11, waiting for transfers between devices, along(): return lax.ppermute(value, 'tp', pairs)  11 us
    gather x3, local copies, waits for them, and re-layouts, local(): jnp.take_along_axis(tree_cache, path[:, None, :, None], axis=2)  4.66 us
  transfers between devices with their start and end apart: 33, of which 16 were waited for; matrix products, arithmetic and copies ran while one was open for 10% of the time, Pallas kernels for 16%

profile of v4, /device:TPU:0, one launch (start us, length us, event | category | flops | bytes accessed | tf_op | source)
XLA Modules:
  0.0 155.5 jit_solution(18228178959144854048)
XLA Ops:
  1.9 1.2 fusion.21
  4.1 1.3 fusion.16
  5.8 2.6 %collective-permute-start.2 = (bf16[2,2,160,256]{3,2,1,0:T(8,128)(2,1)}, bf16[2,2,160,256]{3,2,1,0:T(8,128)(2,1)S(1)}, u32[]{:S(2)}, u32[]{:S(2)}) collective-permute-start(bf16[2,2,160,256]{3,2,1,0:T(8,128)(2,1)} %get-tuple-element.79.rest_6_), channel_id=1, source_target_pairs={{0,8},{4,12},{8,0},{12,4},{16,24},{20,28},{24,16},{28,20},{1,9},{5... | collective-permute-start | bytes 983048 | tf_op jit(solution)/shard_map/ppermute | solution.py:264
  8.6 1.5 collective-permute-start.7
  10.3 6.9 %collective-permute-done.2.rest_7_ = bf16[2,2,160,256]{3,2,1,0:T(8,128)(2,1)S(1)} collective-permute-done((bf16[2,2,160,256]{3,2,1,0:T(8,128)(2,1)}, bf16[2,2,160,256]{3,2,1,0:T(8,128)(2,1)S(1)}, u32[]{:S(2)}, u32[]{:S(2)}) %collective-permute-start.2) | collective-permute-done | bytes 327712 | tf_op jit(solution)/shard_map/ppermute | solution.py:264
  18.0 1.0 collective-permute-done.3
  19.5 1.5 collective-permute-done.6
  22.0 3.8 %collective-permute-done.7.rest_8_ = bf16[2,2,160,256]{3,2,1,0:T(8,128)(2,1)} collective-permute-done((bf16[2,2,160,256]{3,2,1,0:T(8,128)(2,1)}, bf16[2,2,160,256]{3,2,1,0:T(8,128)(2,1)}, u32[]{:S(2)}, u32[]{:S(2)}) %collective-permute-start.7) | collective-permute-done | bytes 327712 | tf_op jit(solution)/shard_map/ppermute | solution.py:264
  26.8 5.3 %shard_map.122 = (bf16[13,48,256]{2,1,0:T(8,128)(2,1)S(1)}, bf16[13,48,256]{2,1,0:T(8,128)(2,1)S(1)}) custom-call(s32[6,4]{1,0:T(8,128)S(1)} %stack.26.slot_ref, bf16[13,48,1024]{2,1,0:T(8,128)(2,1)} %rest_0_.3, bf16[13,2,48,1024]{3,2,1,0:T(8,128)(2,1)S(1)} %copy-done.2, f32[13,48,256]{2,1,0:T(8,128)S(1)} %pad.21.rest_2_, ...), custom_call_target="tpu_custom_call" | custom-call | flops 8099999744 | bytes 1000 | tf_op jit(solution)/shard_map/pallas_call | solution.py:178
  33.2 1.2 collective-permute-start.11
  34.4 1.4 collective-permute-start.12
  36.6 4.4 %collective-permute-start.14 = (bf16[624,256]{1,0:T(8,128)(2,1)S(1)}, bf16[624,256]{1,0:T(8,128)(2,1)S(1)}, u32[]{:S(2)}, u32[]{:S(2)}) collective-permute-start(bf16[624,256]{1,0:T(8,128)(2,1)S(1)} %bitcast.45), channel_id=1, source_target_pairs={{0,1},{1,0},{2,3},{3,2},{4,5},{5,4},{6,7},{7,6},{8,9},{9,8},{10,11... | collective-permute-start | bytes 958472 | tf_op jit(solution)/shard_map/ppermute | solution.py:268
  41.1 1.8 %collective-permute-done.10.rest_7_ = bf16[2,2,160,256]{3,2,1,0:T(8,128)(2,1)S(1)} collective-permute-done((bf16[2,2,160,256]{3,2,1,0:T(8,128)(2,1)S(1)}, bf16[2,2,160,256]{3,2,1,0:T(8,128)(2,1)S(1)}, u32[]{:S(2)}, u32[]{:S(2)}) %collective-permute-start.10) | collective-permute-done | bytes 327712 | tf_op jit(solution)/shard_map/ppermute | solution.py:264
  42.8 5.9 %collective-permute-done.11.rest_8_ = bf16[2,2,160,256]{3,2,1,0:T(8,128)(2,1)S(1)} collective-permute-done((bf16[2,2,160,256]{3,2,1,0:T(8,128)(2,1)S(1)}, bf16[2,2,160,256]{3,2,1,0:T(8,128)(2,1)S(1)}, u32[]{:S(2)}, u32[]{:S(2)}) %collective-permute-start.11) | collective-permute-done | bytes 327712 | tf_op jit(solution)/shard_map/ppermute | solution.py:264
  48.7 1.6 %collective-permute-done.12.rest_9_ = bf16[2,2,160,256]{3,2,1,0:T(8,128)(2,1)S(1)} collective-permute-done((bf16[2,2,160,256]{3,2,1,0:T(8,128)(2,1)S(1)}, bf16[2,2,160,256]{3,2,1,0:T(8,128)(2,1)S(1)}, u32[]{:S(2)}, u32[]{:S(2)}) %collective-permute-start.12) | collective-permute-done | bytes 327712 | tf_op jit(solution)/shard_map/ppermute | solution.py:264
  50.4 1.1 copy-done.18
  51.4 5.1 %shard_map.123 = (bf16[13,48,256]{2,1,0:T(8,128)(2,1)S(1)}, bf16[13,48,256]{2,1,0:T(8,128)(2,1)S(1)}) custom-call(s32[6,4]{1,0:T(8,128)S(1)} %stack.26.slot_ref, bf16[13,48,1024]{2,1,0:T(8,128)(2,1)} %rest_0_.3, bf16[13,2,48,1024]{3,2,1,0:T(8,128)(2,1)S(1)} %copy-done.2, f32[13,48,256]{2,1,0:T(8,128)S(1)} %copy-done.18, ...), custom_call_target="tpu_custom_call" | custom-call | flops 8099999744 | bytes 1000 | tf_op jit(solution)/shard_map/pallas_call | solution.py:178
  57.6 1.5 collective-permute-start.17
  59.1 1.2 collective-permute-start.18
  61.2 4.4 %collective-permute-start.20 = (bf16[624,512]{1,0:T(8,128)(2,1)S(1)}, bf16[624,512]{1,0:T(8,128)(2,1)S(1)}, u32[]{:S(2)}, u32[]{:S(2)}) collective-permute-start(bf16[624,512]{1,0:T(8,128)(2,1)S(1)} %get-tuple-element.74), channel_id=1, source_target_pairs={{0,1},{1,0},{2,3},{3,2},{4,5},{5,4},{6,7},{7,6},{8,9},{9,8},{10,11... | collective-permute-start | bytes 1916936 | tf_op jit(solution)/shard_map/ppermute | solution.py:268
  65.6 1.9 %collective-permute-done.16.rest_7_ = bf16[2,2,160,256]{3,2,1,0:T(8,128)(2,1)S(1)} collective-permute-done((bf16[2,2,160,256]{3,2,1,0:T(8,128)(2,1)}, bf16[2,2,160,256]{3,2,1,0:T(8,128)(2,1)S(1)}, u32[]{:S(2)}, u32[]{:S(2)}) %collective-permute-start.16) | collective-permute-done | bytes 327712 | tf_op jit(solution)/shard_map/ppermute | solution.py:264
  67.5 7.1 %collective-permute-done.17.rest_8_ = bf16[2,2,160,256]{3,2,1,0:T(8,128)(2,1)S(1)} collective-permute-done((bf16[2,2,160,256]{3,2,1,0:T(8,128)(2,1)}, bf16[2,2,160,256]{3,2,1,0:T(8,128)(2,1)S(1)}, u32[]{:S(2)}, u32[]{:S(2)}) %collective-permute-start.17) | collective-permute-done | bytes 327712 | tf_op jit(solution)/shard_map/ppermute | solution.py:264
  74.6 5.1 %shard_map.124 = (bf16[13,48,256]{2,1,0:T(8,128)(2,1)S(1)}, bf16[13,48,256]{2,1,0:T(8,128)(2,1)S(1)}) custom-call(s32[6,4]{1,0:T(8,128)S(1)} %stack.26.slot_ref, bf16[13,48,1024]{2,1,0:T(8,128)(2,1)} %rest_0_.3, bf16[13,2,48,1024]{3,2,1,0:T(8,128)(2,1)S(1)} %copy-done.2, f32[13,48,256]{2,1,0:T(8,128)S(1)} %copy-done.19, ...), custom_call_target="tpu_custom_call" | custom-call | flops 8099999744 | bytes 1000 | tf_op jit(solution)/shard_map/pallas_call | solution.py:178
  79.9 1.3 collective-permute-start.22
  82.0 1.4 collective-permute-start.24
  83.6 1.6 %collective-permute-start.25 = (bf16[624,768]{1,0:T(8,128)(2,1)S(1)}, bf16[624,768]{1,0:T(8,128)(2,1)S(1)}, u32[]{:S(2)}, u32[]{:S(2)}) collective-permute-start(bf16[624,768]{1,0:T(8,128)(2,1)S(1)} %pad_maximum_fusion), channel_id=1, source_target_pairs={{0,1},{1,0},{2,3},{3,2},{4,5},{5,4},{6,7},{7,6},{8,9},{9,8},{10,11... | collective-permute-start | bytes 2875400 | tf_op jit(solution)/shard_map/ppermute | solution.py:268
  86.3 4.2 %collective-permute-done.22.rest_7_ = bf16[2,2,160,256]{3,2,1,0:T(8,128)(2,1)S(1)} collective-permute-done((bf16[2,2,160,256]{3,2,1,0:T(8,128)(2,1)S(1)}, bf16[2,2,160,256]{3,2,1,0:T(8,128)(2,1)S(1)}, u32[]{:S(2)}, u32[]{:S(2)}) %collective-permute-start.22) | collective-permute-done | bytes 327712 | tf_op jit(solution)/shard_map/ppermute | solution.py:264
  90.5 5.9 %collective-permute-done.23.rest_8_ = bf16[2,2,160,256]{3,2,1,0:T(8,128)(2,1)S(1)} collective-permute-done((bf16[2,2,160,256]{3,2,1,0:T(8,128)(2,1)S(1)}, bf16[2,2,160,256]{3,2,1,0:T(8,128)(2,1)S(1)}, u32[]{:S(2)}, u32[]{:S(2)}) %collective-permute-start.23) | collective-permute-done | bytes 327712 | tf_op jit(solution)/shard_map/ppermute | solution.py:264
  96.4 1.6 %collective-permute-done.24.rest_9_ = bf16[2,2,160,256]{3,2,1,0:T(8,128)(2,1)S(1)} collective-permute-done((bf16[2,2,160,256]{3,2,1,0:T(8,128)(2,1)S(1)}, bf16[2,2,160,256]{3,2,1,0:T(8,128)(2,1)S(1)}, u32[]{:S(2)}, u32[]{:S(2)}) %collective-permute-start.24) | collective-permute-done | bytes 327712 | tf_op jit(solution)/shard_map/ppermute | solution.py:264
  98.0 5.1 %shard_map.125 = (bf16[13,48,256]{2,1,0:T(8,128)(2,1)S(1)}, bf16[13,48,256]{2,1,0:T(8,128)(2,1)S(1)}) custom-call(s32[6,4]{1,0:T(8,128)S(1)} %stack.26.slot_ref, bf16[13,48,1024]{2,1,0:T(8,128)(2,1)} %rest_0_.3, bf16[13,2,48,1024]{3,2,1,0:T(8,128)(2,1)S(1)} %copy-done.2, f32[13,48,256]{2,1,0:T(8,128)S(1)} %copy-done.19, ...), custom_call_target="tpu_custom_call" | custom-call | flops 8099999744 | bytes 1000 | tf_op jit(solution)/shard_map/pallas_call | solution.py:178
  103.2 3.3 %collective-permute-done.25.rest_6_ = bf16[624,768]{1,0:T(8,128)(2,1)S(1)} collective-permute-done((bf16[624,768]{1,0:T(8,128)(2,1)S(1)}, bf16[624,768]{1,0:T(8,128)(2,1)S(1)}, u32[]{:S(2)}, u32[]{:S(2)}) %collective-permute-start.25) | collective-permute-done | bytes 958496 | tf_op jit(solution)/shard_map/ppermute | solution.py:268
  106.4 1.6 %collective-permute-done.27 = bf16[13,48,256]{2,1,0:T(8,128)(2,1)S(1)} collective-permute-done((bf16[13,48,256]{2,1,0:T(8,128)(2,1)S(1)}, bf16[13,48,256]{2,1,0:T(8,128)(2,1)S(1)}, u32[]{:S(2)}, u32[]{:S(2)}) %collective-permute-start.27) | collective-permute-done | bytes 319520 | tf_op jit(solution)/shard_map/ppermute | solution.py:264
  108.2 1.0 pad_maximum_fusion.1
  109.2 1.6 %collective-permute-start.28 = (bf16[624,768]{1,0:T(8,128)(2,1)}, bf16[624,768]{1,0:T(8,128)(2,1)}, u32[]{:S(2)}, u32[]{:S(2)}) collective-permute-start(bf16[624,768]{1,0:T(8,128)(2,1)} %pad_maximum_fusion.1), channel_id=1, source_target_pairs={{0,1},{1,0},{2,3},{3,2},{4,5},{5,4},{6,7},{7,6},{8,9},{9,8},{10,11... | collective-permute-start | bytes 2875400 | tf_op jit(solution)/shard_map/ppermute | solution.py:268
  111.7 1.5 collective-permute-start.29
  113.2 4.1 %copy.24 = bf16[13,2,48,1024]{3,1,2,0:T(2,128)(2,1)} copy(bf16[13,2,48,1024]{3,2,1,0:T(8,128)(2,1)S(1)} %copy-done.2) | data formatting | bytes 5111808 | tf_op jit(solution)/shard_map/optimization_barrier | solution.py:340
  117.4 3.4 %copy-done = bf16[4096,1024]{1,0:T(8,128)(2,1)S(1)} copy-done((bf16[4096,1024]{1,0:T(8,128)(2,1)S(1)}, bf16[4096,1024]{1,0:T(8,128)(2,1)}, u32[]{:S(2)}) %copy-start) | copy-done | bytes 8388632
  120.8 3.9 %shard_map.126.rest_0_ = f32[624,1024]{1,0:T(8,128)S(1)} custom-call(s32[1]{0:T(128)} %bitcast.z_ref, bf16[4,1024,1024]{2,1,0:T(8,128)(2,1)S(1)} %bitcast.32, bf16[624,256]{1,0:T(8,128)(2,1)S(1)} %bitcast.46, bf16[624,256]{1,0:T(8,128)(2,1)S(1)} %copy-done.16, bf16[624,256]{1,0:T(8,128)(2,1)S(1)} %bitcast.43, bf16[624,512]{1,0:T(8,128)(2,1)S(1)} %copy-done.10, ...), custom_call_target="tpu_custom_call" | custom-call | flops 2000000000 | bytes 1000 | tf_op jit(solution)/shard_map/pallas_call | solution.py:241
  124.7 1.3 collective-permute-start.30
  126.0 6.8 %collective-permute-done.28.rest_2_ = bf16[624,768]{1,0:T(8,128)(2,1)} collective-permute-done((bf16[624,768]{1,0:T(8,128)(2,1)}, bf16[624,768]{1,0:T(8,128)(2,1)}, u32[]{:S(2)}, u32[]{:S(2)}) %collective-permute-start.28) | collective-permute-done | bytes 958496 | tf_op jit(solution)/shard_map/ppermute | solution.py:268
  134.7 4.5 %gather_fusion = bf16[104,2,1024]{2,1,0:T(2,128)(2,1)} fusion(bf16[13,2,48,1024]{3,1,2,0:T(2,128)(2,1)} %copy.24, s32[104]{0:T(128)S(1)} %reshape.134), kind=kCustom, calls=%fused_computation | custom fusion | bytes 852800 | tf_op jit(solution)/shard_map/jit(take_along_axis)/gather | solution.py:393
  139.2 1.1 fusion.8
  141.1 1.5 collective-permute-start.32
  142.6 3.4 %copy-done.1 = bf16[4096,1024]{1,0:T(8,128)(2,1)S(1)} copy-done((bf16[4096,1024]{1,0:T(8,128)(2,1)S(1)}, bf16[4096,1024]{1,0:T(8,128)(2,1)}, u32[]{:S(2)}) %copy-start.1) | copy-done | bytes 8388632
  146.0 1.1 copy-done.6
  147.1 3.2 %shard_map.127.rest_0_ = f32[624,1024]{1,0:T(8,128)S(1)} custom-call(s32[1]{0:T(128)} %bitcast.z_ref, bf16[4,1024,1024]{2,1,0:T(8,128)(2,1)S(1)} %bitcast.33, f32[624,1024]{1,0:T(8,128)S(1)} %shard_map.126.rest_0_, bf16[624,256]{1,0:T(8,128)(2,1)S(1)} %bitcast.41, bf16[624,768]{1,0:T(8,128)(2,1)} %collective-permute-done.28.rest_2_, ...), custom_call_target="tpu_custom_call", output_to_operand_aliasing={{}: (2, {})} | custom-call | flops 2000000000 | bytes 1000 | tf_op jit(solution)/shard_map/pallas_call | solution.py:241
  150.3 2.4 %shard_map.128.rest_0_ = f32[624,1024]{1,0:T(8,128)S(1)} custom-call(s32[1]{0:T(128)} %bitcast.z_ref, bf16[4,1024,1024]{2,1,0:T(8,128)(2,1)S(1)} %bitcast.34, f32[624,1024]{1,0:T(8,128)S(1)} %shard_map.127.rest_0_, bf16[624,512]{1,0:T(8,128)(2,1)} %collective-permute-done.30.rest_1_, ...), custom_call_target="tpu_custom_call", output_to_operand_aliasing={{}: (2, {})} | custom-call | flops 2000000000 | bytes 1000 | tf_op jit(solution)/shard_map/pallas_call | solution.py:241
  153.7 1.6 %shard_map.129 = bf16[624,1024]{1,0:T(8,128)(2,1)} custom-call(s32[1]{0:T(128)} %bitcast.z_ref, bf16[4,1024,1024]{2,1,0:T(8,128)(2,1)S(1)} %bitcast.35, f32[624,1024]{1,0:T(8,128)S(1)} %shard_map.128.rest_0_, bf16[624,256]{1,0:T(8,128)(2,1)S(1)} %collective-permute-done.32.rest_1_, bf16[624,256]{1,0:T(8,128)(2,1)S(1)} %collective-permute-done.31.rest_2_), custom_call_target="tpu_custom_call" | custom-call | flops 2000000000 | bytes 1000 | tf_op jit(solution)/shard_map/pallas_call | solution.py:241
  (114 shorter events, 15.3 us)
Async XLA Ops:
  0.6 3.4 %collective-permute-start.1 = (bf16[1,2,152,1024]{3,2,1,0:T(8,128)(2,1)}, bf16[1,2,152,1024]{3,2,1,0:T(8,128)(2,1)S(1)}, u32[]{:S(2)}, u32[]{:S(2)}) collective-permute-start(bf16[1,2,152,1024]{3,2,1,0:T(8,128)(2,1)} %param.18), channel_id=1, source_target_pairs={{0,4},{4,0},{8,12},{12,8},{16,20},{20,16},{24,28},{28,24},{1,5},{5... | collective-permute-start | bytes 1867784 | tf_op jit(solution)/shard_map/ppermute | solution.py:264
  1.1 2.0 %collective-permute-start = (s32[1]{0:T(128)}, s32[1]{0:T(128)}, u32[]{:S(2)}, u32[]{:S(2)}) collective-permute-start(s32[1]{0:T(128)} %param.19), channel_id=1, source_target_pairs={{0,4},{4,0},{8,12},{12,8},{16,20},{20,16},{24,28},{28,24},{1,5},{5... | collective-permute-start | bytes 20 | tf_op jit(solution)/shard_map/ppermute | solution.py:264
  3.1 14.8 %copy-start.25 = (s32[13,1]{0,1:T(1,128)S(1)}, s32[13,1]{0,1:T(1,128)}, u32[]{:S(2)}) copy-start(s32[13,1]{0,1:T(1,128)} %param.14) | copy-start | bytes 160
  3.1 14.8 %copy-start.23 = (s32[13,48,48]{2,1,0:T(8,128)S(1)}, s32[13,48,48]{2,1,0:T(8,128)}, u32[]{:S(2)}) copy-start(s32[13,48,48]{2,1,0:T(8,128)} %param.13) | copy-start | bytes 359428
  5.4 20.5 %collective-permute-start.5 = (bf16[13,2,48,1024]{3,2,1,0:T(8,128)(2,1)S(1)}, bf16[13,2,48,1024]{3,2,1,0:T(8,128)(2,1)}, u32[]{:S(2)}, u32[]{:S(2)}) collective-permute-start(bf16[13,2,48,1024]{3,2,1,0:T(8,128)(2,1)S(1)} %copy-done.2), channel_id=1, source_target_pairs={{0,4},{4,0},{8,12},{12,8},{16,20},{20,16},{24,28},{28,24},{1,5},{5... | collective-permute-start | bytes 7667720 | tf_op jit(solution)/shard_map/ppermute | solution.py:264
  5.8 11.3 %collective-permute-start.2 = (bf16[2,2,160,256]{3,2,1,0:T(8,128)(2,1)}, bf16[2,2,160,256]{3,2,1,0:T(8,128)(2,1)S(1)}, u32[]{:S(2)}, u32[]{:S(2)}) collective-permute-start(bf16[2,2,160,256]{3,2,1,0:T(8,128)(2,1)} %get-tuple-element.79.rest_6_), channel_id=1, source_target_pairs={{0,8},{4,12},{8,0},{12,4},{16,24},{20,28},{24,16},{28,20},{1,9},{5... | collective-permute-start | bytes 983048 | tf_op jit(solution)/shard_map/ppermute | solution.py:264
  8.4 17.5 %collective-permute-start.4 = (bf16[13,48,1024]{2,1,0:T(8,128)(2,1)}, bf16[13,48,1024]{2,1,0:T(8,128)(2,1)}, u32[]{:S(2)}, u32[]{:S(2)}) collective-permute-start(bf16[13,48,1024]{2,1,0:T(8,128)(2,1)} %rest_0_.3), channel_id=1, source_target_pairs={{0,4},{4,0},{8,12},{12,8},{16,20},{20,16},{24,28},{28,24},{1,5},{5... | collective-permute-start | bytes 3833864 | tf_op jit(solution)/shard_map/ppermute | solution.py:264
  8.6 17.3 %collective-permute-start.7 = (bf16[2,2,160,256]{3,2,1,0:T(8,128)(2,1)}, bf16[2,2,160,256]{3,2,1,0:T(8,128)(2,1)}, u32[]{:S(2)}, u32[]{:S(2)}) collective-permute-start(bf16[2,2,160,256]{3,2,1,0:T(8,128)(2,1)} %get-tuple-element.79.rest_6_), channel_id=1, source_target_pairs={{0,16},{4,20},{8,24},{12,28},{16,0},{20,4},{24,8},{28,12},{1,17},{... | collective-permute-start | bytes 983048 | tf_op jit(solution)/shard_map/ppermute | solution.py:264
  10.1 15.8 %collective-permute-start.8 = (bf16[2,2,160,256]{3,2,1,0:T(8,128)(2,1)}, bf16[2,2,160,256]{3,2,1,0:T(8,128)(2,1)}, u32[]{:S(2)}, u32[]{:S(2)}) collective-permute-start(bf16[2,2,160,256]{3,2,1,0:T(8,128)(2,1)} %get-tuple-element.79.rest_6_), channel_id=1, source_target_pairs={{0,24},{4,28},{8,16},{12,20},{16,8},{20,12},{24,0},{28,4},{1,25},{... | collective-permute-start | bytes 983048 | tf_op jit(solution)/shard_map/ppermute | solution.py:264
  17.9 1.1 collective-permute-start.3
  18.0 14.2 %copy-start.17 = (f32[13,48,256]{2,1,0:T(8,128)}, f32[13,48,256]{2,1,0:T(8,128)S(1)}, u32[]{:S(2)}) copy-start(f32[13,48,256]{2,1,0:T(8,128)S(1)} %pad.21.rest_2_) | copy-start | bytes 1916932
  19.0 2.0 %collective-permute-start.6 = (s32[13,48,48]{2,1,0:T(8,128)}, s32[13,48,48]{2,1,0:T(8,128)}, u32[]{:S(2)}, u32[]{:S(2)}) collective-permute-start(s32[13,48,48]{2,1,0:T(8,128)} %param.13), channel_id=1, source_target_pairs={{0,4},{4,0},{8,12},{12,8},{16,20},{20,16},{24,28},{28,24},{1,5},{5... | collective-permute-start | bytes 359432 | tf_op jit(solution)/shard_map/ppermute | solution.py:264
  32.2 3.6 %collective-permute-start.9 = (bf16[13,48,256]{2,1,0:T(8,128)(2,1)S(1)}, bf16[13,48,256]{2,1,0:T(8,128)(2,1)S(1)}, u32[]{:S(2)}, u32[]{:S(2)}) collective-permute-start(bf16[13,48,256]{2,1,0:T(8,128)(2,1)S(1)} %get-tuple-element.34), channel_id=1, source_target_pairs={{0,4},{4,0},{8,12},{12,8},{16,20},{20,16},{24,28},{28,24},{1,5},{5... | collective-permute-start | bytes 958472 | tf_op jit(solution)/shard_map/ppermute | solution.py:264
  32.3 10.6 %collective-permute-start.10 = (bf16[2,2,160,256]{3,2,1,0:T(8,128)(2,1)S(1)}, bf16[2,2,160,256]{3,2,1,0:T(8,128)(2,1)S(1)}, u32[]{:S(2)}, u32[]{:S(2)}) collective-permute-start(bf16[2,2,160,256]{3,2,1,0:T(8,128)(2,1)S(1)} %get-tuple-element.36.rest_6_), channel_id=1, source_target_pairs={{0,8},{4,12},{8,0},{12,4},{16,24},{20,28},{24,16},{28,20},{1,9},{5... | collective-permute-start | bytes 983048 | tf_op jit(solution)/shard_map/ppermute | solution.py:264
  33.2 15.5 %collective-permute-start.11 = (bf16[2,2,160,256]{3,2,1,0:T(8,128)(2,1)S(1)}, bf16[2,2,160,256]{3,2,1,0:T(8,128)(2,1)S(1)}, u32[]{:S(2)}, u32[]{:S(2)}) collective-permute-start(bf16[2,2,160,256]{3,2,1,0:T(8,128)(2,1)S(1)} %get-tuple-element.36.rest_6_), channel_id=1, source_target_pairs={{0,16},{4,20},{8,24},{12,28},{16,0},{20,4},{24,8},{28,12},{1,17},{... | collective-permute-start | bytes 983048 | tf_op jit(solution)/shard_map/ppermute | solution.py:264
  34.4 16.0 %collective-permute-start.12 = (bf16[2,2,160,256]{3,2,1,0:T(8,128)(2,1)S(1)}, bf16[2,2,160,256]{3,2,1,0:T(8,128)(2,1)S(1)}, u32[]{:S(2)}, u32[]{:S(2)}) collective-permute-start(bf16[2,2,160,256]{3,2,1,0:T(8,128)(2,1)S(1)} %get-tuple-element.36.rest_6_), channel_id=1, source_target_pairs={{0,24},{4,28},{8,16},{12,20},{16,8},{20,12},{24,0},{28,4},{1,25},{... | collective-permute-start | bytes 983048 | tf_op jit(solution)/shard_map/ppermute | solution.py:264
  35.9 20.7 %copy-start.11 = (bf16[13,48,256]{2,1,0:T(8,128)(2,1)}, bf16[13,48,256]{2,1,0:T(8,128)(2,1)S(1)}, u32[]{:S(2)}) copy-start(bf16[13,48,256]{2,1,0:T(8,128)(2,1)S(1)} %broadcast_select_fusion.3) | copy-start | bytes 958468
  35.9 20.7 %collective-permute-start.13 = (bf16[624,256]{1,0:T(8,128)(2,1)S(1)}, bf16[624,256]{1,0:T(8,128)(2,1)S(1)}, u32[]{:S(2)}, u32[]{:S(2)}) collective-permute-start(bf16[624,256]{1,0:T(8,128)(2,1)S(1)} %bitcast.44), channel_id=1, source_target_pairs={{1,2},{2,1},{5,6},{6,5},{9,10},{10,9},{13,14},{14,13},{17,18},{18,... | collective-permute-start | bytes 958472 | tf_op jit(solution)/shard_map/ppermute | solution.py:268
  36.6 20.0 %collective-permute-start.14 = (bf16[624,256]{1,0:T(8,128)(2,1)S(1)}, bf16[624,256]{1,0:T(8,128)(2,1)S(1)}, u32[]{:S(2)}, u32[]{:S(2)}) collective-permute-start(bf16[624,256]{1,0:T(8,128)(2,1)S(1)} %bitcast.45), channel_id=1, source_target_pairs={{0,1},{1,0},{2,3},{3,2},{4,5},{5,4},{6,7},{7,6},{8,9},{9,8},{10,11... | collective-permute-start | bytes 958472 | tf_op jit(solution)/shard_map/ppermute | solution.py:268
  56.6 18.0 %copy-start.19 = (f32[13,48,256]{2,1,0:T(8,128)S(1)}, f32[13,48,256]{2,1,0:T(8,128)}, u32[]{:S(2)}) copy-start(f32[13,48,256]{2,1,0:T(8,128)} %copy-done.17) | copy-start | bytes 1916932
  56.6 23.1 %copy-start.13 = (bf16[624,256]{1,0:T(8,128)(2,1)}, bf16[624,256]{1,0:T(8,128)(2,1)S(1)}, u32[]{:S(2)}) copy-start(bf16[624,256]{1,0:T(8,128)(2,1)S(1)} %collective-permute-done.13.rest_4_) | copy-start | bytes 958468
  56.6 23.1 %copy-start.15 = (bf16[624,256]{1,0:T(8,128)(2,1)}, bf16[624,256]{1,0:T(8,128)(2,1)S(1)}, u32[]{:S(2)}) copy-start(bf16[624,256]{1,0:T(8,128)(2,1)S(1)} %collective-permute-done.14.rest_1_) | copy-start | bytes 958468
  56.7 3.6 %collective-permute-start.15 = (bf16[13,48,256]{2,1,0:T(8,128)(2,1)S(1)}, bf16[13,48,256]{2,1,0:T(8,128)(2,1)S(1)}, u32[]{:S(2)}, u32[]{:S(2)}) collective-permute-start(bf16[13,48,256]{2,1,0:T(8,128)(2,1)S(1)} %get-tuple-element.40), channel_id=1, source_target_pairs={{0,4},{4,0},{8,12},{12,8},{16,20},{20,16},{24,28},{28,24},{1,5},{5... | collective-permute-start | bytes 958472 | tf_op jit(solution)/shard_map/ppermute | solution.py:264
  56.7 10.8 %collective-permute-start.16 = (bf16[2,2,160,256]{3,2,1,0:T(8,128)(2,1)}, bf16[2,2,160,256]{3,2,1,0:T(8,128)(2,1)S(1)}, u32[]{:S(2)}, u32[]{:S(2)}) collective-permute-start(bf16[2,2,160,256]{3,2,1,0:T(8,128)(2,1)} %get-tuple-element.42.rest_6_), channel_id=1, source_target_pairs={{0,8},{4,12},{8,0},{12,4},{16,24},{20,28},{24,16},{28,20},{1,9},{5... | collective-permute-start | bytes 983048 | tf_op jit(solution)/shard_map/ppermute | solution.py:264
  57.6 17.0 %collective-permute-start.17 = (bf16[2,2,160,256]{3,2,1,0:T(8,128)(2,1)}, bf16[2,2,160,256]{3,2,1,0:T(8,128)(2,1)S(1)}, u32[]{:S(2)}, u32[]{:S(2)}) collective-permute-start(bf16[2,2,160,256]{3,2,1,0:T(8,128)(2,1)} %get-tuple-element.42.rest_6_), channel_id=1, source_target_pairs={{0,16},{4,20},{8,24},{12,28},{16,0},{20,4},{24,8},{28,12},{1,17},{... | collective-permute-start | bytes 983048 | tf_op jit(solution)/shard_map/ppermute | solution.py:264
  59.1 15.5 %collective-permute-start.18 = (bf16[2,2,160,256]{3,2,1,0:T(8,128)(2,1)}, bf16[2,2,160,256]{3,2,1,0:T(8,128)(2,1)S(1)}, u32[]{:S(2)}, u32[]{:S(2)}) collective-permute-start(bf16[2,2,160,256]{3,2,1,0:T(8,128)(2,1)} %get-tuple-element.42.rest_6_), channel_id=1, source_target_pairs={{0,24},{4,28},{8,16},{12,20},{16,8},{20,12},{24,0},{28,4},{1,25},{... | collective-permute-start | bytes 983048 | tf_op jit(solution)/shard_map/ppermute | solution.py:264
  60.5 19.3 %collective-permute-start.19 = (bf16[624,512]{1,0:T(8,128)(2,1)S(1)}, bf16[624,512]{1,0:T(8,128)(2,1)S(1)}, u32[]{:S(2)}, u32[]{:S(2)}) collective-permute-start(bf16[624,512]{1,0:T(8,128)(2,1)S(1)} %get-tuple-element.75), channel_id=1, source_target_pairs={{1,2},{2,1},{5,6},{6,5},{9,10},{10,9},{13,14},{14,13},{17,18},{18,... | collective-permute-start | bytes 1916936 | tf_op jit(solution)/shard_map/ppermute | solution.py:268
  61.2 18.7 %copy-start.20 = (bf16[2,2,160,256]{3,2,1,0:T(8,128)(2,1)S(1)}, bf16[2,2,160,256]{3,2,1,0:T(8,128)(2,1)}, u32[]{:S(2)}) copy-start(bf16[2,2,160,256]{3,2,1,0:T(8,128)(2,1)} %get-tuple-element.48.rest_6_) | copy-start | bytes 983044
  61.2 18.6 %collective-permute-start.20 = (bf16[624,512]{1,0:T(8,128)(2,1)S(1)}, bf16[624,512]{1,0:T(8,128)(2,1)S(1)}, u32[]{:S(2)}, u32[]{:S(2)}) collective-permute-start(bf16[624,512]{1,0:T(8,128)(2,1)S(1)} %get-tuple-element.74), channel_id=1, source_target_pairs={{0,1},{1,0},{2,3},{3,2},{4,5},{5,4},{6,7},{7,6},{8,9},{9,8},{10,11... | collective-permute-start | bytes 1916936 | tf_op jit(solution)/shard_map/ppermute | solution.py:268
  79.8 5.6 %copy-start.3 = (bf16[624,512]{1,0:T(8,128)(2,1)}, bf16[624,512]{1,0:T(8,128)(2,1)S(1)}, u32[]{:S(2)}) copy-start(bf16[624,512]{1,0:T(8,128)(2,1)S(1)} %collective-permute-done.19.rest_7_) | copy-start | bytes 1916932
  79.8 5.5 %copy-start.9 = (bf16[624,512]{1,0:T(8,128)(2,1)}, bf16[624,512]{1,0:T(8,128)(2,1)S(1)}, u32[]{:S(2)}) copy-start(bf16[624,512]{1,0:T(8,128)(2,1)S(1)} %collective-permute-done.20.rest_3_) | copy-start | bytes 1916932
  79.8 3.6 %collective-permute-start.21 = (bf16[13,48,256]{2,1,0:T(8,128)(2,1)S(1)}, bf16[13,48,256]{2,1,0:T(8,128)(2,1)S(1)}, u32[]{:S(2)}, u32[]{:S(2)}) collective-permute-start(bf16[13,48,256]{2,1,0:T(8,128)(2,1)S(1)} %get-tuple-element.46), channel_id=1, source_target_pairs={{0,4},{4,0},{8,12},{12,8},{16,20},{20,16},{24,28},{28,24},{1,5},{5... | collective-permute-start | bytes 958472 | tf_op jit(solution)/shard_map/ppermute | solution.py:264
  79.9 10.6 %collective-permute-start.22 = (bf16[2,2,160,256]{3,2,1,0:T(8,128)(2,1)S(1)}, bf16[2,2,160,256]{3,2,1,0:T(8,128)(2,1)S(1)}, u32[]{:S(2)}, u32[]{:S(2)}) collective-permute-start(bf16[2,2,160,256]{3,2,1,0:T(8,128)(2,1)S(1)} %copy-done.20), channel_id=1, source_target_pairs={{0,8},{4,12},{8,0},{12,4},{16,24},{20,28},{24,16},{28,20},{1,9},{5... | collective-permute-start | bytes 983048 | tf_op jit(solution)/shard_map/ppermute | solution.py:264
  81.2 15.2 %collective-permute-start.23 = (bf16[2,2,160,256]{3,2,1,0:T(8,128)(2,1)S(1)}, bf16[2,2,160,256]{3,2,1,0:T(8,128)(2,1)S(1)}, u32[]{:S(2)}, u32[]{:S(2)}) collective-permute-start(bf16[2,2,160,256]{3,2,1,0:T(8,128)(2,1)S(1)} %copy-done.20), channel_id=1, source_target_pairs={{0,16},{4,20},{8,24},{12,28},{16,0},{20,4},{24,8},{28,12},{1,17},{... | collective-permute-start | bytes 983048 | tf_op jit(solution)/shard_map/ppermute | solution.py:264
  82.0 16.0 %collective-permute-start.24 = (bf16[2,2,160,256]{3,2,1,0:T(8,128)(2,1)S(1)}, bf16[2,2,160,256]{3,2,1,0:T(8,128)(2,1)S(1)}, u32[]{:S(2)}, u32[]{:S(2)}) collective-permute-start(bf16[2,2,160,256]{3,2,1,0:T(8,128)(2,1)S(1)} %copy-done.20), channel_id=1, source_target_pairs={{0,24},{4,28},{8,16},{12,20},{16,8},{20,12},{24,0},{28,4},{1,25},{... | collective-permute-start | bytes 983048 | tf_op jit(solution)/shard_map/ppermute | solution.py:264
  83.6 22.8 %collective-permute-start.25 = (bf16[624,768]{1,0:T(8,128)(2,1)S(1)}, bf16[624,768]{1,0:T(8,128)(2,1)S(1)}, u32[]{:S(2)}, u32[]{:S(2)}) collective-permute-start(bf16[624,768]{1,0:T(8,128)(2,1)S(1)} %pad_maximum_fusion), channel_id=1, source_target_pairs={{0,1},{1,0},{2,3},{3,2},{4,5},{5,4},{6,7},{7,6},{8,9},{9,8},{10,11... | collective-permute-start | bytes 2875400 | tf_op jit(solution)/shard_map/ppermute | solution.py:268
  85.4 17.8 %collective-permute-start.26 = (bf16[624,512]{1,0:T(8,128)(2,1)S(1)}, bf16[624,512]{1,0:T(8,128)(2,1)S(1)}, u32[]{:S(2)}, u32[]{:S(2)}) collective-permute-start(bf16[624,512]{1,0:T(8,128)(2,1)S(1)} %pad_maximum_fusion.4), channel_id=1, source_target_pairs={{1,2},{2,1},{5,6},{6,5},{9,10},{10,9},{13,14},{14,13},{17,18},{18,... | collective-permute-start | bytes 1916936 | tf_op jit(solution)/shard_map/ppermute | solution.py:268
  103.2 8.6 %copy-start.5 = (bf16[624,512]{1,0:T(8,128)(2,1)}, bf16[624,512]{1,0:T(8,128)(2,1)S(1)}, u32[]{:S(2)}) copy-start(bf16[624,512]{1,0:T(8,128)(2,1)S(1)} %collective-permute-done.26.rest_3_) | copy-start | bytes 1916932
  106.4 5.3 %copy-start.7 = (bf16[624,768]{1,0:T(8,128)(2,1)}, bf16[624,768]{1,0:T(8,128)(2,1)S(1)}, u32[]{:S(2)}) copy-start(bf16[624,768]{1,0:T(8,128)(2,1)S(1)} %collective-permute-done.25.rest_6_) | copy-start | bytes 2875396
  106.4 1.6 %collective-permute-start.27 = (bf16[13,48,256]{2,1,0:T(8,128)(2,1)S(1)}, bf16[13,48,256]{2,1,0:T(8,128)(2,1)S(1)}, u32[]{:S(2)}, u32[]{:S(2)}) collective-permute-start(bf16[13,48,256]{2,1,0:T(8,128)(2,1)S(1)} %get-tuple-element.54), channel_id=1, source_target_pairs={{0,4},{4,0},{8,12},{12,8},{16,20},{20,16},{24,28},{28,24},{1,5},{5... | collective-permute-start | bytes 958472 | tf_op jit(solution)/shard_map/ppermute | solution.py:264
  109.2 23.6 %collective-permute-start.28 = (bf16[624,768]{1,0:T(8,128)(2,1)}, bf16[624,768]{1,0:T(8,128)(2,1)}, u32[]{:S(2)}, u32[]{:S(2)}) collective-permute-start(bf16[624,768]{1,0:T(8,128)(2,1)} %pad_maximum_fusion.1), channel_id=1, source_target_pairs={{0,1},{1,0},{2,3},{3,2},{4,5},{5,4},{6,7},{7,6},{8,9},{9,8},{10,11... | collective-permute-start | bytes 2875400 | tf_op jit(solution)/shard_map/ppermute | solution.py:268
  111.7 13.0 %collective-permute-start.29 = (bf16[624,512]{1,0:T(8,128)(2,1)}, bf16[624,512]{1,0:T(8,128)(2,1)}, u32[]{:S(2)}, u32[]{:S(2)}) collective-permute-start(bf16[624,512]{1,0:T(8,128)(2,1)} %pad_maximum_fusion.5), channel_id=1, source_target_pairs={{1,2},{2,1},{5,6},{6,5},{9,10},{10,9},{13,14},{14,13},{17,18},{18,... | collective-permute-start | bytes 1916936 | tf_op jit(solution)/shard_map/ppermute | solution.py:268
  113.2 4.1 %copy-start.12 = (bf16[13,48,256]{2,1,0:T(8,128)(2,1)S(1)}, bf16[13,48,256]{2,1,0:T(8,128)(2,1)}, u32[]{:S(2)}) copy-start(bf16[13,48,256]{2,1,0:T(8,128)(2,1)} %copy-done.11) | copy-start | bytes 958468
  113.2 4.1 %copy-start.14 = (bf16[624,256]{1,0:T(8,128)(2,1)S(1)}, bf16[624,256]{1,0:T(8,128)(2,1)}, u32[]{:S(2)}) copy-start(bf16[624,256]{1,0:T(8,128)(2,1)} %copy-done.13) | copy-start | bytes 958468
  113.2 4.1 %copy-start.16 = (bf16[624,256]{1,0:T(8,128)(2,1)S(1)}, bf16[624,256]{1,0:T(8,128)(2,1)}, u32[]{:S(2)}) copy-start(bf16[624,256]{1,0:T(8,128)(2,1)} %copy-done.15) | copy-start | bytes 958468
  124.7 25.6 %collective-permute-start.30 = (bf16[624,512]{1,0:T(8,128)(2,1)}, bf16[624,512]{1,0:T(8,128)(2,1)}, u32[]{:S(2)}, u32[]{:S(2)}) collective-permute-start(bf16[624,512]{1,0:T(8,128)(2,1)} %collective-permute-done.29.rest_2_), channel_id=1, source_target_pairs={{1,0},{2,3},{5,4},{6,7},{9,8},{10,11},{13,12},{14,15},{17,16},{18,... | collective-permute-start | bytes 1916936 | tf_op jit(solution)/shard_map/ppermute | solution.py:268
  133.8 7.4 %collective-permute-start.31 = (bf16[624,256]{1,0:T(8,128)(2,1)S(1)}, bf16[624,256]{1,0:T(8,128)(2,1)S(1)}, u32[]{:S(2)}, u32[]{:S(2)}) collective-permute-start(bf16[624,256]{1,0:T(8,128)(2,1)S(1)} %slice.52), channel_id=1, source_target_pairs={{1,2},{2,1},{5,6},{6,5},{9,10},{10,9},{13,14},{14,13},{17,18},{18,... | collective-permute-start | bytes 958472 | tf_op jit(solution)/shard_map/ppermute | solution.py:268
  141.1 12.5 %collective-permute-start.32 = (bf16[624,256]{1,0:T(8,128)(2,1)S(1)}, bf16[624,256]{1,0:T(8,128)(2,1)S(1)}, u32[]{:S(2)}, u32[]{:S(2)}) collective-permute-start(bf16[624,256]{1,0:T(8,128)(2,1)S(1)} %collective-permute-done.31.rest_2_), channel_id=1, source_target_pairs={{1,0},{2,3},{5,4},{6,7},{9,8},{10,11},{13,12},{14,15},{17,16},{18,... | collective-permute-start | bytes 958472 | tf_op jit(solution)/shard_map/ppermute | solution.py:268
  (11 other events, 29.2 us)

commit v5 on v4

--- a/solution.py
+++ b/solution.py
@@ -17,7 +17,6 @@
 
 K_FLOPS = 2_700_000_000
 J_FLOPS = 2_000_000_000
-GATE = (0, 1, 1)
 
 
 def cost(flops):
@@ -365,11 +364,9 @@
             raws.append(theirs)
             if i + 1 < n:
                 gather(i + 1)
-                if GATE[0] == 1 or i > 0 and GATE[0] == 2:
-                    theirs = after(theirs, *gathered[i + 1][1:])
-            if i > 0 and GATE[1]:
+            if i > 0:
                 theirs = after(theirs, between[i - 1])
-            if i > 0 and (GATE[2] == 1 or i < n - 1 and GATE[2] == 2 or i == 1 and GATE[2] == 3):
+            if 0 < i < n - 1:
                 theirs = after(theirs, outer[i - 1])
             attn = jnp.where(mine[:, None, None], own, across(theirs, 1)).reshape(req * tree, width)
             owns.append(attn)
@@ -389,7 +386,7 @@
         if i in SPLITS:
             acc = project(after(z, raws[-1]), weight, steps, acc, i == n + 1)
             steps = []
-    path = after(accepted_path, owns[-1])
+    path = after(accepted_path, outer[n - 1])
     accepted_cache = jnp.take_along_axis(tree_cache, path[:, None, :, None], axis=2)
     return acc.reshape(req, tree, out_weight.shape[1]), accepted_cache
 

time: 157 us -> 154 us (0.981)
  waiting for transfers between devices: 55.8 us -> 51.2 us
  local copies, waits for them, and re-layouts: 22.7 us -> 24.5 us
    ppermute x11, waiting for transfers between devices: 11 us -> 7.22 us  [along(): return lax.ppermute(value, 'tp', pairs)]
    unnamed x53, local copies, waits for them, and re-layouts: 11.5 us -> 13.2 us
  transfers between devices with their start and end apart: 33 -> 33, of which waited for: 16 -> 15; matrix products, arithmetic and copies ran while one was open for 10% -> 11% of each run, Pallas kernels for 16% -> 16%
where the time goes in v5:
time: 154 us; the launch traced here: 153 us
  waiting for transfers between devices  51.2 us (33%)
  starting transfers between devices  36.3 us (24%)
  Pallas kernels  31.8 us (21%)
  local copies, waits for them, and re-layouts  24.5 us (16%)
  other arithmetic  6.33 us (4%)
  between operations  2.85 us (2%)
    ppermute x22, waiting for transfers between devices, across(): lax.ppermute(value, 'rep', [(i, i ^ mask) for i in range(lax.axis_size('r...  44 us
    pallas_call x4, Pallas kernels, attend_pairs(): pl.pallas_call(partial(paired_kernel, start=start, inside=inside, n_cache...  20.7 us
    ppermute x11, starting transfers between devices, along(): return lax.ppermute(value, 'tp', pairs)  19.7 us
    ppermute x22, starting transfers between devices, across(): lax.ppermute(value, 'rep', [(i, i ^ mask) for i in range(lax.axis_size('r...  16.6 us
    unnamed x53, local copies, waits for them, and re-layouts  13.2 us
    pallas_call x4, Pallas kernels, project(): pl.pallas_call(partial(project_kernel, steps=tuple(shape), has_acc=acc is...  11.1 us
    ppermute x11, waiting for transfers between devices, along(): return lax.ppermute(value, 'tp', pairs)  7.22 us
    gather x3, local copies, waits for them, and re-layouts, local(): jnp.take_along_axis(tree_cache, path[:, None, :, None], axis=2)  4.66 us
  transfers between devices with their start and end apart: 33, of which 15 were waited for; matrix products, arithmetic and copies ran while one was open for 11% of the time, Pallas kernels for 16%

profile of v5, /device:TPU:0, one launch (start us, length us, event | category | flops | bytes accessed | tf_op | source)
XLA Modules:
  0.0 152.9 jit_solution(16849640284049739821)
XLA Ops:
  1.9 1.2 fusion.21
  4.1 1.3 fusion.16
  5.8 2.6 %collective-permute-start.2 = (bf16[2,2,160,256]{3,2,1,0:T(8,128)(2,1)}, bf16[2,2,160,256]{3,2,1,0:T(8,128)(2,1)S(1)}, u32[]{:S(2)}, u32[]{:S(2)}) collective-permute-start(bf16[2,2,160,256]{3,2,1,0:T(8,128)(2,1)} %get-tuple-element.77.rest_6_), channel_id=1, source_target_pairs={{0,8},{4,12},{8,0},{12,4},{16,24},{20,28},{24,16},{28,20},{1,9},{5... | collective-permute-start | bytes 983048 | tf_op jit(solution)/shard_map/ppermute | solution.py:263
  8.6 1.5 collective-permute-start.7
  10.3 6.9 %collective-permute-done.2.rest_7_ = bf16[2,2,160,256]{3,2,1,0:T(8,128)(2,1)S(1)} collective-permute-done((bf16[2,2,160,256]{3,2,1,0:T(8,128)(2,1)}, bf16[2,2,160,256]{3,2,1,0:T(8,128)(2,1)S(1)}, u32[]{:S(2)}, u32[]{:S(2)}) %collective-permute-start.2) | collective-permute-done | bytes 327712 | tf_op jit(solution)/shard_map/ppermute | solution.py:263
  18.0 1.0 collective-permute-done.3
  19.5 1.5 collective-permute-done.6
  22.0 3.8 %collective-permute-done.7.rest_8_ = bf16[2,2,160,256]{3,2,1,0:T(8,128)(2,1)} collective-permute-done((bf16[2,2,160,256]{3,2,1,0:T(8,128)(2,1)}, bf16[2,2,160,256]{3,2,1,0:T(8,128)(2,1)}, u32[]{:S(2)}, u32[]{:S(2)}) %collective-permute-start.7) | collective-permute-done | bytes 327712 | tf_op jit(solution)/shard_map/ppermute | solution.py:263
  26.8 5.3 %shard_map.122 = (bf16[13,48,256]{2,1,0:T(8,128)(2,1)S(1)}, bf16[13,48,256]{2,1,0:T(8,128)(2,1)S(1)}) custom-call(s32[6,4]{1,0:T(8,128)S(1)} %stack.26.slot_ref, bf16[13,48,1024]{2,1,0:T(8,128)(2,1)} %rest_0_.3, bf16[13,2,48,1024]{3,2,1,0:T(8,128)(2,1)S(1)} %copy-done.2, f32[13,48,256]{2,1,0:T(8,128)S(1)} %pad.21.rest_2_, ...), custom_call_target="tpu_custom_call" | custom-call | flops 8099999744 | bytes 1000 | tf_op jit(solution)/shard_map/pallas_call | solution.py:177
  33.2 1.2 collective-permute-start.11
  34.4 1.4 collective-permute-start.12
  36.6 4.4 %collective-permute-start.14 = (bf16[624,256]{1,0:T(8,128)(2,1)S(1)}, bf16[624,256]{1,0:T(8,128)(2,1)S(1)}, u32[]{:S(2)}, u32[]{:S(2)}) collective-permute-start(bf16[624,256]{1,0:T(8,128)(2,1)S(1)} %bitcast.45), channel_id=1, source_target_pairs={{0,1},{1,0},{2,3},{3,2},{4,5},{5,4},{6,7},{7,6},{8,9},{9,8},{10,11... | collective-permute-start | bytes 958472 | tf_op jit(solution)/shard_map/ppermute | solution.py:267
  41.1 1.8 %collective-permute-done.10.rest_7_ = bf16[2,2,160,256]{3,2,1,0:T(8,128)(2,1)S(1)} collective-permute-done((bf16[2,2,160,256]{3,2,1,0:T(8,128)(2,1)S(1)}, bf16[2,2,160,256]{3,2,1,0:T(8,128)(2,1)S(1)}, u32[]{:S(2)}, u32[]{:S(2)}) %collective-permute-start.10) | collective-permute-done | bytes 327712 | tf_op jit(solution)/shard_map/ppermute | solution.py:263
  42.8 5.9 %collective-permute-done.11.rest_8_ = bf16[2,2,160,256]{3,2,1,0:T(8,128)(2,1)S(1)} collective-permute-done((bf16[2,2,160,256]{3,2,1,0:T(8,128)(2,1)S(1)}, bf16[2,2,160,256]{3,2,1,0:T(8,128)(2,1)S(1)}, u32[]{:S(2)}, u32[]{:S(2)}) %collective-permute-start.11) | collective-permute-done | bytes 327712 | tf_op jit(solution)/shard_map/ppermute | solution.py:263
  48.7 1.6 %collective-permute-done.12.rest_9_ = bf16[2,2,160,256]{3,2,1,0:T(8,128)(2,1)S(1)} collective-permute-done((bf16[2,2,160,256]{3,2,1,0:T(8,128)(2,1)S(1)}, bf16[2,2,160,256]{3,2,1,0:T(8,128)(2,1)S(1)}, u32[]{:S(2)}, u32[]{:S(2)}) %collective-permute-start.12) | collective-permute-done | bytes 327712 | tf_op jit(solution)/shard_map/ppermute | solution.py:263
  50.4 1.1 copy-done.18
  51.4 5.1 %shard_map.123 = (bf16[13,48,256]{2,1,0:T(8,128)(2,1)S(1)}, bf16[13,48,256]{2,1,0:T(8,128)(2,1)S(1)}) custom-call(s32[6,4]{1,0:T(8,128)S(1)} %stack.26.slot_ref, bf16[13,48,1024]{2,1,0:T(8,128)(2,1)} %rest_0_.3, bf16[13,2,48,1024]{3,2,1,0:T(8,128)(2,1)S(1)} %copy-done.2, f32[13,48,256]{2,1,0:T(8,128)S(1)} %copy-done.18, ...), custom_call_target="tpu_custom_call" | custom-call | flops 8099999744 | bytes 1000 | tf_op jit(solution)/shard_map/pallas_call | solution.py:177
  57.6 1.5 collective-permute-start.17
  59.1 1.2 collective-permute-start.18
  61.2 4.4 %collective-permute-start.20 = (bf16[624,512]{1,0:T(8,128)(2,1)S(1)}, bf16[624,512]{1,0:T(8,128)(2,1)S(1)}, u32[]{:S(2)}, u32[]{:S(2)}) collective-permute-start(bf16[624,512]{1,0:T(8,128)(2,1)S(1)} %get-tuple-element.72), channel_id=1, source_target_pairs={{0,1},{1,0},{2,3},{3,2},{4,5},{5,4},{6,7},{7,6},{8,9},{9,8},{10,11... | collective-permute-start | bytes 1916936 | tf_op jit(solution)/shard_map/ppermute | solution.py:267
  65.7 1.9 %collective-permute-done.16.rest_7_ = bf16[2,2,160,256]{3,2,1,0:T(8,128)(2,1)S(1)} collective-permute-done((bf16[2,2,160,256]{3,2,1,0:T(8,128)(2,1)}, bf16[2,2,160,256]{3,2,1,0:T(8,128)(2,1)S(1)}, u32[]{:S(2)}, u32[]{:S(2)}) %collective-permute-start.16) | collective-permute-done | bytes 327712 | tf_op jit(solution)/shard_map/ppermute | solution.py:263
  67.5 7.1 %collective-permute-done.17.rest_8_ = bf16[2,2,160,256]{3,2,1,0:T(8,128)(2,1)S(1)} collective-permute-done((bf16[2,2,160,256]{3,2,1,0:T(8,128)(2,1)}, bf16[2,2,160,256]{3,2,1,0:T(8,128)(2,1)S(1)}, u32[]{:S(2)}, u32[]{:S(2)}) %collective-permute-start.17) | collective-permute-done | bytes 327712 | tf_op jit(solution)/shard_map/ppermute | solution.py:263
  74.6 5.1 %shard_map.124 = (bf16[13,48,256]{2,1,0:T(8,128)(2,1)S(1)}, bf16[13,48,256]{2,1,0:T(8,128)(2,1)S(1)}) custom-call(s32[6,4]{1,0:T(8,128)S(1)} %stack.26.slot_ref, bf16[13,48,1024]{2,1,0:T(8,128)(2,1)} %rest_0_.3, bf16[13,2,48,1024]{3,2,1,0:T(8,128)(2,1)S(1)} %copy-done.2, f32[13,48,256]{2,1,0:T(8,128)S(1)} %copy-done.19, ...), custom_call_target="tpu_custom_call" | custom-call | flops 8099999744 | bytes 1000 | tf_op jit(solution)/shard_map/pallas_call | solution.py:177
  79.9 1.3 collective-permute-start.22
  82.0 1.4 collective-permute-start.24
  84.5 1.6 %collective-permute-start.25 = (bf16[624,768]{1,0:T(8,128)(2,1)S(1)}, bf16[624,768]{1,0:T(8,128)(2,1)S(1)}, u32[]{:S(2)}, u32[]{:S(2)}) collective-permute-start(bf16[624,768]{1,0:T(8,128)(2,1)S(1)} %pad_maximum_fusion), channel_id=1, source_target_pairs={{0,1},{1,0},{2,3},{3,2},{4,5},{5,4},{6,7},{7,6},{8,9},{9,8},{10,11... | collective-permute-start | bytes 2875400 | tf_op jit(solution)/shard_map/ppermute | solution.py:267
  87.1 3.4 %collective-permute-done.22.rest_7_ = bf16[2,2,160,256]{3,2,1,0:T(8,128)(2,1)S(1)} collective-permute-done((bf16[2,2,160,256]{3,2,1,0:T(8,128)(2,1)S(1)}, bf16[2,2,160,256]{3,2,1,0:T(8,128)(2,1)S(1)}, u32[]{:S(2)}, u32[]{:S(2)}) %collective-permute-start.22) | collective-permute-done | bytes 327712 | tf_op jit(solution)/shard_map/ppermute | solution.py:263
  90.4 5.9 %collective-permute-done.23.rest_8_ = bf16[2,2,160,256]{3,2,1,0:T(8,128)(2,1)S(1)} collective-permute-done((bf16[2,2,160,256]{3,2,1,0:T(8,128)(2,1)S(1)}, bf16[2,2,160,256]{3,2,1,0:T(8,128)(2,1)S(1)}, u32[]{:S(2)}, u32[]{:S(2)}) %collective-permute-start.23) | collective-permute-done | bytes 327712 | tf_op jit(solution)/shard_map/ppermute | solution.py:263
  96.3 1.6 %collective-permute-done.24.rest_9_ = bf16[2,2,160,256]{3,2,1,0:T(8,128)(2,1)S(1)} collective-permute-done((bf16[2,2,160,256]{3,2,1,0:T(8,128)(2,1)S(1)}, bf16[2,2,160,256]{3,2,1,0:T(8,128)(2,1)S(1)}, u32[]{:S(2)}, u32[]{:S(2)}) %collective-permute-start.24) | collective-permute-done | bytes 327712 | tf_op jit(solution)/shard_map/ppermute | solution.py:263
  98.0 5.1 %shard_map.125 = (bf16[13,48,256]{2,1,0:T(8,128)(2,1)S(1)}, bf16[13,48,256]{2,1,0:T(8,128)(2,1)S(1)}) custom-call(s32[6,4]{1,0:T(8,128)S(1)} %stack.26.slot_ref, bf16[13,48,1024]{2,1,0:T(8,128)(2,1)} %rest_0_.3, bf16[13,2,48,1024]{3,2,1,0:T(8,128)(2,1)S(1)} %copy-done.2, f32[13,48,256]{2,1,0:T(8,128)S(1)} %copy-done.19, ...), custom_call_target="tpu_custom_call" | custom-call | flops 8099999744 | bytes 1000 | tf_op jit(solution)/shard_map/pallas_call | solution.py:177
  103.2 1.6 %collective-permute-done.27 = bf16[13,48,256]{2,1,0:T(8,128)(2,1)S(1)} collective-permute-done((bf16[13,48,256]{2,1,0:T(8,128)(2,1)S(1)}, bf16[13,48,256]{2,1,0:T(8,128)(2,1)S(1)}, u32[]{:S(2)}, u32[]{:S(2)}) %collective-permute-start.27) | collective-permute-done | bytes 319520 | tf_op jit(solution)/shard_map/ppermute | solution.py:263
  104.9 1.0 pad_maximum_fusion.1
  105.9 1.9 %collective-permute-start.28 = (bf16[624,768]{1,0:T(8,128)(2,1)}, bf16[624,768]{1,0:T(8,128)(2,1)}, u32[]{:S(2)}, u32[]{:S(2)}) collective-permute-start(bf16[624,768]{1,0:T(8,128)(2,1)} %pad_maximum_fusion.1), channel_id=1, source_target_pairs={{0,1},{1,0},{2,3},{3,2},{4,5},{5,4},{6,7},{7,6},{8,9},{9,8},{10,11... | collective-permute-start | bytes 2875400 | tf_op jit(solution)/shard_map/ppermute | solution.py:267
  109.7 1.5 collective-permute-start.29
  111.3 4.1 %copy.24 = bf16[13,2,48,1024]{3,1,2,0:T(2,128)(2,1)} copy(bf16[13,2,48,1024]{3,2,1,0:T(8,128)(2,1)S(1)} %copy-done.2) | data formatting | bytes 5111808 | tf_op jit(solution)/shard_map/optimization_barrier | solution.py:339
  115.4 3.4 %copy-done = bf16[4096,1024]{1,0:T(8,128)(2,1)S(1)} copy-done((bf16[4096,1024]{1,0:T(8,128)(2,1)S(1)}, bf16[4096,1024]{1,0:T(8,128)(2,1)}, u32[]{:S(2)}) %copy-start) | copy-done | bytes 8388632
  118.8 3.9 %shard_map.126.rest_0_ = f32[624,1024]{1,0:T(8,128)S(1)} custom-call(s32[1]{0:T(128)} %bitcast.z_ref, bf16[4,1024,1024]{2,1,0:T(8,128)(2,1)S(1)} %bitcast.32, bf16[624,256]{1,0:T(8,128)(2,1)S(1)} %bitcast.46, bf16[624,256]{1,0:T(8,128)(2,1)S(1)} %copy-done.16, bf16[624,256]{1,0:T(8,128)(2,1)S(1)} %bitcast.43, bf16[624,512]{1,0:T(8,128)(2,1)S(1)} %copy-done.10, ...), custom_call_target="tpu_custom_call" | custom-call | flops 2000000000 | bytes 1000 | tf_op jit(solution)/shard_map/pallas_call | solution.py:240
  122.7 1.3 collective-permute-start.30
  124.0 5.7 %collective-permute-done.28.rest_2_ = bf16[624,768]{1,0:T(8,128)(2,1)} collective-permute-done((bf16[624,768]{1,0:T(8,128)(2,1)}, bf16[624,768]{1,0:T(8,128)(2,1)}, u32[]{:S(2)}, u32[]{:S(2)}) %collective-permute-start.28) | collective-permute-done | bytes 958496 | tf_op jit(solution)/shard_map/ppermute | solution.py:267
  131.7 4.5 %gather_fusion = bf16[104,2,1024]{2,1,0:T(2,128)(2,1)} fusion(bf16[13,2,48,1024]{3,1,2,0:T(2,128)(2,1)} %copy.24, s32[104]{0:T(128)S(1)} %reshape.134), kind=kCustom, calls=%fused_computation | custom fusion | bytes 852800 | tf_op jit(solution)/shard_map/jit(take_along_axis)/gather | solution.py:390
  136.2 1.1 fusion.8
  138.1 1.5 collective-permute-start.32
  139.6 3.4 %copy-done.1 = bf16[4096,1024]{1,0:T(8,128)(2,1)S(1)} copy-done((bf16[4096,1024]{1,0:T(8,128)(2,1)S(1)}, bf16[4096,1024]{1,0:T(8,128)(2,1)}, u32[]{:S(2)}) %copy-start.1) | copy-done | bytes 8388632
  143.0 1.1 copy-done.6
  144.0 3.1 %shard_map.127.rest_0_ = f32[624,1024]{1,0:T(8,128)S(1)} custom-call(s32[1]{0:T(128)} %bitcast.z_ref, bf16[4,1024,1024]{2,1,0:T(8,128)(2,1)S(1)} %bitcast.33, f32[624,1024]{1,0:T(8,128)S(1)} %shard_map.126.rest_0_, bf16[624,256]{1,0:T(8,128)(2,1)S(1)} %bitcast.41, bf16[624,768]{1,0:T(8,128)(2,1)} %collective-permute-done.28.rest_2_, ...), custom_call_target="tpu_custom_call", output_to_operand_aliasing={{}: (2, {})} | custom-call | flops 2000000000 | bytes 1000 | tf_op jit(solution)/shard_map/pallas_call | solution.py:240
  147.2 2.4 %shard_map.128.rest_0_ = f32[624,1024]{1,0:T(8,128)S(1)} custom-call(s32[1]{0:T(128)} %bitcast.z_ref, bf16[4,1024,1024]{2,1,0:T(8,128)(2,1)S(1)} %bitcast.34, f32[624,1024]{1,0:T(8,128)S(1)} %shard_map.127.rest_0_, bf16[624,512]{1,0:T(8,128)(2,1)} %collective-permute-done.30.rest_1_, ...), custom_call_target="tpu_custom_call", output_to_operand_aliasing={{}: (2, {})} | custom-call | flops 2000000000 | bytes 1000 | tf_op jit(solution)/shard_map/pallas_call | solution.py:240
  149.6 1.5 collective-permute-done.32.rest_1_
  151.1 1.6 %shard_map.129 = bf16[624,1024]{1,0:T(8,128)(2,1)} custom-call(s32[1]{0:T(128)} %bitcast.z_ref, bf16[4,1024,1024]{2,1,0:T(8,128)(2,1)S(1)} %bitcast.35, f32[624,1024]{1,0:T(8,128)S(1)} %shard_map.128.rest_0_, bf16[624,256]{1,0:T(8,128)(2,1)S(1)} %collective-permute-done.32.rest_1_, bf16[624,256]{1,0:T(8,128)(2,1)S(1)} %collective-permute-done.31.rest_2_), custom_call_target="tpu_custom_call" | custom-call | flops 2000000000 | bytes 1000 | tf_op jit(solution)/shard_map/pallas_call | solution.py:240
  (114 shorter events, 16.2 us)
Async XLA Ops:
  0.6 3.4 %collective-permute-start.1 = (bf16[1,2,152,1024]{3,2,1,0:T(8,128)(2,1)}, bf16[1,2,152,1024]{3,2,1,0:T(8,128)(2,1)S(1)}, u32[]{:S(2)}, u32[]{:S(2)}) collective-permute-start(bf16[1,2,152,1024]{3,2,1,0:T(8,128)(2,1)} %param.18), channel_id=1, source_target_pairs={{0,4},{4,0},{8,12},{12,8},{16,20},{20,16},{24,28},{28,24},{1,5},{5... | collective-permute-start | bytes 1867784 | tf_op jit(solution)/shard_map/ppermute | solution.py:263
  1.1 2.0 %collective-permute-start = (s32[1]{0:T(128)}, s32[1]{0:T(128)}, u32[]{:S(2)}, u32[]{:S(2)}) collective-permute-start(s32[1]{0:T(128)} %param.19), channel_id=1, source_target_pairs={{0,4},{4,0},{8,12},{12,8},{16,20},{20,16},{24,28},{28,24},{1,5},{5... | collective-permute-start | bytes 20 | tf_op jit(solution)/shard_map/ppermute | solution.py:263
  3.1 14.8 %copy-start.25 = (s32[13,1]{0,1:T(1,128)S(1)}, s32[13,1]{0,1:T(1,128)}, u32[]{:S(2)}) copy-start(s32[13,1]{0,1:T(1,128)} %param.14) | copy-start | bytes 160
  3.1 14.8 %copy-start.23 = (s32[13,48,48]{2,1,0:T(8,128)S(1)}, s32[13,48,48]{2,1,0:T(8,128)}, u32[]{:S(2)}) copy-start(s32[13,48,48]{2,1,0:T(8,128)} %param.13) | copy-start | bytes 359428
  5.4 20.5 %collective-permute-start.5 = (bf16[13,2,48,1024]{3,2,1,0:T(8,128)(2,1)S(1)}, bf16[13,2,48,1024]{3,2,1,0:T(8,128)(2,1)}, u32[]{:S(2)}, u32[]{:S(2)}) collective-permute-start(bf16[13,2,48,1024]{3,2,1,0:T(8,128)(2,1)S(1)} %copy-done.2), channel_id=1, source_target_pairs={{0,4},{4,0},{8,12},{12,8},{16,20},{20,16},{24,28},{28,24},{1,5},{5... | collective-permute-start | bytes 7667720 | tf_op jit(solution)/shard_map/ppermute | solution.py:263
  5.8 11.3 %collective-permute-start.2 = (bf16[2,2,160,256]{3,2,1,0:T(8,128)(2,1)}, bf16[2,2,160,256]{3,2,1,0:T(8,128)(2,1)S(1)}, u32[]{:S(2)}, u32[]{:S(2)}) collective-permute-start(bf16[2,2,160,256]{3,2,1,0:T(8,128)(2,1)} %get-tuple-element.77.rest_6_), channel_id=1, source_target_pairs={{0,8},{4,12},{8,0},{12,4},{16,24},{20,28},{24,16},{28,20},{1,9},{5... | collective-permute-start | bytes 983048 | tf_op jit(solution)/shard_map/ppermute | solution.py:263
  8.4 17.5 %collective-permute-start.4 = (bf16[13,48,1024]{2,1,0:T(8,128)(2,1)}, bf16[13,48,1024]{2,1,0:T(8,128)(2,1)}, u32[]{:S(2)}, u32[]{:S(2)}) collective-permute-start(bf16[13,48,1024]{2,1,0:T(8,128)(2,1)} %rest_0_.3), channel_id=1, source_target_pairs={{0,4},{4,0},{8,12},{12,8},{16,20},{20,16},{24,28},{28,24},{1,5},{5... | collective-permute-start | bytes 3833864 | tf_op jit(solution)/shard_map/ppermute | solution.py:263
  8.6 17.3 %collective-permute-start.7 = (bf16[2,2,160,256]{3,2,1,0:T(8,128)(2,1)}, bf16[2,2,160,256]{3,2,1,0:T(8,128)(2,1)}, u32[]{:S(2)}, u32[]{:S(2)}) collective-permute-start(bf16[2,2,160,256]{3,2,1,0:T(8,128)(2,1)} %get-tuple-element.77.rest_6_), channel_id=1, source_target_pairs={{0,16},{4,20},{8,24},{12,28},{16,0},{20,4},{24,8},{28,12},{1,17},{... | collective-permute-start | bytes 983048 | tf_op jit(solution)/shard_map/ppermute | solution.py:263
  10.1 15.8 %collective-permute-start.8 = (bf16[2,2,160,256]{3,2,1,0:T(8,128)(2,1)}, bf16[2,2,160,256]{3,2,1,0:T(8,128)(2,1)}, u32[]{:S(2)}, u32[]{:S(2)}) collective-permute-start(bf16[2,2,160,256]{3,2,1,0:T(8,128)(2,1)} %get-tuple-element.77.rest_6_), channel_id=1, source_target_pairs={{0,24},{4,28},{8,16},{12,20},{16,8},{20,12},{24,0},{28,4},{1,25},{... | collective-permute-start | bytes 983048 | tf_op jit(solution)/shard_map/ppermute | solution.py:263
  17.9 1.1 collective-permute-start.3
  18.0 14.2 %copy-start.17 = (f32[13,48,256]{2,1,0:T(8,128)}, f32[13,48,256]{2,1,0:T(8,128)S(1)}, u32[]{:S(2)}) copy-start(f32[13,48,256]{2,1,0:T(8,128)S(1)} %pad.21.rest_2_) | copy-start | bytes 1916932
  19.0 2.0 %collective-permute-start.6 = (s32[13,48,48]{2,1,0:T(8,128)}, s32[13,48,48]{2,1,0:T(8,128)}, u32[]{:S(2)}, u32[]{:S(2)}) collective-permute-start(s32[13,48,48]{2,1,0:T(8,128)} %param.13), channel_id=1, source_target_pairs={{0,4},{4,0},{8,12},{12,8},{16,20},{20,16},{24,28},{28,24},{1,5},{5... | collective-permute-start | bytes 359432 | tf_op jit(solution)/shard_map/ppermute | solution.py:263
  32.2 3.6 %collective-permute-start.9 = (bf16[13,48,256]{2,1,0:T(8,128)(2,1)S(1)}, bf16[13,48,256]{2,1,0:T(8,128)(2,1)S(1)}, u32[]{:S(2)}, u32[]{:S(2)}) collective-permute-start(bf16[13,48,256]{2,1,0:T(8,128)(2,1)S(1)} %get-tuple-element.33), channel_id=1, source_target_pairs={{0,4},{4,0},{8,12},{12,8},{16,20},{20,16},{24,28},{28,24},{1,5},{5... | collective-permute-start | bytes 958472 | tf_op jit(solution)/shard_map/ppermute | solution.py:263
  32.2 10.6 %collective-permute-start.10 = (bf16[2,2,160,256]{3,2,1,0:T(8,128)(2,1)S(1)}, bf16[2,2,160,256]{3,2,1,0:T(8,128)(2,1)S(1)}, u32[]{:S(2)}, u32[]{:S(2)}) collective-permute-start(bf16[2,2,160,256]{3,2,1,0:T(8,128)(2,1)S(1)} %get-tuple-element.35.rest_6_), channel_id=1, source_target_pairs={{0,8},{4,12},{8,0},{12,4},{16,24},{20,28},{24,16},{28,20},{1,9},{5... | collective-permute-start | bytes 983048 | tf_op jit(solution)/shard_map/ppermute | solution.py:263
  33.2 15.5 %collective-permute-start.11 = (bf16[2,2,160,256]{3,2,1,0:T(8,128)(2,1)S(1)}, bf16[2,2,160,256]{3,2,1,0:T(8,128)(2,1)S(1)}, u32[]{:S(2)}, u32[]{:S(2)}) collective-permute-start(bf16[2,2,160,256]{3,2,1,0:T(8,128)(2,1)S(1)} %get-tuple-element.35.rest_6_), channel_id=1, source_target_pairs={{0,16},{4,20},{8,24},{12,28},{16,0},{20,4},{24,8},{28,12},{1,17},{... | collective-permute-start | bytes 983048 | tf_op jit(solution)/shard_map/ppermute | solution.py:263
  34.4 16.0 %collective-permute-start.12 = (bf16[2,2,160,256]{3,2,1,0:T(8,128)(2,1)S(1)}, bf16[2,2,160,256]{3,2,1,0:T(8,128)(2,1)S(1)}, u32[]{:S(2)}, u32[]{:S(2)}) collective-permute-start(bf16[2,2,160,256]{3,2,1,0:T(8,128)(2,1)S(1)} %get-tuple-element.35.rest_6_), channel_id=1, source_target_pairs={{0,24},{4,28},{8,16},{12,20},{16,8},{20,12},{24,0},{28,4},{1,25},{... | collective-permute-start | bytes 983048 | tf_op jit(solution)/shard_map/ppermute | solution.py:263
  35.9 20.7 %copy-start.11 = (bf16[13,48,256]{2,1,0:T(8,128)(2,1)}, bf16[13,48,256]{2,1,0:T(8,128)(2,1)S(1)}, u32[]{:S(2)}) copy-start(bf16[13,48,256]{2,1,0:T(8,128)(2,1)S(1)} %broadcast_select_fusion.3) | copy-start | bytes 958468
  35.9 20.7 %collective-permute-start.13 = (bf16[624,256]{1,0:T(8,128)(2,1)S(1)}, bf16[624,256]{1,0:T(8,128)(2,1)S(1)}, u32[]{:S(2)}, u32[]{:S(2)}) collective-permute-start(bf16[624,256]{1,0:T(8,128)(2,1)S(1)} %bitcast.44), channel_id=1, source_target_pairs={{1,2},{2,1},{5,6},{6,5},{9,10},{10,9},{13,14},{14,13},{17,18},{18,... | collective-permute-start | bytes 958472 | tf_op jit(solution)/shard_map/ppermute | solution.py:267
  36.6 20.0 %collective-permute-start.14 = (bf16[624,256]{1,0:T(8,128)(2,1)S(1)}, bf16[624,256]{1,0:T(8,128)(2,1)S(1)}, u32[]{:S(2)}, u32[]{:S(2)}) collective-permute-start(bf16[624,256]{1,0:T(8,128)(2,1)S(1)} %bitcast.45), channel_id=1, source_target_pairs={{0,1},{1,0},{2,3},{3,2},{4,5},{5,4},{6,7},{7,6},{8,9},{9,8},{10,11... | collective-permute-start | bytes 958472 | tf_op jit(solution)/shard_map/ppermute | solution.py:267
  56.6 18.0 %copy-start.19 = (f32[13,48,256]{2,1,0:T(8,128)S(1)}, f32[13,48,256]{2,1,0:T(8,128)}, u32[]{:S(2)}) copy-start(f32[13,48,256]{2,1,0:T(8,128)} %copy-done.17) | copy-start | bytes 1916932
  56.6 4.6 %copy-start.13 = (bf16[624,256]{1,0:T(8,128)(2,1)}, bf16[624,256]{1,0:T(8,128)(2,1)S(1)}, u32[]{:S(2)}) copy-start(bf16[624,256]{1,0:T(8,128)(2,1)S(1)} %collective-permute-done.13.rest_4_) | copy-start | bytes 958468
  56.6 4.6 %copy-start.15 = (bf16[624,256]{1,0:T(8,128)(2,1)}, bf16[624,256]{1,0:T(8,128)(2,1)S(1)}, u32[]{:S(2)}) copy-start(bf16[624,256]{1,0:T(8,128)(2,1)S(1)} %collective-permute-done.14.rest_1_) | copy-start | bytes 958468
  56.6 3.6 %collective-permute-start.15 = (bf16[13,48,256]{2,1,0:T(8,128)(2,1)S(1)}, bf16[13,48,256]{2,1,0:T(8,128)(2,1)S(1)}, u32[]{:S(2)}, u32[]{:S(2)}) collective-permute-start(bf16[13,48,256]{2,1,0:T(8,128)(2,1)S(1)} %get-tuple-element.39), channel_id=1, source_target_pairs={{0,4},{4,0},{8,12},{12,8},{16,20},{20,16},{24,28},{28,24},{1,5},{5... | collective-permute-start | bytes 958472 | tf_op jit(solution)/shard_map/ppermute | solution.py:263
  56.7 10.8 %collective-permute-start.16 = (bf16[2,2,160,256]{3,2,1,0:T(8,128)(2,1)}, bf16[2,2,160,256]{3,2,1,0:T(8,128)(2,1)S(1)}, u32[]{:S(2)}, u32[]{:S(2)}) collective-permute-start(bf16[2,2,160,256]{3,2,1,0:T(8,128)(2,1)} %get-tuple-element.41.rest_6_), channel_id=1, source_target_pairs={{0,8},{4,12},{8,0},{12,4},{16,24},{20,28},{24,16},{28,20},{1,9},{5... | collective-permute-start | bytes 983048 | tf_op jit(solution)/shard_map/ppermute | solution.py:263
  57.6 17.0 %collective-permute-start.17 = (bf16[2,2,160,256]{3,2,1,0:T(8,128)(2,1)}, bf16[2,2,160,256]{3,2,1,0:T(8,128)(2,1)S(1)}, u32[]{:S(2)}, u32[]{:S(2)}) collective-permute-start(bf16[2,2,160,256]{3,2,1,0:T(8,128)(2,1)} %get-tuple-element.41.rest_6_), channel_id=1, source_target_pairs={{0,16},{4,20},{8,24},{12,28},{16,0},{20,4},{24,8},{28,12},{1,17},{... | collective-permute-start | bytes 983048 | tf_op jit(solution)/shard_map/ppermute | solution.py:263
  59.1 15.5 %collective-permute-start.18 = (bf16[2,2,160,256]{3,2,1,0:T(8,128)(2,1)}, bf16[2,2,160,256]{3,2,1,0:T(8,128)(2,1)S(1)}, u32[]{:S(2)}, u32[]{:S(2)}) collective-permute-start(bf16[2,2,160,256]{3,2,1,0:T(8,128)(2,1)} %get-tuple-element.41.rest_6_), channel_id=1, source_target_pairs={{0,24},{4,28},{8,16},{12,20},{16,8},{20,12},{24,0},{28,4},{1,25},{... | collective-permute-start | bytes 983048 | tf_op jit(solution)/shard_map/ppermute | solution.py:263
  60.5 19.3 %collective-permute-start.19 = (bf16[624,512]{1,0:T(8,128)(2,1)S(1)}, bf16[624,512]{1,0:T(8,128)(2,1)S(1)}, u32[]{:S(2)}, u32[]{:S(2)}) collective-permute-start(bf16[624,512]{1,0:T(8,128)(2,1)S(1)} %get-tuple-element.73), channel_id=1, source_target_pairs={{1,2},{2,1},{5,6},{6,5},{9,10},{10,9},{13,14},{14,13},{17,18},{18,... | collective-permute-start | bytes 1916936 | tf_op jit(solution)/shard_map/ppermute | solution.py:267
  61.2 18.6 %copy-start.20 = (bf16[2,2,160,256]{3,2,1,0:T(8,128)(2,1)S(1)}, bf16[2,2,160,256]{3,2,1,0:T(8,128)(2,1)}, u32[]{:S(2)}) copy-start(bf16[2,2,160,256]{3,2,1,0:T(8,128)(2,1)} %get-tuple-element.47.rest_6_) | copy-start | bytes 983044
  61.2 18.5 %collective-permute-start.20 = (bf16[624,512]{1,0:T(8,128)(2,1)S(1)}, bf16[624,512]{1,0:T(8,128)(2,1)S(1)}, u32[]{:S(2)}, u32[]{:S(2)}) collective-permute-start(bf16[624,512]{1,0:T(8,128)(2,1)S(1)} %get-tuple-element.72), channel_id=1, source_target_pairs={{0,1},{1,0},{2,3},{3,2},{4,5},{5,4},{6,7},{7,6},{8,9},{9,8},{10,11... | collective-permute-start | bytes 1916936 | tf_op jit(solution)/shard_map/ppermute | solution.py:267
  79.8 6.4 %copy-start.3 = (bf16[624,512]{1,0:T(8,128)(2,1)}, bf16[624,512]{1,0:T(8,128)(2,1)S(1)}, u32[]{:S(2)}) copy-start(bf16[624,512]{1,0:T(8,128)(2,1)S(1)} %collective-permute-done.19.rest_7_) | copy-start | bytes 1916932
  79.8 4.5 %collective-permute-start.21 = (bf16[13,48,256]{2,1,0:T(8,128)(2,1)S(1)}, bf16[13,48,256]{2,1,0:T(8,128)(2,1)S(1)}, u32[]{:S(2)}, u32[]{:S(2)}) collective-permute-start(bf16[13,48,256]{2,1,0:T(8,128)(2,1)S(1)} %get-tuple-element.45), channel_id=1, source_target_pairs={{0,4},{4,0},{8,12},{12,8},{16,20},{20,16},{24,28},{28,24},{1,5},{5... | collective-permute-start | bytes 958472 | tf_op jit(solution)/shard_map/ppermute | solution.py:263
  79.9 10.6 %collective-permute-start.22 = (bf16[2,2,160,256]{3,2,1,0:T(8,128)(2,1)S(1)}, bf16[2,2,160,256]{3,2,1,0:T(8,128)(2,1)S(1)}, u32[]{:S(2)}, u32[]{:S(2)}) collective-permute-start(bf16[2,2,160,256]{3,2,1,0:T(8,128)(2,1)S(1)} %copy-done.20), channel_id=1, source_target_pairs={{0,8},{4,12},{8,0},{12,4},{16,24},{20,28},{24,16},{28,20},{1,9},{5... | collective-permute-start | bytes 983048 | tf_op jit(solution)/shard_map/ppermute | solution.py:263
  81.2 15.2 %collective-permute-start.23 = (bf16[2,2,160,256]{3,2,1,0:T(8,128)(2,1)S(1)}, bf16[2,2,160,256]{3,2,1,0:T(8,128)(2,1)S(1)}, u32[]{:S(2)}, u32[]{:S(2)}) collective-permute-start(bf16[2,2,160,256]{3,2,1,0:T(8,128)(2,1)S(1)} %copy-done.20), channel_id=1, source_target_pairs={{0,16},{4,20},{8,24},{12,28},{16,0},{20,4},{24,8},{28,12},{1,17},{... | collective-permute-start | bytes 983048 | tf_op jit(solution)/shard_map/ppermute | solution.py:263
  82.0 16.0 %collective-permute-start.24 = (bf16[2,2,160,256]{3,2,1,0:T(8,128)(2,1)S(1)}, bf16[2,2,160,256]{3,2,1,0:T(8,128)(2,1)S(1)}, u32[]{:S(2)}, u32[]{:S(2)}) collective-permute-start(bf16[2,2,160,256]{3,2,1,0:T(8,128)(2,1)S(1)} %copy-done.20), channel_id=1, source_target_pairs={{0,24},{4,28},{8,16},{12,20},{16,8},{20,12},{24,0},{28,4},{1,25},{... | collective-permute-start | bytes 983048 | tf_op jit(solution)/shard_map/ppermute | solution.py:263
  84.5 23.4 %collective-permute-start.25 = (bf16[624,768]{1,0:T(8,128)(2,1)S(1)}, bf16[624,768]{1,0:T(8,128)(2,1)S(1)}, u32[]{:S(2)}, u32[]{:S(2)}) collective-permute-start(bf16[624,768]{1,0:T(8,128)(2,1)S(1)} %pad_maximum_fusion), channel_id=1, source_target_pairs={{0,1},{1,0},{2,3},{3,2},{4,5},{5,4},{6,7},{7,6},{8,9},{9,8},{10,11... | collective-permute-start | bytes 2875400 | tf_op jit(solution)/shard_map/ppermute | solution.py:267
  86.2 16.9 %collective-permute-start.26 = (bf16[624,512]{1,0:T(8,128)(2,1)S(1)}, bf16[624,512]{1,0:T(8,128)(2,1)S(1)}, u32[]{:S(2)}, u32[]{:S(2)}) collective-permute-start(bf16[624,512]{1,0:T(8,128)(2,1)S(1)} %pad_maximum_fusion.4), channel_id=1, source_target_pairs={{1,2},{2,1},{5,6},{6,5},{9,10},{10,9},{13,14},{14,13},{17,18},{18,... | collective-permute-start | bytes 1916936 | tf_op jit(solution)/shard_map/ppermute | solution.py:267
  103.1 6.6 %copy-start.5 = (bf16[624,512]{1,0:T(8,128)(2,1)}, bf16[624,512]{1,0:T(8,128)(2,1)S(1)}, u32[]{:S(2)}) copy-start(bf16[624,512]{1,0:T(8,128)(2,1)S(1)} %collective-permute-done.26.rest_3_) | copy-start | bytes 1916932
  103.1 1.7 %collective-permute-start.27 = (bf16[13,48,256]{2,1,0:T(8,128)(2,1)S(1)}, bf16[13,48,256]{2,1,0:T(8,128)(2,1)S(1)}, u32[]{:S(2)}, u32[]{:S(2)}) collective-permute-start(bf16[13,48,256]{2,1,0:T(8,128)(2,1)S(1)} %get-tuple-element.52), channel_id=1, source_target_pairs={{0,4},{4,0},{8,12},{12,8},{16,20},{20,16},{24,28},{28,24},{1,5},{5... | collective-permute-start | bytes 958472 | tf_op jit(solution)/shard_map/ppermute | solution.py:263
  105.9 23.7 %collective-permute-start.28 = (bf16[624,768]{1,0:T(8,128)(2,1)}, bf16[624,768]{1,0:T(8,128)(2,1)}, u32[]{:S(2)}, u32[]{:S(2)}) collective-permute-start(bf16[624,768]{1,0:T(8,128)(2,1)} %pad_maximum_fusion.1), channel_id=1, source_target_pairs={{0,1},{1,0},{2,3},{3,2},{4,5},{5,4},{6,7},{7,6},{8,9},{9,8},{10,11... | collective-permute-start | bytes 2875400 | tf_op jit(solution)/shard_map/ppermute | solution.py:267
  109.7 12.9 %collective-permute-start.29 = (bf16[624,512]{1,0:T(8,128)(2,1)}, bf16[624,512]{1,0:T(8,128)(2,1)}, u32[]{:S(2)}, u32[]{:S(2)}) collective-permute-start(bf16[624,512]{1,0:T(8,128)(2,1)} %pad_maximum_fusion.5), channel_id=1, source_target_pairs={{1,2},{2,1},{5,6},{6,5},{9,10},{10,9},{13,14},{14,13},{17,18},{18,... | collective-permute-start | bytes 1916936 | tf_op jit(solution)/shard_map/ppermute | solution.py:267
  111.2 4.1 %copy-start.10 = (bf16[624,512]{1,0:T(8,128)(2,1)S(1)}, bf16[624,512]{1,0:T(8,128)(2,1)}, u32[]{:S(2)}) copy-start(bf16[624,512]{1,0:T(8,128)(2,1)} %copy-done.9) | copy-start | bytes 1916932
  111.2 4.1 %copy-start.12 = (bf16[13,48,256]{2,1,0:T(8,128)(2,1)S(1)}, bf16[13,48,256]{2,1,0:T(8,128)(2,1)}, u32[]{:S(2)}) copy-start(bf16[13,48,256]{2,1,0:T(8,128)(2,1)} %copy-done.11) | copy-start | bytes 958468
  111.2 4.1 %copy-start.14 = (bf16[624,256]{1,0:T(8,128)(2,1)S(1)}, bf16[624,256]{1,0:T(8,128)(2,1)}, u32[]{:S(2)}) copy-start(bf16[624,256]{1,0:T(8,128)(2,1)} %copy-done.13) | copy-start | bytes 958468
  111.3 4.1 %copy-start.16 = (bf16[624,256]{1,0:T(8,128)(2,1)S(1)}, bf16[624,256]{1,0:T(8,128)(2,1)}, u32[]{:S(2)}) copy-start(bf16[624,256]{1,0:T(8,128)(2,1)} %copy-done.15) | copy-start | bytes 958468
  118.8 12.6 %copy-start.24 = (s32[13,8]{0,1:T(8,128)S(1)}, s32[13,8]{0,1:T(8,128)}, u32[]{:S(2)}) copy-start(s32[13,8]{0,1:T(8,128)} %param.15) | copy-start | bytes 1252
  122.7 24.5 %collective-permute-start.30 = (bf16[624,512]{1,0:T(8,128)(2,1)}, bf16[624,512]{1,0:T(8,128)(2,1)}, u32[]{:S(2)}, u32[]{:S(2)}) collective-permute-start(bf16[624,512]{1,0:T(8,128)(2,1)} %collective-permute-done.29.rest_2_), channel_id=1, source_target_pairs={{1,0},{2,3},{5,4},{6,7},{9,8},{10,11},{13,12},{14,15},{17,16},{18,... | collective-permute-start | bytes 1916936 | tf_op jit(solution)/shard_map/ppermute | solution.py:267
  130.7 7.4 %collective-permute-start.31 = (bf16[624,256]{1,0:T(8,128)(2,1)S(1)}, bf16[624,256]{1,0:T(8,128)(2,1)S(1)}, u32[]{:S(2)}, u32[]{:S(2)}) collective-permute-start(bf16[624,256]{1,0:T(8,128)(2,1)S(1)} %slice.52), channel_id=1, source_target_pairs={{1,2},{2,1},{5,6},{6,5},{9,10},{10,9},{13,14},{14,13},{17,18},{18,... | collective-permute-start | bytes 958472 | tf_op jit(solution)/shard_map/ppermute | solution.py:267
  138.1 13.1 %collective-permute-start.32 = (bf16[624,256]{1,0:T(8,128)(2,1)S(1)}, bf16[624,256]{1,0:T(8,128)(2,1)S(1)}, u32[]{:S(2)}, u32[]{:S(2)}) collective-permute-start(bf16[624,256]{1,0:T(8,128)(2,1)S(1)} %collective-permute-done.31.rest_2_), channel_id=1, source_target_pairs={{1,0},{2,3},{5,4},{6,7},{9,8},{10,11},{13,12},{14,15},{17,16},{18,... | collective-permute-start | bytes 958472 | tf_op jit(solution)/shard_map/ppermute | solution.py:267
  (11 other events, 23.0 us)

commit v6 on v5

--- a/solution.py
+++ b/solution.py
@@ -252,6 +252,30 @@
     )(z, weight, *given)
 
 
+def accept_kernel(pick_ref, tree_ref, out_ref):
+    for r in range(tree_ref.shape[0]):
+        for k in range(2):
+            rows = jnp.dot(pick_ref[r], tree_ref[r, k], preferred_element_type=jnp.float32)
+            out_ref[r, k] = rows[: out_ref.shape[2]].astype(out_ref.dtype)
+
+
+def accept(path, tree_cache):
+    req, _, tree, cols = tree_cache.shape
+    taken = path.shape[1]
+    order = jnp.arange(tree, dtype=jnp.int32)
+    pick = (path[:, :, None] == order[None, None, :]).astype(jnp.bfloat16)
+    pick = jnp.pad(pick, ((0, 0), (0, -taken % 16), (0, 0)))
+    vmem = pl.BlockSpec(memory_space=pltpu.VMEM)
+    return pl.pallas_call(
+        accept_kernel,
+        in_specs=[vmem, vmem],
+        out_specs=vmem,
+        out_shape=jax.ShapeDtypeStruct((req, 2, taken, cols), jnp.bfloat16),
+        compiler_params=pltpu.CompilerParams(vmem_limit_bytes=VMEM_BYTES),
+        cost_estimate=cost(J_FLOPS),
+    )(pick, tree_cache)
+
+
 def cache_block(prompt, spill, lens, start, width, padded):
     both = jnp.stack([prompt[0, ..., start : start + width], spill[0, ..., start : start + width]])
     both = jnp.pad(both, ((0, 0), (0, 0), (0, padded - both.shape[2]), (0, 0)))
@@ -332,7 +356,7 @@
         start, width = chunks[i]
         block = cache_block(prompt_cache, spill, lens, start, width, padded)
         if i > 0:
-            block = after(block, *gathered[i - 1][1:], *raws[max(i - 2, 0) : i - 1])
+            block = after(block, *gathered[i - 1][1:])
         gathered.append([block] + [across(block, m) for m in (2, 4, 6)])
 
     gather(0)
@@ -387,7 +411,7 @@
             acc = project(after(z, raws[-1]), weight, steps, acc, i == n + 1)
             steps = []
     path = after(accepted_path, outer[n - 1])
-    accepted_cache = jnp.take_along_axis(tree_cache, path[:, None, :, None], axis=2)
+    accepted_cache = accept(path, tree_cache)
     return acc.reshape(req, tree, out_weight.shape[1]), accepted_cache
 
 

time: 154 us -> 153 us (level)
  local copies, waits for them, and re-layouts: 24.5 us -> 16.5 us
  Pallas kernels: 31.8 us -> 37.7 us
  waiting for transfers between devices: 51.2 us -> 56.4 us
  other arithmetic: 6.33 us -> 3.53 us
    gather x3 -> x0, local copies, waits for them, and re-layouts: 4.66 us -> none  [local(): jnp.take_along_axis(tree_cache, path[:, None, :, None], axis=2)]
    optimization_barrier x1, local copies, waits for them, and re-layouts: 4.1 us -> 0.08 us  [after(): return lax.optimization_barrier((value, *earlier))[0]]
    ppermute x11, waiting for transfers between devices: 7.22 us -> 10.5 us  [along(): return lax.ppermute(value, 'tp', pairs)]
    pallas_call x0 -> x1, Pallas kernels: none -> 3.01 us  [accept(): pl.pallas_call(accept_kernel, in_specs=[vmem, vmem], out_specs=vmem, out_...]
    pallas_call x4, Pallas kernels: 20.7 us -> 23.6 us  [attend_pairs(): pl.pallas_call(partial(paired_kernel, start=start, inside=inside, n_cache...]
    ppermute x22, waiting for transfers between devices: 44 us -> 46 us  [across(): lax.ppermute(value, 'rep', [(i, i ^ mask) for i in range(lax.axis_size('r...]
    unnamed x53 -> x38, local copies, waits for them, and re-layouts: 13.2 us -> 14 us
  transfers between devices with their start and end apart: 33 -> 33, of which waited for: 15 -> 16; matrix products, arithmetic and copies ran while one was open for 11% -> 4% of each run, Pallas kernels for 16% -> 20%
where the time goes in v6:
time: 153 us; the launch traced here: 152 us
  waiting for transfers between devices  56.4 us (37%)
  Pallas kernels  37.7 us (25%)
  starting transfers between devices  35.8 us (23%)
  local copies, waits for them, and re-layouts  16.5 us (11%)
  other arithmetic  3.53 us (2%)
  between operations  2.61 us (2%)
    ppermute x22, waiting for transfers between devices, across(): lax.ppermute(value, 'rep', [(i, i ^ mask) for i in range(lax.axis_size('r...  46 us
    pallas_call x4, Pallas kernels, attend_pairs(): pl.pallas_call(partial(paired_kernel, start=start, inside=inside, n_cache...  23.6 us
    ppermute x11, starting transfers between devices, along(): return lax.ppermute(value, 'tp', pairs)  19.1 us
    ppermute x22, starting transfers between devices, across(): lax.ppermute(value, 'rep', [(i, i ^ mask) for i in range(lax.axis_size('r...  16.7 us
    unnamed x38, local copies, waits for them, and re-layouts  14 us
    pallas_call x4, Pallas kernels, project(): pl.pallas_call(partial(project_kernel, steps=tuple(shape), has_acc=acc is...  11.1 us
    ppermute x11, waiting for transfers between devices, along(): return lax.ppermute(value, 'tp', pairs)  10.5 us
  transfers between devices with their start and end apart: 33, of which 16 were waited for; matrix products, arithmetic and copies ran while one was open for 4% of the time, Pallas kernels for 20%

profile of v6, /device:TPU:0, one launch (start us, length us, event | category | flops | bytes accessed | tf_op | source)
XLA Modules:
  0.0 152.5 jit_solution(8832552825808847802)
XLA Ops:
  1.9 1.2 fusion.20
  5.0 2.6 %collective-permute-start.2 = (bf16[2,2,160,256]{3,2,1,0:T(8,128)(2,1)S(1)}, bf16[2,2,160,256]{3,2,1,0:T(8,128)(2,1)S(1)}, u32[]{:S(2)}, u32[]{:S(2)}) collective-permute-start(bf16[2,2,160,256]{3,2,1,0:T(8,128)(2,1)S(1)} %get-tuple-element.73.rest_6_), channel_id=1, source_target_pairs={{0,8},{4,12},{8,0},{12,4},{16,24},{20,28},{24,16},{28,20},{1,9},{5... | collective-permute-start | bytes 983048 | tf_op jit(solution)/shard_map/ppermute | solution.py:287
  7.7 1.5 collective-permute-start.7
  9.4 6.7 %collective-permute-done.2.rest_7_ = bf16[2,2,160,256]{3,2,1,0:T(8,128)(2,1)S(1)} collective-permute-done((bf16[2,2,160,256]{3,2,1,0:T(8,128)(2,1)S(1)}, bf16[2,2,160,256]{3,2,1,0:T(8,128)(2,1)S(1)}, u32[]{:S(2)}, u32[]{:S(2)}) %collective-permute-start.2) | collective-permute-done | bytes 327712 | tf_op jit(solution)/shard_map/ppermute | solution.py:287
  16.2 1.0 collective-permute-done.3
  17.7 1.1 collective-permute-done.6
  18.9 5.8 %collective-permute-done.7.rest_8_ = bf16[2,2,160,256]{3,2,1,0:T(8,128)(2,1)S(1)} collective-permute-done((bf16[2,2,160,256]{3,2,1,0:T(8,128)(2,1)S(1)}, bf16[2,2,160,256]{3,2,1,0:T(8,128)(2,1)S(1)}, u32[]{:S(2)}, u32[]{:S(2)}) %collective-permute-start.7) | collective-permute-done | bytes 327712 | tf_op jit(solution)/shard_map/ppermute | solution.py:287
  24.7 5.9 %shard_map.122 = (bf16[13,48,256]{2,1,0:T(8,128)(2,1)S(1)}, bf16[13,48,256]{2,1,0:T(8,128)(2,1)S(1)}) custom-call(s32[6,4]{1,0:T(8,128)S(1)} %stack.26.slot_ref, bf16[13,48,1024]{2,1,0:T(8,128)(2,1)} %rest_0_.3, bf16[13,2,48,1024]{3,2,1,0:T(8,128)(2,1)} %tree_ref, f32[13,48,256]{2,1,0:T(8,128)S(1)} %pad.27.rest_2_, ...), custom_call_target="tpu_custom_call" | custom-call | flops 8099999744 | bytes 1000 | tf_op jit(solution)/shard_map/pallas_call | solution.py:177
  30.6 1.0 collective-permute-start.10
  31.7 1.1 collective-permute-start.11
  32.8 1.4 collective-permute-start.12
  35.0 4.4 %collective-permute-start.14 = (bf16[624,256]{1,0:T(8,128)(2,1)S(1)}, bf16[624,256]{1,0:T(8,128)(2,1)S(1)}, u32[]{:S(2)}, u32[]{:S(2)}) collective-permute-start(bf16[624,256]{1,0:T(8,128)(2,1)S(1)} %bitcast.35), channel_id=1, source_target_pairs={{0,1},{1,0},{2,3},{3,2},{4,5},{5,4},{6,7},{7,6},{8,9},{9,8},{10,11... | collective-permute-start | bytes 958472 | tf_op jit(solution)/shard_map/ppermute | solution.py:291
  39.5 1.8 %collective-permute-done.10.rest_7_ = bf16[2,2,160,256]{3,2,1,0:T(8,128)(2,1)S(1)} collective-permute-done((bf16[2,2,160,256]{3,2,1,0:T(8,128)(2,1)S(1)}, bf16[2,2,160,256]{3,2,1,0:T(8,128)(2,1)S(1)}, u32[]{:S(2)}, u32[]{:S(2)}) %collective-permute-start.10) | collective-permute-done | bytes 327712 | tf_op jit(solution)/shard_map/ppermute | solution.py:287
  41.2 5.9 %collective-permute-done.11.rest_8_ = bf16[2,2,160,256]{3,2,1,0:T(8,128)(2,1)S(1)} collective-permute-done((bf16[2,2,160,256]{3,2,1,0:T(8,128)(2,1)S(1)}, bf16[2,2,160,256]{3,2,1,0:T(8,128)(2,1)S(1)}, u32[]{:S(2)}, u32[]{:S(2)}) %collective-permute-start.11) | collective-permute-done | bytes 327712 | tf_op jit(solution)/shard_map/ppermute | solution.py:287
  47.1 1.6 %collective-permute-done.12.rest_9_ = bf16[2,2,160,256]{3,2,1,0:T(8,128)(2,1)S(1)} collective-permute-done((bf16[2,2,160,256]{3,2,1,0:T(8,128)(2,1)S(1)}, bf16[2,2,160,256]{3,2,1,0:T(8,128)(2,1)S(1)}, u32[]{:S(2)}, u32[]{:S(2)}) %collective-permute-start.12) | collective-permute-done | bytes 327712 | tf_op jit(solution)/shard_map/ppermute | solution.py:287
  48.8 5.9 %shard_map.123 = (bf16[13,48,256]{2,1,0:T(8,128)(2,1)S(1)}, bf16[13,48,256]{2,1,0:T(8,128)(2,1)S(1)}) custom-call(s32[6,4]{1,0:T(8,128)S(1)} %stack.26.slot_ref, bf16[13,48,1024]{2,1,0:T(8,128)(2,1)} %rest_0_.3, bf16[13,2,48,1024]{3,2,1,0:T(8,128)(2,1)} %tree_ref, f32[13,48,256]{2,1,0:T(8,128)S(1)} %pad.27.rest_2_, ...), custom_call_target="tpu_custom_call" | custom-call | flops 8099999744 | bytes 1000 | tf_op jit(solution)/shard_map/pallas_call | solution.py:177
  55.6 1.5 collective-permute-start.17
  57.2 1.2 collective-permute-start.18
  59.3 4.4 %collective-permute-start.20 = (bf16[624,512]{1,0:T(8,128)(2,1)S(1)}, bf16[624,512]{1,0:T(8,128)(2,1)S(1)}, u32[]{:S(2)}, u32[]{:S(2)}) collective-permute-start(bf16[624,512]{1,0:T(8,128)(2,1)S(1)} %get-tuple-element.68), channel_id=1, source_target_pairs={{0,1},{1,0},{2,3},{3,2},{4,5},{5,4},{6,7},{7,6},{8,9},{9,8},{10,11... | collective-permute-start | bytes 1916936 | tf_op jit(solution)/shard_map/ppermute | solution.py:291
  63.7 1.7 %collective-permute-done.16.rest_7_ = bf16[2,2,160,256]{3,2,1,0:T(8,128)(2,1)S(1)} collective-permute-done((bf16[2,2,160,256]{3,2,1,0:T(8,128)(2,1)S(1)}, bf16[2,2,160,256]{3,2,1,0:T(8,128)(2,1)S(1)}, u32[]{:S(2)}, u32[]{:S(2)}) %collective-permute-start.16) | collective-permute-done | bytes 327712 | tf_op jit(solution)/shard_map/ppermute | solution.py:287
  65.4 7.1 %collective-permute-done.17.rest_8_ = bf16[2,2,160,256]{3,2,1,0:T(8,128)(2,1)S(1)} collective-permute-done((bf16[2,2,160,256]{3,2,1,0:T(8,128)(2,1)S(1)}, bf16[2,2,160,256]{3,2,1,0:T(8,128)(2,1)S(1)}, u32[]{:S(2)}, u32[]{:S(2)}) %collective-permute-start.17) | collective-permute-done | bytes 327712 | tf_op jit(solution)/shard_map/ppermute | solution.py:287
  72.5 5.9 %shard_map.124 = (bf16[13,48,256]{2,1,0:T(8,128)(2,1)S(1)}, bf16[13,48,256]{2,1,0:T(8,128)(2,1)S(1)}) custom-call(s32[6,4]{1,0:T(8,128)S(1)} %stack.26.slot_ref, bf16[13,48,1024]{2,1,0:T(8,128)(2,1)} %rest_0_.3, bf16[13,2,48,1024]{3,2,1,0:T(8,128)(2,1)} %tree_ref, f32[13,48,256]{2,1,0:T(8,128)S(1)} %pad.27.rest_2_, ...), custom_call_target="tpu_custom_call" | custom-call | flops 8099999744 | bytes 1000 | tf_op jit(solution)/shard_map/pallas_call | solution.py:177
  78.5 1.3 collective-permute-start.22
  80.6 1.4 collective-permute-start.24
  82.3 1.6 %collective-permute-start.25 = (bf16[624,768]{1,0:T(8,128)(2,1)S(1)}, bf16[624,768]{1,0:T(8,128)(2,1)S(1)}, u32[]{:S(2)}, u32[]{:S(2)}) collective-permute-start(bf16[624,768]{1,0:T(8,128)(2,1)S(1)} %pad_maximum_fusion), channel_id=1, source_target_pairs={{0,1},{1,0},{2,3},{3,2},{4,5},{5,4},{6,7},{7,6},{8,9},{9,8},{10,11... | collective-permute-start | bytes 2875400 | tf_op jit(solution)/shard_map/ppermute | solution.py:291
  84.8 4.2 %collective-permute-done.22.rest_7_ = bf16[2,2,160,256]{3,2,1,0:T(8,128)(2,1)S(1)} collective-permute-done((bf16[2,2,160,256]{3,2,1,0:T(8,128)(2,1)S(1)}, bf16[2,2,160,256]{3,2,1,0:T(8,128)(2,1)S(1)}, u32[]{:S(2)}, u32[]{:S(2)}) %collective-permute-start.22) | collective-permute-done | bytes 327712 | tf_op jit(solution)/shard_map/ppermute | solution.py:287
  89.1 5.9 %collective-permute-done.23.rest_8_ = bf16[2,2,160,256]{3,2,1,0:T(8,128)(2,1)S(1)} collective-permute-done((bf16[2,2,160,256]{3,2,1,0:T(8,128)(2,1)S(1)}, bf16[2,2,160,256]{3,2,1,0:T(8,128)(2,1)S(1)}, u32[]{:S(2)}, u32[]{:S(2)}) %collective-permute-start.23) | collective-permute-done | bytes 327712 | tf_op jit(solution)/shard_map/ppermute | solution.py:287
  95.0 1.6 %collective-permute-done.24.rest_9_ = bf16[2,2,160,256]{3,2,1,0:T(8,128)(2,1)S(1)} collective-permute-done((bf16[2,2,160,256]{3,2,1,0:T(8,128)(2,1)S(1)}, bf16[2,2,160,256]{3,2,1,0:T(8,128)(2,1)S(1)}, u32[]{:S(2)}, u32[]{:S(2)}) %collective-permute-start.24) | collective-permute-done | bytes 327712 | tf_op jit(solution)/shard_map/ppermute | solution.py:287
  96.6 5.9 %shard_map.125 = (bf16[13,48,256]{2,1,0:T(8,128)(2,1)S(1)}, bf16[13,48,256]{2,1,0:T(8,128)(2,1)S(1)}) custom-call(s32[6,4]{1,0:T(8,128)S(1)} %stack.26.slot_ref, bf16[13,48,1024]{2,1,0:T(8,128)(2,1)} %rest_0_.3, bf16[13,2,48,1024]{3,2,1,0:T(8,128)(2,1)} %tree_ref, f32[13,48,256]{2,1,0:T(8,128)S(1)} %pad.27.rest_2_, ...), custom_call_target="tpu_custom_call" | custom-call | flops 8099999744 | bytes 1000 | tf_op jit(solution)/shard_map/pallas_call | solution.py:177
  102.6 1.6 %collective-permute-done.27 = bf16[13,48,256]{2,1,0:T(8,128)(2,1)S(1)} collective-permute-done((bf16[13,48,256]{2,1,0:T(8,128)(2,1)S(1)}, bf16[13,48,256]{2,1,0:T(8,128)(2,1)S(1)}, u32[]{:S(2)}, u32[]{:S(2)}) %collective-permute-start.27) | collective-permute-done | bytes 319520 | tf_op jit(solution)/shard_map/ppermute | solution.py:287
  104.3 1.0 pad_maximum_fusion.1
  105.3 1.6 %collective-permute-start.28 = (bf16[624,768]{1,0:T(8,128)(2,1)}, bf16[624,768]{1,0:T(8,128)(2,1)}, u32[]{:S(2)}, u32[]{:S(2)}) collective-permute-start(bf16[624,768]{1,0:T(8,128)(2,1)} %pad_maximum_fusion.1), channel_id=1, source_target_pairs={{0,1},{1,0},{2,3},{3,2},{4,5},{5,4},{6,7},{7,6},{8,9},{9,8},{10,11... | collective-permute-start | bytes 2875400 | tf_op jit(solution)/shard_map/ppermute | solution.py:291
  108.8 1.5 collective-permute-start.29
  110.2 3.4 %copy-done = bf16[4096,1024]{1,0:T(8,128)(2,1)S(1)} copy-done((bf16[4096,1024]{1,0:T(8,128)(2,1)S(1)}, bf16[4096,1024]{1,0:T(8,128)(2,1)}, u32[]{:S(2)}) %copy-start) | copy-done | bytes 8388632
  113.6 1.1 copy-done.3
  114.7 1.2 copy-done.7
  115.9 1.1 copy-done.9
  119.9 3.9 %shard_map.126.rest_0_ = f32[624,1024]{1,0:T(8,128)S(1)} custom-call(s32[1]{0:T(128)} %bitcast.z_ref, bf16[4,1024,1024]{2,1,0:T(8,128)(2,1)S(1)} %bitcast.22, bf16[624,256]{1,0:T(8,128)(2,1)S(1)} %bitcast.36, bf16[624,256]{1,0:T(8,128)(2,1)S(1)} %copy-done.15, bf16[624,256]{1,0:T(8,128)(2,1)S(1)} %bitcast.33, bf16[624,512]{1,0:T(8,128)(2,1)S(1)} %copy-done.9, ...), custom_call_target="tpu_custom_call" | custom-call | flops 2000000000 | bytes 1000 | tf_op jit(solution)/shard_map/pallas_call | solution.py:240
  123.8 1.3 collective-permute-start.30
  125.1 3.8 %collective-permute-done.28.rest_2_ = bf16[624,768]{1,0:T(8,128)(2,1)} collective-permute-done((bf16[624,768]{1,0:T(8,128)(2,1)}, bf16[624,768]{1,0:T(8,128)(2,1)}, u32[]{:S(2)}, u32[]{:S(2)}) %collective-permute-start.28) | collective-permute-done | bytes 958496 | tf_op jit(solution)/shard_map/ppermute | solution.py:291
  130.8 3.0 %shard_map.130 = bf16[13,2,8,1024]{3,2,1,0:T(8,128)(2,1)} custom-call(bf16[13,16,48]{2,1,0:T(8,128)(2,1)S(1)} %pad_convert_fusion.pick_ref, bf16[13,2,48,1024]{3,2,1,0:T(8,128)(2,1)} %tree_ref), custom_call_target="tpu_custom_call" | custom-call | flops 2000000000 | bytes 1000 | tf_op jit(solution)/shard_map/pallas_call | solution.py:269
  133.8 1.3 collective-permute-start.32
  135.1 3.4 %copy-done.1 = bf16[4096,1024]{1,0:T(8,128)(2,1)S(1)} copy-done((bf16[4096,1024]{1,0:T(8,128)(2,1)S(1)}, bf16[4096,1024]{1,0:T(8,128)(2,1)}, u32[]{:S(2)}) %copy-start.1) | copy-done | bytes 8388632
  138.5 3.2 %shard_map.127.rest_0_ = f32[624,1024]{1,0:T(8,128)S(1)} custom-call(s32[1]{0:T(128)} %bitcast.z_ref, bf16[4,1024,1024]{2,1,0:T(8,128)(2,1)S(1)} %bitcast.23, f32[624,1024]{1,0:T(8,128)S(1)} %shard_map.126.rest_0_, bf16[624,256]{1,0:T(8,128)(2,1)S(1)} %bitcast.31, bf16[624,768]{1,0:T(8,128)(2,1)} %collective-permute-done.28.rest_2_, ...), custom_call_target="tpu_custom_call", output_to_operand_aliasing={{}: (2, {})} | custom-call | flops 2000000000 | bytes 1000 | tf_op jit(solution)/shard_map/pallas_call | solution.py:240
  141.7 3.3 %collective-permute-done.30.rest_1_ = bf16[624,512]{1,0:T(8,128)(2,1)} collective-permute-done((bf16[624,512]{1,0:T(8,128)(2,1)}, bf16[624,512]{1,0:T(8,128)(2,1)}, u32[]{:S(2)}, u32[]{:S(2)}) %collective-permute-start.30) | collective-permute-done | bytes 639008 | tf_op jit(solution)/shard_map/ppermute | solution.py:291
  144.9 2.4 %shard_map.128.rest_0_ = f32[624,1024]{1,0:T(8,128)S(1)} custom-call(s32[1]{0:T(128)} %bitcast.z_ref, bf16[4,1024,1024]{2,1,0:T(8,128)(2,1)S(1)} %bitcast.24, f32[624,1024]{1,0:T(8,128)S(1)} %shard_map.127.rest_0_, bf16[624,512]{1,0:T(8,128)(2,1)} %collective-permute-done.30.rest_1_, ...), custom_call_target="tpu_custom_call", output_to_operand_aliasing={{}: (2, {})} | custom-call | flops 2000000000 | bytes 1000 | tf_op jit(solution)/shard_map/pallas_call | solution.py:240
  147.4 3.3 %collective-permute-done.32.rest_1_ = bf16[624,256]{1,0:T(8,128)(2,1)S(1)} collective-permute-done((bf16[624,256]{1,0:T(8,128)(2,1)S(1)}, bf16[624,256]{1,0:T(8,128)(2,1)S(1)}, u32[]{:S(2)}, u32[]{:S(2)}) %collective-permute-start.32) | collective-permute-done | bytes 319520 | tf_op jit(solution)/shard_map/ppermute | solution.py:291
  150.7 1.6 %shard_map.129 = bf16[624,1024]{1,0:T(8,128)(2,1)} custom-call(s32[1]{0:T(128)} %bitcast.z_ref, bf16[4,1024,1024]{2,1,0:T(8,128)(2,1)S(1)} %bitcast.25, f32[624,1024]{1,0:T(8,128)S(1)} %shard_map.128.rest_0_, bf16[624,256]{1,0:T(8,128)(2,1)S(1)} %collective-permute-done.32.rest_1_, bf16[624,256]{1,0:T(8,128)(2,1)S(1)} %collective-permute-done.31.rest_2_), custom_call_target="tpu_custom_call" | custom-call | flops 2000000000 | bytes 1000 | tf_op jit(solution)/shard_map/pallas_call | solution.py:240
  (95 shorter events, 14.3 us)
Async XLA Ops:
  0.6 3.2 %collective-permute-start.1 = (bf16[1,2,152,1024]{3,2,1,0:T(8,128)(2,1)}, bf16[1,2,152,1024]{3,2,1,0:T(8,128)(2,1)S(1)}, u32[]{:S(2)}, u32[]{:S(2)}) collective-permute-start(bf16[1,2,152,1024]{3,2,1,0:T(8,128)(2,1)} %param.18), channel_id=1, source_target_pairs={{0,4},{4,0},{8,12},{12,8},{16,20},{20,16},{24,28},{28,24},{1,5},{5... | collective-permute-start | bytes 1867784 | tf_op jit(solution)/shard_map/ppermute | solution.py:287
  1.1 1.9 %collective-permute-start = (s32[1]{0:T(128)}, s32[1]{0:T(128)}, u32[]{:S(2)}, u32[]{:S(2)}) collective-permute-start(s32[1]{0:T(128)} %param.19), channel_id=1, source_target_pairs={{0,4},{4,0},{8,12},{12,8},{16,20},{20,16},{24,28},{28,24},{1,5},{5... | collective-permute-start | bytes 20 | tf_op jit(solution)/shard_map/ppermute | solution.py:287
  3.9 12.2 %copy-start.18 = (s32[13,1]{0,1:T(1,128)S(1)}, s32[13,1]{0,1:T(1,128)}, u32[]{:S(2)}) copy-start(s32[13,1]{0,1:T(1,128)} %param.14) | copy-start | bytes 160
  3.9 12.2 %copy-start.16 = (s32[13,48,48]{2,1,0:T(8,128)S(1)}, s32[13,48,48]{2,1,0:T(8,128)}, u32[]{:S(2)}) copy-start(s32[13,48,48]{2,1,0:T(8,128)} %param.13) | copy-start | bytes 359428
  4.5 20.2 %collective-permute-start.5 = (bf16[13,2,48,1024]{3,2,1,0:T(8,128)(2,1)}, bf16[13,2,48,1024]{3,2,1,0:T(8,128)(2,1)}, u32[]{:S(2)}, u32[]{:S(2)}) collective-permute-start(bf16[13,2,48,1024]{3,2,1,0:T(8,128)(2,1)} %tree_ref), channel_id=1, source_target_pairs={{0,4},{4,0},{8,12},{12,8},{16,20},{20,16},{24,28},{28,24},{1,5},{5... | collective-permute-start | bytes 7667720 | tf_op jit(solution)/shard_map/ppermute | solution.py:287
  5.0 11.1 %collective-permute-start.2 = (bf16[2,2,160,256]{3,2,1,0:T(8,128)(2,1)S(1)}, bf16[2,2,160,256]{3,2,1,0:T(8,128)(2,1)S(1)}, u32[]{:S(2)}, u32[]{:S(2)}) collective-permute-start(bf16[2,2,160,256]{3,2,1,0:T(8,128)(2,1)S(1)} %get-tuple-element.73.rest_6_), channel_id=1, source_target_pairs={{0,8},{4,12},{8,0},{12,4},{16,24},{20,28},{24,16},{28,20},{1,9},{5... | collective-permute-start | bytes 983048 | tf_op jit(solution)/shard_map/ppermute | solution.py:287
  7.5 17.2 %collective-permute-start.4 = (bf16[13,48,1024]{2,1,0:T(8,128)(2,1)}, bf16[13,48,1024]{2,1,0:T(8,128)(2,1)}, u32[]{:S(2)}, u32[]{:S(2)}) collective-permute-start(bf16[13,48,1024]{2,1,0:T(8,128)(2,1)} %rest_0_.3), channel_id=1, source_target_pairs={{0,4},{4,0},{8,12},{12,8},{16,20},{20,16},{24,28},{28,24},{1,5},{5... | collective-permute-start | bytes 3833864 | tf_op jit(solution)/shard_map/ppermute | solution.py:287
  7.7 17.0 %collective-permute-start.7 = (bf16[2,2,160,256]{3,2,1,0:T(8,128)(2,1)S(1)}, bf16[2,2,160,256]{3,2,1,0:T(8,128)(2,1)S(1)}, u32[]{:S(2)}, u32[]{:S(2)}) collective-permute-start(bf16[2,2,160,256]{3,2,1,0:T(8,128)(2,1)S(1)} %get-tuple-element.73.rest_6_), channel_id=1, source_target_pairs={{0,16},{4,20},{8,24},{12,28},{16,0},{20,4},{24,8},{28,12},{1,17},{... | collective-permute-start | bytes 983048 | tf_op jit(solution)/shard_map/ppermute | solution.py:287
  9.2 15.5 %collective-permute-start.8 = (bf16[2,2,160,256]{3,2,1,0:T(8,128)(2,1)S(1)}, bf16[2,2,160,256]{3,2,1,0:T(8,128)(2,1)}, u32[]{:S(2)}, u32[]{:S(2)}) collective-permute-start(bf16[2,2,160,256]{3,2,1,0:T(8,128)(2,1)S(1)} %get-tuple-element.73.rest_6_), channel_id=1, source_target_pairs={{0,24},{4,28},{8,16},{12,20},{16,8},{20,12},{24,0},{28,4},{1,25},{... | collective-permute-start | bytes 983048 | tf_op jit(solution)/shard_map/ppermute | solution.py:287
  16.1 1.1 collective-permute-start.3
  17.2 1.6 %collective-permute-start.6 = (s32[13,48,48]{2,1,0:T(8,128)S(1)}, s32[13,48,48]{2,1,0:T(8,128)S(1)}, u32[]{:S(2)}, u32[]{:S(2)}) collective-permute-start(s32[13,48,48]{2,1,0:T(8,128)S(1)} %copy-done.16), channel_id=1, source_target_pairs={{0,4},{4,0},{8,12},{12,8},{16,20},{20,16},{24,28},{28,24},{1,5},{5... | collective-permute-start | bytes 359432 | tf_op jit(solution)/shard_map/ppermute | solution.py:287
  30.6 3.6 %collective-permute-start.9 = (bf16[13,48,256]{2,1,0:T(8,128)(2,1)S(1)}, bf16[13,48,256]{2,1,0:T(8,128)(2,1)S(1)}, u32[]{:S(2)}, u32[]{:S(2)}) collective-permute-start(bf16[13,48,256]{2,1,0:T(8,128)(2,1)S(1)} %get-tuple-element.33), channel_id=1, source_target_pairs={{0,4},{4,0},{8,12},{12,8},{16,20},{20,16},{24,28},{28,24},{1,5},{5... | collective-permute-start | bytes 958472 | tf_op jit(solution)/shard_map/ppermute | solution.py:287
  30.6 10.6 %collective-permute-start.10 = (bf16[2,2,160,256]{3,2,1,0:T(8,128)(2,1)S(1)}, bf16[2,2,160,256]{3,2,1,0:T(8,128)(2,1)S(1)}, u32[]{:S(2)}, u32[]{:S(2)}) collective-permute-start(bf16[2,2,160,256]{3,2,1,0:T(8,128)(2,1)S(1)} %get-tuple-element.35.rest_6_), channel_id=1, source_target_pairs={{0,8},{4,12},{8,0},{12,4},{16,24},{20,28},{24,16},{28,20},{1,9},{5... | collective-permute-start | bytes 983048 | tf_op jit(solution)/shard_map/ppermute | solution.py:287
  31.7 15.4 %collective-permute-start.11 = (bf16[2,2,160,256]{3,2,1,0:T(8,128)(2,1)S(1)}, bf16[2,2,160,256]{3,2,1,0:T(8,128)(2,1)S(1)}, u32[]{:S(2)}, u32[]{:S(2)}) collective-permute-start(bf16[2,2,160,256]{3,2,1,0:T(8,128)(2,1)S(1)} %get-tuple-element.35.rest_6_), channel_id=1, source_target_pairs={{0,16},{4,20},{8,24},{12,28},{16,0},{20,4},{24,8},{28,12},{1,17},{... | collective-permute-start | bytes 983048 | tf_op jit(solution)/shard_map/ppermute | solution.py:287
  32.8 16.0 %collective-permute-start.12 = (bf16[2,2,160,256]{3,2,1,0:T(8,128)(2,1)S(1)}, bf16[2,2,160,256]{3,2,1,0:T(8,128)(2,1)S(1)}, u32[]{:S(2)}, u32[]{:S(2)}) collective-permute-start(bf16[2,2,160,256]{3,2,1,0:T(8,128)(2,1)S(1)} %get-tuple-element.35.rest_6_), channel_id=1, source_target_pairs={{0,24},{4,28},{8,16},{12,20},{16,8},{20,12},{24,0},{28,4},{1,25},{... | collective-permute-start | bytes 983048 | tf_op jit(solution)/shard_map/ppermute | solution.py:287
  34.3 20.3 %copy-start.10 = (bf16[13,48,256]{2,1,0:T(8,128)(2,1)}, bf16[13,48,256]{2,1,0:T(8,128)(2,1)S(1)}, u32[]{:S(2)}) copy-start(bf16[13,48,256]{2,1,0:T(8,128)(2,1)S(1)} %broadcast_select_fusion.3) | copy-start | bytes 958468
  34.3 20.3 %collective-permute-start.13 = (bf16[624,256]{1,0:T(8,128)(2,1)S(1)}, bf16[624,256]{1,0:T(8,128)(2,1)S(1)}, u32[]{:S(2)}, u32[]{:S(2)}) collective-permute-start(bf16[624,256]{1,0:T(8,128)(2,1)S(1)} %bitcast.34), channel_id=1, source_target_pairs={{1,2},{2,1},{5,6},{6,5},{9,10},{10,9},{13,14},{14,13},{17,18},{18,... | collective-permute-start | bytes 958472 | tf_op jit(solution)/shard_map/ppermute | solution.py:291
  35.0 19.7 %collective-permute-start.14 = (bf16[624,256]{1,0:T(8,128)(2,1)S(1)}, bf16[624,256]{1,0:T(8,128)(2,1)S(1)}, u32[]{:S(2)}, u32[]{:S(2)}) collective-permute-start(bf16[624,256]{1,0:T(8,128)(2,1)S(1)} %bitcast.35), channel_id=1, source_target_pairs={{0,1},{1,0},{2,3},{3,2},{4,5},{5,4},{6,7},{7,6},{8,9},{9,8},{10,11... | collective-permute-start | bytes 958472 | tf_op jit(solution)/shard_map/ppermute | solution.py:291
  54.7 3.9 %copy-start.12 = (bf16[624,256]{1,0:T(8,128)(2,1)}, bf16[624,256]{1,0:T(8,128)(2,1)S(1)}, u32[]{:S(2)}) copy-start(bf16[624,256]{1,0:T(8,128)(2,1)S(1)} %collective-permute-done.13.rest_4_) | copy-start | bytes 958468
  54.7 3.9 %copy-start.14 = (bf16[624,256]{1,0:T(8,128)(2,1)}, bf16[624,256]{1,0:T(8,128)(2,1)S(1)}, u32[]{:S(2)}) copy-start(bf16[624,256]{1,0:T(8,128)(2,1)S(1)} %collective-permute-done.14.rest_1_) | copy-start | bytes 958468
  54.7 3.6 %collective-permute-start.15 = (bf16[13,48,256]{2,1,0:T(8,128)(2,1)S(1)}, bf16[13,48,256]{2,1,0:T(8,128)(2,1)S(1)}, u32[]{:S(2)}, u32[]{:S(2)}) collective-permute-start(bf16[13,48,256]{2,1,0:T(8,128)(2,1)S(1)} %get-tuple-element.39), channel_id=1, source_target_pairs={{0,4},{4,0},{8,12},{12,8},{16,20},{20,16},{24,28},{28,24},{1,5},{5... | collective-permute-start | bytes 958472 | tf_op jit(solution)/shard_map/ppermute | solution.py:287
  54.8 10.6 %collective-permute-start.16 = (bf16[2,2,160,256]{3,2,1,0:T(8,128)(2,1)S(1)}, bf16[2,2,160,256]{3,2,1,0:T(8,128)(2,1)S(1)}, u32[]{:S(2)}, u32[]{:S(2)}) collective-permute-start(bf16[2,2,160,256]{3,2,1,0:T(8,128)(2,1)S(1)} %get-tuple-element.41.rest_6_), channel_id=1, source_target_pairs={{0,8},{4,12},{8,0},{12,4},{16,24},{20,28},{24,16},{28,20},{1,9},{5... | collective-permute-start | bytes 983048 | tf_op jit(solution)/shard_map/ppermute | solution.py:287
  55.6 16.8 %collective-permute-start.17 = (bf16[2,2,160,256]{3,2,1,0:T(8,128)(2,1)S(1)}, bf16[2,2,160,256]{3,2,1,0:T(8,128)(2,1)S(1)}, u32[]{:S(2)}, u32[]{:S(2)}) collective-permute-start(bf16[2,2,160,256]{3,2,1,0:T(8,128)(2,1)S(1)} %get-tuple-element.41.rest_6_), channel_id=1, source_target_pairs={{0,16},{4,20},{8,24},{12,28},{16,0},{20,4},{24,8},{28,12},{1,17},{... | collective-permute-start | bytes 983048 | tf_op jit(solution)/shard_map/ppermute | solution.py:287
  57.2 15.3 %collective-permute-start.18 = (bf16[2,2,160,256]{3,2,1,0:T(8,128)(2,1)S(1)}, bf16[2,2,160,256]{3,2,1,0:T(8,128)(2,1)S(1)}, u32[]{:S(2)}, u32[]{:S(2)}) collective-permute-start(bf16[2,2,160,256]{3,2,1,0:T(8,128)(2,1)S(1)} %get-tuple-element.41.rest_6_), channel_id=1, source_target_pairs={{0,24},{4,28},{8,16},{12,20},{16,8},{20,12},{24,0},{28,4},{1,25},{... | collective-permute-start | bytes 983048 | tf_op jit(solution)/shard_map/ppermute | solution.py:287
  58.6 19.8 %collective-permute-start.19 = (bf16[624,512]{1,0:T(8,128)(2,1)S(1)}, bf16[624,512]{1,0:T(8,128)(2,1)S(1)}, u32[]{:S(2)}, u32[]{:S(2)}) collective-permute-start(bf16[624,512]{1,0:T(8,128)(2,1)S(1)} %get-tuple-element.69), channel_id=1, source_target_pairs={{1,2},{2,1},{5,6},{6,5},{9,10},{10,9},{13,14},{14,13},{17,18},{18,... | collective-permute-start | bytes 1916936 | tf_op jit(solution)/shard_map/ppermute | solution.py:291
  59.3 19.1 %collective-permute-start.20 = (bf16[624,512]{1,0:T(8,128)(2,1)S(1)}, bf16[624,512]{1,0:T(8,128)(2,1)S(1)}, u32[]{:S(2)}, u32[]{:S(2)}) collective-permute-start(bf16[624,512]{1,0:T(8,128)(2,1)S(1)} %get-tuple-element.68), channel_id=1, source_target_pairs={{0,1},{1,0},{2,3},{3,2},{4,5},{5,4},{6,7},{7,6},{8,9},{9,8},{10,11... | collective-permute-start | bytes 1916936 | tf_op jit(solution)/shard_map/ppermute | solution.py:291
  78.4 3.9 %copy-start.2 = (bf16[624,512]{1,0:T(8,128)(2,1)}, bf16[624,512]{1,0:T(8,128)(2,1)S(1)}, u32[]{:S(2)}) copy-start(bf16[624,512]{1,0:T(8,128)(2,1)S(1)} %collective-permute-done.19.rest_7_) | copy-start | bytes 1916932
  78.4 3.8 %copy-start.8 = (bf16[624,512]{1,0:T(8,128)(2,1)}, bf16[624,512]{1,0:T(8,128)(2,1)S(1)}, u32[]{:S(2)}) copy-start(bf16[624,512]{1,0:T(8,128)(2,1)S(1)} %collective-permute-done.20.rest_3_) | copy-start | bytes 1916932
  78.4 3.7 %collective-permute-start.21 = (bf16[13,48,256]{2,1,0:T(8,128)(2,1)S(1)}, bf16[13,48,256]{2,1,0:T(8,128)(2,1)S(1)}, u32[]{:S(2)}, u32[]{:S(2)}) collective-permute-start(bf16[13,48,256]{2,1,0:T(8,128)(2,1)S(1)} %get-tuple-element.45), channel_id=1, source_target_pairs={{0,4},{4,0},{8,12},{12,8},{16,20},{20,16},{24,28},{28,24},{1,5},{5... | collective-permute-start | bytes 958472 | tf_op jit(solution)/shard_map/ppermute | solution.py:287
  78.5 10.6 %collective-permute-start.22 = (bf16[2,2,160,256]{3,2,1,0:T(8,128)(2,1)S(1)}, bf16[2,2,160,256]{3,2,1,0:T(8,128)(2,1)S(1)}, u32[]{:S(2)}, u32[]{:S(2)}) collective-permute-start(bf16[2,2,160,256]{3,2,1,0:T(8,128)(2,1)S(1)} %get-tuple-element.47.rest_6_), channel_id=1, source_target_pairs={{0,8},{4,12},{8,0},{12,4},{16,24},{20,28},{24,16},{28,20},{1,9},{5... | collective-permute-start | bytes 983048 | tf_op jit(solution)/shard_map/ppermute | solution.py:287
  79.8 15.2 %collective-permute-start.23 = (bf16[2,2,160,256]{3,2,1,0:T(8,128)(2,1)S(1)}, bf16[2,2,160,256]{3,2,1,0:T(8,128)(2,1)S(1)}, u32[]{:S(2)}, u32[]{:S(2)}) collective-permute-start(bf16[2,2,160,256]{3,2,1,0:T(8,128)(2,1)S(1)} %get-tuple-element.47.rest_6_), channel_id=1, source_target_pairs={{0,16},{4,20},{8,24},{12,28},{16,0},{20,4},{24,8},{28,12},{1,17},{... | collective-permute-start | bytes 983048 | tf_op jit(solution)/shard_map/ppermute | solution.py:287
  80.6 16.0 %collective-permute-start.24 = (bf16[2,2,160,256]{3,2,1,0:T(8,128)(2,1)S(1)}, bf16[2,2,160,256]{3,2,1,0:T(8,128)(2,1)S(1)}, u32[]{:S(2)}, u32[]{:S(2)}) collective-permute-start(bf16[2,2,160,256]{3,2,1,0:T(8,128)(2,1)S(1)} %get-tuple-element.47.rest_6_), channel_id=1, source_target_pairs={{0,24},{4,28},{8,16},{12,20},{16,8},{20,12},{24,0},{28,4},{1,25},{... | collective-permute-start | bytes 983048 | tf_op jit(solution)/shard_map/ppermute | solution.py:287
  82.3 24.6 %collective-permute-start.25 = (bf16[624,768]{1,0:T(8,128)(2,1)S(1)}, bf16[624,768]{1,0:T(8,128)(2,1)S(1)}, u32[]{:S(2)}, u32[]{:S(2)}) collective-permute-start(bf16[624,768]{1,0:T(8,128)(2,1)S(1)} %pad_maximum_fusion), channel_id=1, source_target_pairs={{0,1},{1,0},{2,3},{3,2},{4,5},{5,4},{6,7},{7,6},{8,9},{9,8},{10,11... | collective-permute-start | bytes 2875400 | tf_op jit(solution)/shard_map/ppermute | solution.py:291
  84.0 18.5 %collective-permute-start.26 = (bf16[624,512]{1,0:T(8,128)(2,1)S(1)}, bf16[624,512]{1,0:T(8,128)(2,1)S(1)}, u32[]{:S(2)}, u32[]{:S(2)}) collective-permute-start(bf16[624,512]{1,0:T(8,128)(2,1)S(1)} %pad_maximum_fusion.4), channel_id=1, source_target_pairs={{1,2},{2,1},{5,6},{6,5},{9,10},{10,9},{13,14},{14,13},{17,18},{18,... | collective-permute-start | bytes 1916936 | tf_op jit(solution)/shard_map/ppermute | solution.py:291
  102.5 2.8 %copy-start.4 = (bf16[624,512]{1,0:T(8,128)(2,1)}, bf16[624,512]{1,0:T(8,128)(2,1)S(1)}, u32[]{:S(2)}) copy-start(bf16[624,512]{1,0:T(8,128)(2,1)S(1)} %collective-permute-done.26.rest_3_) | copy-start | bytes 1916932
  102.5 1.7 %collective-permute-start.27 = (bf16[13,48,256]{2,1,0:T(8,128)(2,1)S(1)}, bf16[13,48,256]{2,1,0:T(8,128)(2,1)S(1)}, u32[]{:S(2)}, u32[]{:S(2)}) collective-permute-start(bf16[13,48,256]{2,1,0:T(8,128)(2,1)S(1)} %get-tuple-element.52), channel_id=1, source_target_pairs={{0,4},{4,0},{8,12},{12,8},{16,20},{20,16},{24,28},{28,24},{1,5},{5... | collective-permute-start | bytes 958472 | tf_op jit(solution)/shard_map/ppermute | solution.py:287
  105.3 23.6 %collective-permute-start.28 = (bf16[624,768]{1,0:T(8,128)(2,1)}, bf16[624,768]{1,0:T(8,128)(2,1)}, u32[]{:S(2)}, u32[]{:S(2)}) collective-permute-start(bf16[624,768]{1,0:T(8,128)(2,1)} %pad_maximum_fusion.1), channel_id=1, source_target_pairs={{0,1},{1,0},{2,3},{3,2},{4,5},{5,4},{6,7},{7,6},{8,9},{9,8},{10,11... | collective-permute-start | bytes 2875400 | tf_op jit(solution)/shard_map/ppermute | solution.py:291
  108.8 15.0 %collective-permute-start.29 = (bf16[624,512]{1,0:T(8,128)(2,1)}, bf16[624,512]{1,0:T(8,128)(2,1)}, u32[]{:S(2)}, u32[]{:S(2)}) collective-permute-start(bf16[624,512]{1,0:T(8,128)(2,1)} %pad_maximum_fusion.5), channel_id=1, source_target_pairs={{1,2},{2,1},{5,6},{6,5},{9,10},{10,9},{13,14},{14,13},{17,18},{18,... | collective-permute-start | bytes 1916936 | tf_op jit(solution)/shard_map/ppermute | solution.py:291
  110.2 3.4 %copy-start = (bf16[4096,1024]{1,0:T(8,128)(2,1)S(1)}, bf16[4096,1024]{1,0:T(8,128)(2,1)}, u32[]{:S(2)}) copy-start(bf16[4096,1024]{1,0:T(8,128)(2,1)} %param.20) | copy-start | bytes 25165828
  113.6 1.1 copy-start.3
  114.7 1.2 copy-start.7
  115.9 1.1 copy-start.9
  119.9 10.7 %copy-start.17 = (s32[13,8]{0,1:T(8,128)S(1)}, s32[13,8]{0,1:T(8,128)}, u32[]{:S(2)}) copy-start(s32[13,8]{0,1:T(8,128)} %param.15) | copy-start | bytes 1252
  123.8 21.2 %collective-permute-start.30 = (bf16[624,512]{1,0:T(8,128)(2,1)}, bf16[624,512]{1,0:T(8,128)(2,1)}, u32[]{:S(2)}, u32[]{:S(2)}) collective-permute-start(bf16[624,512]{1,0:T(8,128)(2,1)} %collective-permute-done.29.rest_2_), channel_id=1, source_target_pairs={{1,0},{2,3},{5,4},{6,7},{9,8},{10,11},{13,12},{14,15},{17,16},{18,... | collective-permute-start | bytes 1916936 | tf_op jit(solution)/shard_map/ppermute | solution.py:291
  129.9 3.9 %collective-permute-start.31 = (bf16[624,256]{1,0:T(8,128)(2,1)S(1)}, bf16[624,256]{1,0:T(8,128)(2,1)S(1)}, u32[]{:S(2)}, u32[]{:S(2)}) collective-permute-start(bf16[624,256]{1,0:T(8,128)(2,1)S(1)} %slice.50), channel_id=1, source_target_pairs={{1,2},{2,1},{5,6},{6,5},{9,10},{10,9},{13,14},{14,13},{17,18},{18,... | collective-permute-start | bytes 958472 | tf_op jit(solution)/shard_map/ppermute | solution.py:291
  130.8 4.3 %copy-start.5 = (bf16[624,512]{1,0:T(8,128)(2,1)S(1)}, bf16[624,512]{1,0:T(8,128)(2,1)}, u32[]{:S(2)}) copy-start(bf16[624,512]{1,0:T(8,128)(2,1)} %copy-done.4) | copy-start | bytes 1916932
  133.8 16.9 %collective-permute-start.32 = (bf16[624,256]{1,0:T(8,128)(2,1)S(1)}, bf16[624,256]{1,0:T(8,128)(2,1)S(1)}, u32[]{:S(2)}, u32[]{:S(2)}) collective-permute-start(bf16[624,256]{1,0:T(8,128)(2,1)S(1)} %collective-permute-done.31.rest_2_), channel_id=1, source_target_pairs={{1,0},{2,3},{5,4},{6,7},{9,8},{10,11},{13,12},{14,15},{17,16},{18,... | collective-permute-start | bytes 958472 | tf_op jit(solution)/shard_map/ppermute | solution.py:291
  135.1 3.4 %copy-start.1 = (bf16[4096,1024]{1,0:T(8,128)(2,1)S(1)}, bf16[4096,1024]{1,0:T(8,128)(2,1)}, u32[]{:S(2)}) copy-start(bf16[4096,1024]{1,0:T(8,128)(2,1)} %param.20) | copy-start | bytes 25165828
  (4 other events, 3.8 us)

commit v7 on v6

--- a/solution.py
+++ b/solution.py
@@ -11,7 +11,7 @@
 HD = 128
 NEG_FILL = -1e30
 HEAD_CHUNKS = (2, 2, 2, 2)
-SPLITS = (2, 3, 4, 5)
+SPLITS = (2, 3, 5)
 FRONT = 1
 
 

time: 153 us -> 155 us (1.013)
  waiting for transfers between devices: 56.4 us -> 58.8 us
    ppermute x11, waiting for transfers between devices: 10.5 us -> 12.8 us  [along(): return lax.ppermute(value, 'tp', pairs)]
    pallas_call x4 -> x3, Pallas kernels: 11.1 us -> 10.7 us  [project(): pl.pallas_call(partial(project_kernel, steps=tuple(shape), has_acc=acc is...]
  transfers between devices with their start and end apart: 33 -> 33, of which waited for: 16 -> 16; matrix products, arithmetic and copies ran while one was open for 4% -> 3% of each run, Pallas kernels for 20% -> 18%
where the time goes in v7:
time: 155 us
  waiting for transfers between devices  58.8 us (38%)
  Pallas kernels  37.2 us (24%)
  starting transfers between devices  36 us (23%)
  local copies, waits for them, and re-layouts  16.5 us (11%)
  other arithmetic  3.53 us (2%)
  between operations  2.6 us (2%)
    ppermute x22, waiting for transfers between devices, across(): lax.ppermute(value, 'rep', [(i, i ^ mask) for i in range(lax.axis_size('r...  46 us
    pallas_call x4, Pallas kernels, attend_pairs(): pl.pallas_call(partial(paired_kernel, start=start, inside=inside, n_cache...  23.5 us
    ppermute x11, starting transfers between devices, along(): return lax.ppermute(value, 'tp', pairs)  19.3 us
    ppermute x22, starting transfers between devices, across(): lax.ppermute(value, 'rep', [(i, i ^ mask) for i in range(lax.axis_size('r...  16.7 us
    unnamed x38, local copies, waits for them, and re-layouts  14 us
    ppermute x11, waiting for transfers between devices, along(): return lax.ppermute(value, 'tp', pairs)  12.8 us
    pallas_call x3, Pallas kernels, project(): pl.pallas_call(partial(project_kernel, steps=tuple(shape), has_acc=acc is...  10.7 us
  transfers between devices with their start and end apart: 33, of which 16 were waited for; matrix products, arithmetic and copies ran while one was open for 3% of the time, Pallas kernels for 18%

profile of v7, /device:TPU:0, one launch (start us, length us, event | category | flops | bytes accessed | tf_op | source)
XLA Modules:
  0.0 154.6 jit_solution(6466095484238552204)
XLA Ops:
  1.9 1.2 fusion.20
  5.0 2.6 %collective-permute-start.2 = (bf16[2,2,160,256]{3,2,1,0:T(8,128)(2,1)S(1)}, bf16[2,2,160,256]{3,2,1,0:T(8,128)(2,1)S(1)}, u32[]{:S(2)}, u32[]{:S(2)}) collective-permute-start(bf16[2,2,160,256]{3,2,1,0:T(8,128)(2,1)S(1)} %get-tuple-element.73.rest_6_), channel_id=1, source_target_pairs={{0,8},{4,12},{8,0},{12,4},{16,24},{20,28},{24,16},{28,20},{1,9},{5... | collective-permute-start | bytes 983048 | tf_op jit(solution)/shard_map/ppermute | solution.py:287
  7.7 1.5 collective-permute-start.7
  9.4 6.7 %collective-permute-done.2.rest_7_ = bf16[2,2,160,256]{3,2,1,0:T(8,128)(2,1)S(1)} collective-permute-done((bf16[2,2,160,256]{3,2,1,0:T(8,128)(2,1)S(1)}, bf16[2,2,160,256]{3,2,1,0:T(8,128)(2,1)S(1)}, u32[]{:S(2)}, u32[]{:S(2)}) %collective-permute-start.2) | collective-permute-done | bytes 327712 | tf_op jit(solution)/shard_map/ppermute | solution.py:287
  16.2 1.0 collective-permute-done.3
  17.7 1.1 collective-permute-done.6
  18.9 5.8 %collective-permute-done.7.rest_8_ = bf16[2,2,160,256]{3,2,1,0:T(8,128)(2,1)S(1)} collective-permute-done((bf16[2,2,160,256]{3,2,1,0:T(8,128)(2,1)S(1)}, bf16[2,2,160,256]{3,2,1,0:T(8,128)(2,1)S(1)}, u32[]{:S(2)}, u32[]{:S(2)}) %collective-permute-start.7) | collective-permute-done | bytes 327712 | tf_op jit(solution)/shard_map/ppermute | solution.py:287
  24.7 5.9 %shard_map.122 = (bf16[13,48,256]{2,1,0:T(8,128)(2,1)S(1)}, bf16[13,48,256]{2,1,0:T(8,128)(2,1)S(1)}) custom-call(s32[6,4]{1,0:T(8,128)S(1)} %stack.26.slot_ref, bf16[13,48,1024]{2,1,0:T(8,128)(2,1)} %rest_0_.3, bf16[13,2,48,1024]{3,2,1,0:T(8,128)(2,1)} %tree_ref, f32[13,48,256]{2,1,0:T(8,128)S(1)} %pad.27.rest_2_, ...), custom_call_target="tpu_custom_call" | custom-call | flops 8099999744 | bytes 1000 | tf_op jit(solution)/shard_map/pallas_call | solution.py:177
  30.6 1.0 collective-permute-start.10
  31.7 1.1 collective-permute-start.11
  32.8 1.4 collective-permute-start.12
  35.0 4.4 %collective-permute-start.14 = (bf16[624,256]{1,0:T(8,128)(2,1)S(1)}, bf16[624,256]{1,0:T(8,128)(2,1)S(1)}, u32[]{:S(2)}, u32[]{:S(2)}) collective-permute-start(bf16[624,256]{1,0:T(8,128)(2,1)S(1)} %bitcast.34), channel_id=1, source_target_pairs={{0,1},{1,0},{2,3},{3,2},{4,5},{5,4},{6,7},{7,6},{8,9},{9,8},{10,11... | collective-permute-start | bytes 958472 | tf_op jit(solution)/shard_map/ppermute | solution.py:291
  39.5 1.8 %collective-permute-done.10.rest_7_ = bf16[2,2,160,256]{3,2,1,0:T(8,128)(2,1)S(1)} collective-permute-done((bf16[2,2,160,256]{3,2,1,0:T(8,128)(2,1)S(1)}, bf16[2,2,160,256]{3,2,1,0:T(8,128)(2,1)S(1)}, u32[]{:S(2)}, u32[]{:S(2)}) %collective-permute-start.10) | collective-permute-done | bytes 327712 | tf_op jit(solution)/shard_map/ppermute | solution.py:287
  41.2 5.9 %collective-permute-done.11.rest_8_ = bf16[2,2,160,256]{3,2,1,0:T(8,128)(2,1)S(1)} collective-permute-done((bf16[2,2,160,256]{3,2,1,0:T(8,128)(2,1)S(1)}, bf16[2,2,160,256]{3,2,1,0:T(8,128)(2,1)S(1)}, u32[]{:S(2)}, u32[]{:S(2)}) %collective-permute-start.11) | collective-permute-done | bytes 327712 | tf_op jit(solution)/shard_map/ppermute | solution.py:287
  47.1 1.6 %collective-permute-done.12.rest_9_ = bf16[2,2,160,256]{3,2,1,0:T(8,128)(2,1)S(1)} collective-permute-done((bf16[2,2,160,256]{3,2,1,0:T(8,128)(2,1)S(1)}, bf16[2,2,160,256]{3,2,1,0:T(8,128)(2,1)S(1)}, u32[]{:S(2)}, u32[]{:S(2)}) %collective-permute-start.12) | collective-permute-done | bytes 327712 | tf_op jit(solution)/shard_map/ppermute | solution.py:287
  48.7 5.9 %shard_map.123 = (bf16[13,48,256]{2,1,0:T(8,128)(2,1)S(1)}, bf16[13,48,256]{2,1,0:T(8,128)(2,1)S(1)}) custom-call(s32[6,4]{1,0:T(8,128)S(1)} %stack.26.slot_ref, bf16[13,48,1024]{2,1,0:T(8,128)(2,1)} %rest_0_.3, bf16[13,2,48,1024]{3,2,1,0:T(8,128)(2,1)} %tree_ref, f32[13,48,256]{2,1,0:T(8,128)S(1)} %pad.27.rest_2_, ...), custom_call_target="tpu_custom_call" | custom-call | flops 8099999744 | bytes 1000 | tf_op jit(solution)/shard_map/pallas_call | solution.py:177
  55.6 1.5 collective-permute-start.17
  57.2 1.2 collective-permute-start.18
  59.3 4.4 %collective-permute-start.20 = (bf16[624,512]{1,0:T(8,128)(2,1)S(1)}, bf16[624,512]{1,0:T(8,128)(2,1)S(1)}, u32[]{:S(2)}, u32[]{:S(2)}) collective-permute-start(bf16[624,512]{1,0:T(8,128)(2,1)S(1)} %get-tuple-element.68), channel_id=1, source_target_pairs={{0,1},{1,0},{2,3},{3,2},{4,5},{5,4},{6,7},{7,6},{8,9},{9,8},{10,11... | collective-permute-start | bytes 1916936 | tf_op jit(solution)/shard_map/ppermute | solution.py:291
  63.7 1.7 %collective-permute-done.16.rest_7_ = bf16[2,2,160,256]{3,2,1,0:T(8,128)(2,1)S(1)} collective-permute-done((bf16[2,2,160,256]{3,2,1,0:T(8,128)(2,1)S(1)}, bf16[2,2,160,256]{3,2,1,0:T(8,128)(2,1)S(1)}, u32[]{:S(2)}, u32[]{:S(2)}) %collective-permute-start.16) | collective-permute-done | bytes 327712 | tf_op jit(solution)/shard_map/ppermute | solution.py:287
  65.3 7.1 %collective-permute-done.17.rest_8_ = bf16[2,2,160,256]{3,2,1,0:T(8,128)(2,1)S(1)} collective-permute-done((bf16[2,2,160,256]{3,2,1,0:T(8,128)(2,1)S(1)}, bf16[2,2,160,256]{3,2,1,0:T(8,128)(2,1)S(1)}, u32[]{:S(2)}, u32[]{:S(2)}) %collective-permute-start.17) | collective-permute-done | bytes 327712 | tf_op jit(solution)/shard_map/ppermute | solution.py:287
  72.5 5.9 %shard_map.124 = (bf16[13,48,256]{2,1,0:T(8,128)(2,1)S(1)}, bf16[13,48,256]{2,1,0:T(8,128)(2,1)S(1)}) custom-call(s32[6,4]{1,0:T(8,128)S(1)} %stack.26.slot_ref, bf16[13,48,1024]{2,1,0:T(8,128)(2,1)} %rest_0_.3, bf16[13,2,48,1024]{3,2,1,0:T(8,128)(2,1)} %tree_ref, f32[13,48,256]{2,1,0:T(8,128)S(1)} %pad.27.rest_2_, ...), custom_call_target="tpu_custom_call" | custom-call | flops 8099999744 | bytes 1000 | tf_op jit(solution)/shard_map/pallas_call | solution.py:177
  78.5 1.3 collective-permute-start.22
  80.6 1.4 collective-permute-start.24
  82.3 1.6 %collective-permute-start.25 = (bf16[624,768]{1,0:T(8,128)(2,1)S(1)}, bf16[624,768]{1,0:T(8,128)(2,1)S(1)}, u32[]{:S(2)}, u32[]{:S(2)}) collective-permute-start(bf16[624,768]{1,0:T(8,128)(2,1)S(1)} %pad_maximum_fusion), channel_id=1, source_target_pairs={{0,1},{1,0},{2,3},{3,2},{4,5},{5,4},{6,7},{7,6},{8,9},{9,8},{10,11... | collective-permute-start | bytes 2875400 | tf_op jit(solution)/shard_map/ppermute | solution.py:291
  84.8 4.2 %collective-permute-done.22.rest_7_ = bf16[2,2,160,256]{3,2,1,0:T(8,128)(2,1)S(1)} collective-permute-done((bf16[2,2,160,256]{3,2,1,0:T(8,128)(2,1)S(1)}, bf16[2,2,160,256]{3,2,1,0:T(8,128)(2,1)S(1)}, u32[]{:S(2)}, u32[]{:S(2)}) %collective-permute-start.22) | collective-permute-done | bytes 327712 | tf_op jit(solution)/shard_map/ppermute | solution.py:287
  89.0 5.9 %collective-permute-done.23.rest_8_ = bf16[2,2,160,256]{3,2,1,0:T(8,128)(2,1)S(1)} collective-permute-done((bf16[2,2,160,256]{3,2,1,0:T(8,128)(2,1)S(1)}, bf16[2,2,160,256]{3,2,1,0:T(8,128)(2,1)S(1)}, u32[]{:S(2)}, u32[]{:S(2)}) %collective-permute-start.23) | collective-permute-done | bytes 327712 | tf_op jit(solution)/shard_map/ppermute | solution.py:287
  94.9 1.6 %collective-permute-done.24.rest_9_ = bf16[2,2,160,256]{3,2,1,0:T(8,128)(2,1)S(1)} collective-permute-done((bf16[2,2,160,256]{3,2,1,0:T(8,128)(2,1)S(1)}, bf16[2,2,160,256]{3,2,1,0:T(8,128)(2,1)S(1)}, u32[]{:S(2)}, u32[]{:S(2)}) %collective-permute-start.24) | collective-permute-done | bytes 327712 | tf_op jit(solution)/shard_map/ppermute | solution.py:287
  96.6 5.9 %shard_map.125 = (bf16[13,48,256]{2,1,0:T(8,128)(2,1)S(1)}, bf16[13,48,256]{2,1,0:T(8,128)(2,1)S(1)}) custom-call(s32[6,4]{1,0:T(8,128)S(1)} %stack.26.slot_ref, bf16[13,48,1024]{2,1,0:T(8,128)(2,1)} %rest_0_.3, bf16[13,2,48,1024]{3,2,1,0:T(8,128)(2,1)} %tree_ref, f32[13,48,256]{2,1,0:T(8,128)S(1)} %pad.27.rest_2_, ...), custom_call_target="tpu_custom_call" | custom-call | flops 8099999744 | bytes 1000 | tf_op jit(solution)/shard_map/pallas_call | solution.py:177
  102.6 1.6 %collective-permute-done.27 = bf16[13,48,256]{2,1,0:T(8,128)(2,1)S(1)} collective-permute-done((bf16[13,48,256]{2,1,0:T(8,128)(2,1)S(1)}, bf16[13,48,256]{2,1,0:T(8,128)(2,1)S(1)}, u32[]{:S(2)}, u32[]{:S(2)}) %collective-permute-start.27) | collective-permute-done | bytes 319520 | tf_op jit(solution)/shard_map/ppermute | solution.py:287
  104.3 1.0 pad_maximum_fusion.1
  105.3 1.6 %collective-permute-start.28 = (bf16[624,768]{1,0:T(8,128)(2,1)}, bf16[624,768]{1,0:T(8,128)(2,1)}, u32[]{:S(2)}, u32[]{:S(2)}) collective-permute-start(bf16[624,768]{1,0:T(8,128)(2,1)} %pad_maximum_fusion.1), channel_id=1, source_target_pairs={{0,1},{1,0},{2,3},{3,2},{4,5},{5,4},{6,7},{7,6},{8,9},{9,8},{10,11... | collective-permute-start | bytes 2875400 | tf_op jit(solution)/shard_map/ppermute | solution.py:291
  108.7 1.5 collective-permute-start.29
  110.2 3.4 %copy-done = bf16[4096,1024]{1,0:T(8,128)(2,1)S(1)} copy-done((bf16[4096,1024]{1,0:T(8,128)(2,1)S(1)}, bf16[4096,1024]{1,0:T(8,128)(2,1)}, u32[]{:S(2)}) %copy-start) | copy-done | bytes 8388632
  113.6 1.1 copy-done.3
  114.7 1.2 copy-done.7
  115.9 1.1 copy-done.9
  119.9 3.9 %shard_map.126.rest_0_ = f32[624,1024]{1,0:T(8,128)S(1)} custom-call(s32[1]{0:T(128)} %bitcast.z_ref, bf16[4,1024,1024]{2,1,0:T(8,128)(2,1)S(1)} %bitcast.22, bf16[624,256]{1,0:T(8,128)(2,1)S(1)} %bitcast.35, bf16[624,256]{1,0:T(8,128)(2,1)S(1)} %copy-done.15, bf16[624,256]{1,0:T(8,128)(2,1)S(1)} %bitcast.32, bf16[624,512]{1,0:T(8,128)(2,1)S(1)} %copy-done.9, ...), custom_call_target="tpu_custom_call" | custom-call | flops 2000000000 | bytes 1000 | tf_op jit(solution)/shard_map/pallas_call | solution.py:240
  123.7 1.3 collective-permute-start.30
  125.0 3.8 %collective-permute-done.28.rest_2_ = bf16[624,768]{1,0:T(8,128)(2,1)} collective-permute-done((bf16[624,768]{1,0:T(8,128)(2,1)}, bf16[624,768]{1,0:T(8,128)(2,1)}, u32[]{:S(2)}, u32[]{:S(2)}) %collective-permute-start.28) | collective-permute-done | bytes 958496 | tf_op jit(solution)/shard_map/ppermute | solution.py:291
  128.9 1.0 slice.50
  130.8 1.4 collective-permute-start.32
  132.2 3.0 %shard_map.129 = bf16[13,2,8,1024]{3,2,1,0:T(8,128)(2,1)} custom-call(bf16[13,16,48]{2,1,0:T(8,128)(2,1)S(1)} %pad_convert_fusion.pick_ref, bf16[13,2,48,1024]{3,2,1,0:T(8,128)(2,1)} %tree_ref), custom_call_target="tpu_custom_call" | custom-call | flops 2000000000 | bytes 1000 | tf_op jit(solution)/shard_map/pallas_call | solution.py:269
  135.2 3.4 %copy-done.1 = bf16[4096,1024]{1,0:T(8,128)(2,1)S(1)} copy-done((bf16[4096,1024]{1,0:T(8,128)(2,1)S(1)}, bf16[4096,1024]{1,0:T(8,128)(2,1)}, u32[]{:S(2)}) %copy-start.1) | copy-done | bytes 8388632
  138.5 3.2 %shard_map.127.rest_0_ = f32[624,1024]{1,0:T(8,128)S(1)} custom-call(s32[1]{0:T(128)} %bitcast.z_ref, bf16[4,1024,1024]{2,1,0:T(8,128)(2,1)S(1)} %bitcast.23, f32[624,1024]{1,0:T(8,128)S(1)} %shard_map.126.rest_0_, bf16[624,256]{1,0:T(8,128)(2,1)S(1)} %bitcast.30, bf16[624,768]{1,0:T(8,128)(2,1)} %collective-permute-done.28.rest_2_, ...), custom_call_target="tpu_custom_call", output_to_operand_aliasing={{}: (2, {})} | custom-call | flops 2000000000 | bytes 1000 | tf_op jit(solution)/shard_map/pallas_call | solution.py:240
  141.7 3.2 %collective-permute-done.30.rest_1_ = bf16[624,512]{1,0:T(8,128)(2,1)} collective-permute-done((bf16[624,512]{1,0:T(8,128)(2,1)}, bf16[624,512]{1,0:T(8,128)(2,1)}, u32[]{:S(2)}, u32[]{:S(2)}) %collective-permute-start.30) | collective-permute-done | bytes 639008 | tf_op jit(solution)/shard_map/ppermute | solution.py:291
  144.9 5.8 %collective-permute-done.32.rest_3_ = bf16[624,256]{1,0:T(8,128)(2,1)S(1)} collective-permute-done((bf16[624,256]{1,0:T(8,128)(2,1)S(1)}, bf16[624,256]{1,0:T(8,128)(2,1)S(1)}, u32[]{:S(2)}, u32[]{:S(2)}) %collective-permute-start.32) | collective-permute-done | bytes 319520 | tf_op jit(solution)/shard_map/ppermute | solution.py:291
  150.7 3.7 %shard_map.128 = bf16[624,1024]{1,0:T(8,128)(2,1)} custom-call(s32[1]{0:T(128)} %bitcast.z_ref, bf16[4,1024,1024]{2,1,0:T(8,128)(2,1)S(1)} %bitcast.24, f32[624,1024]{1,0:T(8,128)S(1)} %shard_map.127.rest_0_, bf16[624,512]{1,0:T(8,128)(2,1)} %collective-permute-done.30.rest_1_, bf16[624,512]{1,0:T(8,128)(2,1)} %collective-permute-done.29.rest_2_, ...), custom_call_target="tpu_custom_call" | custom-call | flops 2000000000 | bytes 1000 | tf_op jit(solution)/shard_map/pallas_call | solution.py:240
  (94 shorter events, 13.4 us)
Async XLA Ops:
  0.6 3.2 %collective-permute-start.1 = (bf16[1,2,152,1024]{3,2,1,0:T(8,128)(2,1)}, bf16[1,2,152,1024]{3,2,1,0:T(8,128)(2,1)S(1)}, u32[]{:S(2)}, u32[]{:S(2)}) collective-permute-start(bf16[1,2,152,1024]{3,2,1,0:T(8,128)(2,1)} %param.18), channel_id=1, source_target_pairs={{0,4},{4,0},{8,12},{12,8},{16,20},{20,16},{24,28},{28,24},{1,5},{5... | collective-permute-start | bytes 1867784 | tf_op jit(solution)/shard_map/ppermute | solution.py:287
  1.1 1.9 %collective-permute-start = (s32[1]{0:T(128)}, s32[1]{0:T(128)}, u32[]{:S(2)}, u32[]{:S(2)}) collective-permute-start(s32[1]{0:T(128)} %param.19), channel_id=1, source_target_pairs={{0,4},{4,0},{8,12},{12,8},{16,20},{20,16},{24,28},{28,24},{1,5},{5... | collective-permute-start | bytes 20 | tf_op jit(solution)/shard_map/ppermute | solution.py:287
  3.9 12.2 %copy-start.18 = (s32[13,1]{0,1:T(1,128)S(1)}, s32[13,1]{0,1:T(1,128)}, u32[]{:S(2)}) copy-start(s32[13,1]{0,1:T(1,128)} %param.14) | copy-start | bytes 160
  3.9 12.2 %copy-start.16 = (s32[13,48,48]{2,1,0:T(8,128)S(1)}, s32[13,48,48]{2,1,0:T(8,128)}, u32[]{:S(2)}) copy-start(s32[13,48,48]{2,1,0:T(8,128)} %param.13) | copy-start | bytes 359428
  4.5 20.2 %collective-permute-start.5 = (bf16[13,2,48,1024]{3,2,1,0:T(8,128)(2,1)}, bf16[13,2,48,1024]{3,2,1,0:T(8,128)(2,1)}, u32[]{:S(2)}, u32[]{:S(2)}) collective-permute-start(bf16[13,2,48,1024]{3,2,1,0:T(8,128)(2,1)} %tree_ref), channel_id=1, source_target_pairs={{0,4},{4,0},{8,12},{12,8},{16,20},{20,16},{24,28},{28,24},{1,5},{5... | collective-permute-start | bytes 7667720 | tf_op jit(solution)/shard_map/ppermute | solution.py:287
  5.0 11.1 %collective-permute-start.2 = (bf16[2,2,160,256]{3,2,1,0:T(8,128)(2,1)S(1)}, bf16[2,2,160,256]{3,2,1,0:T(8,128)(2,1)S(1)}, u32[]{:S(2)}, u32[]{:S(2)}) collective-permute-start(bf16[2,2,160,256]{3,2,1,0:T(8,128)(2,1)S(1)} %get-tuple-element.73.rest_6_), channel_id=1, source_target_pairs={{0,8},{4,12},{8,0},{12,4},{16,24},{20,28},{24,16},{28,20},{1,9},{5... | collective-permute-start | bytes 983048 | tf_op jit(solution)/shard_map/ppermute | solution.py:287
  7.5 17.2 %collective-permute-start.4 = (bf16[13,48,1024]{2,1,0:T(8,128)(2,1)}, bf16[13,48,1024]{2,1,0:T(8,128)(2,1)}, u32[]{:S(2)}, u32[]{:S(2)}) collective-permute-start(bf16[13,48,1024]{2,1,0:T(8,128)(2,1)} %rest_0_.3), channel_id=1, source_target_pairs={{0,4},{4,0},{8,12},{12,8},{16,20},{20,16},{24,28},{28,24},{1,5},{5... | collective-permute-start | bytes 3833864 | tf_op jit(solution)/shard_map/ppermute | solution.py:287
  7.7 17.0 %collective-permute-start.7 = (bf16[2,2,160,256]{3,2,1,0:T(8,128)(2,1)S(1)}, bf16[2,2,160,256]{3,2,1,0:T(8,128)(2,1)S(1)}, u32[]{:S(2)}, u32[]{:S(2)}) collective-permute-start(bf16[2,2,160,256]{3,2,1,0:T(8,128)(2,1)S(1)} %get-tuple-element.73.rest_6_), channel_id=1, source_target_pairs={{0,16},{4,20},{8,24},{12,28},{16,0},{20,4},{24,8},{28,12},{1,17},{... | collective-permute-start | bytes 983048 | tf_op jit(solution)/shard_map/ppermute | solution.py:287
  9.2 15.5 %collective-permute-start.8 = (bf16[2,2,160,256]{3,2,1,0:T(8,128)(2,1)S(1)}, bf16[2,2,160,256]{3,2,1,0:T(8,128)(2,1)}, u32[]{:S(2)}, u32[]{:S(2)}) collective-permute-start(bf16[2,2,160,256]{3,2,1,0:T(8,128)(2,1)S(1)} %get-tuple-element.73.rest_6_), channel_id=1, source_target_pairs={{0,24},{4,28},{8,16},{12,20},{16,8},{20,12},{24,0},{28,4},{1,25},{... | collective-permute-start | bytes 983048 | tf_op jit(solution)/shard_map/ppermute | solution.py:287
  16.1 1.1 collective-permute-start.3
  17.2 1.6 %collective-permute-start.6 = (s32[13,48,48]{2,1,0:T(8,128)S(1)}, s32[13,48,48]{2,1,0:T(8,128)S(1)}, u32[]{:S(2)}, u32[]{:S(2)}) collective-permute-start(s32[13,48,48]{2,1,0:T(8,128)S(1)} %copy-done.16), channel_id=1, source_target_pairs={{0,4},{4,0},{8,12},{12,8},{16,20},{20,16},{24,28},{28,24},{1,5},{5... | collective-permute-start | bytes 359432 | tf_op jit(solution)/shard_map/ppermute | solution.py:287
  30.6 3.6 %collective-permute-start.9 = (bf16[13,48,256]{2,1,0:T(8,128)(2,1)S(1)}, bf16[13,48,256]{2,1,0:T(8,128)(2,1)S(1)}, u32[]{:S(2)}, u32[]{:S(2)}) collective-permute-start(bf16[13,48,256]{2,1,0:T(8,128)(2,1)S(1)} %get-tuple-element.33), channel_id=1, source_target_pairs={{0,4},{4,0},{8,12},{12,8},{16,20},{20,16},{24,28},{28,24},{1,5},{5... | collective-permute-start | bytes 958472 | tf_op jit(solution)/shard_map/ppermute | solution.py:287
  30.6 10.6 %collective-permute-start.10 = (bf16[2,2,160,256]{3,2,1,0:T(8,128)(2,1)S(1)}, bf16[2,2,160,256]{3,2,1,0:T(8,128)(2,1)S(1)}, u32[]{:S(2)}, u32[]{:S(2)}) collective-permute-start(bf16[2,2,160,256]{3,2,1,0:T(8,128)(2,1)S(1)} %get-tuple-element.35.rest_6_), channel_id=1, source_target_pairs={{0,8},{4,12},{8,0},{12,4},{16,24},{20,28},{24,16},{28,20},{1,9},{5... | collective-permute-start | bytes 983048 | tf_op jit(solution)/shard_map/ppermute | solution.py:287
  31.7 15.4 %collective-permute-start.11 = (bf16[2,2,160,256]{3,2,1,0:T(8,128)(2,1)S(1)}, bf16[2,2,160,256]{3,2,1,0:T(8,128)(2,1)S(1)}, u32[]{:S(2)}, u32[]{:S(2)}) collective-permute-start(bf16[2,2,160,256]{3,2,1,0:T(8,128)(2,1)S(1)} %get-tuple-element.35.rest_6_), channel_id=1, source_target_pairs={{0,16},{4,20},{8,24},{12,28},{16,0},{20,4},{24,8},{28,12},{1,17},{... | collective-permute-start | bytes 983048 | tf_op jit(solution)/shard_map/ppermute | solution.py:287
  32.8 16.0 %collective-permute-start.12 = (bf16[2,2,160,256]{3,2,1,0:T(8,128)(2,1)S(1)}, bf16[2,2,160,256]{3,2,1,0:T(8,128)(2,1)S(1)}, u32[]{:S(2)}, u32[]{:S(2)}) collective-permute-start(bf16[2,2,160,256]{3,2,1,0:T(8,128)(2,1)S(1)} %get-tuple-element.35.rest_6_), channel_id=1, source_target_pairs={{0,24},{4,28},{8,16},{12,20},{16,8},{20,12},{24,0},{28,4},{1,25},{... | collective-permute-start | bytes 983048 | tf_op jit(solution)/shard_map/ppermute | solution.py:287
  34.3 20.3 %copy-start.10 = (bf16[13,48,256]{2,1,0:T(8,128)(2,1)}, bf16[13,48,256]{2,1,0:T(8,128)(2,1)S(1)}, u32[]{:S(2)}) copy-start(bf16[13,48,256]{2,1,0:T(8,128)(2,1)S(1)} %broadcast_select_fusion.3) | copy-start | bytes 958468
  34.3 20.3 %collective-permute-start.13 = (bf16[624,256]{1,0:T(8,128)(2,1)S(1)}, bf16[624,256]{1,0:T(8,128)(2,1)S(1)}, u32[]{:S(2)}, u32[]{:S(2)}) collective-permute-start(bf16[624,256]{1,0:T(8,128)(2,1)S(1)} %bitcast.33), channel_id=1, source_target_pairs={{1,2},{2,1},{5,6},{6,5},{9,10},{10,9},{13,14},{14,13},{17,18},{18,... | collective-permute-start | bytes 958472 | tf_op jit(solution)/shard_map/ppermute | solution.py:291
  35.0 19.7 %collective-permute-start.14 = (bf16[624,256]{1,0:T(8,128)(2,1)S(1)}, bf16[624,256]{1,0:T(8,128)(2,1)S(1)}, u32[]{:S(2)}, u32[]{:S(2)}) collective-permute-start(bf16[624,256]{1,0:T(8,128)(2,1)S(1)} %bitcast.34), channel_id=1, source_target_pairs={{0,1},{1,0},{2,3},{3,2},{4,5},{5,4},{6,7},{7,6},{8,9},{9,8},{10,11... | collective-permute-start | bytes 958472 | tf_op jit(solution)/shard_map/ppermute | solution.py:291
  54.7 3.9 %copy-start.12 = (bf16[624,256]{1,0:T(8,128)(2,1)}, bf16[624,256]{1,0:T(8,128)(2,1)S(1)}, u32[]{:S(2)}) copy-start(bf16[624,256]{1,0:T(8,128)(2,1)S(1)} %collective-permute-done.13.rest_4_) | copy-start | bytes 958468
  54.7 3.9 %copy-start.14 = (bf16[624,256]{1,0:T(8,128)(2,1)}, bf16[624,256]{1,0:T(8,128)(2,1)S(1)}, u32[]{:S(2)}) copy-start(bf16[624,256]{1,0:T(8,128)(2,1)S(1)} %collective-permute-done.14.rest_1_) | copy-start | bytes 958468
  54.7 3.6 %collective-permute-start.15 = (bf16[13,48,256]{2,1,0:T(8,128)(2,1)S(1)}, bf16[13,48,256]{2,1,0:T(8,128)(2,1)S(1)}, u32[]{:S(2)}, u32[]{:S(2)}) collective-permute-start(bf16[13,48,256]{2,1,0:T(8,128)(2,1)S(1)} %get-tuple-element.39), channel_id=1, source_target_pairs={{0,4},{4,0},{8,12},{12,8},{16,20},{20,16},{24,28},{28,24},{1,5},{5... | collective-permute-start | bytes 958472 | tf_op jit(solution)/shard_map/ppermute | solution.py:287
  54.8 10.6 %collective-permute-start.16 = (bf16[2,2,160,256]{3,2,1,0:T(8,128)(2,1)S(1)}, bf16[2,2,160,256]{3,2,1,0:T(8,128)(2,1)S(1)}, u32[]{:S(2)}, u32[]{:S(2)}) collective-permute-start(bf16[2,2,160,256]{3,2,1,0:T(8,128)(2,1)S(1)} %get-tuple-element.41.rest_6_), channel_id=1, source_target_pairs={{0,8},{4,12},{8,0},{12,4},{16,24},{20,28},{24,16},{28,20},{1,9},{5... | collective-permute-start | bytes 983048 | tf_op jit(solution)/shard_map/ppermute | solution.py:287
  55.6 16.8 %collective-permute-start.17 = (bf16[2,2,160,256]{3,2,1,0:T(8,128)(2,1)S(1)}, bf16[2,2,160,256]{3,2,1,0:T(8,128)(2,1)S(1)}, u32[]{:S(2)}, u32[]{:S(2)}) collective-permute-start(bf16[2,2,160,256]{3,2,1,0:T(8,128)(2,1)S(1)} %get-tuple-element.41.rest_6_), channel_id=1, source_target_pairs={{0,16},{4,20},{8,24},{12,28},{16,0},{20,4},{24,8},{28,12},{1,17},{... | collective-permute-start | bytes 983048 | tf_op jit(solution)/shard_map/ppermute | solution.py:287
  57.2 15.3 %collective-permute-start.18 = (bf16[2,2,160,256]{3,2,1,0:T(8,128)(2,1)S(1)}, bf16[2,2,160,256]{3,2,1,0:T(8,128)(2,1)S(1)}, u32[]{:S(2)}, u32[]{:S(2)}) collective-permute-start(bf16[2,2,160,256]{3,2,1,0:T(8,128)(2,1)S(1)} %get-tuple-element.41.rest_6_), channel_id=1, source_target_pairs={{0,24},{4,28},{8,16},{12,20},{16,8},{20,12},{24,0},{28,4},{1,25},{... | collective-permute-start | bytes 983048 | tf_op jit(solution)/shard_map/ppermute | solution.py:287
  58.5 19.8 %collective-permute-start.19 = (bf16[624,512]{1,0:T(8,128)(2,1)S(1)}, bf16[624,512]{1,0:T(8,128)(2,1)S(1)}, u32[]{:S(2)}, u32[]{:S(2)}) collective-permute-start(bf16[624,512]{1,0:T(8,128)(2,1)S(1)} %get-tuple-element.69), channel_id=1, source_target_pairs={{1,2},{2,1},{5,6},{6,5},{9,10},{10,9},{13,14},{14,13},{17,18},{18,... | collective-permute-start | bytes 1916936 | tf_op jit(solution)/shard_map/ppermute | solution.py:291
  59.3 19.1 %collective-permute-start.20 = (bf16[624,512]{1,0:T(8,128)(2,1)S(1)}, bf16[624,512]{1,0:T(8,128)(2,1)S(1)}, u32[]{:S(2)}, u32[]{:S(2)}) collective-permute-start(bf16[624,512]{1,0:T(8,128)(2,1)S(1)} %get-tuple-element.68), channel_id=1, source_target_pairs={{0,1},{1,0},{2,3},{3,2},{4,5},{5,4},{6,7},{7,6},{8,9},{9,8},{10,11... | collective-permute-start | bytes 1916936 | tf_op jit(solution)/shard_map/ppermute | solution.py:291
  78.4 3.9 %copy-start.2 = (bf16[624,512]{1,0:T(8,128)(2,1)}, bf16[624,512]{1,0:T(8,128)(2,1)S(1)}, u32[]{:S(2)}) copy-start(bf16[624,512]{1,0:T(8,128)(2,1)S(1)} %collective-permute-done.19.rest_7_) | copy-start | bytes 1916932
  78.4 3.8 %copy-start.8 = (bf16[624,512]{1,0:T(8,128)(2,1)}, bf16[624,512]{1,0:T(8,128)(2,1)S(1)}, u32[]{:S(2)}) copy-start(bf16[624,512]{1,0:T(8,128)(2,1)S(1)} %collective-permute-done.20.rest_3_) | copy-start | bytes 1916932
  78.4 3.7 %collective-permute-start.21 = (bf16[13,48,256]{2,1,0:T(8,128)(2,1)S(1)}, bf16[13,48,256]{2,1,0:T(8,128)(2,1)S(1)}, u32[]{:S(2)}, u32[]{:S(2)}) collective-permute-start(bf16[13,48,256]{2,1,0:T(8,128)(2,1)S(1)} %get-tuple-element.45), channel_id=1, source_target_pairs={{0,4},{4,0},{8,12},{12,8},{16,20},{20,16},{24,28},{28,24},{1,5},{5... | collective-permute-start | bytes 958472 | tf_op jit(solution)/shard_map/ppermute | solution.py:287
  78.5 10.6 %collective-permute-start.22 = (bf16[2,2,160,256]{3,2,1,0:T(8,128)(2,1)S(1)}, bf16[2,2,160,256]{3,2,1,0:T(8,128)(2,1)S(1)}, u32[]{:S(2)}, u32[]{:S(2)}) collective-permute-start(bf16[2,2,160,256]{3,2,1,0:T(8,128)(2,1)S(1)} %get-tuple-element.47.rest_6_), channel_id=1, source_target_pairs={{0,8},{4,12},{8,0},{12,4},{16,24},{20,28},{24,16},{28,20},{1,9},{5... | collective-permute-start | bytes 983048 | tf_op jit(solution)/shard_map/ppermute | solution.py:287
  79.8 15.2 %collective-permute-start.23 = (bf16[2,2,160,256]{3,2,1,0:T(8,128)(2,1)S(1)}, bf16[2,2,160,256]{3,2,1,0:T(8,128)(2,1)S(1)}, u32[]{:S(2)}, u32[]{:S(2)}) collective-permute-start(bf16[2,2,160,256]{3,2,1,0:T(8,128)(2,1)S(1)} %get-tuple-element.47.rest_6_), channel_id=1, source_target_pairs={{0,16},{4,20},{8,24},{12,28},{16,0},{20,4},{24,8},{28,12},{1,17},{... | collective-permute-start | bytes 983048 | tf_op jit(solution)/shard_map/ppermute | solution.py:287
  80.6 16.0 %collective-permute-start.24 = (bf16[2,2,160,256]{3,2,1,0:T(8,128)(2,1)S(1)}, bf16[2,2,160,256]{3,2,1,0:T(8,128)(2,1)S(1)}, u32[]{:S(2)}, u32[]{:S(2)}) collective-permute-start(bf16[2,2,160,256]{3,2,1,0:T(8,128)(2,1)S(1)} %get-tuple-element.47.rest_6_), channel_id=1, source_target_pairs={{0,24},{4,28},{8,16},{12,20},{16,8},{20,12},{24,0},{28,4},{1,25},{... | collective-permute-start | bytes 983048 | tf_op jit(solution)/shard_map/ppermute | solution.py:287
  82.3 24.6 %collective-permute-start.25 = (bf16[624,768]{1,0:T(8,128)(2,1)S(1)}, bf16[624,768]{1,0:T(8,128)(2,1)S(1)}, u32[]{:S(2)}, u32[]{:S(2)}) collective-permute-start(bf16[624,768]{1,0:T(8,128)(2,1)S(1)} %pad_maximum_fusion), channel_id=1, source_target_pairs={{0,1},{1,0},{2,3},{3,2},{4,5},{5,4},{6,7},{7,6},{8,9},{9,8},{10,11... | collective-permute-start | bytes 2875400 | tf_op jit(solution)/shard_map/ppermute | solution.py:291
  83.9 18.5 %collective-permute-start.26 = (bf16[624,512]{1,0:T(8,128)(2,1)S(1)}, bf16[624,512]{1,0:T(8,128)(2,1)S(1)}, u32[]{:S(2)}, u32[]{:S(2)}) collective-permute-start(bf16[624,512]{1,0:T(8,128)(2,1)S(1)} %pad_maximum_fusion.4), channel_id=1, source_target_pairs={{1,2},{2,1},{5,6},{6,5},{9,10},{10,9},{13,14},{14,13},{17,18},{18,... | collective-permute-start | bytes 1916936 | tf_op jit(solution)/shard_map/ppermute | solution.py:291
  102.5 2.8 %copy-start.4 = (bf16[624,512]{1,0:T(8,128)(2,1)}, bf16[624,512]{1,0:T(8,128)(2,1)S(1)}, u32[]{:S(2)}) copy-start(bf16[624,512]{1,0:T(8,128)(2,1)S(1)} %collective-permute-done.26.rest_3_) | copy-start | bytes 1916932
  102.5 1.7 %collective-permute-start.27 = (bf16[13,48,256]{2,1,0:T(8,128)(2,1)S(1)}, bf16[13,48,256]{2,1,0:T(8,128)(2,1)S(1)}, u32[]{:S(2)}, u32[]{:S(2)}) collective-permute-start(bf16[13,48,256]{2,1,0:T(8,128)(2,1)S(1)} %get-tuple-element.52), channel_id=1, source_target_pairs={{0,4},{4,0},{8,12},{12,8},{16,20},{20,16},{24,28},{28,24},{1,5},{5... | collective-permute-start | bytes 958472 | tf_op jit(solution)/shard_map/ppermute | solution.py:287
  105.3 23.6 %collective-permute-start.28 = (bf16[624,768]{1,0:T(8,128)(2,1)}, bf16[624,768]{1,0:T(8,128)(2,1)}, u32[]{:S(2)}, u32[]{:S(2)}) collective-permute-start(bf16[624,768]{1,0:T(8,128)(2,1)} %pad_maximum_fusion.1), channel_id=1, source_target_pairs={{0,1},{1,0},{2,3},{3,2},{4,5},{5,4},{6,7},{7,6},{8,9},{9,8},{10,11... | collective-permute-start | bytes 2875400 | tf_op jit(solution)/shard_map/ppermute | solution.py:291
  108.7 15.0 %collective-permute-start.29 = (bf16[624,512]{1,0:T(8,128)(2,1)}, bf16[624,512]{1,0:T(8,128)(2,1)}, u32[]{:S(2)}, u32[]{:S(2)}) collective-permute-start(bf16[624,512]{1,0:T(8,128)(2,1)} %pad_maximum_fusion.5), channel_id=1, source_target_pairs={{1,2},{2,1},{5,6},{6,5},{9,10},{10,9},{13,14},{14,13},{17,18},{18,... | collective-permute-start | bytes 1916936 | tf_op jit(solution)/shard_map/ppermute | solution.py:291
  110.2 3.4 %copy-start = (bf16[4096,1024]{1,0:T(8,128)(2,1)S(1)}, bf16[4096,1024]{1,0:T(8,128)(2,1)}, u32[]{:S(2)}) copy-start(bf16[4096,1024]{1,0:T(8,128)(2,1)} %param.20) | copy-start | bytes 25165828
  113.6 1.1 copy-start.3
  114.7 1.2 copy-start.7
  115.9 1.1 copy-start.9
  119.9 10.7 %copy-start.17 = (s32[13,8]{0,1:T(8,128)S(1)}, s32[13,8]{0,1:T(8,128)}, u32[]{:S(2)}) copy-start(s32[13,8]{0,1:T(8,128)} %param.15) | copy-start | bytes 1252
  123.7 21.2 %collective-permute-start.30 = (bf16[624,512]{1,0:T(8,128)(2,1)}, bf16[624,512]{1,0:T(8,128)(2,1)}, u32[]{:S(2)}, u32[]{:S(2)}) collective-permute-start(bf16[624,512]{1,0:T(8,128)(2,1)} %collective-permute-done.29.rest_2_), channel_id=1, source_target_pairs={{1,0},{2,3},{5,4},{6,7},{9,8},{10,11},{13,12},{14,15},{17,16},{18,... | collective-permute-start | bytes 1916936 | tf_op jit(solution)/shard_map/ppermute | solution.py:291
  129.9 0.9 collective-permute-start.31
  130.8 4.4 %copy-start.5 = (bf16[624,512]{1,0:T(8,128)(2,1)S(1)}, bf16[624,512]{1,0:T(8,128)(2,1)}, u32[]{:S(2)}) copy-start(bf16[624,512]{1,0:T(8,128)(2,1)} %copy-done.4) | copy-start | bytes 1916932
  130.8 19.9 %collective-permute-start.32 = (bf16[624,256]{1,0:T(8,128)(2,1)S(1)}, bf16[624,256]{1,0:T(8,128)(2,1)S(1)}, u32[]{:S(2)}, u32[]{:S(2)}) collective-permute-start(bf16[624,256]{1,0:T(8,128)(2,1)S(1)} %collective-permute-done.31.rest_4_), channel_id=1, source_target_pairs={{1,0},{2,3},{5,4},{6,7},{9,8},{10,11},{13,12},{14,15},{17,16},{18,... | collective-permute-start | bytes 958472 | tf_op jit(solution)/shard_map/ppermute | solution.py:291
  135.2 3.4 %copy-start.1 = (bf16[4096,1024]{1,0:T(8,128)(2,1)S(1)}, bf16[4096,1024]{1,0:T(8,128)(2,1)}, u32[]{:S(2)}) copy-start(bf16[4096,1024]{1,0:T(8,128)(2,1)} %param.20) | copy-start | bytes 25165828
  (4 other events, 3.8 us)
